TPU v7x, 128 devices: a whole 4x4x4 slice. The times are simulated.
128 devices in a mesh: gx: 4 (over x), gy: 4 (over y), gz: 8 (over z, core).
Axes of the slice: x: 4, y: 4, z: 4, core: 2. Of those that a mesh axis runs over, the one named last changes fastest.
Arguments:
- latent: bfloat16 [4, 4, 8, 1024, 128], P('gx', 'gy', 'gz'), may hold values from -6 to 6
- destination: int32 [4, 4, 8, 1024, 1], P('gx', 'gy', 'gz'), may hold values from 0 to 127, as said below
- neighbours: int32 [4, 4, 8, 3456, 24], P('gx', 'gy', 'gz'), may hold values from 0 to 5247
- valid: int32 [4, 4, 8, 3456, 24], P('gx', 'gy', 'gz'), may hold values 0 or 1
- ghost_index: int32 [4, 4, 8, 8, 32], P('gx', 'gy', 'gz'), may hold values from 0 to 3455
- edge_first: bfloat16 [2, 256, 128], replicated, may hold values from -0.375 to 0.375
- edge_second: bfloat16 [2, 128, 128], replicated, may hold values from -0.5 to 0.5
- edge_third: bfloat16 [2, 128, 128], replicated, may hold values from -0.25 to 0.25
- node_first: bfloat16 [2, 256, 128], replicated, may hold values from -0.375 to 0.375
- node_second: bfloat16 [2, 128, 128], replicated, may hold values from -0.5 to 0.5
- node_third: bfloat16 [2, 128, 128], replicated, may hold values from -0.5 to 0.5
Outputs:
- settled: bfloat16 [4, 4, 8, 3456, 128], P('gx', 'gy', 'gz')
Inputs may be any that keep to these rules, and one draw needn't show every extreme that they name: Each particle's destination is its own bin or one of the bins beside it, diagonals included; at most 128 particles of one bin have one destination, and exactly 128 of every bin stay in it. `neighbours`: rows below 3456 are the bin's own slots, the others its ghosts.
All inputs are finite; a program needn't handle non-finite values. No bound on the sum of `valid` on one device may be relied on, other than what follows from the above.
Results may differ from a plain program's by a relative error of at most 0.011.
Values may be sent and summed in bfloat16 or wider, within the bound.
No kernel may reach another device: no remote copies, remote signals or barrier semaphores. Data moves between devices by JAX's collectives and lax.ppermute only.
A program may use at most 64 MiB of HBM per device.

v0:
```python
import jax
import jax.numpy as jnp
import numpy as np
from jax import lax
from jax.sharding import PartitionSpec as P

outer_slabs = np.array(
    [p for p in range(64) if p // 16 in (0, 3) or p // 4 % 4 in (0, 3) or p % 4 in (0, 3)],
    dtype=np.int32,
)


def with_halo(block, sides, width):
    for axis, dim in sides:
        count = lax.axis_size(axis)
        forward = [(i, i + 1) for i in range(count - 1)]
        backward = [(target, source) for source, target in forward]
        low = lax.ppermute(
            lax.slice_in_dim(block, block.shape[dim] - width, None, axis=dim), axis, forward
        )
        high = lax.ppermute(lax.slice_in_dim(block, 0, width, axis=dim), axis, backward)
        block = jnp.concatenate([low, block, high], axis=dim)
    return block


def layer_norm(values):
    mean = jnp.mean(values, axis=1, keepdims=True)
    centred = values - mean
    var = jnp.mean(centred * centred, axis=1, keepdims=True)
    return centred / jnp.sqrt(var + 1e-05)


def message_pass(state, ghosts, nbr_rows, valid_rows, live_rows, weights):
    efirst, esecond, ethird, nfirst, nsecond, nthird = weights
    width = state.shape[1]
    rows = state.shape[0]
    degree = nbr_rows.shape[1]
    table = jnp.concatenate([state, ghosts], axis=0)
    sender_weight = efirst[width:]
    recv_part = jnp.dot(state, efirst[:width], preferred_element_type=jnp.float32)
    blocks = 27

    def edge_block(pieces):
        recv, nbr, mask = pieces
        fetched = jnp.take(table, nbr.reshape(-1), axis=0)
        sender = jnp.dot(fetched, sender_weight, preferred_element_type=jnp.float32).reshape(
            -1, degree, width
        )
        hidden = jnp.maximum(recv[:, None, :] + sender, 0.0)
        hidden = hidden.astype(jnp.bfloat16).reshape(-1, width)
        hidden = jnp.maximum(
            jnp.dot(hidden, esecond, preferred_element_type=jnp.float32), 0.0
        ).astype(jnp.bfloat16)
        message = jnp.dot(hidden, ethird, preferred_element_type=jnp.float32).reshape(
            -1, degree, width
        )
        return jnp.sum(message * mask[:, :, None], axis=1)

    aggregate = lax.map(
        edge_block,
        (
            recv_part.reshape(blocks, -1, width),
            nbr_rows.reshape(blocks, -1, degree),
            valid_rows.astype(jnp.float32).reshape(blocks, -1, degree),
        ),
    )
    aggregate = aggregate.reshape(rows, width).astype(jnp.bfloat16)
    hidden = jnp.dot(state, nfirst[:width], preferred_element_type=jnp.float32) + jnp.dot(
        aggregate, nfirst[width:], preferred_element_type=jnp.float32
    )
    hidden = jnp.maximum(hidden, 0.0).astype(jnp.bfloat16)
    hidden = jnp.maximum(jnp.dot(hidden, nsecond, preferred_element_type=jnp.float32), 0.0).astype(
        jnp.bfloat16
    )
    update = jnp.dot(hidden, nthird, preferred_element_type=jnp.float32)
    return (live_rows[:, None] * (state.astype(jnp.float32) + layer_norm(update))).astype(
        jnp.bfloat16
    )


def body(
    latent,
    destination,
    neighbours,
    valid,
    ghost_index,
    edge_first,
    edge_second,
    edge_third,
    node_first,
    node_second,
    node_third,
):
    rows = latent[0, 0, 0]
    dest = destination[0, 0, 0, :, 0]
    count_p, width = rows.shape
    size_second = lax.axis_size("gy")
    size_third = lax.axis_size("gz")
    capacity = count_p // 8
    first = lax.axis_index("gx")
    second = lax.axis_index("gy")
    third = lax.axis_index("gz")
    code = (
        (dest // (size_second * size_third) - first + 1) * 9
        + (dest // size_third % size_second - second + 1) * 3
        + (dest % size_third - third + 1)
    )
    onehot = code[:, None] == jnp.arange(27, dtype=jnp.int32)[None, :]
    lower = (
        lax.broadcasted_iota(jnp.int32, (count_p, count_p), 0)
        > lax.broadcasted_iota(jnp.int32, (count_p, count_p), 1)
    ).astype(jnp.bfloat16)
    before = jnp.dot(lower, onehot.astype(jnp.bfloat16), preferred_element_type=jnp.float32)
    rank = jnp.sum(before * onehot.astype(jnp.float32), axis=1).astype(jnp.int32)
    counts = jnp.sum(onehot.astype(jnp.float32), axis=0).astype(jnp.bfloat16).reshape(3, 3, 3, 1)
    slot_rank = jnp.arange(capacity, dtype=jnp.int32)

    def place(offset):
        chosen = ((code[None, :] == offset) & (rank[None, :] == slot_rank[:, None])).astype(
            jnp.bfloat16
        )
        return jnp.dot(chosen, rows, preferred_element_type=jnp.float32).astype(jnp.bfloat16)

    buffer = lax.map(place, jnp.arange(27, dtype=jnp.int32)).reshape(3, 3, 3, capacity, width)
    framed, framed_counts = (
        with_halo(buffer, (("gx", 0), ("gy", 1), ("gz", 2)), 1),
        with_halo(counts, (("gx", 0), ("gy", 1), ("gz", 2)), 1),
    )
    moved = framed[0::2, 0::2, 0::2]
    sent = framed_counts[0::2, 0::2, 0::2]
    state = moved.reshape(27 * capacity, width)
    live = (
        (jnp.arange(capacity, dtype=jnp.float32)[None, :] < sent.reshape(27, 1).astype(jnp.float32))
        .astype(jnp.float32)
        .reshape(-1)
    )
    nbr = neighbours[0, 0, 0]
    mask = valid[0, 0, 0]
    gidx = ghost_index[0, 0, 0].reshape(-1)
    slab_rows = ghost_index.shape[4]
    for layer in range(edge_first.shape[0]):
        weights = (
            edge_first[layer],
            edge_second[layer],
            edge_third[layer],
            node_first[layer],
            node_second[layer],
            node_third[layer],
        )
        slabs = jnp.take(state, gidx, axis=0).reshape(2, 2, 2, slab_rows, width)
        window = with_halo(slabs, (("gx", 0), ("gy", 1), ("gz", 2)), 1)
        ghosts = window.reshape(64, slab_rows, width)[outer_slabs].reshape(56 * slab_rows, width)
        state = message_pass(state, ghosts, nbr, mask, live, weights)
    return state.reshape(1, 1, 1, 27 * capacity, width)


def solution(mesh):
    return jax.shard_map(
        body,
        mesh=mesh,
        in_specs=(
            P("gx", "gy", "gz", None, None),
            P("gx", "gy", "gz", None, None),
            P("gx", "gy", "gz", None, None),
            P("gx", "gy", "gz", None, None),
            P("gx", "gy", "gz", None, None),
            P(),
            P(),
            P(),
            P(),
            P(),
            P(),
        ),
        out_specs=P("gx", "gy", "gz", None, None),
        check_vma=False,
    )
```

profile of v0, /device:TPU:106, one launch (start us, length us, event | category | flops | bytes accessed | tf_op | source)
XLA Modules:
  0.0 1258.9 jit_solution(5047529521826143831)
XLA Ops:
  1.3 66.0 %while.33 = (s32[]{:T(128)}, bf16[27,128,128]{2,1,0:T(8,128)(2,1)S(1)}, s32[27]{0:T(128)S(1)}, s32[1024]{0:T(1024)S(1)}, s32[1024]{0:T(1024)S(1)}, /*index=5*/bf16[1024,128]{1,0:T(8,128)(2,1)}, s32[]{:T(128)}) while((s32[]{:T(128)}, bf16[27,128,128]{2,1,0:T(8,128)(2,1)S(1)}, s32[27]{0:T(128)S(1)}, s32[1024]{0:T(1024)S(1)}, ...), condition=%wide.region_3.4_spmd.clone, body=%wide.region_2.3_spmd.clone.sunk | while | flops 33833984 | bytes 305249 | solution.py:124
  154.4 529.9 %while.31 = (s32[]{:T(128)}, bf16[27,128,128]{2,1,0:T(8,128)(2,1)}, f32[27,128,128]{2,1,0:T(8,128)}, s32[27,128,24]{2,1,0:T(8,128)}, bf16[5248,128]{1,0:T(8,128)...) while((s32[]{:T(128)}, bf16[27,128,128]{2,1,0:T(8,128)(2,1)}, ...), condition=%wide.region_6.9_spmd, body=%wide.region_4.8_spmd.sunk | while | flops 305149952 | bytes 10758769 | solution.py:59
  155.4 11.4 gather_fusion
  175.0 11.4 gather_fusion
  194.6 11.4 gather_fusion
  214.3 11.4 gather_fusion
  233.9 11.4 gather_fusion
  253.5 11.4 gather_fusion
  273.1 11.4 gather_fusion
  292.8 11.4 gather_fusion
  312.4 11.4 gather_fusion
  332.0 11.4 gather_fusion
  351.7 11.4 gather_fusion
  371.3 11.4 gather_fusion
  390.9 11.4 gather_fusion
  410.5 11.4 gather_fusion
  430.2 11.4 gather_fusion
  449.8 11.4 gather_fusion
  469.4 11.4 gather_fusion
  489.0 11.4 gather_fusion
  508.7 11.4 gather_fusion
  528.3 11.4 gather_fusion
  547.9 11.4 gather_fusion
  567.5 11.4 gather_fusion
  587.2 11.4 gather_fusion
  606.8 11.4 gather_fusion
  626.4 11.4 gather_fusion
  646.0 11.4 gather_fusion
  665.7 11.4 gather_fusion
  719.7 529.5 %while.32 = (s32[]{:T(128)}, bf16[27,128,128]{2,1,0:T(8,128)(2,1)}, f32[27,128,128]{2,1,0:T(8,128)}, s32[27,128,24]{2,1,0:T(8,128)}, bf16[5248,128]{1,0:T(8,128)...) while((s32[]{:T(128)}, bf16[27,128,128]{2,1,0:T(8,128)(2,1)}, ...), condition=%wide.region_11.14_spmd, body=%wide.region_9.13_spmd.sunk | while | flops 305149952 | bytes 10758769 | solution.py:59
  799.1 11.4 gather_fusion.1
  1014.8 11.4 gather_fusion.1
  (860 shorter events, 924.6 us)
Async XLA Ops:
  1.3 78.3 %copy-start.16 = (s32[1,1,1,8,32]{4,3,2,1,0:T(8,128)S(1)}, s32[1,1,1,8,32]{4,3,2,1,0:T(8,128)}, u32[]{:S(2)}) copy-start(s32[1,1,1,8,32]{4,3,2,1,0:T(8,128)} %param.28) | copy-start | bytes 3076
  67.3 20.6 %copy-start.12 = (bf16[2,128,128]{2,1,0:T(8,128)(2,1)S(1)}, bf16[2,128,128]{2,1,0:T(8,128)(2,1)}, u32[]{:S(2)}) copy-start(bf16[2,128,128]{2,1,0:T(8,128)(2,1)} %param.31) | copy-start | bytes 196612
  67.4 12.3 collective-permute-start.6
  70.9 10.4 collective-permute-start.7
  73.7 36.3 %collective-permute-start = (bf16[1,3,3,1]{2,1,3,0:T(4,128)(2,1)S(1)}, bf16[1,3,3,1]{2,1,3,0:T(4,128)(2,1)S(1)}, u32[]{:S(2)}, u32[]{:S(2)}) collective-permute-start(bf16[1,3,3,1]{2,1,3,0:T(4,128)(2,1)S(1)} %slice.191), channel_id=1, source_target_pairs={{0,32},{32,64},{64,96},{1,33},{33,65},{65,97},{2,34},{34,66},{66,9... | collective-permute-start | bytes 62 | tf_op jit(solution)/shard_map/ppermute | solution.py:18
  77.1 32.8 %collective-permute-start.1 = (bf16[1,3,3,1]{2,1,0,3:T(4,128)(2,1)S(1)}, bf16[1,3,3,1]{2,1,0,3:T(4,128)(2,1)S(1)}, u32[]{:S(2)}, u32[]{:S(2)}) collective-permute-start(bf16[1,3,3,1]{2,1,0,3:T(4,128)(2,1)S(1)} %bitcast.200), channel_id=1, source_target_pairs={{32,0},{64,32},{96,64},{33,1},{65,33},{97,65},{34,2},{66,34},{98,6... | collective-permute-start | bytes 62 | tf_op jit(solution)/shard_map/ppermute | solution.py:21
  81.4 13.7 %collective-permute-start.8 = (bf16[5,1,3,128,128]{4,3,2,1,0:T(8,128)(2,1)S(1)}, bf16[5,1,3,128,128]{4,3,2,1,0:T(8,128)(2,1)S(1)}, u32[]{:S(2)}, u32[]{:S(2)}) collective-permute-start(bf16[5,1,3,128,128]{4,3,2,1,0:T(8,128)(2,1)S(1)} %get-tuple-element.223), channel_id=1, source_target_pairs={{0,8},{8,16},{16,24},{1,9},{9,17},{17,25},{2,10},{10,18},{18,26},{... | collective-permute-start | bytes 1474568 | tf_op jit(solution)/shard_map/ppermute | solution.py:18
  84.9 13.4 %collective-permute-start.9 = (bf16[5,1,3,128,128]{4,3,2,1,0:T(8,128)(2,1)S(1)}, bf16[5,1,3,128,128]{4,3,2,1,0:T(8,128)(2,1)S(1)}, u32[]{:S(2)}, u32[]{:S(2)}) collective-permute-start(bf16[5,1,3,128,128]{4,3,2,1,0:T(8,128)(2,1)S(1)} %get-tuple-element.224), channel_id=1, source_target_pairs={{8,0},{16,8},{24,16},{9,1},{17,9},{25,17},{10,2},{18,10},{26,18},{... | collective-permute-start | bytes 1474568 | tf_op jit(solution)/shard_map/ppermute | solution.py:21
  87.3 39.9 %copy-start.17 = (pred[256]{0:T(512)(128)(4,1)}, pred[256]{0:T(512)(128)(4,1)S(1)}, u32[]{:S(2)}) copy-start(pred[256]{0:T(512)(128)(4,1)S(1)} %compare_and_fusion.2) | copy-start | bytes 772
  99.7 24.6 %collective-permute-start.10 = (bf16[5,5,1,128,128]{4,3,2,1,0:T(8,128)(2,1)}, bf16[5,5,1,128,128]{4,3,2,1,0:T(8,128)(2,1)}, u32[]{:S(2)}, u32[]{:S(2)}) collective-permute-start(bf16[5,5,1,128,128]{4,3,2,1,0:T(8,128)(2,1)} %get-tuple-element.221), channel_id=1, source_target_pairs={{0,1},{1,2},{2,3},{3,4},{4,5},{5,6},{6,7},{8,9},{9,10},{10,11},{11... | collective-permute-start | bytes 2457608 | tf_op jit(solution)/shard_map/ppermute | solution.py:18
  101.6 22.7 %collective-permute-start.11 = (bf16[5,5,1,128,128]{4,3,2,1,0:T(8,128)(2,1)}, bf16[5,5,1,128,128]{4,3,2,1,0:T(8,128)(2,1)}, u32[]{:S(2)}, u32[]{:S(2)}) collective-permute-start(bf16[5,5,1,128,128]{4,3,2,1,0:T(8,128)(2,1)} %get-tuple-element.222), channel_id=1, source_target_pairs={{1,0},{2,1},{3,2},{4,3},{5,4},{6,5},{7,6},{9,8},{10,9},{11,10},{12... | collective-permute-start | bytes 2457608 | tf_op jit(solution)/shard_map/ppermute | solution.py:21
  105.3 21.0 %copy-start.14 = (s32[1024]{0:T(1024)}, s32[1024]{0:T(1024)S(1)}, u32[]{:S(2)}) copy-start(s32[1024]{0:T(1024)S(1)} %pad_clamp_fusion.1) | copy-start | bytes 12292
  109.9 42.7 %copy-start.15 = (s32[1024]{0:T(1024)}, s32[1024]{0:T(1024)S(1)}, u32[]{:S(2)}) copy-start(s32[1024]{0:T(1024)S(1)} %pad_clamp_fusion) | copy-start | bytes 12292
  110.0 5.9 collective-permute-start.2
  113.2 5.5 collective-permute-start.3
  118.7 14.4 %collective-permute-start.4 = (bf16[5,5,1,1]{2,1,0,3:T(8,128)(2,1)S(1)}, bf16[5,5,1,1]{2,1,0,3:T(8,128)(2,1)S(1)}, u32[]{:S(2)}, u32[]{:S(2)}) collective-permute-start(bf16[5,5,1,1]{2,1,0,3:T(8,128)(2,1)S(1)} %get-tuple-element.245), channel_id=1, source_target_pairs={{0,1},{1,2},{2,3},{3,4},{4,5},{5,6},{6,7},{8,9},{9,10},{10,11},{11... | collective-permute-start | bytes 158 | tf_op jit(solution)/shard_map/ppermute | solution.py:18
  120.7 12.5 collective-permute-start.5
  126.3 26.9 %copy-start = (bf16[3,3,3,128,128]{4,3,2,1,0:T(8,128)(2,1)}, bf16[3,3,3,128,128]{4,3,2,1,0:T(8,128)(2,1)S(1)}, u32[]{:S(2)}) copy-start(bf16[3,3,3,128,128]{4,3,2,1,0:T(8,128)(2,1)S(1)} %slice.207) | copy-start | bytes 2654212
  127.3 6.4 collective-permute-start.12
  130.4 5.8 collective-permute-start.13
  136.3 6.2 collective-permute-start.14
  138.2 6.2 collective-permute-start.15
  144.4 7.2 collective-permute-start.16
  146.3 6.1 collective-permute-start.17
  692.4 26.1 %copy-start.2 = (bf16[3456,128]{1,0:T(8,128)(2,1)}, bf16[3456,128]{1,0:T(8,128)(2,1)S(1)}, u32[]{:S(2)}) copy-start(bf16[3456,128]{1,0:T(8,128)(2,1)S(1)} %multiply_convert_fusion.1) | copy-start | bytes 2654212
  693.5 5.9 collective-permute-start.18
  695.4 5.8 collective-permute-start.19
  701.3 7.5 collective-permute-start.20
  703.2 6.2 collective-permute-start.21
  709.4 8.1 collective-permute-start.22
  711.4 6.2 collective-permute-start.23
  719.7 529.5 %copy-start.10 = (bf16[2,128,128]{2,1,0:T(8,128)(2,1)S(1)}, bf16[2,128,128]{2,1,0:T(8,128)(2,1)}, u32[]{:S(2)}) copy-start(bf16[2,128,128]{2,1,0:T(8,128)(2,1)} %param.33) | copy-start | bytes 196612
  (12 other events, 92.2 us)
where the time goes:
time: 1280 us; the launch traced here: 1260 us
  local copies, waits for them, and re-layouts  829 us (65%)
  matrix products  275 us (21%)
  starting transfers between devices  69.3 us (5%)
  other arithmetic  61 us (5%)
  waiting for transfers between devices  22.2 us (2%)
    gather x54, local copies, waits for them, and re-layouts, edge_block(): fetched = jnp.take(table, nbr.reshape(-1), axis=0)  618 us
    dot_general x54, matrix products, edge_block(): jnp.dot(hidden, esecond, preferred_element_type=jnp.float32)  149 us
    dot_general x54, matrix products, edge_block(): jnp.dot(hidden, ethird, preferred_element_type=jnp.float32)  79.7 us
    add x108, local copies, waits for them, and re-layouts, edge_block(): hidden = jnp.maximum(recv[:, None, :] + sender, 0.0)  51.5 us
    mul x54, local copies, waits for them, and re-layouts, edge_block(): return jnp.sum(message * mask[:, :, None], axis=1)  46 us
    dynamic_slice x54, local copies, waits for them, and re-layouts, message_pass(): lax.map(edge_block, (recv_part.reshape(blocks, -1, width), nbr_rows.resha...  45.6 us
    ppermute x12, starting transfers between devices, with_halo(): lax.ppermute(lax.slice_in_dim(block, 0, width, axis=dim), axis, backward)  39.2 us
    dynamic_update_slice x54, local copies, waits for them, and re-layouts, message_pass(): lax.map(edge_block, (recv_part.reshape(blocks, -1, width), nbr_rows.resha...  33.7 us
  transfers between devices with their start and end apart: 24, of which 10 were waited for; matrix products, arithmetic and copies ran while one was open for 1% of the time, Pallas kernels for 0%

commit v1 on v0

v1 whole, which is shorter than its diff:
```python
import jax
import jax.numpy as jnp
import numpy as np
from jax import lax
from jax.experimental import pallas as pl
from jax.experimental.pallas import tpu as pltpu
from jax.sharding import PartitionSpec as P

F32 = jnp.float32
BF16 = jnp.bfloat16
I32 = jnp.int32
W = 128
CODES = 27
ROWS = CODES * W
DEG = 24
SLAB = 32
OUTER = [
    p for p in range(64) if p // 16 in (0, 3) or p // 4 % 4 in (0, 3) or p % 4 in (0, 3)
]
GHOSTS = len(OUTER) * SLAB
NODES = ROWS + GHOSTS
DUMMY = NODES
MARK = 2.0**100
CH = 4
HALO_AXES = ("gx", "gy", "gz")
VMEM_LIMIT = 56 * 2**20


def dot(a, b):
    return jnp.dot(a, b, preferred_element_type=F32)


def vmem():
    return pl.BlockSpec(memory_space=pltpu.VMEM)


def smem():
    return pl.BlockSpec(memory_space=pltpu.SMEM)


def iota(shape, dim):
    return lax.broadcasted_iota(I32, shape, dim)


def pack_kernel(dest_ref, rows_ref, out_ref, slot_ref):
    n_y, n_z = 4, 8
    ix, iy, iz = (lax.axis_index(a) for a in HALO_AXES)
    tri = (iota((W, W), 0) < iota((W, W), 1)).astype(BF16)
    ones = jnp.ones((W, W), BF16)
    off = jnp.zeros((32, W), F32)
    for j in range(8):
        d = dest_ref[:, j * W : (j + 1) * W]
        code = (
            (lax.shift_right_logical(d, 5) - ix + 1) * 9
            + ((lax.shift_right_logical(d, 3) & (n_y - 1)) - iy + 1) * 3
            + ((d & (n_z - 1)) - iz + 1)
        )
        hit = iota((32, W), 0) == code
        one = jnp.where(hit, 1.0, 0.0).astype(BF16)
        before = dot(one, tri) + off
        rank = jnp.sum(jnp.where(hit, before, 0.0), axis=0, keepdims=True)
        slot_ref[:, j * W : (j + 1) * W] = code * W + rank.astype(I32)
        off = off + dot(one, ones)
    slot = slot_ref[...]
    rows = rows_ref[...]
    for c in range(CODES):
        chosen = jnp.where(slot == iota((W, 1024), 0) + c * W, 1.0, 0.0).astype(BF16)
        got = dot(chosen, rows)
        alive = iota((W, W), 0).astype(F32) < off[c : c + 1, :]
        out_ref[c] = jnp.where(alive, got, MARK).astype(BF16)


def pack(dest, rows):
    return pl.pallas_call(
        pack_kernel,
        out_shape=jax.ShapeDtypeStruct((CODES, W, W), BF16),
        in_specs=[vmem(), vmem()],
        out_specs=vmem(),
        scratch_shapes=[pltpu.VMEM((1, 1024), I32)],
        compiler_params=pltpu.CompilerParams(vmem_limit_bytes=VMEM_LIMIT),
        name="pack",
    )(dest, rows)


def receive_kernel(gidx_ref, raw_ref, state_ref, cnt_ref, slab_ref, full, picked):
    sizes = (4, 4, 8)
    pos = [lax.axis_index(a) for a in HALO_AXES]
    cnt_ref[...] = jnp.zeros_like(cnt_ref)
    for c in range(CODES):
        offs = (c // 9 - 1, c // 3 % 3 - 1, c % 3 - 1)
        inside = jnp.int32(1)
        for p, o, s in zip(pos, offs, sizes):
            if o < 0:
                inside = inside * (p > 0).astype(I32)
            if o > 0:
                inside = inside * (p < s - 1).astype(I32)
        x = raw_ref[c].astype(F32)
        alive = x < MARK * 0.5
        count = jnp.sum(jnp.where(alive, 1.0, 0.0), axis=0, keepdims=True).astype(I32)
        cnt_ref[c : c + 1, :] = count * inside
        clean = jnp.where(alive, x, 0.0)
        full[c * W : (c + 1) * W, :] = clean
        state_ref[c * W : (c + 1) * W, :] = clean.astype(BF16)
    pick_slabs(gidx_ref, full, picked)
    slab_ref[...] = picked[...].astype(BF16)


def pick_slabs(gidx_ref, full, picked):
    def some(b, carry):
        for r in range(16):
            picked[pl.ds(b * 16 + r, 1), :] = full[pl.ds(gidx_ref[b * 16 + r], 1), :]
        return carry

    lax.fori_loop(0, 16, some, 0)


def receive(gidx, raw):
    return pl.pallas_call(
        receive_kernel,
        out_shape=[
            jax.ShapeDtypeStruct((ROWS, W), BF16),
            jax.ShapeDtypeStruct((32, W), I32),
            jax.ShapeDtypeStruct((8 * SLAB, W), BF16),
        ],
        in_specs=[smem(), vmem()],
        out_specs=[vmem()] * 3,
        scratch_shapes=[pltpu.VMEM((ROWS, W), F32), pltpu.VMEM((8 * SLAB, W), F32)],
        compiler_params=pltpu.CompilerParams(vmem_limit_bytes=VMEM_LIMIT),
        name="receive",
    )(gidx, raw)


def index_kernel(nbr_ref, valid_ref, idx_ref, steps_ref):
    steps_ref[...] = jnp.zeros_like(steps_ref) + DEG
    for c in range(CODES):
        cols = slice(c * W, (c + 1) * W)
        idx_ref[c * DEG : (c + 1) * DEG, :] = jnp.where(
            valid_ref[:, cols] > 0, nbr_ref[:, cols], DUMMY
        )


def indices(nbr, valid):
    return pl.pallas_call(
        index_kernel,
        out_shape=[
            jax.ShapeDtypeStruct((CODES * DEG, W), I32),
            jax.ShapeDtypeStruct((32, W), I32),
        ],
        in_specs=[vmem()] * 2,
        out_specs=[vmem()] * 2,
        compiler_params=pltpu.CompilerParams(vmem_limit_bytes=VMEM_LIMIT),
        name="indices",
    )(nbr, valid)


def layer_kernel(
    idx_ref,
    steps_ref,
    cnt_ref,
    gidx_ref,
    state_ref,
    mid_ref,
    low_ref,
    high_ref,
    efirst_ref,
    esecond_ref,
    ethird_ref,
    nfirst_ref,
    nsecond_ref,
    nthird_ref,
    out_ref,
    slab_ref,
    table,
    recv,
    ghosts,
    hidden,
    deep,
    agg,
    full,
    picked,
    where_ref,
):
    w_recv = efirst_ref[0:W, :]
    w_send = efirst_ref[W : 2 * W, :]
    w_both = jnp.concatenate([w_recv, w_send], axis=1)

    for s, p in enumerate(OUTER):
        a, b, c = p // 16, p // 4 % 4, p % 4
        if c == 0:
            slab = low_ref[a, b]
        elif c == 3:
            slab = high_ref[a, b]
        else:
            slab = mid_ref[a, b, c - 1]
        ghosts[s * SLAB : (s + 1) * SLAB, :] = slab

    def own(i, carry):
        rows = pl.ds(i * 384, 384)
        both = dot(state_ref[rows, :], w_both)
        recv[rows, :] = both[:, :W]
        table[rows, :] = both[:, W:]
        return carry

    lax.fori_loop(0, ROWS // 384, own, 0)

    def far(i, carry):
        table[pl.ds(ROWS + i * 256, 256), :] = dot(ghosts[pl.ds(i * 256, 256), :], w_send)
        return carry

    lax.fori_loop(0, GHOSTS // 256, far, 0)
    table[NODES : NODES + 8, :] = jnp.full((8, W), -MARK, F32)

    w_second = esecond_ref[...]
    sub = iota((8, W), 0)

    def sender(c, carry):
        groups = lax.shift_right_logical(cnt_ref[c, 0] + 7, 3)

        def gather(g, chunk):
            q0 = pl.multiple_of(g * 8, 8)
            base = c * (DEG * W) + q0
            mine = recv[pl.ds(pl.multiple_of(c * W + q0, 8), 8), :]
            count = lax.shift_right_logical(steps_ref[c, q0] + (CH - 1), 2)
            where_ref[g] = chunk
            where_ref[32 + g] = count

            def some(t, carry):
                first = base + t * (CH * W)
                for pair in range(CH // 2):
                    both = []
                    for k in (2 * pair, 2 * pair + 1):
                        got = None
                        for r in range(8):
                            at = idx_ref[first + (k * W + r)]
                            row = jnp.broadcast_to(table[pl.ds(at, 1), :], (8, W))
                            got = row if got is None else jnp.where(sub == r, row, got)
                        both.append(jnp.maximum(got + mine, 0.0))
                    dst = pl.multiple_of((chunk + t) * (CH * 8) + pair * 16, 16)
                    hidden[pl.ds(dst, 16), :] = jnp.concatenate(both, axis=0).astype(BF16)
                return carry

            lax.fori_loop(0, count, some, 0)
            return chunk + count

        chunks = lax.fori_loop(0, groups, gather, jnp.int32(0))

        def multiply(i, carry):
            h = hidden[pl.ds(pl.multiple_of(i * 256, 256), 256), :]
            d = jnp.maximum(dot(h, w_second), 0.0).astype(BF16).astype(F32)
            d = jnp.sum(d.reshape(8, CH, 8, W), axis=1)
            deep[pl.ds(pl.multiple_of(i * 64, 64), 64), :] = d.reshape(64, W)
            return carry

        lax.fori_loop(0, lax.shift_right_logical(chunks + 7, 3), multiply, 0)

        def collect(g, carry):
            first = where_ref[g]
            count = where_ref[32 + g]
            total = jnp.zeros((8, W), F32)
            for j in range(DEG // CH):
                piece = deep[pl.ds(pl.multiple_of((first + j) * 8, 8), 8), :]
                total = total + jnp.where(j < count, piece, 0.0)
            agg[pl.ds(pl.multiple_of(c * W + g * 8, 8), 8), :] = total
            return carry

        lax.fori_loop(0, groups, collect, 0)
        return carry

    lax.fori_loop(0, CODES, sender, 0)

    w_third = ethird_ref[...]
    n_state = nfirst_ref[0:W, :]
    n_agg = nfirst_ref[W : 2 * W, :]
    n_second = nsecond_ref[...]
    n_third = nthird_ref[...]

    def node(i, carry):
        rows = pl.ds(pl.multiple_of(i * 384, 384), 384)
        live = jnp.concatenate(
            [iota((W, W), 0) < cnt_ref[i * 3 + j, 0] for j in range(3)], axis=0
        )
        summed = jnp.where(live, agg[rows, :], 0.0)
        top = summed.astype(BF16)
        rest = (summed - top.astype(F32)).astype(BF16)
        total = (dot(top, w_third) + dot(rest, w_third)).astype(BF16)
        state = state_ref[rows, :]
        h = jnp.maximum(dot(state, n_state) + dot(total, n_agg), 0.0).astype(BF16)
        h = jnp.maximum(dot(h, n_second), 0.0).astype(BF16)
        update = dot(h, n_third)
        mean = jnp.mean(update, axis=1, keepdims=True)
        centred = update - mean
        var = jnp.mean(centred * centred, axis=1, keepdims=True)
        new = state.astype(F32) + centred * lax.rsqrt(var + 1e-05)
        new = jnp.where(live, new, 0.0)
        full[rows, :] = new
        out_ref[rows, :] = new.astype(BF16)
        return carry

    lax.fori_loop(0, ROWS // 384, node, 0)
    pick_slabs(gidx_ref, full, picked)
    slab_ref[...] = picked[...].astype(BF16)


def one_layer(idx, steps, cnt, gidx, state, mid, low, high, weights):
    return pl.pallas_call(
        layer_kernel,
        out_shape=[
            jax.ShapeDtypeStruct((ROWS, W), BF16),
            jax.ShapeDtypeStruct((8 * SLAB, W), BF16),
        ],
        in_specs=[smem()] * 4 + [vmem()] * 10,
        out_specs=[vmem()] * 2,
        scratch_shapes=[
            pltpu.VMEM((NODES + 8, W), F32),
            pltpu.VMEM((ROWS, W), F32),
            pltpu.VMEM((GHOSTS, W), BF16),
            pltpu.VMEM((3072 + 256, W), BF16),
            pltpu.VMEM((768 + 64, W), F32),
            pltpu.VMEM((ROWS, W), F32),
            pltpu.VMEM((ROWS, W), F32),
            pltpu.VMEM((8 * SLAB, W), F32),
            pltpu.SMEM((64,), I32),
        ],
        compiler_params=pltpu.CompilerParams(vmem_limit_bytes=VMEM_LIMIT),
        name="layer",
    )(idx, steps, cnt, gidx, state, mid, low, high, *weights)


def both_ways(up, down, axis):
    n = lax.axis_size(axis)
    forward = [(i, i + 1) for i in range(n - 1)]
    backward = [(b, a) for a, b in forward]
    return lax.ppermute(up, axis, forward), lax.ppermute(down, axis, backward)


def migrate(buffer):
    for dim, axis in enumerate(HALO_AXES):
        take = lambda i: lax.index_in_dim(buffer, i, dim, keepdims=True)
        low, high = both_ways(take(2), take(0), axis)
        buffer = jnp.concatenate([low, take(1), high], axis=dim)
    return buffer


def surround(slabs):
    block = slabs.reshape(2, 2, 2, SLAB, W)
    for dim, axis in enumerate(HALO_AXES[:2]):
        low, high = both_ways(
            lax.slice_in_dim(block, 1, 2, axis=dim), lax.slice_in_dim(block, 0, 1, axis=dim), axis
        )
        block = jnp.concatenate([low, block, high], axis=dim)
    low, high = both_ways(block[:, :, 1], block[:, :, 0], "gz")
    return block, low, high


def body(
    latent,
    destination,
    neighbours,
    valid,
    ghost_index,
    edge_first,
    edge_second,
    edge_third,
    node_first,
    node_second,
    node_third,
):
    dest = destination.reshape(1, 1024)
    nbr = neighbours[0, 0, 0].T
    mask = valid[0, 0, 0].T
    gidx = ghost_index.reshape(-1)
    buffer = pack(dest, latent[0, 0, 0])
    idx, steps = indices(nbr, mask)
    idx = idx.reshape(-1)
    moved = migrate(buffer.reshape(3, 3, 3, W, W))
    state, cnt, slabs = receive(gidx, moved.reshape(CODES, W, W))
    for layer in range(edge_first.shape[0]):
        weights = [
            w[layer]
            for w in (edge_first, edge_second, edge_third, node_first, node_second, node_third)
        ]
        mid, low, high = surround(slabs)
        state, slabs = one_layer(idx, steps, cnt, gidx, state, mid, low, high, weights)
    return state.reshape(1, 1, 1, ROWS, W)


def solution(mesh):
    spread = P("gx", "gy", "gz", None, None)
    return jax.shard_map(
        body,
        mesh=mesh,
        in_specs=(spread,) * 5 + (P(),) * 6,
        out_specs=spread,
        check_vma=False,
    )
```

time: 1280 us -> 297 us (0.23); the launches traced: 1260 us -> 295 us
  local copies, waits for them, and re-layouts: 829 us -> 8.52 us
  matrix products: 275 us -> 0 us
  Pallas kernels: 0 us -> 200 us
  other arithmetic: 61 us -> 1.26 us
  starting transfers between devices: 69.3 us -> 52 us
    gather x58 -> x0, local copies, waits for them, and re-layouts: 621 us -> none  [the longest x54 618 us: edge_block(): fetched = jnp.take(table, nbr.reshape(-1), axis=0)]
    dot_general x144 -> x0, matrix products: 275 us -> none  [the longest x54 149 us: edge_block(): jnp.dot(hidden, esecond, preferred_element_type=jnp.float32)]
    pallas_call x0 -> x5, Pallas kernels: none -> 200 us  [the longest x2 190 us: one_layer(): pl.pallas_call(layer_kernel, out_shape=[jax.ShapeDtypeStruct((ROWS, W), B...]
    dynamic_slice x81 -> x0, local copies, waits for them, and re-layouts: 61.7 us -> none  [the longest x54 45.6 us: message_pass(): lax.map(edge_block, (recv_part.reshape(blocks, -1, width), nbr_rows.resha...]
    add x108 -> x0, local copies, waits for them, and re-layouts: 51.5 us -> none  [edge_block(): hidden = jnp.maximum(recv[:, None, :] + sender, 0.0)]
    mul x54 -> x0, local copies, waits for them, and re-layouts: 46 us -> none  [edge_block(): return jnp.sum(message * mask[:, :, None], axis=1)]
    dynamic_update_slice x54 -> x0, local copies, waits for them, and re-layouts: 33.7 us -> none  [message_pass(): lax.map(edge_block, (recv_part.reshape(blocks, -1, width), nbr_rows.resha...]
    reduce_sum x57 -> x0, other arithmetic: 31.9 us -> none  [the longest x54 29.8 us: edge_block(): return jnp.sum(message * mask[:, :, None], axis=1)]
  transfers between devices with their start and end apart: 24 -> 18, of which waited for: 10 -> 13; matrix products, arithmetic and copies ran while one was open for 1% -> 1% of each run, Pallas kernels for 0% -> 1%
where the time goes in v1:
time: 297 us; the launch traced here: 295 us
  Pallas kernels  200 us (67%)
  starting transfers between devices  52 us (18%)
  waiting for transfers between devices  33.3 us (11%)
  local copies, waits for them, and re-layouts  8.52 us (3%)
    pallas_call x2, Pallas kernels, one_layer(): pl.pallas_call(layer_kernel, out_shape=[jax.ShapeDtypeStruct((ROWS, W), B...  190 us
    ppermute x18, starting transfers between devices, both_ways(): return (lax.ppermute(up, axis, forward), lax.ppermute(down, axis, backward))  52 us
    ppermute x18, waiting for transfers between devices, both_ways(): return (lax.ppermute(up, axis, forward), lax.ppermute(down, axis, backward))  33.3 us
  transfers between devices with their start and end apart: 18, of which 13 were waited for; matrix products, arithmetic and copies ran while one was open for 1% of the time, Pallas kernels for 1%

profile of v1, /device:TPU:106, one launch (start us, length us, event | category | flops | bytes accessed | tf_op | source)
XLA Modules:
  0.0 295.3 jit_solution(15338298808717357901)
XLA Ops:
  0.0 5.0 %pack.1 = bf16[27,128,128]{2,1,0:T(8,128)(2,1)} custom-call(s32[1,1024]{1,0:T(1,128)} %bitcast.69, bf16[1024,128]{1,0:T(8,128)(2,1)} %bitcast.64), custom_call_target="tpu_custom_call" | custom-call | tf_op jit(solution)/shard_map/pack/pallas_call | solution.py:74
  6.3 2.4 collective-permute-start.1
  8.7 3.4 %collective-permute-start = (bf16[1,3,3,128,128]{4,3,2,1,0:T(8,128)(2,1)S(1)}, bf16[1,3,3,128,128]{4,3,2,1,0:T(8,128)(2,1)S(1)}, u32[]{:S(2)}, u32[]{:S(2)}) collective-permute-start(bf16[1,3,3,128,128]{4,3,2,1,0:T(8,128)(2,1)S(1)} %bitcast.60), channel_id=1, source_target_pairs={{0,32},{32,64},{64,96},{1,33},{33,65},{65,97},{2,34},{34,66},{66,9... | collective-permute-start | bytes 884744 | tf_op jit(solution)/shard_map/ppermute | solution.py:333
  12.1 4.8 %collective-permute-done.1 = bf16[1,3,3,128,128]{4,3,2,1,0:T(8,128)(2,1)S(1)} collective-permute-done((bf16[1,3,3,128,128]{4,3,2,1,0:T(8,128)(2,1)S(1)}, bf16[1,3,3,128,128]{4,3,2,1,0:T(8,128)(2,1)S(1)}, u32[]{:S(2)}, u32[]{:S(2)}) %collective-permute-start.1) | collective-permute-done | bytes 294944 | tf_op jit(solution)/shard_map/ppermute | solution.py:333
  16.9 2.2 collective-permute-done
  19.2 3.5 %collective-permute-start.2 = (bf16[3,1,3,128,128]{4,3,2,1,0:T(8,128)(2,1)S(1)}, bf16[3,1,3,128,128]{4,3,2,1,0:T(8,128)(2,1)S(1)}, u32[]{:S(2)}, u32[]{:S(2)}) collective-permute-start(bf16[3,1,3,128,128]{4,3,2,1,0:T(8,128)(2,1)S(1)} %get-tuple-element.24), channel_id=1, source_target_pairs={{0,8},{8,16},{16,24},{1,9},{9,17},{17,25},{2,10},{10,18},{18,26},{... | collective-permute-start | bytes 884744 | tf_op jit(solution)/shard_map/ppermute | solution.py:333
  22.7 2.4 collective-permute-start.3
  25.1 3.6 %collective-permute-done.2 = bf16[3,1,3,128,128]{4,3,2,1,0:T(8,128)(2,1)S(1)} collective-permute-done((bf16[3,1,3,128,128]{4,3,2,1,0:T(8,128)(2,1)S(1)}, bf16[3,1,3,128,128]{4,3,2,1,0:T(8,128)(2,1)S(1)}, u32[]{:S(2)}, u32[]{:S(2)}) %collective-permute-start.2) | collective-permute-done | bytes 294944 | tf_op jit(solution)/shard_map/ppermute | solution.py:333
  28.7 3.2 %collective-permute-done.3 = bf16[3,1,3,128,128]{4,3,2,1,0:T(8,128)(2,1)S(1)} collective-permute-done((bf16[3,1,3,128,128]{4,3,2,1,0:T(8,128)(2,1)S(1)}, bf16[3,1,3,128,128]{4,3,2,1,0:T(8,128)(2,1)S(1)}, u32[]{:S(2)}, u32[]{:S(2)}) %collective-permute-start.3) | collective-permute-done | bytes 294944 | tf_op jit(solution)/shard_map/ppermute | solution.py:333
  32.1 1.9 collective-permute-start.4
  34.0 3.6 %collective-permute-start.5 = (bf16[3,3,1,128,128]{4,3,2,1,0:T(8,128)(2,1)S(1)}, bf16[3,3,1,128,128]{4,3,2,1,0:T(8,128)(2,1)S(1)}, u32[]{:S(2)}, u32[]{:S(2)}) collective-permute-start(bf16[3,3,1,128,128]{4,3,2,1,0:T(8,128)(2,1)S(1)} %get-tuple-element.22), channel_id=1, source_target_pairs={{1,0},{2,1},{3,2},{4,3},{5,4},{6,5},{7,6},{9,8},{10,9},{11,10},{12... | collective-permute-start | bytes 884744 | tf_op jit(solution)/shard_map/ppermute | solution.py:333
  38.3 1.9 collective-permute-done.4
  42.9 2.8 receive.1
  46.5 3.4 %collective-permute-start.6 = (bf16[1,2,2,32,128]{4,3,1,0,2:T(8,128)(2,1)S(1)}, bf16[1,2,2,32,128]{4,3,1,0,2:T(8,128)(2,1)S(1)}, u32[]{:S(2)}, u32[]{:S(2)}) collective-permute-start(bf16[1,2,2,32,128]{4,3,1,0,2:T(8,128)(2,1)S(1)} %copy.14), channel_id=1, source_target_pairs={{0,32},{32,64},{64,96},{1,33},{33,65},{65,97},{2,34},{34,66},{66,9... | collective-permute-start | bytes 98312 | tf_op jit(solution)/shard_map/ppermute | solution.py:333
  50.7 2.6 collective-permute-start.7
  53.3 3.3 %collective-permute-done.7 = bf16[1,2,2,32,128]{4,3,1,0,2:T(8,128)(2,1)S(1)} collective-permute-done((bf16[1,2,2,32,128]{4,3,1,0,2:T(8,128)(2,1)S(1)}, bf16[1,2,2,32,128]{4,3,1,0,2:T(8,128)(2,1)S(1)}, u32[]{:S(2)}, u32[]{:S(2)}) %collective-permute-start.7) | collective-permute-done | bytes 32800 | tf_op jit(solution)/shard_map/ppermute | solution.py:333
  56.7 3.3 %collective-permute-start.8 = (bf16[4,1,2,32,128]{4,3,1,0,2:T(8,128)(2,1)S(1)}, bf16[4,1,2,32,128]{4,3,1,0,2:T(8,128)(2,1)S(1)}, u32[]{:S(2)}, u32[]{:S(2)}) collective-permute-start(bf16[4,1,2,32,128]{4,3,1,0,2:T(8,128)(2,1)S(1)} %get-tuple-element.40), channel_id=1, source_target_pairs={{0,8},{8,16},{16,24},{1,9},{9,17},{17,25},{2,10},{10,18},{18,26},{... | collective-permute-start | bytes 196616 | tf_op jit(solution)/shard_map/ppermute | solution.py:333
  60.0 2.7 collective-permute-start.9
  66.2 2.1 collective-permute-start.11
  68.3 2.4 collective-permute-start.10
  72.1 2.5 collective-permute-done.10.low_ref
  75.2 95.1 %layer.2 = (bf16[3456,128]{1,0:T(8,128)(2,1)}, bf16[256,128]{1,0:T(8,128)(2,1)}) custom-call(s32[82944]{0:T(1024)} %bitcast.55, s32[32,128]{1,0:T(8,128)} %get-tuple-element.14.steps_ref, s32[32,128]{1,0:T(8,128)} %get-tuple-element.15.cnt_ref, s32[256]{0:T(256)} %reshape.30.gidx_ref, bf16[3456,128]{1,0:T(8,128)(2,1)} %get-tuple-element.16.state_ref, ...), custom_call_target="tpu_custom_call" | custom-call | tf_op jit(solution)/shard_map/layer/pallas_call | solution.py:305
  171.1 6.3 %collective-permute-start.12 = (bf16[1,2,2,32,128]{4,3,1,0,2:T(8,128)(2,1)S(1)}, bf16[1,2,2,32,128]{4,3,1,0,2:T(8,128)(2,1)S(1)}, u32[]{:S(2)}, u32[]{:S(2)}) collective-permute-start(bf16[1,2,2,32,128]{4,3,1,0,2:T(8,128)(2,1)S(1)} %copy.18), channel_id=1, source_target_pairs={{0,32},{32,64},{64,96},{1,33},{33,65},{65,97},{2,34},{34,66},{66,9... | collective-permute-start | bytes 98312 | tf_op jit(solution)/shard_map/ppermute | solution.py:333
  177.4 1.9 collective-permute-start.13
  179.4 3.8 %collective-permute-done.13 = bf16[1,2,2,32,128]{4,3,1,0,2:T(8,128)(2,1)S(1)} collective-permute-done((bf16[1,2,2,32,128]{4,3,1,0,2:T(8,128)(2,1)S(1)}, bf16[1,2,2,32,128]{4,3,1,0,2:T(8,128)(2,1)S(1)}, u32[]{:S(2)}, u32[]{:S(2)}) %collective-permute-start.13) | collective-permute-done | bytes 32800 | tf_op jit(solution)/shard_map/ppermute | solution.py:333
  183.2 1.9 collective-permute-start.14
  185.2 3.9 %collective-permute-start.15 = (bf16[4,1,2,32,128]{4,3,1,0,2:T(8,128)(2,1)S(1)}, bf16[4,1,2,32,128]{4,3,1,0,2:T(8,128)(2,1)S(1)}, u32[]{:S(2)}, u32[]{:S(2)}) collective-permute-start(bf16[4,1,2,32,128]{4,3,1,0,2:T(8,128)(2,1)S(1)} %get-tuple-element.39), channel_id=1, source_target_pairs={{8,0},{16,8},{24,16},{9,1},{17,9},{25,17},{10,2},{18,10},{26,18},{... | collective-permute-start | bytes 196616 | tf_op jit(solution)/shard_map/ppermute | solution.py:333
  189.4 1.9 collective-permute-done.15
  191.4 1.9 collective-permute-start.17
  193.3 2.4 collective-permute-start.16
  196.5 3.1 %collective-permute-done.16.low_ref = bf16[4,4,32,128]{3,2,1,0:T(8,128)(2,1)S(1)} collective-permute-done((bf16[4,4,32,128]{3,2,1,0:T(8,128)(2,1)S(1)}, bf16[4,4,32,128]{3,2,1,0:T(8,128)(2,1)S(1)}, u32[]{:S(2)}, u32[]{:S(2)}) %collective-permute-start.16) | collective-permute-done | bytes 131104 | tf_op jit(solution)/shard_map/ppermute | solution.py:333
  200.3 95.0 %layer.3 = (bf16[3456,128]{1,0:T(8,128)(2,1)}, bf16[256,128]{1,0:T(8,128)(2,1)}) custom-call(s32[82944]{0:T(1024)} %bitcast.56, s32[32,128]{1,0:T(8,128)} %get-tuple-element.14.steps_ref, s32[32,128]{1,0:T(8,128)} %get-tuple-element.15.cnt_ref, s32[256]{0:T(256)} %reshape.30.gidx_ref, bf16[3456,128]{1,0:T(8,128)(2,1)} %get-tuple-element.18.state_ref, ...), custom_call_target="tpu_custom_call" | custom-call | tf_op jit(solution)/shard_map/layer/pallas_call | solution.py:305
  (65 shorter events, 14.7 us)
Async XLA Ops:
  6.3 10.6 %collective-permute-start.1 = (bf16[1,3,3,128,128]{4,3,2,1,0:T(8,128)(2,1)S(1)}, bf16[1,3,3,128,128]{4,3,2,1,0:T(8,128)(2,1)S(1)}, u32[]{:S(2)}, u32[]{:S(2)}) collective-permute-start(bf16[1,3,3,128,128]{4,3,2,1,0:T(8,128)(2,1)S(1)} %bitcast.61), channel_id=1, source_target_pairs={{32,0},{64,32},{96,64},{33,1},{65,33},{97,65},{34,2},{66,34},{98,6... | collective-permute-start | bytes 884744 | tf_op jit(solution)/shard_map/ppermute | solution.py:333
  8.7 10.4 %collective-permute-start = (bf16[1,3,3,128,128]{4,3,2,1,0:T(8,128)(2,1)S(1)}, bf16[1,3,3,128,128]{4,3,2,1,0:T(8,128)(2,1)S(1)}, u32[]{:S(2)}, u32[]{:S(2)}) collective-permute-start(bf16[1,3,3,128,128]{4,3,2,1,0:T(8,128)(2,1)S(1)} %bitcast.60), channel_id=1, source_target_pairs={{0,32},{32,64},{64,96},{1,33},{33,65},{65,97},{2,34},{34,66},{66,9... | collective-permute-start | bytes 884744 | tf_op jit(solution)/shard_map/ppermute | solution.py:333
  19.2 9.4 %collective-permute-start.2 = (bf16[3,1,3,128,128]{4,3,2,1,0:T(8,128)(2,1)S(1)}, bf16[3,1,3,128,128]{4,3,2,1,0:T(8,128)(2,1)S(1)}, u32[]{:S(2)}, u32[]{:S(2)}) collective-permute-start(bf16[3,1,3,128,128]{4,3,2,1,0:T(8,128)(2,1)S(1)} %get-tuple-element.24), channel_id=1, source_target_pairs={{0,8},{8,16},{16,24},{1,9},{9,17},{17,25},{2,10},{10,18},{18,26},{... | collective-permute-start | bytes 884744 | tf_op jit(solution)/shard_map/ppermute | solution.py:333
  22.7 9.2 %collective-permute-start.3 = (bf16[3,1,3,128,128]{4,3,2,1,0:T(8,128)(2,1)S(1)}, bf16[3,1,3,128,128]{4,3,2,1,0:T(8,128)(2,1)S(1)}, u32[]{:S(2)}, u32[]{:S(2)}) collective-permute-start(bf16[3,1,3,128,128]{4,3,2,1,0:T(8,128)(2,1)S(1)} %get-tuple-element.25), channel_id=1, source_target_pairs={{8,0},{16,8},{24,16},{9,1},{17,9},{25,17},{10,2},{18,10},{26,18},{... | collective-permute-start | bytes 884744 | tf_op jit(solution)/shard_map/ppermute | solution.py:333
  32.0 5.7 %copy-start.12 = (s32[1,1,1,8,32]{4,3,2,1,0:T(8,128)S(1)}, s32[1,1,1,8,32]{4,3,2,1,0:T(8,128)}, u32[]{:S(2)}) copy-start(s32[1,1,1,8,32]{4,3,2,1,0:T(8,128)} %param.15) | copy-start | bytes 3076
  32.1 8.0 %collective-permute-start.4 = (bf16[3,3,1,128,128]{4,3,2,1,0:T(8,128)(2,1)S(1)}, bf16[3,3,1,128,128]{4,3,2,1,0:T(8,128)(2,1)S(1)}, u32[]{:S(2)}, u32[]{:S(2)}) collective-permute-start(bf16[3,3,1,128,128]{4,3,2,1,0:T(8,128)(2,1)S(1)} %get-tuple-element.21), channel_id=1, source_target_pairs={{0,1},{1,2},{2,3},{3,4},{4,5},{5,6},{6,7},{8,9},{9,10},{10,11},{11... | collective-permute-start | bytes 884744 | tf_op jit(solution)/shard_map/ppermute | solution.py:333
  34.0 7.9 %collective-permute-start.5 = (bf16[3,3,1,128,128]{4,3,2,1,0:T(8,128)(2,1)S(1)}, bf16[3,3,1,128,128]{4,3,2,1,0:T(8,128)(2,1)S(1)}, u32[]{:S(2)}, u32[]{:S(2)}) collective-permute-start(bf16[3,3,1,128,128]{4,3,2,1,0:T(8,128)(2,1)S(1)} %get-tuple-element.22), channel_id=1, source_target_pairs={{1,0},{2,1},{3,2},{4,3},{5,4},{6,5},{7,6},{9,8},{10,9},{11,10},{12... | collective-permute-start | bytes 884744 | tf_op jit(solution)/shard_map/ppermute | solution.py:333
  42.9 7.0 %copy-start.7 = (bf16[2,256,128]{2,1,0:T(8,128)(2,1)S(1)}, bf16[2,256,128]{2,1,0:T(8,128)(2,1)}, u32[]{:S(2)}) copy-start(bf16[2,256,128]{2,1,0:T(8,128)(2,1)} %param.16) | copy-start | bytes 393220
  45.7 4.2 %copy-start.6 = (bf16[2,256,128]{2,1,0:T(8,128)(2,1)S(1)}, bf16[2,256,128]{2,1,0:T(8,128)(2,1)}, u32[]{:S(2)}) copy-start(bf16[2,256,128]{2,1,0:T(8,128)(2,1)} %param.19) | copy-start | bytes 393220
  46.5 6.7 %collective-permute-start.6 = (bf16[1,2,2,32,128]{4,3,1,0,2:T(8,128)(2,1)S(1)}, bf16[1,2,2,32,128]{4,3,1,0,2:T(8,128)(2,1)S(1)}, u32[]{:S(2)}, u32[]{:S(2)}) collective-permute-start(bf16[1,2,2,32,128]{4,3,1,0,2:T(8,128)(2,1)S(1)} %copy.14), channel_id=1, source_target_pairs={{0,32},{32,64},{64,96},{1,33},{33,65},{65,97},{2,34},{34,66},{66,9... | collective-permute-start | bytes 98312 | tf_op jit(solution)/shard_map/ppermute | solution.py:333
  50.7 2.6 copy-start.1
  50.7 5.9 %collective-permute-start.7 = (bf16[1,2,2,32,128]{4,3,1,0,2:T(8,128)(2,1)S(1)}, bf16[1,2,2,32,128]{4,3,1,0,2:T(8,128)(2,1)S(1)}, u32[]{:S(2)}, u32[]{:S(2)}) collective-permute-start(bf16[1,2,2,32,128]{4,3,1,0,2:T(8,128)(2,1)S(1)} %copy.15), channel_id=1, source_target_pairs={{32,0},{64,32},{96,64},{33,1},{65,33},{97,65},{34,2},{66,34},{98,6... | collective-permute-start | bytes 98312 | tf_op jit(solution)/shard_map/ppermute | solution.py:333
  56.6 6.0 %copy-start.8 = (bf16[2,128,128]{2,1,0:T(8,128)(2,1)S(1)}, bf16[2,128,128]{2,1,0:T(8,128)(2,1)}, u32[]{:S(2)}) copy-start(bf16[2,128,128]{2,1,0:T(8,128)(2,1)} %param.18) | copy-start | bytes 196612
  56.6 6.0 %copy-start.9 = (bf16[2,128,128]{2,1,0:T(8,128)(2,1)S(1)}, bf16[2,128,128]{2,1,0:T(8,128)(2,1)}, u32[]{:S(2)}) copy-start(bf16[2,128,128]{2,1,0:T(8,128)(2,1)} %param.17) | copy-start | bytes 196612
  56.7 8.5 %collective-permute-start.8 = (bf16[4,1,2,32,128]{4,3,1,0,2:T(8,128)(2,1)S(1)}, bf16[4,1,2,32,128]{4,3,1,0,2:T(8,128)(2,1)S(1)}, u32[]{:S(2)}, u32[]{:S(2)}) collective-permute-start(bf16[4,1,2,32,128]{4,3,1,0,2:T(8,128)(2,1)S(1)} %get-tuple-element.40), channel_id=1, source_target_pairs={{0,8},{8,16},{16,24},{1,9},{9,17},{17,25},{2,10},{10,18},{18,26},{... | collective-permute-start | bytes 196616 | tf_op jit(solution)/shard_map/ppermute | solution.py:333
  60.0 6.2 %collective-permute-start.9 = (bf16[4,1,2,32,128]{4,3,1,0,2:T(8,128)(2,1)S(1)}, bf16[4,1,2,32,128]{4,3,1,0,2:T(8,128)(2,1)S(1)}, u32[]{:S(2)}, u32[]{:S(2)}) collective-permute-start(bf16[4,1,2,32,128]{4,3,1,0,2:T(8,128)(2,1)S(1)} %get-tuple-element.41), channel_id=1, source_target_pairs={{8,0},{16,8},{24,16},{9,1},{17,9},{25,17},{10,2},{18,10},{26,18},{... | collective-permute-start | bytes 196616 | tf_op jit(solution)/shard_map/ppermute | solution.py:333
  66.2 4.5 %copy-start.10 = (bf16[2,128,128]{2,1,0:T(8,128)(2,1)S(1)}, bf16[2,128,128]{2,1,0:T(8,128)(2,1)}, u32[]{:S(2)}) copy-start(bf16[2,128,128]{2,1,0:T(8,128)(2,1)} %param.21) | copy-start | bytes 196612
  66.2 4.5 %copy-start.11 = (bf16[2,128,128]{2,1,0:T(8,128)(2,1)S(1)}, bf16[2,128,128]{2,1,0:T(8,128)(2,1)}, u32[]{:S(2)}) copy-start(bf16[2,128,128]{2,1,0:T(8,128)(2,1)} %param.20) | copy-start | bytes 196612
  66.2 5.9 %collective-permute-start.11 = (bf16[4,4,32,128]{3,2,1,0:T(8,128)(2,1)S(1)}, bf16[4,4,32,128]{3,2,1,0:T(8,128)(2,1)S(1)}, u32[]{:S(2)}, u32[]{:S(2)}) collective-permute-start(bf16[4,4,32,128]{3,2,1,0:T(8,128)(2,1)S(1)} %get-tuple-element.32), channel_id=1, source_target_pairs={{1,0},{2,1},{3,2},{4,3},{5,4},{6,5},{7,6},{9,8},{10,9},{11,10},{12... | collective-permute-start | bytes 393224 | tf_op jit(solution)/shard_map/ppermute | solution.py:333
  68.3 6.3 %collective-permute-start.10 = (bf16[4,4,32,128]{3,2,1,0:T(8,128)(2,1)S(1)}, bf16[4,4,32,128]{3,2,1,0:T(8,128)(2,1)S(1)}, u32[]{:S(2)}, u32[]{:S(2)}) collective-permute-start(bf16[4,4,32,128]{3,2,1,0:T(8,128)(2,1)S(1)} %get-tuple-element.33), channel_id=1, source_target_pairs={{0,1},{1,2},{2,3},{3,4},{4,5},{5,6},{6,7},{8,9},{9,10},{10,11},{11... | collective-permute-start | bytes 393224 | tf_op jit(solution)/shard_map/ppermute | solution.py:333
  72.1 2.5 copy-start.3
  74.6 0.6 copy-start.5
  171.1 8.2 %collective-permute-start.12 = (bf16[1,2,2,32,128]{4,3,1,0,2:T(8,128)(2,1)S(1)}, bf16[1,2,2,32,128]{4,3,1,0,2:T(8,128)(2,1)S(1)}, u32[]{:S(2)}, u32[]{:S(2)}) collective-permute-start(bf16[1,2,2,32,128]{4,3,1,0,2:T(8,128)(2,1)S(1)} %copy.18), channel_id=1, source_target_pairs={{0,32},{32,64},{64,96},{1,33},{33,65},{65,97},{2,34},{34,66},{66,9... | collective-permute-start | bytes 98312 | tf_op jit(solution)/shard_map/ppermute | solution.py:333
  177.4 2.0 copy-start
  177.4 5.8 %collective-permute-start.13 = (bf16[1,2,2,32,128]{4,3,1,0,2:T(8,128)(2,1)S(1)}, bf16[1,2,2,32,128]{4,3,1,0,2:T(8,128)(2,1)S(1)}, u32[]{:S(2)}, u32[]{:S(2)}) collective-permute-start(bf16[1,2,2,32,128]{4,3,1,0,2:T(8,128)(2,1)S(1)} %copy.19), channel_id=1, source_target_pairs={{32,0},{64,32},{96,64},{33,1},{65,33},{97,65},{34,2},{66,34},{98,6... | collective-permute-start | bytes 98312 | tf_op jit(solution)/shard_map/ppermute | solution.py:333
  183.2 6.2 %collective-permute-start.14 = (bf16[4,1,2,32,128]{4,3,1,0,2:T(8,128)(2,1)S(1)}, bf16[4,1,2,32,128]{4,3,1,0,2:T(8,128)(2,1)S(1)}, u32[]{:S(2)}, u32[]{:S(2)}) collective-permute-start(bf16[4,1,2,32,128]{4,3,1,0,2:T(8,128)(2,1)S(1)} %get-tuple-element.38), channel_id=1, source_target_pairs={{0,8},{8,16},{16,24},{1,9},{9,17},{17,25},{2,10},{10,18},{18,26},{... | collective-permute-start | bytes 196616 | tf_op jit(solution)/shard_map/ppermute | solution.py:333
  185.2 6.2 %collective-permute-start.15 = (bf16[4,1,2,32,128]{4,3,1,0,2:T(8,128)(2,1)S(1)}, bf16[4,1,2,32,128]{4,3,1,0,2:T(8,128)(2,1)S(1)}, u32[]{:S(2)}, u32[]{:S(2)}) collective-permute-start(bf16[4,1,2,32,128]{4,3,1,0,2:T(8,128)(2,1)S(1)} %get-tuple-element.39), channel_id=1, source_target_pairs={{8,0},{16,8},{24,16},{9,1},{17,9},{25,17},{10,2},{18,10},{26,18},{... | collective-permute-start | bytes 196616 | tf_op jit(solution)/shard_map/ppermute | solution.py:333
  191.4 5.1 %collective-permute-start.17 = (bf16[4,4,32,128]{3,2,1,0:T(8,128)(2,1)S(1)}, bf16[4,4,32,128]{3,2,1,0:T(8,128)(2,1)S(1)}, u32[]{:S(2)}, u32[]{:S(2)}) collective-permute-start(bf16[4,4,32,128]{3,2,1,0:T(8,128)(2,1)S(1)} %get-tuple-element.30), channel_id=1, source_target_pairs={{1,0},{2,1},{3,2},{4,3},{5,4},{6,5},{7,6},{9,8},{10,9},{11,10},{12... | collective-permute-start | bytes 393224 | tf_op jit(solution)/shard_map/ppermute | solution.py:333
  193.3 6.3 %collective-permute-start.16 = (bf16[4,4,32,128]{3,2,1,0:T(8,128)(2,1)S(1)}, bf16[4,4,32,128]{3,2,1,0:T(8,128)(2,1)S(1)}, u32[]{:S(2)}, u32[]{:S(2)}) collective-permute-start(bf16[4,4,32,128]{3,2,1,0:T(8,128)(2,1)S(1)} %get-tuple-element.31), channel_id=1, source_target_pairs={{0,1},{1,2},{2,3},{3,4},{4,5},{5,6},{6,7},{8,9},{9,10},{10,11},{11... | collective-permute-start | bytes 393224 | tf_op jit(solution)/shard_map/ppermute | solution.py:333
  196.5 3.1 %copy-start.2 = (bf16[4,4,32,128]{3,2,1,0:T(8,128)(2,1)}, bf16[4,4,32,128]{3,2,1,0:T(8,128)(2,1)S(1)}, u32[]{:S(2)}) copy-start(bf16[4,4,32,128]{3,2,1,0:T(8,128)(2,1)S(1)} %collective-permute-done.17.high_ref) | copy-start | bytes 393220
  199.6 0.7 copy-start.4

commit v2 on v1

--- a/solution.py
+++ b/solution.py
@@ -98,9 +98,9 @@
         alive = x < MARK * 0.5
         count = jnp.sum(jnp.where(alive, 1.0, 0.0), axis=0, keepdims=True).astype(I32)
         cnt_ref[c : c + 1, :] = count * inside
-        clean = jnp.where(alive, x, 0.0)
-        full[c * W : (c + 1) * W, :] = clean
-        state_ref[c * W : (c + 1) * W, :] = clean.astype(BF16)
+        present = iota((W, W), 0) < count * inside
+        full[c * W : (c + 1) * W, :] = jnp.where(present, x, MARK)
+        state_ref[c * W : (c + 1) * W, :] = jnp.where(present, x, 0.0).astype(BF16)
     pick_slabs(gidx_ref, full, picked)
     slab_ref[...] = picked[...].astype(BF16)
 
@@ -130,27 +130,106 @@
     )(gidx, raw)
 
 
-def index_kernel(nbr_ref, valid_ref, idx_ref, steps_ref):
-    steps_ref[...] = jnp.zeros_like(steps_ref) + DEG
+def sort_pairs(count):
+    pairs = []
+    size = 1
+    while size < count:
+        size *= 2
+    p = 1
+    while p < size:
+        k = p
+        while k >= 1:
+            for j in range(k % p, size - k, 2 * k):
+                for i in range(min(k, size - j - k)):
+                    if (i + j) // (2 * p) == (i + j + k) // (2 * p) and i + j + k < count:
+                        pairs.append((i + j, i + j + k))
+            k //= 2
+        p *= 2
+    return pairs
+
+
+def fill_ghosts(mid_ref, low_ref, high_ref, ghosts):
+    for s, p in enumerate(OUTER):
+        a, b, c = p // 16, p // 4 % 4, p % 4
+        if c == 0:
+            slab = low_ref[a, b]
+        elif c == 3:
+            slab = high_ref[a, b]
+        else:
+            slab = mid_ref[a, b, c - 1]
+        ghosts[s * SLAB : (s + 1) * SLAB, :] = slab
+
+
+def index_kernel(
+    nbr_ref, valid_ref, cnt_ref, mid_ref, low_ref, high_ref, idx_ref, steps_ref, dead_ref, ghosts, held
+):
+    fill_ghosts(mid_ref, low_ref, high_ref, ghosts)
+    alive = jnp.where(ghosts[...].astype(F32) < MARK * 0.5, 1.0, 0.0).astype(BF16)
+    at = iota((W, GHOSTS), 1)
+    bit = jnp.left_shift(1, at & 15).astype(F32)
+    spread = jnp.where(lax.shift_right_logical(at, 4) == iota((W, GHOSTS), 0), bit, 0.0)
+    words = dot(spread.astype(BF16), alive)
+    eye = iota((W, W), 0) == iota((W, W), 1)
+    words = jnp.sum(jnp.where(eye, words, 0.0), axis=0, keepdims=True).astype(I32)
+    words = jnp.broadcast_to(words, (8, W))
+    counts = cnt_ref[...]
+    diag = iota((32, W), 0) == iota((32, W), 1)
+    by_code = jnp.sum(jnp.where(diag, counts.astype(F32), 0.0), axis=0, keepdims=True)
+    by_code = jnp.broadcast_to(by_code.astype(I32), (8, W))
+
+    held[...] = jnp.zeros_like(held) - 1
     for c in range(CODES):
         cols = slice(c * W, (c + 1) * W)
-        idx_ref[c * DEG : (c + 1) * DEG, :] = jnp.where(
-            valid_ref[:, cols] > 0, nbr_ref[:, cols], DUMMY
-        )
-
-
-def indices(nbr, valid):
+        held[c * DEG : (c + 1) * DEG, :] = jnp.where(valid_ref[:, cols] > 0, nbr_ref[:, cols], -1)
+
+    for b in range(4):
+        here = iota((8, W), 1) < counts[b * 8 : (b + 1) * 8, :]
+        keys = []
+        dead = jnp.zeros((8, W), F32)
+        for k in range(DEG):
+            node = held[pl.ds(b * 8 * DEG + k, 8, stride=DEG), :]
+            far = jnp.maximum(node - ROWS, 0)
+            word = jnp.take_along_axis(words, lax.shift_right_logical(far, 4), axis=1)
+            flag = lax.shift_right_logical(word, far & 15) & 1
+            near = jnp.minimum(jnp.maximum(node, 0), ROWS - 1)
+            limit = jnp.take_along_axis(by_code, lax.shift_right_logical(near, 7), axis=1)
+            lives = jnp.where(node >= ROWS, flag, jnp.where((near & (W - 1)) < limit, 1, 0))
+            real = node >= 0
+            key = jnp.where(here & real & (lives > 0), node, DUMMY)
+            dead = dead + jnp.where(here & real & (lives == 0), 1.0, 0.0)
+            keys.append(key.astype(F32))
+        for i, j in sort_pairs(DEG):
+            keys[i], keys[j] = jnp.minimum(keys[i], keys[j]), jnp.maximum(keys[i], keys[j])
+        used = jnp.zeros((8, W), F32)
+        for k in range(DEG):
+            used = used + jnp.where(keys[k] < DUMMY, 1.0, 0.0)
+            idx_ref[k * 32 + b * 8 : k * 32 + (b + 1) * 8, :] = keys[k].astype(I32)
+        for shift in (1, 2, 4, 8):
+            used = jnp.maximum(used, pltpu.roll(used, W - shift, 1))
+        steps_ref[b * 8 : (b + 1) * 8, :] = used.astype(I32)
+        dead_ref[b * 8 : (b + 1) * 8, :] = dead
+
+
+def indices(nbr, valid, cnt, mid, low, high):
     return pl.pallas_call(
         index_kernel,
         out_shape=[
-            jax.ShapeDtypeStruct((CODES * DEG, W), I32),
+            jax.ShapeDtypeStruct((DEG * 32, W), I32),
             jax.ShapeDtypeStruct((32, W), I32),
+            jax.ShapeDtypeStruct((32, W), F32),
         ],
-        in_specs=[vmem()] * 2,
-        out_specs=[vmem()] * 2,
+        in_specs=[vmem()] * 6,
+        out_specs=[vmem()] * 3,
+        scratch_shapes=[pltpu.VMEM((GHOSTS, W), BF16), pltpu.VMEM((32 * DEG, W), I32)],
         compiler_params=pltpu.CompilerParams(vmem_limit_bytes=VMEM_LIMIT),
         name="indices",
-    )(nbr, valid)
+    )(nbr, valid, cnt, mid, low, high)
+
+
+GROUP = 16
+FIRST = 8
+TAILS = (0, 2, 4, 6, 8, 10, 12, 16)
+DUMP = ROWS
 
 
 def layer_kernel(
@@ -158,6 +237,7 @@
     steps_ref,
     cnt_ref,
     gidx_ref,
+    dead_ref,
     state_ref,
     mid_ref,
     low_ref,
@@ -174,28 +254,17 @@
     recv,
     ghosts,
     hidden,
-    deep,
     agg,
     full,
     picked,
-    where_ref,
 ):
     w_recv = efirst_ref[0:W, :]
     w_send = efirst_ref[W : 2 * W, :]
     w_both = jnp.concatenate([w_recv, w_send], axis=1)
-
-    for s, p in enumerate(OUTER):
-        a, b, c = p // 16, p // 4 % 4, p % 4
-        if c == 0:
-            slab = low_ref[a, b]
-        elif c == 3:
-            slab = high_ref[a, b]
-        else:
-            slab = mid_ref[a, b, c - 1]
-        ghosts[s * SLAB : (s + 1) * SLAB, :] = slab
+    fill_ghosts(mid_ref, low_ref, high_ref, ghosts)
 
     def own(i, carry):
-        rows = pl.ds(i * 384, 384)
+        rows = pl.ds(pl.multiple_of(i * 384, 384), 384)
         both = dot(state_ref[rows, :], w_both)
         recv[rows, :] = both[:, :W]
         table[rows, :] = both[:, W:]
@@ -204,7 +273,9 @@
     lax.fori_loop(0, ROWS // 384, own, 0)
 
     def far(i, carry):
-        table[pl.ds(ROWS + i * 256, 256), :] = dot(ghosts[pl.ds(i * 256, 256), :], w_send)
+        x = ghosts[pl.ds(pl.multiple_of(i * 256, 256), 256), :].astype(F32)
+        x = jnp.where(x < MARK * 0.5, x, 0.0).astype(BF16)
+        table[pl.ds(pl.multiple_of(ROWS + i * 256, 128), 256), :] = dot(x, w_send)
         return carry
 
     lax.fori_loop(0, GHOSTS // 256, far, 0)
@@ -213,73 +284,79 @@
     w_second = esecond_ref[...]
     sub = iota((8, W), 0)
 
-    def sender(c, carry):
-        groups = lax.shift_right_logical(cnt_ref[c, 0] + 7, 3)
-
-        def gather(g, chunk):
-            q0 = pl.multiple_of(g * 8, 8)
-            base = c * (DEG * W) + q0
-            mine = recv[pl.ds(pl.multiple_of(c * W + q0, 8), 8), :]
-            count = lax.shift_right_logical(steps_ref[c, q0] + (CH - 1), 2)
-            where_ref[g] = chunk
-            where_ref[32 + g] = count
-
-            def some(t, carry):
-                first = base + t * (CH * W)
-                for pair in range(CH // 2):
-                    both = []
-                    for k in (2 * pair, 2 * pair + 1):
-                        got = None
-                        for r in range(8):
-                            at = idx_ref[first + (k * W + r)]
-                            row = jnp.broadcast_to(table[pl.ds(at, 1), :], (8, W))
-                            got = row if got is None else jnp.where(sub == r, row, got)
-                        both.append(jnp.maximum(got + mine, 0.0))
-                    dst = pl.multiple_of((chunk + t) * (CH * 8) + pair * 16, 16)
-                    hidden[pl.ds(dst, 16), :] = jnp.concatenate(both, axis=0).astype(BF16)
-                return carry
-
-            lax.fori_loop(0, count, some, 0)
-            return chunk + count
-
-        chunks = lax.fori_loop(0, groups, gather, jnp.int32(0))
-
-        def multiply(i, carry):
-            h = hidden[pl.ds(pl.multiple_of(i * 256, 256), 256), :]
-            d = jnp.maximum(dot(h, w_second), 0.0).astype(BF16).astype(F32)
-            d = jnp.sum(d.reshape(8, CH, 8, W), axis=1)
-            deep[pl.ds(pl.multiple_of(i * 64, 64), 64), :] = d.reshape(64, W)
-            return carry
-
-        lax.fori_loop(0, lax.shift_right_logical(chunks + 7, 3), multiply, 0)
-
-        def collect(g, carry):
-            first = where_ref[g]
-            count = where_ref[32 + g]
-            total = jnp.zeros((8, W), F32)
-            for j in range(DEG // CH):
-                piece = deep[pl.ds(pl.multiple_of((first + j) * 8, 8), 8), :]
-                total = total + jnp.where(j < count, piece, 0.0)
-            agg[pl.ds(pl.multiple_of(c * W + g * 8, 8), 8), :] = total
-            return carry
-
-        lax.fori_loop(0, groups, collect, 0)
-        return carry
-
-    lax.fori_loop(0, CODES, sender, 0)
+    def finish(h, row):
+        d = jnp.maximum(dot(h, w_second), 0.0)
+        agg[pl.ds(pl.multiple_of(row, GROUP), GROUP), :] = jnp.sum(
+            d.reshape(DEG, GROUP, W), axis=0
+        )
+
+    def step(base, mine, k):
+        both = []
+        for half in range(2):
+            got = None
+            for r in range(8):
+                at = idx_ref[base + (k * (32 * W) + half * 8 + r)]
+                row = jnp.broadcast_to(table[pl.ds(at, 1), :], (8, W))
+                got = row if got is None else jnp.where(sub == r, row, got)
+            both.append(jnp.maximum(got + mine[half], 0.0))
+        hidden[k * GROUP : (k + 1) * GROUP, :] = jnp.concatenate(both, axis=0).astype(BF16)
+
+    def sender(c, last):
+        groups = lax.shift_right_logical(cnt_ref[c, 0] + (GROUP - 1), 4)
+
+        def gather(g, last):
+            q0 = pl.multiple_of(g * GROUP, GROUP)
+            base = c * W + q0
+            mine = [recv[pl.ds(pl.multiple_of(base + h * 8, 8), 8), :] for h in range(2)]
+            finish(hidden[...], last)
+            for k in range(FIRST):
+                step(base, mine, k)
+            more = steps_ref[c, q0] - FIRST
+            which = sum((more > t).astype(I32) for t in TAILS[:-1])
+
+            def tail(size):
+                def run():
+                    for k in range(FIRST, FIRST + size):
+                        step(base, mine, k)
+                    if FIRST + size < DEG:
+                        hidden[(FIRST + size) * GROUP :, :] = jnp.zeros(
+                            ((DEG - FIRST - size) * GROUP, W), BF16
+                        )
+
+                return run
+
+            lax.switch(which, [tail(t) for t in TAILS])
+            return base
+
+        return lax.fori_loop(0, groups, gather, last)
+
+    last = lax.fori_loop(0, CODES, sender, jnp.int32(DUMP))
+    finish(hidden[...], last)
 
     w_third = ethird_ref[...]
     n_state = nfirst_ref[0:W, :]
     n_agg = nfirst_ref[W : 2 * W, :]
     n_second = nsecond_ref[...]
     n_third = nthird_ref[...]
+    eye = iota((W, W), 0) == iota((W, W), 1)
+    ones = jnp.ones((W, W), BF16)
 
     def node(i, carry):
         rows = pl.ds(pl.multiple_of(i * 384, 384), 384)
         live = jnp.concatenate(
             [iota((W, W), 0) < cnt_ref[i * 3 + j, 0] for j in range(3)], axis=0
         )
-        summed = jnp.where(live, agg[rows, :], 0.0)
+        times = jnp.concatenate(
+            [
+                jnp.where(eye, jnp.broadcast_to(dead_ref[pl.ds(i * 3 + j, 1), :], (W, W)), 0.0)
+                for j in range(3)
+            ],
+            axis=0,
+        )
+        times = dot(times.astype(BF16), ones)
+        alone = jnp.maximum(recv[rows, :], 0.0).astype(BF16)
+        alone = jnp.maximum(dot(alone, w_second), 0.0)
+        summed = jnp.where(live, agg[rows, :] + times * alone, 0.0)
         top = summed.astype(BF16)
         rest = (summed - top.astype(F32)).astype(BF16)
         total = (dot(top, w_third) + dot(rest, w_third)).astype(BF16)
@@ -291,9 +368,8 @@
         centred = update - mean
         var = jnp.mean(centred * centred, axis=1, keepdims=True)
         new = state.astype(F32) + centred * lax.rsqrt(var + 1e-05)
-        new = jnp.where(live, new, 0.0)
-        full[rows, :] = new
-        out_ref[rows, :] = new.astype(BF16)
+        full[rows, :] = jnp.where(live, new, MARK)
+        out_ref[rows, :] = jnp.where(live, new, 0.0).astype(BF16)
         return carry
 
     lax.fori_loop(0, ROWS // 384, node, 0)
@@ -301,29 +377,27 @@
     slab_ref[...] = picked[...].astype(BF16)
 
 
-def one_layer(idx, steps, cnt, gidx, state, mid, low, high, weights):
+def one_layer(idx, steps, cnt, gidx, dead, state, mid, low, high, weights):
     return pl.pallas_call(
         layer_kernel,
         out_shape=[
             jax.ShapeDtypeStruct((ROWS, W), BF16),
             jax.ShapeDtypeStruct((8 * SLAB, W), BF16),
         ],
-        in_specs=[smem()] * 4 + [vmem()] * 10,
+        in_specs=[smem()] * 4 + [vmem()] * 11,
         out_specs=[vmem()] * 2,
         scratch_shapes=[
             pltpu.VMEM((NODES + 8, W), F32),
             pltpu.VMEM((ROWS, W), F32),
             pltpu.VMEM((GHOSTS, W), BF16),
-            pltpu.VMEM((3072 + 256, W), BF16),
-            pltpu.VMEM((768 + 64, W), F32),
-            pltpu.VMEM((ROWS, W), F32),
+            pltpu.VMEM((DEG * GROUP, W), BF16),
+            pltpu.VMEM((ROWS + GROUP, W), F32),
             pltpu.VMEM((ROWS, W), F32),
             pltpu.VMEM((8 * SLAB, W), F32),
-            pltpu.SMEM((64,), I32),
         ],
         compiler_params=pltpu.CompilerParams(vmem_limit_bytes=VMEM_LIMIT),
         name="layer",
-    )(idx, steps, cnt, gidx, state, mid, low, high, *weights)
+    )(idx, steps, cnt, gidx, dead, state, mid, low, high, *weights)
 
 
 def both_ways(up, down, axis):
@@ -370,8 +444,6 @@
     mask = valid[0, 0, 0].T
     gidx = ghost_index.reshape(-1)
     buffer = pack(dest, latent[0, 0, 0])
-    idx, steps = indices(nbr, mask)
-    idx = idx.reshape(-1)
     moved = migrate(buffer.reshape(3, 3, 3, W, W))
     state, cnt, slabs = receive(gidx, moved.reshape(CODES, W, W))
     for layer in range(edge_first.shape[0]):
@@ -380,7 +452,10 @@
             for w in (edge_first, edge_second, edge_third, node_first, node_second, node_third)
         ]
         mid, low, high = surround(slabs)
-        state, slabs = one_layer(idx, steps, cnt, gidx, state, mid, low, high, weights)
+        if layer == 0:
+            idx, steps, dead = indices(nbr, mask, cnt, mid, low, high)
+            idx = idx.reshape(-1)
+        state, slabs = one_layer(idx, steps, cnt, gidx, dead, state, mid, low, high, weights)
     return state.reshape(1, 1, 1, ROWS, W)
 
 

time: 297 us -> 211 us (0.71)
  Pallas kernels: 200 us -> 114 us
    pallas_call x2, Pallas kernels: 190 us -> 104 us  [one_layer(): pl.pallas_call(layer_kernel, out_shape=[jax.ShapeDtypeStruct((ROWS, W), B...]
  transfers between devices with their start and end apart: 18 -> 18, of which waited for: 13 -> 13; matrix products, arithmetic and copies ran while one was open for 1% -> 2% of each run, Pallas kernels for 1% -> 0%
where the time goes in v2:
time: 211 us; the launch traced here: 209 us
  Pallas kernels  114 us (54%)
  starting transfers between devices  49.7 us (24%)
  waiting for transfers between devices  34.7 us (16%)
  local copies, waits for them, and re-layouts  8.61 us (4%)
    pallas_call x2, Pallas kernels, one_layer(): pl.pallas_call(layer_kernel, out_shape=[jax.ShapeDtypeStruct((ROWS, W), B...  104 us
    ppermute x18, starting transfers between devices, both_ways(): return (lax.ppermute(up, axis, forward), lax.ppermute(down, axis, backward))  49.7 us
    ppermute x18, waiting for transfers between devices, both_ways(): return (lax.ppermute(up, axis, forward), lax.ppermute(down, axis, backward))  34.7 us
    pallas_call x1, Pallas kernels, pack(): pl.pallas_call(pack_kernel, out_shape=jax.ShapeDtypeStruct((CODES, W, W),...  5.04 us
  transfers between devices with their start and end apart: 18, of which 13 were waited for; matrix products, arithmetic and copies ran while one was open for 2% of the time, Pallas kernels for 0%

profile of v2, /device:TPU:106, one launch (start us, length us, event | category | flops | bytes accessed | tf_op | source)
XLA Modules:
  0.0 209.1 jit_solution(13279728625770669504)
XLA Ops:
  0.0 5.0 %pack.1 = bf16[27,128,128]{2,1,0:T(8,128)(2,1)} custom-call(s32[1,1024]{1,0:T(1,128)} %bitcast.69, bf16[1024,128]{1,0:T(8,128)(2,1)} %bitcast.64), custom_call_target="tpu_custom_call" | custom-call | tf_op jit(solution)/shard_map/pack/pallas_call | solution.py:74
  6.3 2.4 %collective-permute-start.1 = (bf16[1,3,3,128,128]{4,3,2,1,0:T(8,128)(2,1)S(1)}, bf16[1,3,3,128,128]{4,3,2,1,0:T(8,128)(2,1)S(1)}, u32[]{:S(2)}, u32[]{:S(2)}) collective-permute-start(bf16[1,3,3,128,128]{4,3,2,1,0:T(8,128)(2,1)S(1)} %bitcast.61), channel_id=1, source_target_pairs={{32,0},{64,32},{96,64},{33,1},{65,33},{97,65},{34,2},{66,34},{98,6... | collective-permute-start | bytes 884744 | tf_op jit(solution)/shard_map/ppermute | solution.py:407
  8.7 3.4 %collective-permute-start = (bf16[1,3,3,128,128]{4,3,2,1,0:T(8,128)(2,1)S(1)}, bf16[1,3,3,128,128]{4,3,2,1,0:T(8,128)(2,1)S(1)}, u32[]{:S(2)}, u32[]{:S(2)}) collective-permute-start(bf16[1,3,3,128,128]{4,3,2,1,0:T(8,128)(2,1)S(1)} %bitcast.60), channel_id=1, source_target_pairs={{0,32},{32,64},{64,96},{1,33},{33,65},{65,97},{2,34},{34,66},{66,9... | collective-permute-start | bytes 884744 | tf_op jit(solution)/shard_map/ppermute | solution.py:407
  12.1 4.8 %collective-permute-done.1 = bf16[1,3,3,128,128]{4,3,2,1,0:T(8,128)(2,1)S(1)} collective-permute-done((bf16[1,3,3,128,128]{4,3,2,1,0:T(8,128)(2,1)S(1)}, bf16[1,3,3,128,128]{4,3,2,1,0:T(8,128)(2,1)S(1)}, u32[]{:S(2)}, u32[]{:S(2)}) %collective-permute-start.1) | collective-permute-done | bytes 294944 | tf_op jit(solution)/shard_map/ppermute | solution.py:407
  16.9 2.2 %collective-permute-done = bf16[1,3,3,128,128]{4,3,2,1,0:T(8,128)(2,1)S(1)} collective-permute-done((bf16[1,3,3,128,128]{4,3,2,1,0:T(8,128)(2,1)S(1)}, bf16[1,3,3,128,128]{4,3,2,1,0:T(8,128)(2,1)S(1)}, u32[]{:S(2)}, u32[]{:S(2)}) %collective-permute-start) | collective-permute-done | bytes 294944 | tf_op jit(solution)/shard_map/ppermute | solution.py:407
  19.2 3.5 %collective-permute-start.2 = (bf16[3,1,3,128,128]{4,3,2,1,0:T(8,128)(2,1)S(1)}, bf16[3,1,3,128,128]{4,3,2,1,0:T(8,128)(2,1)S(1)}, u32[]{:S(2)}, u32[]{:S(2)}) collective-permute-start(bf16[3,1,3,128,128]{4,3,2,1,0:T(8,128)(2,1)S(1)} %get-tuple-element.26), channel_id=1, source_target_pairs={{0,8},{8,16},{16,24},{1,9},{9,17},{17,25},{2,10},{10,18},{18,26},{... | collective-permute-start | bytes 884744 | tf_op jit(solution)/shard_map/ppermute | solution.py:407
  22.7 2.4 %collective-permute-start.3 = (bf16[3,1,3,128,128]{4,3,2,1,0:T(8,128)(2,1)S(1)}, bf16[3,1,3,128,128]{4,3,2,1,0:T(8,128)(2,1)S(1)}, u32[]{:S(2)}, u32[]{:S(2)}) collective-permute-start(bf16[3,1,3,128,128]{4,3,2,1,0:T(8,128)(2,1)S(1)} %get-tuple-element.27), channel_id=1, source_target_pairs={{8,0},{16,8},{24,16},{9,1},{17,9},{25,17},{10,2},{18,10},{26,18},{... | collective-permute-start | bytes 884744 | tf_op jit(solution)/shard_map/ppermute | solution.py:407
  25.1 3.6 %collective-permute-done.2 = bf16[3,1,3,128,128]{4,3,2,1,0:T(8,128)(2,1)S(1)} collective-permute-done((bf16[3,1,3,128,128]{4,3,2,1,0:T(8,128)(2,1)S(1)}, bf16[3,1,3,128,128]{4,3,2,1,0:T(8,128)(2,1)S(1)}, u32[]{:S(2)}, u32[]{:S(2)}) %collective-permute-start.2) | collective-permute-done | bytes 294944 | tf_op jit(solution)/shard_map/ppermute | solution.py:407
  28.7 3.2 %collective-permute-done.3 = bf16[3,1,3,128,128]{4,3,2,1,0:T(8,128)(2,1)S(1)} collective-permute-done((bf16[3,1,3,128,128]{4,3,2,1,0:T(8,128)(2,1)S(1)}, bf16[3,1,3,128,128]{4,3,2,1,0:T(8,128)(2,1)S(1)}, u32[]{:S(2)}, u32[]{:S(2)}) %collective-permute-start.3) | collective-permute-done | bytes 294944 | tf_op jit(solution)/shard_map/ppermute | solution.py:407
  32.1 1.9 collective-permute-start.4
  34.0 3.6 %collective-permute-start.5 = (bf16[3,3,1,128,128]{4,3,2,1,0:T(8,128)(2,1)S(1)}, bf16[3,3,1,128,128]{4,3,2,1,0:T(8,128)(2,1)S(1)}, u32[]{:S(2)}, u32[]{:S(2)}) collective-permute-start(bf16[3,3,1,128,128]{4,3,2,1,0:T(8,128)(2,1)S(1)} %get-tuple-element.24), channel_id=1, source_target_pairs={{1,0},{2,1},{3,2},{4,3},{5,4},{6,5},{7,6},{9,8},{10,9},{11,10},{12... | collective-permute-start | bytes 884744 | tf_op jit(solution)/shard_map/ppermute | solution.py:407
  42.9 3.0 %receive.1 = (bf16[3456,128]{1,0:T(8,128)(2,1)}, s32[32,128]{1,0:T(8,128)}, bf16[256,128]{1,0:T(8,128)(2,1)}) custom-call(s32[256]{0:T(256)} %reshape.29.gidx_ref, bf16[27,128,128]{2,1,0:T(8,128)(2,1)} %bitcast.54), custom_call_target="tpu_custom_call" | custom-call | tf_op jit(solution)/shard_map/receive/pallas_call | solution.py:118
  46.7 3.4 %collective-permute-start.6 = (bf16[1,2,2,32,128]{4,3,1,0,2:T(8,128)(2,1)S(1)}, bf16[1,2,2,32,128]{4,3,1,0,2:T(8,128)(2,1)S(1)}, u32[]{:S(2)}, u32[]{:S(2)}) collective-permute-start(bf16[1,2,2,32,128]{4,3,1,0,2:T(8,128)(2,1)S(1)} %copy.15), channel_id=1, source_target_pairs={{0,32},{32,64},{64,96},{1,33},{33,65},{65,97},{2,34},{34,66},{66,9... | collective-permute-start | bytes 98312 | tf_op jit(solution)/shard_map/ppermute | solution.py:407
  50.8 2.6 %collective-permute-start.7 = (bf16[1,2,2,32,128]{4,3,1,0,2:T(8,128)(2,1)S(1)}, bf16[1,2,2,32,128]{4,3,1,0,2:T(8,128)(2,1)S(1)}, u32[]{:S(2)}, u32[]{:S(2)}) collective-permute-start(bf16[1,2,2,32,128]{4,3,1,0,2:T(8,128)(2,1)S(1)} %copy.16), channel_id=1, source_target_pairs={{32,0},{64,32},{96,64},{33,1},{65,33},{97,65},{34,2},{66,34},{98,6... | collective-permute-start | bytes 98312 | tf_op jit(solution)/shard_map/ppermute | solution.py:407
  53.5 3.3 %collective-permute-done.7 = bf16[1,2,2,32,128]{4,3,1,0,2:T(8,128)(2,1)S(1)} collective-permute-done((bf16[1,2,2,32,128]{4,3,1,0,2:T(8,128)(2,1)S(1)}, bf16[1,2,2,32,128]{4,3,1,0,2:T(8,128)(2,1)S(1)}, u32[]{:S(2)}, u32[]{:S(2)}) %collective-permute-start.7) | collective-permute-done | bytes 32800 | tf_op jit(solution)/shard_map/ppermute | solution.py:407
  56.8 3.3 %collective-permute-start.8 = (bf16[4,1,2,32,128]{4,3,1,0,2:T(8,128)(2,1)S(1)}, bf16[4,1,2,32,128]{4,3,1,0,2:T(8,128)(2,1)S(1)}, u32[]{:S(2)}, u32[]{:S(2)}) collective-permute-start(bf16[4,1,2,32,128]{4,3,1,0,2:T(8,128)(2,1)S(1)} %get-tuple-element.42), channel_id=1, source_target_pairs={{0,8},{8,16},{16,24},{1,9},{9,17},{17,25},{2,10},{10,18},{18,26},{... | collective-permute-start | bytes 196616 | tf_op jit(solution)/shard_map/ppermute | solution.py:407
  60.1 2.7 %collective-permute-start.9 = (bf16[4,1,2,32,128]{4,3,1,0,2:T(8,128)(2,1)S(1)}, bf16[4,1,2,32,128]{4,3,1,0,2:T(8,128)(2,1)S(1)}, u32[]{:S(2)}, u32[]{:S(2)}) collective-permute-start(bf16[4,1,2,32,128]{4,3,1,0,2:T(8,128)(2,1)S(1)} %get-tuple-element.43), channel_id=1, source_target_pairs={{8,0},{16,8},{24,16},{9,1},{17,9},{25,17},{10,2},{18,10},{26,18},{... | collective-permute-start | bytes 196616 | tf_op jit(solution)/shard_map/ppermute | solution.py:407
  63.5 2.8 %collective-permute-done.9 = bf16[4,1,2,32,128]{4,3,1,0,2:T(8,128)(2,1)S(1)} collective-permute-done((bf16[4,1,2,32,128]{4,3,1,0,2:T(8,128)(2,1)S(1)}, bf16[4,1,2,32,128]{4,3,1,0,2:T(8,128)(2,1)S(1)}, u32[]{:S(2)}, u32[]{:S(2)}) %collective-permute-start.9) | collective-permute-done | bytes 65568 | tf_op jit(solution)/shard_map/ppermute | solution.py:407
  66.4 2.1 collective-permute-start.11
  68.5 2.4 %collective-permute-start.10 = (bf16[4,4,32,128]{3,2,1,0:T(8,128)(2,1)S(1)}, bf16[4,4,32,128]{3,2,1,0:T(8,128)(2,1)S(1)}, u32[]{:S(2)}, u32[]{:S(2)}) collective-permute-start(bf16[4,4,32,128]{3,2,1,0:T(8,128)(2,1)S(1)} %get-tuple-element.35), channel_id=1, source_target_pairs={{0,1},{1,2},{2,3},{3,4},{4,5},{5,6},{6,7},{8,9},{9,10},{10,11},{11... | collective-permute-start | bytes 393224 | tf_op jit(solution)/shard_map/ppermute | solution.py:407
  72.3 2.5 %collective-permute-done.10.low_ref = bf16[4,4,32,128]{3,2,1,0:T(8,128)(2,1)S(1)} collective-permute-done((bf16[4,4,32,128]{3,2,1,0:T(8,128)(2,1)S(1)}, bf16[4,4,32,128]{3,2,1,0:T(8,128)(2,1)S(1)}, u32[]{:S(2)}, u32[]{:S(2)}) %collective-permute-start.10) | collective-permute-done | bytes 131104 | tf_op jit(solution)/shard_map/ppermute | solution.py:407
  75.4 3.0 %indices.1 = (s32[768,128]{1,0:T(8,128)}, s32[32,128]{1,0:T(8,128)}, f32[32,128]{1,0:T(8,128)}) custom-call(s32[24,3456]{1,0:T(8,128)} %bitcast.58, s32[24,3456]{1,0:T(8,128)} %bitcast.59, s32[32,128]{1,0:T(8,128)} %get-tuple-element.14.cnt_ref, bf16[4,4,2,32,128]{4,3,2,1,0:T(8,128)(2,1)} %copy.18.mid_ref, bf16[4,4,32,128]{3,2,1,0:T(8,128)(2,1)} %copy-done.1, ...), custom_call_target="tpu_custom_call" | custom-call | tf_op jit(solution)/shard_map/indices/pallas_call | solution.py:214
  78.3 51.8 %layer.2 = (bf16[3456,128]{1,0:T(8,128)(2,1)}, bf16[256,128]{1,0:T(8,128)(2,1)}) custom-call(s32[98304]{0:T(1024)} %bitcast.55, s32[32,128]{1,0:T(8,128)} %get-tuple-element.17.steps_ref, s32[32,128]{1,0:T(8,128)} %get-tuple-element.14.cnt_ref, s32[256]{0:T(256)} %reshape.29.gidx_ref, f32[32,128]{1,0:T(8,128)} %get-tuple-element.18.dead_ref, ...), custom_call_target="tpu_custom_call" | custom-call | tf_op jit(solution)/shard_map/layer/pallas_call | solution.py:381
  130.9 3.2 %collective-permute-start.12 = (bf16[1,2,2,32,128]{4,3,1,0,2:T(8,128)(2,1)S(1)}, bf16[1,2,2,32,128]{4,3,1,0,2:T(8,128)(2,1)S(1)}, u32[]{:S(2)}, u32[]{:S(2)}) collective-permute-start(bf16[1,2,2,32,128]{4,3,1,0,2:T(8,128)(2,1)S(1)} %copy.20), channel_id=1, source_target_pairs={{0,32},{32,64},{64,96},{1,33},{33,65},{65,97},{2,34},{34,66},{66,9... | collective-permute-start | bytes 98312 | tf_op jit(solution)/shard_map/ppermute | solution.py:407
  134.1 2.7 %collective-permute-start.13 = (bf16[1,2,2,32,128]{4,3,1,0,2:T(8,128)(2,1)S(1)}, bf16[1,2,2,32,128]{4,3,1,0,2:T(8,128)(2,1)S(1)}, u32[]{:S(2)}, u32[]{:S(2)}) collective-permute-start(bf16[1,2,2,32,128]{4,3,1,0,2:T(8,128)(2,1)S(1)} %copy.21), channel_id=1, source_target_pairs={{32,0},{64,32},{96,64},{33,1},{65,33},{97,65},{34,2},{66,34},{98,6... | collective-permute-start | bytes 98312 | tf_op jit(solution)/shard_map/ppermute | solution.py:407
  136.8 3.1 %collective-permute-done.13 = bf16[1,2,2,32,128]{4,3,1,0,2:T(8,128)(2,1)S(1)} collective-permute-done((bf16[1,2,2,32,128]{4,3,1,0,2:T(8,128)(2,1)S(1)}, bf16[1,2,2,32,128]{4,3,1,0,2:T(8,128)(2,1)S(1)}, u32[]{:S(2)}, u32[]{:S(2)}) %collective-permute-start.13) | collective-permute-done | bytes 32800 | tf_op jit(solution)/shard_map/ppermute | solution.py:407
  140.0 2.3 %collective-permute-start.14 = (bf16[4,1,2,32,128]{4,3,1,0,2:T(8,128)(2,1)S(1)}, bf16[4,1,2,32,128]{4,3,1,0,2:T(8,128)(2,1)S(1)}, u32[]{:S(2)}, u32[]{:S(2)}) collective-permute-start(bf16[4,1,2,32,128]{4,3,1,0,2:T(8,128)(2,1)S(1)} %get-tuple-element.40), channel_id=1, source_target_pairs={{0,8},{8,16},{16,24},{1,9},{9,17},{17,25},{2,10},{10,18},{18,26},{... | collective-permute-start | bytes 196616 | tf_op jit(solution)/shard_map/ppermute | solution.py:407
  142.3 3.5 %collective-permute-start.15 = (bf16[4,1,2,32,128]{4,3,1,0,2:T(8,128)(2,1)S(1)}, bf16[4,1,2,32,128]{4,3,1,0,2:T(8,128)(2,1)S(1)}, u32[]{:S(2)}, u32[]{:S(2)}) collective-permute-start(bf16[4,1,2,32,128]{4,3,1,0,2:T(8,128)(2,1)S(1)} %get-tuple-element.41), channel_id=1, source_target_pairs={{8,0},{16,8},{24,16},{9,1},{17,9},{25,17},{10,2},{18,10},{26,18},{... | collective-permute-start | bytes 196616 | tf_op jit(solution)/shard_map/ppermute | solution.py:407
  146.1 2.3 %collective-permute-done.15 = bf16[4,1,2,32,128]{4,3,1,0,2:T(8,128)(2,1)S(1)} collective-permute-done((bf16[4,1,2,32,128]{4,3,1,0,2:T(8,128)(2,1)S(1)}, bf16[4,1,2,32,128]{4,3,1,0,2:T(8,128)(2,1)S(1)}, u32[]{:S(2)}, u32[]{:S(2)}) %collective-permute-start.15) | collective-permute-done | bytes 65568 | tf_op jit(solution)/shard_map/ppermute | solution.py:407
  150.4 2.4 %collective-permute-start.16 = (bf16[4,4,32,128]{3,2,1,0:T(8,128)(2,1)S(1)}, bf16[4,4,32,128]{3,2,1,0:T(8,128)(2,1)S(1)}, u32[]{:S(2)}, u32[]{:S(2)}) collective-permute-start(bf16[4,4,32,128]{3,2,1,0:T(8,128)(2,1)S(1)} %get-tuple-element.33), channel_id=1, source_target_pairs={{0,1},{1,2},{2,3},{3,4},{4,5},{5,6},{6,7},{8,9},{9,10},{10,11},{11... | collective-permute-start | bytes 393224 | tf_op jit(solution)/shard_map/ppermute | solution.py:407
  153.6 3.1 %collective-permute-done.16.low_ref = bf16[4,4,32,128]{3,2,1,0:T(8,128)(2,1)S(1)} collective-permute-done((bf16[4,4,32,128]{3,2,1,0:T(8,128)(2,1)S(1)}, bf16[4,4,32,128]{3,2,1,0:T(8,128)(2,1)S(1)}, u32[]{:S(2)}, u32[]{:S(2)}) %collective-permute-start.16) | collective-permute-done | bytes 131104 | tf_op jit(solution)/shard_map/ppermute | solution.py:407
  157.4 51.7 %layer.3 = (bf16[3456,128]{1,0:T(8,128)(2,1)}, bf16[256,128]{1,0:T(8,128)(2,1)}) custom-call(s32[98304]{0:T(1024)} %bitcast.56, s32[32,128]{1,0:T(8,128)} %get-tuple-element.17.steps_ref, s32[32,128]{1,0:T(8,128)} %get-tuple-element.14.cnt_ref, s32[256]{0:T(256)} %reshape.29.gidx_ref, f32[32,128]{1,0:T(8,128)} %get-tuple-element.18.dead_ref, ...), custom_call_target="tpu_custom_call" | custom-call | tf_op jit(solution)/shard_map/layer/pallas_call | solution.py:381
  (65 shorter events, 15.6 us)
Async XLA Ops:
  6.3 10.6 %collective-permute-start.1 = (bf16[1,3,3,128,128]{4,3,2,1,0:T(8,128)(2,1)S(1)}, bf16[1,3,3,128,128]{4,3,2,1,0:T(8,128)(2,1)S(1)}, u32[]{:S(2)}, u32[]{:S(2)}) collective-permute-start(bf16[1,3,3,128,128]{4,3,2,1,0:T(8,128)(2,1)S(1)} %bitcast.61), channel_id=1, source_target_pairs={{32,0},{64,32},{96,64},{33,1},{65,33},{97,65},{34,2},{66,34},{98,6... | collective-permute-start | bytes 884744 | tf_op jit(solution)/shard_map/ppermute | solution.py:407
  8.7 10.4 %collective-permute-start = (bf16[1,3,3,128,128]{4,3,2,1,0:T(8,128)(2,1)S(1)}, bf16[1,3,3,128,128]{4,3,2,1,0:T(8,128)(2,1)S(1)}, u32[]{:S(2)}, u32[]{:S(2)}) collective-permute-start(bf16[1,3,3,128,128]{4,3,2,1,0:T(8,128)(2,1)S(1)} %bitcast.60), channel_id=1, source_target_pairs={{0,32},{32,64},{64,96},{1,33},{33,65},{65,97},{2,34},{34,66},{66,9... | collective-permute-start | bytes 884744 | tf_op jit(solution)/shard_map/ppermute | solution.py:407
  19.2 9.4 %collective-permute-start.2 = (bf16[3,1,3,128,128]{4,3,2,1,0:T(8,128)(2,1)S(1)}, bf16[3,1,3,128,128]{4,3,2,1,0:T(8,128)(2,1)S(1)}, u32[]{:S(2)}, u32[]{:S(2)}) collective-permute-start(bf16[3,1,3,128,128]{4,3,2,1,0:T(8,128)(2,1)S(1)} %get-tuple-element.26), channel_id=1, source_target_pairs={{0,8},{8,16},{16,24},{1,9},{9,17},{17,25},{2,10},{10,18},{18,26},{... | collective-permute-start | bytes 884744 | tf_op jit(solution)/shard_map/ppermute | solution.py:407
  22.7 9.2 %collective-permute-start.3 = (bf16[3,1,3,128,128]{4,3,2,1,0:T(8,128)(2,1)S(1)}, bf16[3,1,3,128,128]{4,3,2,1,0:T(8,128)(2,1)S(1)}, u32[]{:S(2)}, u32[]{:S(2)}) collective-permute-start(bf16[3,1,3,128,128]{4,3,2,1,0:T(8,128)(2,1)S(1)} %get-tuple-element.27), channel_id=1, source_target_pairs={{8,0},{16,8},{24,16},{9,1},{17,9},{25,17},{10,2},{18,10},{26,18},{... | collective-permute-start | bytes 884744 | tf_op jit(solution)/shard_map/ppermute | solution.py:407
  32.0 5.7 %copy-start.12 = (s32[1,1,1,8,32]{4,3,2,1,0:T(8,128)S(1)}, s32[1,1,1,8,32]{4,3,2,1,0:T(8,128)}, u32[]{:S(2)}) copy-start(s32[1,1,1,8,32]{4,3,2,1,0:T(8,128)} %param.15) | copy-start | bytes 3076
  32.1 8.0 %collective-permute-start.4 = (bf16[3,3,1,128,128]{4,3,2,1,0:T(8,128)(2,1)S(1)}, bf16[3,3,1,128,128]{4,3,2,1,0:T(8,128)(2,1)S(1)}, u32[]{:S(2)}, u32[]{:S(2)}) collective-permute-start(bf16[3,3,1,128,128]{4,3,2,1,0:T(8,128)(2,1)S(1)} %get-tuple-element.23), channel_id=1, source_target_pairs={{0,1},{1,2},{2,3},{3,4},{4,5},{5,6},{6,7},{8,9},{9,10},{10,11},{11... | collective-permute-start | bytes 884744 | tf_op jit(solution)/shard_map/ppermute | solution.py:407
  34.0 7.9 %collective-permute-start.5 = (bf16[3,3,1,128,128]{4,3,2,1,0:T(8,128)(2,1)S(1)}, bf16[3,3,1,128,128]{4,3,2,1,0:T(8,128)(2,1)S(1)}, u32[]{:S(2)}, u32[]{:S(2)}) collective-permute-start(bf16[3,3,1,128,128]{4,3,2,1,0:T(8,128)(2,1)S(1)} %get-tuple-element.24), channel_id=1, source_target_pairs={{1,0},{2,1},{3,2},{4,3},{5,4},{6,5},{7,6},{9,8},{10,9},{11,10},{12... | collective-permute-start | bytes 884744 | tf_op jit(solution)/shard_map/ppermute | solution.py:407
  42.9 7.2 %copy-start.5 = (bf16[2,256,128]{2,1,0:T(8,128)(2,1)S(1)}, bf16[2,256,128]{2,1,0:T(8,128)(2,1)}, u32[]{:S(2)}) copy-start(bf16[2,256,128]{2,1,0:T(8,128)(2,1)} %param.16) | copy-start | bytes 393220
  45.9 4.2 %copy-start.4 = (bf16[2,256,128]{2,1,0:T(8,128)(2,1)S(1)}, bf16[2,256,128]{2,1,0:T(8,128)(2,1)}, u32[]{:S(2)}) copy-start(bf16[2,256,128]{2,1,0:T(8,128)(2,1)} %param.19) | copy-start | bytes 393220
  46.7 6.7 %collective-permute-start.6 = (bf16[1,2,2,32,128]{4,3,1,0,2:T(8,128)(2,1)S(1)}, bf16[1,2,2,32,128]{4,3,1,0,2:T(8,128)(2,1)S(1)}, u32[]{:S(2)}, u32[]{:S(2)}) collective-permute-start(bf16[1,2,2,32,128]{4,3,1,0,2:T(8,128)(2,1)S(1)} %copy.15), channel_id=1, source_target_pairs={{0,32},{32,64},{64,96},{1,33},{33,65},{65,97},{2,34},{34,66},{66,9... | collective-permute-start | bytes 98312 | tf_op jit(solution)/shard_map/ppermute | solution.py:407
  50.8 2.6 %copy-start.3 = (bf16[256,128]{1,0:T(8,128)(2,1)S(1)}, bf16[256,128]{1,0:T(8,128)(2,1)}, u32[]{:S(2)}) copy-start(bf16[256,128]{1,0:T(8,128)(2,1)} %get-tuple-element.15) | copy-start | bytes 196612
  50.8 5.9 %collective-permute-start.7 = (bf16[1,2,2,32,128]{4,3,1,0,2:T(8,128)(2,1)S(1)}, bf16[1,2,2,32,128]{4,3,1,0,2:T(8,128)(2,1)S(1)}, u32[]{:S(2)}, u32[]{:S(2)}) collective-permute-start(bf16[1,2,2,32,128]{4,3,1,0,2:T(8,128)(2,1)S(1)} %copy.16), channel_id=1, source_target_pairs={{32,0},{64,32},{96,64},{33,1},{65,33},{97,65},{34,2},{66,34},{98,6... | collective-permute-start | bytes 98312 | tf_op jit(solution)/shard_map/ppermute | solution.py:407
  56.8 6.0 %copy-start.8 = (bf16[2,128,128]{2,1,0:T(8,128)(2,1)S(1)}, bf16[2,128,128]{2,1,0:T(8,128)(2,1)}, u32[]{:S(2)}) copy-start(bf16[2,128,128]{2,1,0:T(8,128)(2,1)} %param.18) | copy-start | bytes 196612
  56.8 6.0 %copy-start.9 = (bf16[2,128,128]{2,1,0:T(8,128)(2,1)S(1)}, bf16[2,128,128]{2,1,0:T(8,128)(2,1)}, u32[]{:S(2)}) copy-start(bf16[2,128,128]{2,1,0:T(8,128)(2,1)} %param.17) | copy-start | bytes 196612
  56.8 6.7 %collective-permute-start.8 = (bf16[4,1,2,32,128]{4,3,1,0,2:T(8,128)(2,1)S(1)}, bf16[4,1,2,32,128]{4,3,1,0,2:T(8,128)(2,1)S(1)}, u32[]{:S(2)}, u32[]{:S(2)}) collective-permute-start(bf16[4,1,2,32,128]{4,3,1,0,2:T(8,128)(2,1)S(1)} %get-tuple-element.42), channel_id=1, source_target_pairs={{0,8},{8,16},{16,24},{1,9},{9,17},{17,25},{2,10},{10,18},{18,26},{... | collective-permute-start | bytes 196616 | tf_op jit(solution)/shard_map/ppermute | solution.py:407
  60.1 6.2 %collective-permute-start.9 = (bf16[4,1,2,32,128]{4,3,1,0,2:T(8,128)(2,1)S(1)}, bf16[4,1,2,32,128]{4,3,1,0,2:T(8,128)(2,1)S(1)}, u32[]{:S(2)}, u32[]{:S(2)}) collective-permute-start(bf16[4,1,2,32,128]{4,3,1,0,2:T(8,128)(2,1)S(1)} %get-tuple-element.43), channel_id=1, source_target_pairs={{8,0},{16,8},{24,16},{9,1},{17,9},{25,17},{10,2},{18,10},{26,18},{... | collective-permute-start | bytes 196616 | tf_op jit(solution)/shard_map/ppermute | solution.py:407
  66.3 4.5 %copy-start.10 = (bf16[2,128,128]{2,1,0:T(8,128)(2,1)S(1)}, bf16[2,128,128]{2,1,0:T(8,128)(2,1)}, u32[]{:S(2)}) copy-start(bf16[2,128,128]{2,1,0:T(8,128)(2,1)} %param.21) | copy-start | bytes 196612
  66.4 4.5 %copy-start.11 = (bf16[2,128,128]{2,1,0:T(8,128)(2,1)S(1)}, bf16[2,128,128]{2,1,0:T(8,128)(2,1)}, u32[]{:S(2)}) copy-start(bf16[2,128,128]{2,1,0:T(8,128)(2,1)} %param.20) | copy-start | bytes 196612
  66.4 5.9 %collective-permute-start.11 = (bf16[4,4,32,128]{3,2,1,0:T(8,128)(2,1)S(1)}, bf16[4,4,32,128]{3,2,1,0:T(8,128)(2,1)S(1)}, u32[]{:S(2)}, u32[]{:S(2)}) collective-permute-start(bf16[4,4,32,128]{3,2,1,0:T(8,128)(2,1)S(1)} %get-tuple-element.34), channel_id=1, source_target_pairs={{1,0},{2,1},{3,2},{4,3},{5,4},{6,5},{7,6},{9,8},{10,9},{11,10},{12... | collective-permute-start | bytes 393224 | tf_op jit(solution)/shard_map/ppermute | solution.py:407
  68.5 6.3 %collective-permute-start.10 = (bf16[4,4,32,128]{3,2,1,0:T(8,128)(2,1)S(1)}, bf16[4,4,32,128]{3,2,1,0:T(8,128)(2,1)S(1)}, u32[]{:S(2)}, u32[]{:S(2)}) collective-permute-start(bf16[4,4,32,128]{3,2,1,0:T(8,128)(2,1)S(1)} %get-tuple-element.35), channel_id=1, source_target_pairs={{0,1},{1,2},{2,3},{3,4},{4,5},{5,6},{6,7},{8,9},{9,10},{10,11},{11... | collective-permute-start | bytes 393224 | tf_op jit(solution)/shard_map/ppermute | solution.py:407
  72.3 2.5 %copy-start = (bf16[4,4,32,128]{3,2,1,0:T(8,128)(2,1)}, bf16[4,4,32,128]{3,2,1,0:T(8,128)(2,1)S(1)}, u32[]{:S(2)}) copy-start(bf16[4,4,32,128]{3,2,1,0:T(8,128)(2,1)S(1)} %collective-permute-done.11.high_ref) | copy-start | bytes 393220
  74.7 0.7 copy-start.1
  130.9 5.9 %collective-permute-start.12 = (bf16[1,2,2,32,128]{4,3,1,0,2:T(8,128)(2,1)S(1)}, bf16[1,2,2,32,128]{4,3,1,0,2:T(8,128)(2,1)S(1)}, u32[]{:S(2)}, u32[]{:S(2)}) collective-permute-start(bf16[1,2,2,32,128]{4,3,1,0,2:T(8,128)(2,1)S(1)} %copy.20), channel_id=1, source_target_pairs={{0,32},{32,64},{64,96},{1,33},{33,65},{65,97},{2,34},{34,66},{66,9... | collective-permute-start | bytes 98312 | tf_op jit(solution)/shard_map/ppermute | solution.py:407
  134.1 2.7 %copy-start.2 = (bf16[256,128]{1,0:T(8,128)(2,1)S(1)}, bf16[256,128]{1,0:T(8,128)(2,1)}, u32[]{:S(2)}) copy-start(bf16[256,128]{1,0:T(8,128)(2,1)} %get-tuple-element.21) | copy-start | bytes 196612
  134.1 5.8 %collective-permute-start.13 = (bf16[1,2,2,32,128]{4,3,1,0,2:T(8,128)(2,1)S(1)}, bf16[1,2,2,32,128]{4,3,1,0,2:T(8,128)(2,1)S(1)}, u32[]{:S(2)}, u32[]{:S(2)}) collective-permute-start(bf16[1,2,2,32,128]{4,3,1,0,2:T(8,128)(2,1)S(1)} %copy.21), channel_id=1, source_target_pairs={{32,0},{64,32},{96,64},{33,1},{65,33},{97,65},{34,2},{66,34},{98,6... | collective-permute-start | bytes 98312 | tf_op jit(solution)/shard_map/ppermute | solution.py:407
  140.0 6.2 %collective-permute-start.14 = (bf16[4,1,2,32,128]{4,3,1,0,2:T(8,128)(2,1)S(1)}, bf16[4,1,2,32,128]{4,3,1,0,2:T(8,128)(2,1)S(1)}, u32[]{:S(2)}, u32[]{:S(2)}) collective-permute-start(bf16[4,1,2,32,128]{4,3,1,0,2:T(8,128)(2,1)S(1)} %get-tuple-element.40), channel_id=1, source_target_pairs={{0,8},{8,16},{16,24},{1,9},{9,17},{17,25},{2,10},{10,18},{18,26},{... | collective-permute-start | bytes 196616 | tf_op jit(solution)/shard_map/ppermute | solution.py:407
  142.3 6.2 %collective-permute-start.15 = (bf16[4,1,2,32,128]{4,3,1,0,2:T(8,128)(2,1)S(1)}, bf16[4,1,2,32,128]{4,3,1,0,2:T(8,128)(2,1)S(1)}, u32[]{:S(2)}, u32[]{:S(2)}) collective-permute-start(bf16[4,1,2,32,128]{4,3,1,0,2:T(8,128)(2,1)S(1)} %get-tuple-element.41), channel_id=1, source_target_pairs={{8,0},{16,8},{24,16},{9,1},{17,9},{25,17},{10,2},{18,10},{26,18},{... | collective-permute-start | bytes 196616 | tf_op jit(solution)/shard_map/ppermute | solution.py:407
  148.5 5.1 %collective-permute-start.17 = (bf16[4,4,32,128]{3,2,1,0:T(8,128)(2,1)S(1)}, bf16[4,4,32,128]{3,2,1,0:T(8,128)(2,1)S(1)}, u32[]{:S(2)}, u32[]{:S(2)}) collective-permute-start(bf16[4,4,32,128]{3,2,1,0:T(8,128)(2,1)S(1)} %get-tuple-element.32), channel_id=1, source_target_pairs={{1,0},{2,1},{3,2},{4,3},{5,4},{6,5},{7,6},{9,8},{10,9},{11,10},{12... | collective-permute-start | bytes 393224 | tf_op jit(solution)/shard_map/ppermute | solution.py:407
  150.4 6.3 %collective-permute-start.16 = (bf16[4,4,32,128]{3,2,1,0:T(8,128)(2,1)S(1)}, bf16[4,4,32,128]{3,2,1,0:T(8,128)(2,1)S(1)}, u32[]{:S(2)}, u32[]{:S(2)}) collective-permute-start(bf16[4,4,32,128]{3,2,1,0:T(8,128)(2,1)S(1)} %get-tuple-element.33), channel_id=1, source_target_pairs={{0,1},{1,2},{2,3},{3,4},{4,5},{5,6},{6,7},{8,9},{9,10},{10,11},{11... | collective-permute-start | bytes 393224 | tf_op jit(solution)/shard_map/ppermute | solution.py:407
  153.6 3.1 %copy-start.6 = (bf16[4,4,32,128]{3,2,1,0:T(8,128)(2,1)}, bf16[4,4,32,128]{3,2,1,0:T(8,128)(2,1)S(1)}, u32[]{:S(2)}) copy-start(bf16[4,4,32,128]{3,2,1,0:T(8,128)(2,1)S(1)} %collective-permute-done.17.high_ref) | copy-start | bytes 393220
  156.7 0.7 copy-start.7

commit v3 on v2

--- a/solution.py
+++ b/solution.py
@@ -23,6 +23,7 @@
 MARK = 2.0**100
 CH = 4
 HALO_AXES = ("gx", "gy", "gz")
+GRID = (4, 4, 8)
 VMEM_LIMIT = 56 * 2**20
 
 
@@ -83,13 +84,12 @@
 
 
 def receive_kernel(gidx_ref, raw_ref, state_ref, cnt_ref, slab_ref, full, picked):
-    sizes = (4, 4, 8)
     pos = [lax.axis_index(a) for a in HALO_AXES]
     cnt_ref[...] = jnp.zeros_like(cnt_ref)
     for c in range(CODES):
         offs = (c // 9 - 1, c // 3 % 3 - 1, c % 3 - 1)
         inside = jnp.int32(1)
-        for p, o, s in zip(pos, offs, sizes):
+        for p, o, s in zip(pos, offs, GRID):
             if o < 0:
                 inside = inside * (p > 0).astype(I32)
             if o > 0:
@@ -148,22 +148,41 @@
     return pairs
 
 
-def fill_ghosts(mid_ref, low_ref, high_ref, ghosts):
+def fill_ghosts(pos_ref, mid_ref, low_ref, high_ref, ghosts):
+    first = [pos_ref[i] == 0 for i in range(3)]
+    final = [pos_ref[i] == n - 1 for i, n in enumerate(GRID)]
     for s, p in enumerate(OUTER):
         a, b, c = p // 16, p // 4 % 4, p % 4
+        absent = None
+        for i, at in enumerate((a, b, c)):
+            if at in (0, 3):
+                edge = first[i] if at == 0 else final[i]
+                absent = edge if absent is None else absent | edge
         if c == 0:
             slab = low_ref[a, b]
         elif c == 3:
             slab = high_ref[a, b]
         else:
             slab = mid_ref[a, b, c - 1]
+        slab = jnp.where(absent, MARK, slab.astype(F32)).astype(BF16)
         ghosts[s * SLAB : (s + 1) * SLAB, :] = slab
 
 
 def index_kernel(
-    nbr_ref, valid_ref, cnt_ref, mid_ref, low_ref, high_ref, idx_ref, steps_ref, dead_ref, ghosts, held
+    pos_ref,
+    nbr_ref,
+    valid_ref,
+    cnt_ref,
+    mid_ref,
+    low_ref,
+    high_ref,
+    idx_ref,
+    steps_ref,
+    dead_ref,
+    ghosts,
+    held,
 ):
-    fill_ghosts(mid_ref, low_ref, high_ref, ghosts)
+    fill_ghosts(pos_ref, mid_ref, low_ref, high_ref, ghosts)
     alive = jnp.where(ghosts[...].astype(F32) < MARK * 0.5, 1.0, 0.0).astype(BF16)
     at = iota((W, GHOSTS), 1)
     bit = jnp.left_shift(1, at & 15).astype(F32)
@@ -203,14 +222,14 @@
         used = jnp.zeros((8, W), F32)
         for k in range(DEG):
             used = used + jnp.where(keys[k] < DUMMY, 1.0, 0.0)
-            idx_ref[k * 32 + b * 8 : k * 32 + (b + 1) * 8, :] = keys[k].astype(I32)
+            idx_ref[pl.ds(b * 8 * DEG + k, 8, stride=DEG), :] = keys[k].astype(I32)
         for shift in (1, 2, 4, 8):
             used = jnp.maximum(used, pltpu.roll(used, W - shift, 1))
         steps_ref[b * 8 : (b + 1) * 8, :] = used.astype(I32)
         dead_ref[b * 8 : (b + 1) * 8, :] = dead
 
 
-def indices(nbr, valid, cnt, mid, low, high):
+def indices(pos, nbr, valid, cnt, mid, low, high):
     return pl.pallas_call(
         index_kernel,
         out_shape=[
@@ -218,22 +237,24 @@
             jax.ShapeDtypeStruct((32, W), I32),
             jax.ShapeDtypeStruct((32, W), F32),
         ],
-        in_specs=[vmem()] * 6,
+        in_specs=[smem()] + [vmem()] * 6,
         out_specs=[vmem()] * 3,
         scratch_shapes=[pltpu.VMEM((GHOSTS, W), BF16), pltpu.VMEM((32 * DEG, W), I32)],
         compiler_params=pltpu.CompilerParams(vmem_limit_bytes=VMEM_LIMIT),
         name="indices",
-    )(nbr, valid, cnt, mid, low, high)
+    )(pos, nbr, valid, cnt, mid, low, high)
 
 
 GROUP = 16
 FIRST = 8
 TAILS = (0, 2, 4, 6, 8, 10, 12, 16)
 DUMP = ROWS
+PARTS = ((0, 3), (3, 11), (11, CODES))
 
 
 def layer_kernel(
-    idx_ref,
+    idx_hbm,
+    pos_ref,
     steps_ref,
     cnt_ref,
     gidx_ref,
@@ -257,11 +278,18 @@
     agg,
     full,
     picked,
+    idx_ref,
+    sems,
 ):
+    copies = []
+    for i, (lo, hi) in enumerate(PARTS):
+        words = pl.ds(lo * DEG * W, (hi - lo) * DEG * W)
+        copies.append(pltpu.make_async_copy(idx_hbm.at[words], idx_ref.at[words], sems.at[i]))
+        copies[-1].start()
     w_recv = efirst_ref[0:W, :]
     w_send = efirst_ref[W : 2 * W, :]
     w_both = jnp.concatenate([w_recv, w_send], axis=1)
-    fill_ghosts(mid_ref, low_ref, high_ref, ghosts)
+    fill_ghosts(pos_ref, mid_ref, low_ref, high_ref, ghosts)
 
     def own(i, carry):
         rows = pl.ds(pl.multiple_of(i * 384, 384), 384)
@@ -295,7 +323,7 @@
         for half in range(2):
             got = None
             for r in range(8):
-                at = idx_ref[base + (k * (32 * W) + half * 8 + r)]
+                at = idx_ref[base + (k * W + half * 8 + r)]
                 row = jnp.broadcast_to(table[pl.ds(at, 1), :], (8, W))
                 got = row if got is None else jnp.where(sub == r, row, got)
             both.append(jnp.maximum(got + mine[half], 0.0))
@@ -303,11 +331,14 @@
 
     def sender(c, last):
         groups = lax.shift_right_logical(cnt_ref[c, 0] + (GROUP - 1), 4)
+        for (lo, _), copy in zip(PARTS, copies):
+            pl.when(c == lo)(copy.wait)
 
         def gather(g, last):
             q0 = pl.multiple_of(g * GROUP, GROUP)
-            base = c * W + q0
-            mine = [recv[pl.ds(pl.multiple_of(base + h * 8, 8), 8), :] for h in range(2)]
+            home = c * W + q0
+            base = c * (DEG * W) + q0
+            mine = [recv[pl.ds(pl.multiple_of(home + h * 8, 8), 8), :] for h in range(2)]
             finish(hidden[...], last)
             for k in range(FIRST):
                 step(base, mine, k)
@@ -326,7 +357,7 @@
                 return run
 
             lax.switch(which, [tail(t) for t in TAILS])
-            return base
+            return home
 
         return lax.fori_loop(0, groups, gather, last)
 
@@ -377,14 +408,14 @@
     slab_ref[...] = picked[...].astype(BF16)
 
 
-def one_layer(idx, steps, cnt, gidx, dead, state, mid, low, high, weights):
+def one_layer(idx, pos, steps, cnt, gidx, dead, state, mid, low, high, weights):
     return pl.pallas_call(
         layer_kernel,
         out_shape=[
             jax.ShapeDtypeStruct((ROWS, W), BF16),
             jax.ShapeDtypeStruct((8 * SLAB, W), BF16),
         ],
-        in_specs=[smem()] * 4 + [vmem()] * 11,
+        in_specs=[pl.BlockSpec(memory_space=pl.ANY)] + [smem()] * 4 + [vmem()] * 11,
         out_specs=[vmem()] * 2,
         scratch_shapes=[
             pltpu.VMEM((NODES + 8, W), F32),
@@ -394,15 +425,17 @@
             pltpu.VMEM((ROWS + GROUP, W), F32),
             pltpu.VMEM((ROWS, W), F32),
             pltpu.VMEM((8 * SLAB, W), F32),
+            pltpu.SMEM((ROWS * DEG,), I32),
+            pltpu.SemaphoreType.DMA((len(PARTS),)),
         ],
         compiler_params=pltpu.CompilerParams(vmem_limit_bytes=VMEM_LIMIT),
         name="layer",
-    )(idx, steps, cnt, gidx, dead, state, mid, low, high, *weights)
+    )(idx, pos, steps, cnt, gidx, dead, state, mid, low, high, *weights)
 
 
 def both_ways(up, down, axis):
     n = lax.axis_size(axis)
-    forward = [(i, i + 1) for i in range(n - 1)]
+    forward = [(i, (i + 1) % n) for i in range(n)]
     backward = [(b, a) for a, b in forward]
     return lax.ppermute(up, axis, forward), lax.ppermute(down, axis, backward)
 
@@ -443,6 +476,7 @@
     nbr = neighbours[0, 0, 0].T
     mask = valid[0, 0, 0].T
     gidx = ghost_index.reshape(-1)
+    pos = jnp.stack([lax.axis_index(a) for a in HALO_AXES]).astype(I32)
     buffer = pack(dest, latent[0, 0, 0])
     moved = migrate(buffer.reshape(3, 3, 3, W, W))
     state, cnt, slabs = receive(gidx, moved.reshape(CODES, W, W))
@@ -453,9 +487,9 @@
         ]
         mid, low, high = surround(slabs)
         if layer == 0:
-            idx, steps, dead = indices(nbr, mask, cnt, mid, low, high)
+            idx, steps, dead = indices(pos, nbr, mask, cnt, mid, low, high)
             idx = idx.reshape(-1)
-        state, slabs = one_layer(idx, steps, cnt, gidx, dead, state, mid, low, high, weights)
+        state, slabs = one_layer(idx, pos, steps, cnt, gidx, dead, state, mid, low, high, weights)
     return state.reshape(1, 1, 1, ROWS, W)
 
 

time: 211 us -> 166 us (0.79)
  starting transfers between devices: 49.7 us -> 16.8 us
  Pallas kernels: 114 us -> 101 us
    ppermute x18, starting transfers between devices: 49.7 us -> 16.8 us  [both_ways(): return (lax.ppermute(up, axis, forward), lax.ppermute(down, axis, backward))]
    pallas_call x2, Pallas kernels: 104 us -> 90 us  [one_layer(): pl.pallas_call(layer_kernel, out_shape=[jax.ShapeDtypeStruct((ROWS, W), B...]
  transfers between devices with their start and end apart: 18 -> 18, of which waited for: 13 -> 16; matrix products, arithmetic and copies ran while one was open for 2% -> 3% of each run, Pallas kernels for 0% -> 0%
where the time goes in v3:
time: 166 us; the launch traced here: 165 us
  Pallas kernels  101 us (61%)
  waiting for transfers between devices  36.5 us (22%)
  starting transfers between devices  16.8 us (10%)
  local copies, waits for them, and re-layouts  8.9 us (5%)
  other arithmetic  1.85 us (1%)
    pallas_call x2, Pallas kernels, one_layer(): pl.pallas_call(layer_kernel, out_shape=[jax.ShapeDtypeStruct((ROWS, W), B...  90 us
    ppermute x18, waiting for transfers between devices, both_ways(): return (lax.ppermute(up, axis, forward), lax.ppermute(down, axis, backward))  36.5 us
    ppermute x18, starting transfers between devices, both_ways(): return (lax.ppermute(up, axis, forward), lax.ppermute(down, axis, backward))  16.8 us
    pallas_call x1, Pallas kernels, pack(): pl.pallas_call(pack_kernel, out_shape=jax.ShapeDtypeStruct((CODES, W, W),...  5.04 us
  transfers between devices with their start and end apart: 18, of which 16 were waited for; matrix products, arithmetic and copies ran while one was open for 3% of the time, Pallas kernels for 0%

profile of v3, /device:TPU:106, one launch (start us, length us, event | category | flops | bytes accessed | tf_op | source)
XLA Modules:
  0.0 165.2 jit_solution(5376279223688981556)
XLA Ops:
  0.0 5.0 %pack.1 = bf16[27,128,128]{2,1,0:T(8,128)(2,1)} custom-call(s32[1,1024]{1,0:T(1,128)} %bitcast.72, bf16[1024,128]{1,0:T(8,128)(2,1)} %bitcast.67), custom_call_target="tpu_custom_call" | custom-call | tf_op jit(solution)/shard_map/pack/pallas_call | solution.py:75
  5.0 1.2 fusion.2
  6.9 1.5 collective-permute-start
  8.4 6.7 %collective-permute-done.1 = bf16[1,3,3,128,128]{4,3,2,1,0:T(8,128)(2,1)S(1)} collective-permute-done((bf16[1,3,3,128,128]{4,3,2,1,0:T(8,128)(2,1)S(1)}, bf16[1,3,3,128,128]{4,3,2,1,0:T(8,128)(2,1)S(1)}, u32[]{:S(2)}, u32[]{:S(2)}) %collective-permute-start.1) | collective-permute-done | bytes 294944 | tf_op jit(solution)/shard_map/ppermute | solution.py:440
  15.1 1.3 collective-permute-done
  16.5 1.6 collective-permute-start.2
  18.6 5.8 %collective-permute-done.2 = bf16[3,1,3,128,128]{4,3,2,1,0:T(8,128)(2,1)S(1)} collective-permute-done((bf16[3,1,3,128,128]{4,3,2,1,0:T(8,128)(2,1)S(1)}, bf16[3,1,3,128,128]{4,3,2,1,0:T(8,128)(2,1)S(1)}, u32[]{:S(2)}, u32[]{:S(2)}) %collective-permute-start.2) | collective-permute-done | bytes 294944 | tf_op jit(solution)/shard_map/ppermute | solution.py:440
  24.5 1.3 collective-permute-done.3
  26.0 1.7 %collective-permute-start.5 = (bf16[3,3,1,128,128]{4,3,2,1,0:T(8,128)(2,1)S(1)}, bf16[3,3,1,128,128]{4,3,2,1,0:T(8,128)(2,1)S(1)}, u32[]{:S(2)}, u32[]{:S(2)}) collective-permute-start(bf16[3,3,1,128,128]{4,3,2,1,0:T(8,128)(2,1)S(1)} %get-tuple-element.24), channel_id=1, source_target_pairs={{1,0},{2,1},{3,2},{4,3},{5,4},{6,5},{7,6},{0,7},{9,8},{10,9},{11,1... | collective-permute-start | bytes 884744 | tf_op jit(solution)/shard_map/ppermute | solution.py:440
  28.4 3.7 %collective-permute-done.4 = bf16[3,3,1,128,128]{4,3,2,1,0:T(8,128)(2,1)S(1)} collective-permute-done((bf16[3,3,1,128,128]{4,3,2,1,0:T(8,128)(2,1)S(1)}, bf16[3,3,1,128,128]{4,3,2,1,0:T(8,128)(2,1)S(1)}, u32[]{:S(2)}, u32[]{:S(2)}) %collective-permute-start.4) | collective-permute-done | bytes 294944 | tf_op jit(solution)/shard_map/ppermute | solution.py:440
  32.1 1.0 pad_maximum_fusion.2
  33.1 3.0 %receive.1 = (bf16[3456,128]{1,0:T(8,128)(2,1)}, s32[32,128]{1,0:T(8,128)}, bf16[256,128]{1,0:T(8,128)(2,1)}) custom-call(s32[256]{0:T(256)} %reshape.29.gidx_ref, bf16[27,128,128]{2,1,0:T(8,128)(2,1)} %bitcast.57), custom_call_target="tpu_custom_call" | custom-call | tf_op jit(solution)/shard_map/receive/pallas_call | solution.py:118
  36.1 0.8 fusion.6
  37.9 2.5 %collective-permute-start.7 = (bf16[1,2,2,32,128]{4,3,1,0,2:T(8,128)(2,1)S(1)}, bf16[1,2,2,32,128]{4,3,1,0,2:T(8,128)(2,1)S(1)}, u32[]{:S(2)}, u32[]{:S(2)}) collective-permute-start(bf16[1,2,2,32,128]{4,3,1,0,2:T(8,128)(2,1)S(1)} %copy.16), channel_id=1, source_target_pairs={{32,0},{64,32},{96,64},{0,96},{33,1},{65,33},{97,65},{1,97},{34,2}... | collective-permute-start | bytes 98312 | tf_op jit(solution)/shard_map/ppermute | solution.py:440
  40.4 1.3 collective-permute-done.6
  42.3 1.4 collective-permute-start.8
  43.7 0.7 collective-permute-start.9
  45.1 1.6 collective-permute-done.8
  46.7 1.3 collective-permute-done.9
  50.9 1.6 collective-permute-done.10.low_ref
  53.1 3.0 %indices.1 = (s32[768,128]{1,0:T(8,128)}, s32[32,128]{1,0:T(8,128)}, f32[32,128]{1,0:T(8,128)}) custom-call(s32[3]{0:T(128)} %pad_add_fusion.pos_ref, s32[24,3456]{1,0:T(8,128)} %bitcast.61, s32[24,3456]{1,0:T(8,128)} %bitcast.62, s32[32,128]{1,0:T(8,128)} %get-tuple-element.14.cnt_ref, bf16[4,4,2,32,128]{4,3,2,1,0:T(8,128)(2,1)} %copy.18.mid_ref, ...), custom_call_target="tpu_custom_call" | custom-call | tf_op jit(solution)/shard_map/indices/pallas_call | solution.py:233
  56.2 45.0 %layer.2 = (bf16[3456,128]{1,0:T(8,128)(2,1)}, bf16[256,128]{1,0:T(8,128)(2,1)}) custom-call(s32[98304]{0:T(1024)} %bitcast.58, s32[3]{0:T(128)} %pad_add_fusion.pos_ref, s32[32,128]{1,0:T(8,128)} %get-tuple-element.17.steps_ref, s32[32,128]{1,0:T(8,128)} %get-tuple-element.14.cnt_ref, s32[256]{0:T(256)} %reshape.29.gidx_ref, ...), custom_call_target="tpu_custom_call" | custom-call | tf_op jit(solution)/shard_map/layer/pallas_call | solution.py:412
  101.2 0.8 fusion.5
  102.0 2.5 %collective-permute-start.12 = (bf16[1,2,2,32,128]{4,3,1,0,2:T(8,128)(2,1)S(1)}, bf16[1,2,2,32,128]{4,3,1,0,2:T(8,128)(2,1)S(1)}, u32[]{:S(2)}, u32[]{:S(2)}) collective-permute-start(bf16[1,2,2,32,128]{4,3,1,0,2:T(8,128)(2,1)S(1)} %copy.20), channel_id=1, source_target_pairs={{0,32},{32,64},{64,96},{96,0},{1,33},{33,65},{65,97},{97,1},{2,34}... | collective-permute-start | bytes 98312 | tf_op jit(solution)/shard_map/ppermute | solution.py:440
  104.5 1.6 collective-permute-done.12
  106.1 2.3 %collective-permute-done.13 = bf16[1,2,2,32,128]{4,3,1,0,2:T(8,128)(2,1)S(1)} collective-permute-done((bf16[1,2,2,32,128]{4,3,1,0,2:T(8,128)(2,1)S(1)}, bf16[1,2,2,32,128]{4,3,1,0,2:T(8,128)(2,1)S(1)}, u32[]{:S(2)}, u32[]{:S(2)}) %collective-permute-start.13) | collective-permute-done | bytes 32800 | tf_op jit(solution)/shard_map/ppermute | solution.py:440
  108.4 2.4 %collective-permute-start.14 = (bf16[4,1,2,32,128]{4,3,1,0,2:T(8,128)(2,1)S(1)}, bf16[4,1,2,32,128]{4,3,1,0,2:T(8,128)(2,1)S(1)}, u32[]{:S(2)}, u32[]{:S(2)}) collective-permute-start(bf16[4,1,2,32,128]{4,3,1,0,2:T(8,128)(2,1)S(1)} %get-tuple-element.40), channel_id=1, source_target_pairs={{0,8},{8,16},{16,24},{24,0},{1,9},{9,17},{17,25},{25,1},{2,10},{10... | collective-permute-start | bytes 196616 | tf_op jit(solution)/shard_map/ppermute | solution.py:440
  110.8 1.9 %collective-permute-done.14 = bf16[4,1,2,32,128]{4,3,1,0,2:T(8,128)(2,1)S(1)} collective-permute-done((bf16[4,1,2,32,128]{4,3,1,0,2:T(8,128)(2,1)S(1)}, bf16[4,1,2,32,128]{4,3,1,0,2:T(8,128)(2,1)S(1)}, u32[]{:S(2)}, u32[]{:S(2)}) %collective-permute-start.14) | collective-permute-done | bytes 65568 | tf_op jit(solution)/shard_map/ppermute | solution.py:440
  112.8 2.3 %collective-permute-done.15 = bf16[4,1,2,32,128]{4,3,1,0,2:T(8,128)(2,1)S(1)} collective-permute-done((bf16[4,1,2,32,128]{4,3,1,0,2:T(8,128)(2,1)S(1)}, bf16[4,1,2,32,128]{4,3,1,0,2:T(8,128)(2,1)S(1)}, u32[]{:S(2)}, u32[]{:S(2)}) %collective-permute-start.15) | collective-permute-done | bytes 65568 | tf_op jit(solution)/shard_map/ppermute | solution.py:440
  116.4 1.3 collective-permute-done.17.high_ref
  117.7 1.9 %collective-permute-done.16.low_ref = bf16[4,4,32,128]{3,2,1,0:T(8,128)(2,1)S(1)} collective-permute-done((bf16[4,4,32,128]{3,2,1,0:T(8,128)(2,1)S(1)}, bf16[4,4,32,128]{3,2,1,0:T(8,128)(2,1)S(1)}, u32[]{:S(2)}, u32[]{:S(2)}) %collective-permute-start.16) | collective-permute-done | bytes 131104 | tf_op jit(solution)/shard_map/ppermute | solution.py:440
  120.2 45.0 %layer.3 = (bf16[3456,128]{1,0:T(8,128)(2,1)}, bf16[256,128]{1,0:T(8,128)(2,1)}) custom-call(s32[98304]{0:T(1024)} %bitcast.59, s32[3]{0:T(128)} %pad_add_fusion.pos_ref, s32[32,128]{1,0:T(8,128)} %get-tuple-element.17.steps_ref, s32[32,128]{1,0:T(8,128)} %get-tuple-element.14.cnt_ref, s32[256]{0:T(256)} %reshape.29.gidx_ref, ...), custom_call_target="tpu_custom_call" | custom-call | tf_op jit(solution)/shard_map/layer/pallas_call | solution.py:412
  (66 shorter events, 9.9 us)
Async XLA Ops:
  6.3 8.8 %collective-permute-start.1 = (bf16[1,3,3,128,128]{4,3,2,1,0:T(8,128)(2,1)S(1)}, bf16[1,3,3,128,128]{4,3,2,1,0:T(8,128)(2,1)S(1)}, u32[]{:S(2)}, u32[]{:S(2)}) collective-permute-start(bf16[1,3,3,128,128]{4,3,2,1,0:T(8,128)(2,1)S(1)} %bitcast.64), channel_id=1, source_target_pairs={{32,0},{64,32},{96,64},{0,96},{33,1},{65,33},{97,65},{1,97},{34,2}... | collective-permute-start | bytes 884744 | tf_op jit(solution)/shard_map/ppermute | solution.py:440
  6.9 9.5 %collective-permute-start = (bf16[1,3,3,128,128]{4,3,2,1,0:T(8,128)(2,1)S(1)}, bf16[1,3,3,128,128]{4,3,2,1,0:T(8,128)(2,1)S(1)}, u32[]{:S(2)}, u32[]{:S(2)}) collective-permute-start(bf16[1,3,3,128,128]{4,3,2,1,0:T(8,128)(2,1)S(1)} %bitcast.63), channel_id=1, source_target_pairs={{0,32},{32,64},{64,96},{96,0},{1,33},{33,65},{65,97},{97,1},{2,34}... | collective-permute-start | bytes 884744 | tf_op jit(solution)/shard_map/ppermute | solution.py:440
  16.5 7.9 %collective-permute-start.2 = (bf16[3,1,3,128,128]{4,3,2,1,0:T(8,128)(2,1)S(1)}, bf16[3,1,3,128,128]{4,3,2,1,0:T(8,128)(2,1)S(1)}, u32[]{:S(2)}, u32[]{:S(2)}) collective-permute-start(bf16[3,1,3,128,128]{4,3,2,1,0:T(8,128)(2,1)S(1)} %get-tuple-element.26), channel_id=1, source_target_pairs={{0,8},{8,16},{16,24},{24,0},{1,9},{9,17},{17,25},{25,1},{2,10},{10... | collective-permute-start | bytes 884744 | tf_op jit(solution)/shard_map/ppermute | solution.py:440
  18.2 7.6 %collective-permute-start.3 = (bf16[3,1,3,128,128]{4,3,2,1,0:T(8,128)(2,1)S(1)}, bf16[3,1,3,128,128]{4,3,2,1,0:T(8,128)(2,1)S(1)}, u32[]{:S(2)}, u32[]{:S(2)}) collective-permute-start(bf16[3,1,3,128,128]{4,3,2,1,0:T(8,128)(2,1)S(1)} %get-tuple-element.27), channel_id=1, source_target_pairs={{8,0},{16,8},{24,16},{0,24},{9,1},{17,9},{25,17},{1,25},{10,2},{18... | collective-permute-start | bytes 884744 | tf_op jit(solution)/shard_map/ppermute | solution.py:440
  25.9 1.9 %copy-start.12 = (s32[1,1,1,8,32]{4,3,2,1,0:T(8,128)S(1)}, s32[1,1,1,8,32]{4,3,2,1,0:T(8,128)}, u32[]{:S(2)}) copy-start(s32[1,1,1,8,32]{4,3,2,1,0:T(8,128)} %param.15) | copy-start | bytes 3076
  26.0 6.2 %collective-permute-start.4 = (bf16[3,3,1,128,128]{4,3,2,1,0:T(8,128)(2,1)S(1)}, bf16[3,3,1,128,128]{4,3,2,1,0:T(8,128)(2,1)S(1)}, u32[]{:S(2)}, u32[]{:S(2)}) collective-permute-start(bf16[3,3,1,128,128]{4,3,2,1,0:T(8,128)(2,1)S(1)} %get-tuple-element.23), channel_id=1, source_target_pairs={{0,1},{1,2},{2,3},{3,4},{4,5},{5,6},{6,7},{7,0},{8,9},{9,10},{10,1... | collective-permute-start | bytes 884744 | tf_op jit(solution)/shard_map/ppermute | solution.py:440
  26.0 6.1 %collective-permute-start.5 = (bf16[3,3,1,128,128]{4,3,2,1,0:T(8,128)(2,1)S(1)}, bf16[3,3,1,128,128]{4,3,2,1,0:T(8,128)(2,1)S(1)}, u32[]{:S(2)}, u32[]{:S(2)}) collective-permute-start(bf16[3,3,1,128,128]{4,3,2,1,0:T(8,128)(2,1)S(1)} %get-tuple-element.24), channel_id=1, source_target_pairs={{1,0},{2,1},{3,2},{4,3},{5,4},{6,5},{7,6},{0,7},{9,8},{10,9},{11,1... | collective-permute-start | bytes 884744 | tf_op jit(solution)/shard_map/ppermute | solution.py:440
  33.1 4.1 %copy-start.7 = (bf16[2,256,128]{2,1,0:T(8,128)(2,1)S(1)}, bf16[2,256,128]{2,1,0:T(8,128)(2,1)}, u32[]{:S(2)}) copy-start(bf16[2,256,128]{2,1,0:T(8,128)(2,1)} %param.16) | copy-start | bytes 393220
  36.1 1.1 copy-start.6
  36.9 4.8 %collective-permute-start.6 = (bf16[1,2,2,32,128]{4,3,1,0,2:T(8,128)(2,1)S(1)}, bf16[1,2,2,32,128]{4,3,1,0,2:T(8,128)(2,1)S(1)}, u32[]{:S(2)}, u32[]{:S(2)}) collective-permute-start(bf16[1,2,2,32,128]{4,3,1,0,2:T(8,128)(2,1)S(1)} %copy.15), channel_id=1, source_target_pairs={{0,32},{32,64},{64,96},{96,0},{1,33},{33,65},{65,97},{97,1},{2,34}... | collective-permute-start | bytes 98312 | tf_op jit(solution)/shard_map/ppermute | solution.py:440
  37.9 3.8 %copy-start.3 = (bf16[256,128]{1,0:T(8,128)(2,1)S(1)}, bf16[256,128]{1,0:T(8,128)(2,1)}, u32[]{:S(2)}) copy-start(bf16[256,128]{1,0:T(8,128)(2,1)} %get-tuple-element.15) | copy-start | bytes 196612
  37.9 4.4 %collective-permute-start.7 = (bf16[1,2,2,32,128]{4,3,1,0,2:T(8,128)(2,1)S(1)}, bf16[1,2,2,32,128]{4,3,1,0,2:T(8,128)(2,1)S(1)}, u32[]{:S(2)}, u32[]{:S(2)}) collective-permute-start(bf16[1,2,2,32,128]{4,3,1,0,2:T(8,128)(2,1)S(1)} %copy.16), channel_id=1, source_target_pairs={{32,0},{64,32},{96,64},{0,96},{33,1},{65,33},{97,65},{1,97},{34,2}... | collective-permute-start | bytes 98312 | tf_op jit(solution)/shard_map/ppermute | solution.py:440
  42.3 2.1 %copy-start.8 = (bf16[2,128,128]{2,1,0:T(8,128)(2,1)S(1)}, bf16[2,128,128]{2,1,0:T(8,128)(2,1)}, u32[]{:S(2)}) copy-start(bf16[2,128,128]{2,1,0:T(8,128)(2,1)} %param.18) | copy-start | bytes 196612
  42.3 2.1 %copy-start.9 = (bf16[2,128,128]{2,1,0:T(8,128)(2,1)S(1)}, bf16[2,128,128]{2,1,0:T(8,128)(2,1)}, u32[]{:S(2)}) copy-start(bf16[2,128,128]{2,1,0:T(8,128)(2,1)} %param.17) | copy-start | bytes 196612
  42.3 4.3 %collective-permute-start.8 = (bf16[4,1,2,32,128]{4,3,1,0,2:T(8,128)(2,1)S(1)}, bf16[4,1,2,32,128]{4,3,1,0,2:T(8,128)(2,1)S(1)}, u32[]{:S(2)}, u32[]{:S(2)}) collective-permute-start(bf16[4,1,2,32,128]{4,3,1,0,2:T(8,128)(2,1)S(1)} %get-tuple-element.42), channel_id=1, source_target_pairs={{0,8},{8,16},{16,24},{24,0},{1,9},{9,17},{17,25},{25,1},{2,10},{10... | collective-permute-start | bytes 196616 | tf_op jit(solution)/shard_map/ppermute | solution.py:440
  43.7 4.3 %collective-permute-start.9 = (bf16[4,1,2,32,128]{4,3,1,0,2:T(8,128)(2,1)S(1)}, bf16[4,1,2,32,128]{4,3,1,0,2:T(8,128)(2,1)S(1)}, u32[]{:S(2)}, u32[]{:S(2)}) collective-permute-start(bf16[4,1,2,32,128]{4,3,1,0,2:T(8,128)(2,1)S(1)} %get-tuple-element.43), channel_id=1, source_target_pairs={{8,0},{16,8},{24,16},{0,24},{9,1},{17,9},{25,17},{1,25},{10,2},{18... | collective-permute-start | bytes 196616 | tf_op jit(solution)/shard_map/ppermute | solution.py:440
  48.0 0.8 copy-start.10
  48.0 0.9 copy-start.11
  48.0 2.8 %collective-permute-start.11 = (bf16[4,4,32,128]{3,2,1,0:T(8,128)(2,1)S(1)}, bf16[4,4,32,128]{3,2,1,0:T(8,128)(2,1)S(1)}, u32[]{:S(2)}, u32[]{:S(2)}) collective-permute-start(bf16[4,4,32,128]{3,2,1,0:T(8,128)(2,1)S(1)} %get-tuple-element.34), channel_id=1, source_target_pairs={{1,0},{2,1},{3,2},{4,3},{5,4},{6,5},{7,6},{0,7},{9,8},{10,9},{11,1... | collective-permute-start | bytes 393224 | tf_op jit(solution)/shard_map/ppermute | solution.py:440
  48.1 4.4 %collective-permute-start.10 = (bf16[4,4,32,128]{3,2,1,0:T(8,128)(2,1)S(1)}, bf16[4,4,32,128]{3,2,1,0:T(8,128)(2,1)S(1)}, u32[]{:S(2)}, u32[]{:S(2)}) collective-permute-start(bf16[4,4,32,128]{3,2,1,0:T(8,128)(2,1)S(1)} %get-tuple-element.35), channel_id=1, source_target_pairs={{0,1},{1,2},{2,3},{3,4},{4,5},{5,6},{6,7},{7,0},{8,9},{9,10},{10,1... | collective-permute-start | bytes 393224 | tf_op jit(solution)/shard_map/ppermute | solution.py:440
  50.9 1.6 copy-start
  52.5 0.7 copy-start.1
  102.0 4.1 %collective-permute-start.12 = (bf16[1,2,2,32,128]{4,3,1,0,2:T(8,128)(2,1)S(1)}, bf16[1,2,2,32,128]{4,3,1,0,2:T(8,128)(2,1)S(1)}, u32[]{:S(2)}, u32[]{:S(2)}) collective-permute-start(bf16[1,2,2,32,128]{4,3,1,0,2:T(8,128)(2,1)S(1)} %copy.20), channel_id=1, source_target_pairs={{0,32},{32,64},{64,96},{96,0},{1,33},{33,65},{65,97},{97,1},{2,34}... | collective-permute-start | bytes 98312 | tf_op jit(solution)/shard_map/ppermute | solution.py:440
  104.5 1.6 copy-start.2
  104.5 3.9 %collective-permute-start.13 = (bf16[1,2,2,32,128]{4,3,1,0,2:T(8,128)(2,1)S(1)}, bf16[1,2,2,32,128]{4,3,1,0,2:T(8,128)(2,1)S(1)}, u32[]{:S(2)}, u32[]{:S(2)}) collective-permute-start(bf16[1,2,2,32,128]{4,3,1,0,2:T(8,128)(2,1)S(1)} %copy.21), channel_id=1, source_target_pairs={{32,0},{64,32},{96,64},{0,96},{33,1},{65,33},{97,65},{1,97},{34,2}... | collective-permute-start | bytes 98312 | tf_op jit(solution)/shard_map/ppermute | solution.py:440
  108.4 4.3 %collective-permute-start.14 = (bf16[4,1,2,32,128]{4,3,1,0,2:T(8,128)(2,1)S(1)}, bf16[4,1,2,32,128]{4,3,1,0,2:T(8,128)(2,1)S(1)}, u32[]{:S(2)}, u32[]{:S(2)}) collective-permute-start(bf16[4,1,2,32,128]{4,3,1,0,2:T(8,128)(2,1)S(1)} %get-tuple-element.40), channel_id=1, source_target_pairs={{0,8},{8,16},{16,24},{24,0},{1,9},{9,17},{17,25},{25,1},{2,10},{10... | collective-permute-start | bytes 196616 | tf_op jit(solution)/shard_map/ppermute | solution.py:440
  110.8 4.3 %collective-permute-start.15 = (bf16[4,1,2,32,128]{4,3,1,0,2:T(8,128)(2,1)S(1)}, bf16[4,1,2,32,128]{4,3,1,0,2:T(8,128)(2,1)S(1)}, u32[]{:S(2)}, u32[]{:S(2)}) collective-permute-start(bf16[4,1,2,32,128]{4,3,1,0,2:T(8,128)(2,1)S(1)} %get-tuple-element.41), channel_id=1, source_target_pairs={{8,0},{16,8},{24,16},{0,24},{9,1},{17,9},{25,17},{1,25},{10,2},{18... | collective-permute-start | bytes 196616 | tf_op jit(solution)/shard_map/ppermute | solution.py:440
  115.1 2.5 %collective-permute-start.17 = (bf16[4,4,32,128]{3,2,1,0:T(8,128)(2,1)S(1)}, bf16[4,4,32,128]{3,2,1,0:T(8,128)(2,1)S(1)}, u32[]{:S(2)}, u32[]{:S(2)}) collective-permute-start(bf16[4,4,32,128]{3,2,1,0:T(8,128)(2,1)S(1)} %get-tuple-element.32), channel_id=1, source_target_pairs={{1,0},{2,1},{3,2},{4,3},{5,4},{6,5},{7,6},{0,7},{9,8},{10,9},{11,1... | collective-permute-start | bytes 393224 | tf_op jit(solution)/shard_map/ppermute | solution.py:440
  115.2 4.4 %collective-permute-start.16 = (bf16[4,4,32,128]{3,2,1,0:T(8,128)(2,1)S(1)}, bf16[4,4,32,128]{3,2,1,0:T(8,128)(2,1)S(1)}, u32[]{:S(2)}, u32[]{:S(2)}) collective-permute-start(bf16[4,4,32,128]{3,2,1,0:T(8,128)(2,1)S(1)} %get-tuple-element.33), channel_id=1, source_target_pairs={{0,1},{1,2},{2,3},{3,4},{4,5},{5,6},{6,7},{7,0},{8,9},{9,10},{10,1... | collective-permute-start | bytes 393224 | tf_op jit(solution)/shard_map/ppermute | solution.py:440
  117.7 1.9 %copy-start.4 = (bf16[4,4,32,128]{3,2,1,0:T(8,128)(2,1)}, bf16[4,4,32,128]{3,2,1,0:T(8,128)(2,1)S(1)}, u32[]{:S(2)}) copy-start(bf16[4,4,32,128]{3,2,1,0:T(8,128)(2,1)S(1)} %collective-permute-done.17.high_ref) | copy-start | bytes 393220
  119.6 0.6 copy-start.5

commit v4 on v3

--- a/solution.py
+++ b/solution.py
@@ -246,8 +246,9 @@
 
 
 GROUP = 16
-FIRST = 8
-TAILS = (0, 2, 4, 6, 8, 10, 12, 16)
+SPAN = 27
+FIRST = 13
+TAILS = (0, 1, 2, 3, 5, 7, 11)
 DUMP = ROWS
 PARTS = ((0, 3), (3, 11), (11, CODES))
 
@@ -292,28 +293,28 @@
     fill_ghosts(pos_ref, mid_ref, low_ref, high_ref, ghosts)
 
     def own(i, carry):
-        rows = pl.ds(pl.multiple_of(i * 384, 384), 384)
+        rows = pl.ds(pl.multiple_of(i * 1152, 1152), 1152)
         both = dot(state_ref[rows, :], w_both)
         recv[rows, :] = both[:, :W]
         table[rows, :] = both[:, W:]
         return carry
 
-    lax.fori_loop(0, ROWS // 384, own, 0)
+    lax.fori_loop(0, ROWS // 1152, own, 0)
 
     def far(i, carry):
-        x = ghosts[pl.ds(pl.multiple_of(i * 256, 256), 256), :].astype(F32)
+        x = ghosts[pl.ds(pl.multiple_of(i * 896, 128), 896), :].astype(F32)
         x = jnp.where(x < MARK * 0.5, x, 0.0).astype(BF16)
-        table[pl.ds(pl.multiple_of(ROWS + i * 256, 128), 256), :] = dot(x, w_send)
+        table[pl.ds(pl.multiple_of(ROWS + i * 896, 128), 896), :] = dot(x, w_send)
         return carry
 
-    lax.fori_loop(0, GHOSTS // 256, far, 0)
+    lax.fori_loop(0, GHOSTS // 896, far, 0)
     table[NODES : NODES + 8, :] = jnp.full((8, W), -MARK, F32)
 
     w_second = esecond_ref[...]
     sub = iota((8, W), 0)
 
     def finish(h, row):
-        d = jnp.maximum(dot(h, w_second), 0.0)
+        d = jnp.maximum(dot(h, w_second), 0.0).astype(BF16).astype(F32)
         agg[pl.ds(pl.multiple_of(row, GROUP), GROUP), :] = jnp.sum(
             d.reshape(DEG, GROUP, W), axis=0
         )
@@ -373,14 +374,14 @@
     ones = jnp.ones((W, W), BF16)
 
     def node(i, carry):
-        rows = pl.ds(pl.multiple_of(i * 384, 384), 384)
+        rows = pl.ds(pl.multiple_of(i * (SPAN * W), SPAN * W), SPAN * W)
         live = jnp.concatenate(
-            [iota((W, W), 0) < cnt_ref[i * 3 + j, 0] for j in range(3)], axis=0
+            [iota((W, W), 0) < cnt_ref[i * SPAN + j, 0] for j in range(SPAN)], axis=0
         )
         times = jnp.concatenate(
             [
-                jnp.where(eye, jnp.broadcast_to(dead_ref[pl.ds(i * 3 + j, 1), :], (W, W)), 0.0)
-                for j in range(3)
+                jnp.where(eye, jnp.broadcast_to(dead_ref[pl.ds(i * SPAN + j, 1), :], (W, W)), 0.0)
+                for j in range(SPAN)
             ],
             axis=0,
         )
@@ -403,7 +404,7 @@
         out_ref[rows, :] = jnp.where(live, new, 0.0).astype(BF16)
         return carry
 
-    lax.fori_loop(0, ROWS // 384, node, 0)
+    lax.fori_loop(0, ROWS // (SPAN * W), node, 0)
     pick_slabs(gidx_ref, full, picked)
     slab_ref[...] = picked[...].astype(BF16)
 

time: 166 us -> 140 us (0.84)
  Pallas kernels: 101 us -> 75.1 us
    pallas_call x2, Pallas kernels: 90 us -> 64.1 us  [one_layer(): pl.pallas_call(layer_kernel, out_shape=[jax.ShapeDtypeStruct((ROWS, W), B...]
where the time goes in v4:
time: 140 us; the launch traced here: 139 us
  Pallas kernels  75.1 us (54%)
  waiting for transfers between devices  35.2 us (25%)
  starting transfers between devices  17.5 us (12%)
  local copies, waits for them, and re-layouts  8.9 us (6%)
  other arithmetic  1.85 us (1%)
    pallas_call x2, Pallas kernels, one_layer(): pl.pallas_call(layer_kernel, out_shape=[jax.ShapeDtypeStruct((ROWS, W), B...  64.1 us
    ppermute x18, waiting for transfers between devices, both_ways(): return (lax.ppermute(up, axis, forward), lax.ppermute(down, axis, backward))  35.2 us
    ppermute x18, starting transfers between devices, both_ways(): return (lax.ppermute(up, axis, forward), lax.ppermute(down, axis, backward))  17.5 us
    pallas_call x1, Pallas kernels, pack(): pl.pallas_call(pack_kernel, out_shape=jax.ShapeDtypeStruct((CODES, W, W),...  5.05 us
    pallas_call x1, Pallas kernels, indices(): pl.pallas_call(index_kernel, out_shape=[jax.ShapeDtypeStruct((DEG * 32, W...  3.03 us
    pallas_call x1, Pallas kernels, receive(): pl.pallas_call(receive_kernel, out_shape=[jax.ShapeDtypeStruct((ROWS, W),...  2.96 us
  transfers between devices with their start and end apart: 18, of which 16 were waited for; matrix products, arithmetic and copies ran while one was open for 3% of the time, Pallas kernels for 0%

profile of v4, /device:TPU:106, one launch (start us, length us, event | category | flops | bytes accessed | tf_op | source)
XLA Modules:
  0.0 138.9 jit_solution(13758639621663671054)
XLA Ops:
  0.0 5.0 %pack.1 = bf16[27,128,128]{2,1,0:T(8,128)(2,1)} custom-call(s32[1,1024]{1,0:T(1,128)} %bitcast.72, bf16[1024,128]{1,0:T(8,128)(2,1)} %bitcast.67), custom_call_target="tpu_custom_call" | custom-call | tf_op jit(solution)/shard_map/pack/pallas_call | solution.py:75
  5.0 1.2 fusion.2
  6.9 1.5 %collective-permute-start = (bf16[1,3,3,128,128]{4,3,2,1,0:T(8,128)(2,1)S(1)}, bf16[1,3,3,128,128]{4,3,2,1,0:T(8,128)(2,1)S(1)}, u32[]{:S(2)}, u32[]{:S(2)}) collective-permute-start(bf16[1,3,3,128,128]{4,3,2,1,0:T(8,128)(2,1)S(1)} %bitcast.63), channel_id=1, source_target_pairs={{0,32},{32,64},{64,96},{96,0},{1,33},{33,65},{65,97},{97,1},{2,34}... | collective-permute-start | bytes 884744 | tf_op jit(solution)/shard_map/ppermute | solution.py:441
  8.4 6.7 %collective-permute-done.1 = bf16[1,3,3,128,128]{4,3,2,1,0:T(8,128)(2,1)S(1)} collective-permute-done((bf16[1,3,3,128,128]{4,3,2,1,0:T(8,128)(2,1)S(1)}, bf16[1,3,3,128,128]{4,3,2,1,0:T(8,128)(2,1)S(1)}, u32[]{:S(2)}, u32[]{:S(2)}) %collective-permute-start.1) | collective-permute-done | bytes 294944 | tf_op jit(solution)/shard_map/ppermute | solution.py:441
  15.1 1.3 collective-permute-done
  16.5 1.6 %collective-permute-start.2 = (bf16[3,1,3,128,128]{4,3,2,1,0:T(8,128)(2,1)S(1)}, bf16[3,1,3,128,128]{4,3,2,1,0:T(8,128)(2,1)S(1)}, u32[]{:S(2)}, u32[]{:S(2)}) collective-permute-start(bf16[3,1,3,128,128]{4,3,2,1,0:T(8,128)(2,1)S(1)} %get-tuple-element.26), channel_id=1, source_target_pairs={{0,8},{8,16},{16,24},{24,0},{1,9},{9,17},{17,25},{25,1},{2,10},{10... | collective-permute-start | bytes 884744 | tf_op jit(solution)/shard_map/ppermute | solution.py:441
  18.6 5.8 %collective-permute-done.2 = bf16[3,1,3,128,128]{4,3,2,1,0:T(8,128)(2,1)S(1)} collective-permute-done((bf16[3,1,3,128,128]{4,3,2,1,0:T(8,128)(2,1)S(1)}, bf16[3,1,3,128,128]{4,3,2,1,0:T(8,128)(2,1)S(1)}, u32[]{:S(2)}, u32[]{:S(2)}) %collective-permute-start.2) | collective-permute-done | bytes 294944 | tf_op jit(solution)/shard_map/ppermute | solution.py:441
  24.5 1.3 collective-permute-done.3
  26.0 1.7 %collective-permute-start.5 = (bf16[3,3,1,128,128]{4,3,2,1,0:T(8,128)(2,1)S(1)}, bf16[3,3,1,128,128]{4,3,2,1,0:T(8,128)(2,1)S(1)}, u32[]{:S(2)}, u32[]{:S(2)}) collective-permute-start(bf16[3,3,1,128,128]{4,3,2,1,0:T(8,128)(2,1)S(1)} %get-tuple-element.24), channel_id=1, source_target_pairs={{1,0},{2,1},{3,2},{4,3},{5,4},{6,5},{7,6},{0,7},{9,8},{10,9},{11,1... | collective-permute-start | bytes 884744 | tf_op jit(solution)/shard_map/ppermute | solution.py:441
  28.4 3.7 %collective-permute-done.4 = bf16[3,3,1,128,128]{4,3,2,1,0:T(8,128)(2,1)S(1)} collective-permute-done((bf16[3,3,1,128,128]{4,3,2,1,0:T(8,128)(2,1)S(1)}, bf16[3,3,1,128,128]{4,3,2,1,0:T(8,128)(2,1)S(1)}, u32[]{:S(2)}, u32[]{:S(2)}) %collective-permute-start.4) | collective-permute-done | bytes 294944 | tf_op jit(solution)/shard_map/ppermute | solution.py:441
  32.1 1.0 pad_maximum_fusion.2
  33.1 3.0 %receive.1 = (bf16[3456,128]{1,0:T(8,128)(2,1)}, s32[32,128]{1,0:T(8,128)}, bf16[256,128]{1,0:T(8,128)(2,1)}) custom-call(s32[256]{0:T(256)} %reshape.29.gidx_ref, bf16[27,128,128]{2,1,0:T(8,128)(2,1)} %bitcast.57), custom_call_target="tpu_custom_call" | custom-call | tf_op jit(solution)/shard_map/receive/pallas_call | solution.py:118
  36.1 0.8 fusion.6
  37.9 2.5 %collective-permute-start.7 = (bf16[1,2,2,32,128]{4,3,1,0,2:T(8,128)(2,1)S(1)}, bf16[1,2,2,32,128]{4,3,1,0,2:T(8,128)(2,1)S(1)}, u32[]{:S(2)}, u32[]{:S(2)}) collective-permute-start(bf16[1,2,2,32,128]{4,3,1,0,2:T(8,128)(2,1)S(1)} %copy.16), channel_id=1, source_target_pairs={{32,0},{64,32},{96,64},{0,96},{33,1},{65,33},{97,65},{1,97},{34,2}... | collective-permute-start | bytes 98312 | tf_op jit(solution)/shard_map/ppermute | solution.py:441
  40.4 1.3 collective-permute-done.6
  42.3 1.4 collective-permute-start.8
  43.7 0.7 collective-permute-start.9
  45.1 1.6 %collective-permute-done.8 = bf16[4,1,2,32,128]{4,3,1,0,2:T(8,128)(2,1)S(1)} collective-permute-done((bf16[4,1,2,32,128]{4,3,1,0,2:T(8,128)(2,1)S(1)}, bf16[4,1,2,32,128]{4,3,1,0,2:T(8,128)(2,1)S(1)}, u32[]{:S(2)}, u32[]{:S(2)}) %collective-permute-start.8) | collective-permute-done | bytes 65568 | tf_op jit(solution)/shard_map/ppermute | solution.py:441
  46.7 1.3 collective-permute-done.9
  50.9 1.6 %collective-permute-done.10.low_ref = bf16[4,4,32,128]{3,2,1,0:T(8,128)(2,1)S(1)} collective-permute-done((bf16[4,4,32,128]{3,2,1,0:T(8,128)(2,1)S(1)}, bf16[4,4,32,128]{3,2,1,0:T(8,128)(2,1)S(1)}, u32[]{:S(2)}, u32[]{:S(2)}) %collective-permute-start.10) | collective-permute-done | bytes 131104 | tf_op jit(solution)/shard_map/ppermute | solution.py:441
  53.1 3.0 %indices.1 = (s32[768,128]{1,0:T(8,128)}, s32[32,128]{1,0:T(8,128)}, f32[32,128]{1,0:T(8,128)}) custom-call(s32[3]{0:T(128)} %pad_add_fusion.pos_ref, s32[24,3456]{1,0:T(8,128)} %bitcast.61, s32[24,3456]{1,0:T(8,128)} %bitcast.62, s32[32,128]{1,0:T(8,128)} %get-tuple-element.14.cnt_ref, bf16[4,4,2,32,128]{4,3,2,1,0:T(8,128)(2,1)} %copy.18.mid_ref, ...), custom_call_target="tpu_custom_call" | custom-call | tf_op jit(solution)/shard_map/indices/pallas_call | solution.py:233
  56.2 32.1 %layer.2 = (bf16[3456,128]{1,0:T(8,128)(2,1)}, bf16[256,128]{1,0:T(8,128)(2,1)}) custom-call(s32[98304]{0:T(1024)} %bitcast.58, s32[3]{0:T(128)} %pad_add_fusion.pos_ref, s32[32,128]{1,0:T(8,128)} %get-tuple-element.17.steps_ref, s32[32,128]{1,0:T(8,128)} %get-tuple-element.14.cnt_ref, s32[256]{0:T(256)} %reshape.29.gidx_ref, ...), custom_call_target="tpu_custom_call" | custom-call | tf_op jit(solution)/shard_map/layer/pallas_call | solution.py:413
  88.2 0.8 fusion.5
  89.0 3.5 %collective-permute-start.12 = (bf16[1,2,2,32,128]{4,3,1,0,2:T(8,128)(2,1)S(1)}, bf16[1,2,2,32,128]{4,3,1,0,2:T(8,128)(2,1)S(1)}, u32[]{:S(2)}, u32[]{:S(2)}) collective-permute-start(bf16[1,2,2,32,128]{4,3,1,0,2:T(8,128)(2,1)S(1)} %copy.20), channel_id=1, source_target_pairs={{0,32},{32,64},{64,96},{96,0},{1,33},{33,65},{65,97},{97,1},{2,34}... | collective-permute-start | bytes 98312 | tf_op jit(solution)/shard_map/ppermute | solution.py:441
  92.5 1.6 %collective-permute-done.12 = bf16[1,2,2,32,128]{4,3,1,0,2:T(8,128)(2,1)S(1)} collective-permute-done((bf16[1,2,2,32,128]{4,3,1,0,2:T(8,128)(2,1)S(1)}, bf16[1,2,2,32,128]{4,3,1,0,2:T(8,128)(2,1)S(1)}, u32[]{:S(2)}, u32[]{:S(2)}) %collective-permute-start.12) | collective-permute-done | bytes 32800 | tf_op jit(solution)/shard_map/ppermute | solution.py:441
  94.1 2.3 %collective-permute-done.13 = bf16[1,2,2,32,128]{4,3,1,0,2:T(8,128)(2,1)S(1)} collective-permute-done((bf16[1,2,2,32,128]{4,3,1,0,2:T(8,128)(2,1)S(1)}, bf16[1,2,2,32,128]{4,3,1,0,2:T(8,128)(2,1)S(1)}, u32[]{:S(2)}, u32[]{:S(2)}) %collective-permute-start.13) | collective-permute-done | bytes 32800 | tf_op jit(solution)/shard_map/ppermute | solution.py:441
  96.5 0.8 collective-permute-start.14
  97.3 1.3 collective-permute-start.15
  98.6 2.2 %collective-permute-done.14 = bf16[4,1,2,32,128]{4,3,1,0,2:T(8,128)(2,1)S(1)} collective-permute-done((bf16[4,1,2,32,128]{4,3,1,0,2:T(8,128)(2,1)S(1)}, bf16[4,1,2,32,128]{4,3,1,0,2:T(8,128)(2,1)S(1)}, u32[]{:S(2)}, u32[]{:S(2)}) %collective-permute-start.14) | collective-permute-done | bytes 65568 | tf_op jit(solution)/shard_map/ppermute | solution.py:441
  102.9 1.3 collective-permute-done.17.high_ref
  104.1 1.9 %collective-permute-done.16.low_ref = bf16[4,4,32,128]{3,2,1,0:T(8,128)(2,1)S(1)} collective-permute-done((bf16[4,4,32,128]{3,2,1,0:T(8,128)(2,1)S(1)}, bf16[4,4,32,128]{3,2,1,0:T(8,128)(2,1)S(1)}, u32[]{:S(2)}, u32[]{:S(2)}) %collective-permute-start.16) | collective-permute-done | bytes 131104 | tf_op jit(solution)/shard_map/ppermute | solution.py:441
  106.7 32.0 %layer.3 = (bf16[3456,128]{1,0:T(8,128)(2,1)}, bf16[256,128]{1,0:T(8,128)(2,1)}) custom-call(s32[98304]{0:T(1024)} %bitcast.59, s32[3]{0:T(128)} %pad_add_fusion.pos_ref, s32[32,128]{1,0:T(8,128)} %get-tuple-element.17.steps_ref, s32[32,128]{1,0:T(8,128)} %get-tuple-element.14.cnt_ref, s32[256]{0:T(256)} %reshape.29.gidx_ref, ...), custom_call_target="tpu_custom_call" | custom-call | tf_op jit(solution)/shard_map/layer/pallas_call | solution.py:413
  (66 shorter events, 10.7 us)
Async XLA Ops:
  6.3 8.8 %collective-permute-start.1 = (bf16[1,3,3,128,128]{4,3,2,1,0:T(8,128)(2,1)S(1)}, bf16[1,3,3,128,128]{4,3,2,1,0:T(8,128)(2,1)S(1)}, u32[]{:S(2)}, u32[]{:S(2)}) collective-permute-start(bf16[1,3,3,128,128]{4,3,2,1,0:T(8,128)(2,1)S(1)} %bitcast.64), channel_id=1, source_target_pairs={{32,0},{64,32},{96,64},{0,96},{33,1},{65,33},{97,65},{1,97},{34,2}... | collective-permute-start | bytes 884744 | tf_op jit(solution)/shard_map/ppermute | solution.py:441
  6.9 9.5 %collective-permute-start = (bf16[1,3,3,128,128]{4,3,2,1,0:T(8,128)(2,1)S(1)}, bf16[1,3,3,128,128]{4,3,2,1,0:T(8,128)(2,1)S(1)}, u32[]{:S(2)}, u32[]{:S(2)}) collective-permute-start(bf16[1,3,3,128,128]{4,3,2,1,0:T(8,128)(2,1)S(1)} %bitcast.63), channel_id=1, source_target_pairs={{0,32},{32,64},{64,96},{96,0},{1,33},{33,65},{65,97},{97,1},{2,34}... | collective-permute-start | bytes 884744 | tf_op jit(solution)/shard_map/ppermute | solution.py:441
  16.5 7.9 %collective-permute-start.2 = (bf16[3,1,3,128,128]{4,3,2,1,0:T(8,128)(2,1)S(1)}, bf16[3,1,3,128,128]{4,3,2,1,0:T(8,128)(2,1)S(1)}, u32[]{:S(2)}, u32[]{:S(2)}) collective-permute-start(bf16[3,1,3,128,128]{4,3,2,1,0:T(8,128)(2,1)S(1)} %get-tuple-element.26), channel_id=1, source_target_pairs={{0,8},{8,16},{16,24},{24,0},{1,9},{9,17},{17,25},{25,1},{2,10},{10... | collective-permute-start | bytes 884744 | tf_op jit(solution)/shard_map/ppermute | solution.py:441
  18.2 7.6 %collective-permute-start.3 = (bf16[3,1,3,128,128]{4,3,2,1,0:T(8,128)(2,1)S(1)}, bf16[3,1,3,128,128]{4,3,2,1,0:T(8,128)(2,1)S(1)}, u32[]{:S(2)}, u32[]{:S(2)}) collective-permute-start(bf16[3,1,3,128,128]{4,3,2,1,0:T(8,128)(2,1)S(1)} %get-tuple-element.27), channel_id=1, source_target_pairs={{8,0},{16,8},{24,16},{0,24},{9,1},{17,9},{25,17},{1,25},{10,2},{18... | collective-permute-start | bytes 884744 | tf_op jit(solution)/shard_map/ppermute | solution.py:441
  25.9 1.9 %copy-start.12 = (s32[1,1,1,8,32]{4,3,2,1,0:T(8,128)S(1)}, s32[1,1,1,8,32]{4,3,2,1,0:T(8,128)}, u32[]{:S(2)}) copy-start(s32[1,1,1,8,32]{4,3,2,1,0:T(8,128)} %param.15) | copy-start | bytes 3076
  26.0 6.2 %collective-permute-start.4 = (bf16[3,3,1,128,128]{4,3,2,1,0:T(8,128)(2,1)S(1)}, bf16[3,3,1,128,128]{4,3,2,1,0:T(8,128)(2,1)S(1)}, u32[]{:S(2)}, u32[]{:S(2)}) collective-permute-start(bf16[3,3,1,128,128]{4,3,2,1,0:T(8,128)(2,1)S(1)} %get-tuple-element.23), channel_id=1, source_target_pairs={{0,1},{1,2},{2,3},{3,4},{4,5},{5,6},{6,7},{7,0},{8,9},{9,10},{10,1... | collective-permute-start | bytes 884744 | tf_op jit(solution)/shard_map/ppermute | solution.py:441
  26.0 6.1 %collective-permute-start.5 = (bf16[3,3,1,128,128]{4,3,2,1,0:T(8,128)(2,1)S(1)}, bf16[3,3,1,128,128]{4,3,2,1,0:T(8,128)(2,1)S(1)}, u32[]{:S(2)}, u32[]{:S(2)}) collective-permute-start(bf16[3,3,1,128,128]{4,3,2,1,0:T(8,128)(2,1)S(1)} %get-tuple-element.24), channel_id=1, source_target_pairs={{1,0},{2,1},{3,2},{4,3},{5,4},{6,5},{7,6},{0,7},{9,8},{10,9},{11,1... | collective-permute-start | bytes 884744 | tf_op jit(solution)/shard_map/ppermute | solution.py:441
  33.1 4.1 %copy-start.7 = (bf16[2,256,128]{2,1,0:T(8,128)(2,1)S(1)}, bf16[2,256,128]{2,1,0:T(8,128)(2,1)}, u32[]{:S(2)}) copy-start(bf16[2,256,128]{2,1,0:T(8,128)(2,1)} %param.16) | copy-start | bytes 393220
  36.1 1.1 copy-start.6
  36.9 4.8 %collective-permute-start.6 = (bf16[1,2,2,32,128]{4,3,1,0,2:T(8,128)(2,1)S(1)}, bf16[1,2,2,32,128]{4,3,1,0,2:T(8,128)(2,1)S(1)}, u32[]{:S(2)}, u32[]{:S(2)}) collective-permute-start(bf16[1,2,2,32,128]{4,3,1,0,2:T(8,128)(2,1)S(1)} %copy.15), channel_id=1, source_target_pairs={{0,32},{32,64},{64,96},{96,0},{1,33},{33,65},{65,97},{97,1},{2,34}... | collective-permute-start | bytes 98312 | tf_op jit(solution)/shard_map/ppermute | solution.py:441
  37.9 3.8 %copy-start.3 = (bf16[256,128]{1,0:T(8,128)(2,1)S(1)}, bf16[256,128]{1,0:T(8,128)(2,1)}, u32[]{:S(2)}) copy-start(bf16[256,128]{1,0:T(8,128)(2,1)} %get-tuple-element.15) | copy-start | bytes 196612
  37.9 4.3 %collective-permute-start.7 = (bf16[1,2,2,32,128]{4,3,1,0,2:T(8,128)(2,1)S(1)}, bf16[1,2,2,32,128]{4,3,1,0,2:T(8,128)(2,1)S(1)}, u32[]{:S(2)}, u32[]{:S(2)}) collective-permute-start(bf16[1,2,2,32,128]{4,3,1,0,2:T(8,128)(2,1)S(1)} %copy.16), channel_id=1, source_target_pairs={{32,0},{64,32},{96,64},{0,96},{33,1},{65,33},{97,65},{1,97},{34,2}... | collective-permute-start | bytes 98312 | tf_op jit(solution)/shard_map/ppermute | solution.py:441
  42.3 2.1 %copy-start.8 = (bf16[2,128,128]{2,1,0:T(8,128)(2,1)S(1)}, bf16[2,128,128]{2,1,0:T(8,128)(2,1)}, u32[]{:S(2)}) copy-start(bf16[2,128,128]{2,1,0:T(8,128)(2,1)} %param.18) | copy-start | bytes 196612
  42.3 2.1 %copy-start.9 = (bf16[2,128,128]{2,1,0:T(8,128)(2,1)S(1)}, bf16[2,128,128]{2,1,0:T(8,128)(2,1)}, u32[]{:S(2)}) copy-start(bf16[2,128,128]{2,1,0:T(8,128)(2,1)} %param.17) | copy-start | bytes 196612
  42.3 4.3 %collective-permute-start.8 = (bf16[4,1,2,32,128]{4,3,1,0,2:T(8,128)(2,1)S(1)}, bf16[4,1,2,32,128]{4,3,1,0,2:T(8,128)(2,1)S(1)}, u32[]{:S(2)}, u32[]{:S(2)}) collective-permute-start(bf16[4,1,2,32,128]{4,3,1,0,2:T(8,128)(2,1)S(1)} %get-tuple-element.42), channel_id=1, source_target_pairs={{0,8},{8,16},{16,24},{24,0},{1,9},{9,17},{17,25},{25,1},{2,10},{10... | collective-permute-start | bytes 196616 | tf_op jit(solution)/shard_map/ppermute | solution.py:441
  43.7 4.3 %collective-permute-start.9 = (bf16[4,1,2,32,128]{4,3,1,0,2:T(8,128)(2,1)S(1)}, bf16[4,1,2,32,128]{4,3,1,0,2:T(8,128)(2,1)S(1)}, u32[]{:S(2)}, u32[]{:S(2)}) collective-permute-start(bf16[4,1,2,32,128]{4,3,1,0,2:T(8,128)(2,1)S(1)} %get-tuple-element.43), channel_id=1, source_target_pairs={{8,0},{16,8},{24,16},{0,24},{9,1},{17,9},{25,17},{1,25},{10,2},{18... | collective-permute-start | bytes 196616 | tf_op jit(solution)/shard_map/ppermute | solution.py:441
  48.0 0.8 copy-start.10
  48.0 0.9 copy-start.11
  48.0 2.8 %collective-permute-start.11 = (bf16[4,4,32,128]{3,2,1,0:T(8,128)(2,1)S(1)}, bf16[4,4,32,128]{3,2,1,0:T(8,128)(2,1)S(1)}, u32[]{:S(2)}, u32[]{:S(2)}) collective-permute-start(bf16[4,4,32,128]{3,2,1,0:T(8,128)(2,1)S(1)} %get-tuple-element.34), channel_id=1, source_target_pairs={{1,0},{2,1},{3,2},{4,3},{5,4},{6,5},{7,6},{0,7},{9,8},{10,9},{11,1... | collective-permute-start | bytes 393224 | tf_op jit(solution)/shard_map/ppermute | solution.py:441
  48.1 4.4 %collective-permute-start.10 = (bf16[4,4,32,128]{3,2,1,0:T(8,128)(2,1)S(1)}, bf16[4,4,32,128]{3,2,1,0:T(8,128)(2,1)S(1)}, u32[]{:S(2)}, u32[]{:S(2)}) collective-permute-start(bf16[4,4,32,128]{3,2,1,0:T(8,128)(2,1)S(1)} %get-tuple-element.35), channel_id=1, source_target_pairs={{0,1},{1,2},{2,3},{3,4},{4,5},{5,6},{6,7},{7,0},{8,9},{9,10},{10,1... | collective-permute-start | bytes 393224 | tf_op jit(solution)/shard_map/ppermute | solution.py:441
  50.9 1.6 %copy-start = (bf16[4,4,32,128]{3,2,1,0:T(8,128)(2,1)}, bf16[4,4,32,128]{3,2,1,0:T(8,128)(2,1)S(1)}, u32[]{:S(2)}) copy-start(bf16[4,4,32,128]{3,2,1,0:T(8,128)(2,1)S(1)} %collective-permute-done.11.high_ref) | copy-start | bytes 393220
  52.5 0.7 copy-start.1
  89.0 5.1 %collective-permute-start.12 = (bf16[1,2,2,32,128]{4,3,1,0,2:T(8,128)(2,1)S(1)}, bf16[1,2,2,32,128]{4,3,1,0,2:T(8,128)(2,1)S(1)}, u32[]{:S(2)}, u32[]{:S(2)}) collective-permute-start(bf16[1,2,2,32,128]{4,3,1,0,2:T(8,128)(2,1)S(1)} %copy.20), channel_id=1, source_target_pairs={{0,32},{32,64},{64,96},{96,0},{1,33},{33,65},{65,97},{97,1},{2,34}... | collective-permute-start | bytes 98312 | tf_op jit(solution)/shard_map/ppermute | solution.py:441
  92.5 1.6 %copy-start.2 = (bf16[256,128]{1,0:T(8,128)(2,1)S(1)}, bf16[256,128]{1,0:T(8,128)(2,1)}, u32[]{:S(2)}) copy-start(bf16[256,128]{1,0:T(8,128)(2,1)} %get-tuple-element.21) | copy-start | bytes 196612
  92.5 3.9 %collective-permute-start.13 = (bf16[1,2,2,32,128]{4,3,1,0,2:T(8,128)(2,1)S(1)}, bf16[1,2,2,32,128]{4,3,1,0,2:T(8,128)(2,1)S(1)}, u32[]{:S(2)}, u32[]{:S(2)}) collective-permute-start(bf16[1,2,2,32,128]{4,3,1,0,2:T(8,128)(2,1)S(1)} %copy.21), channel_id=1, source_target_pairs={{32,0},{64,32},{96,64},{0,96},{33,1},{65,33},{97,65},{1,97},{34,2}... | collective-permute-start | bytes 98312 | tf_op jit(solution)/shard_map/ppermute | solution.py:441
  96.5 4.3 %collective-permute-start.14 = (bf16[4,1,2,32,128]{4,3,1,0,2:T(8,128)(2,1)S(1)}, bf16[4,1,2,32,128]{4,3,1,0,2:T(8,128)(2,1)S(1)}, u32[]{:S(2)}, u32[]{:S(2)}) collective-permute-start(bf16[4,1,2,32,128]{4,3,1,0,2:T(8,128)(2,1)S(1)} %get-tuple-element.40), channel_id=1, source_target_pairs={{0,8},{8,16},{16,24},{24,0},{1,9},{9,17},{17,25},{25,1},{2,10},{10... | collective-permute-start | bytes 196616 | tf_op jit(solution)/shard_map/ppermute | solution.py:441
  97.3 4.3 %collective-permute-start.15 = (bf16[4,1,2,32,128]{4,3,1,0,2:T(8,128)(2,1)S(1)}, bf16[4,1,2,32,128]{4,3,1,0,2:T(8,128)(2,1)S(1)}, u32[]{:S(2)}, u32[]{:S(2)}) collective-permute-start(bf16[4,1,2,32,128]{4,3,1,0,2:T(8,128)(2,1)S(1)} %get-tuple-element.41), channel_id=1, source_target_pairs={{8,0},{16,8},{24,16},{0,24},{9,1},{17,9},{25,17},{1,25},{10,2},{18... | collective-permute-start | bytes 196616 | tf_op jit(solution)/shard_map/ppermute | solution.py:441
  101.6 2.5 %collective-permute-start.17 = (bf16[4,4,32,128]{3,2,1,0:T(8,128)(2,1)S(1)}, bf16[4,4,32,128]{3,2,1,0:T(8,128)(2,1)S(1)}, u32[]{:S(2)}, u32[]{:S(2)}) collective-permute-start(bf16[4,4,32,128]{3,2,1,0:T(8,128)(2,1)S(1)} %get-tuple-element.32), channel_id=1, source_target_pairs={{1,0},{2,1},{3,2},{4,3},{5,4},{6,5},{7,6},{0,7},{9,8},{10,9},{11,1... | collective-permute-start | bytes 393224 | tf_op jit(solution)/shard_map/ppermute | solution.py:441
  101.6 4.4 %collective-permute-start.16 = (bf16[4,4,32,128]{3,2,1,0:T(8,128)(2,1)S(1)}, bf16[4,4,32,128]{3,2,1,0:T(8,128)(2,1)S(1)}, u32[]{:S(2)}, u32[]{:S(2)}) collective-permute-start(bf16[4,4,32,128]{3,2,1,0:T(8,128)(2,1)S(1)} %get-tuple-element.33), channel_id=1, source_target_pairs={{0,1},{1,2},{2,3},{3,4},{4,5},{5,6},{6,7},{7,0},{8,9},{9,10},{10,1... | collective-permute-start | bytes 393224 | tf_op jit(solution)/shard_map/ppermute | solution.py:441
  104.1 1.9 %copy-start.4 = (bf16[4,4,32,128]{3,2,1,0:T(8,128)(2,1)}, bf16[4,4,32,128]{3,2,1,0:T(8,128)(2,1)S(1)}, u32[]{:S(2)}) copy-start(bf16[4,4,32,128]{3,2,1,0:T(8,128)(2,1)S(1)} %collective-permute-done.17.high_ref) | copy-start | bytes 393220
  106.0 0.6 copy-start.5

commit v5 on v4

--- a/solution.py
+++ b/solution.py
@@ -17,11 +17,11 @@
 OUTER = [
     p for p in range(64) if p // 16 in (0, 3) or p // 4 % 4 in (0, 3) or p % 4 in (0, 3)
 ]
+AROUND = 6
 GHOSTS = len(OUTER) * SLAB
 NODES = ROWS + GHOSTS
 DUMMY = NODES
 MARK = 2.0**100
-CH = 4
 HALO_AXES = ("gx", "gy", "gz")
 GRID = (4, 4, 8)
 VMEM_LIMIT = 56 * 2**20
@@ -43,7 +43,7 @@
     return lax.broadcasted_iota(I32, shape, dim)
 
 
-def pack_kernel(dest_ref, rows_ref, out_ref, slot_ref):
+def pack_kernel(dest_ref, rows_ref, down_ref, mid_ref, up_ref, slot_ref):
     n_y, n_z = 4, 8
     ix, iy, iz = (lax.axis_index(a) for a in HALO_AXES)
     tri = (iota((W, W), 0) < iota((W, W), 1)).astype(BF16)
@@ -64,26 +64,31 @@
         off = off + dot(one, ones)
     slot = slot_ref[...]
     rows = rows_ref[...]
-    for c in range(CODES):
-        chosen = jnp.where(slot == iota((W, 1024), 0) + c * W, 1.0, 0.0).astype(BF16)
+    for part, out_ref in enumerate((down_ref, mid_ref, up_ref)):
+        first = part * 9 * W
+        chosen = jnp.where(slot == iota((9 * W, 1024), 0) + first, 1.0, 0.0).astype(BF16)
         got = dot(chosen, rows)
-        alive = iota((W, W), 0).astype(F32) < off[c : c + 1, :]
-        out_ref[c] = jnp.where(alive, got, MARK).astype(BF16)
+        for c in range(9):
+            alive = iota((W, W), 0).astype(F32) < off[part * 9 + c : part * 9 + c + 1, :]
+            block = jnp.where(alive, got[c * W : (c + 1) * W, :], MARK)
+            out_ref[c // 3, c % 3] = block.astype(BF16)
 
 
 def pack(dest, rows):
     return pl.pallas_call(
         pack_kernel,
-        out_shape=jax.ShapeDtypeStruct((CODES, W, W), BF16),
+        out_shape=[jax.ShapeDtypeStruct((3, 3, W, W), BF16)] * 3,
         in_specs=[vmem(), vmem()],
-        out_specs=vmem(),
+        out_specs=[vmem()] * 3,
         scratch_shapes=[pltpu.VMEM((1, 1024), I32)],
         compiler_params=pltpu.CompilerParams(vmem_limit_bytes=VMEM_LIMIT),
         name="pack",
     )(dest, rows)
 
 
-def receive_kernel(gidx_ref, raw_ref, state_ref, cnt_ref, slab_ref, full, picked):
+def receive_kernel(
+    gidx_ref, mid_ref, low_ref, high_ref, state_ref, cnt_ref, down_ref, up_ref, full, picked
+):
     pos = [lax.axis_index(a) for a in HALO_AXES]
     cnt_ref[...] = jnp.zeros_like(cnt_ref)
     for c in range(CODES):
@@ -94,40 +99,46 @@
                 inside = inside * (p > 0).astype(I32)
             if o > 0:
                 inside = inside * (p < s - 1).astype(I32)
-        x = raw_ref[c].astype(F32)
+        if c % 3 == 1:
+            x = mid_ref[c // 9, c // 3 % 3].astype(F32)
+        else:
+            x = (low_ref if c % 3 == 0 else high_ref)[c // 9, c // 3 % 3].astype(F32)
         alive = x < MARK * 0.5
         count = jnp.sum(jnp.where(alive, 1.0, 0.0), axis=0, keepdims=True).astype(I32)
         cnt_ref[c : c + 1, :] = count * inside
         present = iota((W, W), 0) < count * inside
         full[c * W : (c + 1) * W, :] = jnp.where(present, x, MARK)
         state_ref[c * W : (c + 1) * W, :] = jnp.where(present, x, 0.0).astype(BF16)
-    pick_slabs(gidx_ref, full, picked)
-    slab_ref[...] = picked[...].astype(BF16)
-
-
-def pick_slabs(gidx_ref, full, picked):
+    pick_slabs(gidx_ref, full, picked, down_ref, up_ref)
+
+
+def pick_slabs(gidx_ref, full, picked, down_ref, up_ref):
     def some(b, carry):
         for r in range(16):
             picked[pl.ds(b * 16 + r, 1), :] = full[pl.ds(gidx_ref[b * 16 + r], 1), :]
         return carry
 
     lax.fori_loop(0, 16, some, 0)
-
-
-def receive(gidx, raw):
+    for s in range(8):
+        out_ref = up_ref if s // 4 else down_ref
+        out_ref[s // 2 % 2, s % 2] = picked[s * SLAB : (s + 1) * SLAB, :].astype(BF16)
+
+
+def receive(gidx, mid, low, high):
     return pl.pallas_call(
         receive_kernel,
         out_shape=[
             jax.ShapeDtypeStruct((ROWS, W), BF16),
             jax.ShapeDtypeStruct((32, W), I32),
-            jax.ShapeDtypeStruct((8 * SLAB, W), BF16),
+            jax.ShapeDtypeStruct((2, 2, SLAB, W), BF16),
+            jax.ShapeDtypeStruct((2, 2, SLAB, W), BF16),
         ],
-        in_specs=[smem(), vmem()],
-        out_specs=[vmem()] * 3,
+        in_specs=[smem()] + [vmem()] * 3,
+        out_specs=[vmem()] * 4,
         scratch_shapes=[pltpu.VMEM((ROWS, W), F32), pltpu.VMEM((8 * SLAB, W), F32)],
         compiler_params=pltpu.CompilerParams(vmem_limit_bytes=VMEM_LIMIT),
         name="receive",
-    )(gidx, raw)
+    )(gidx, mid, low, high)
 
 
 def sort_pairs(count):
@@ -148,7 +159,7 @@
     return pairs
 
 
-def fill_ghosts(pos_ref, mid_ref, low_ref, high_ref, ghosts):
+def fill_ghosts(pos_ref, around, ghosts):
     first = [pos_ref[i] == 0 for i in range(3)]
     final = [pos_ref[i] == n - 1 for i, n in enumerate(GRID)]
     for s, p in enumerate(OUTER):
@@ -158,12 +169,13 @@
             if at in (0, 3):
                 edge = first[i] if at == 0 else final[i]
                 absent = edge if absent is None else absent | edge
-        if c == 0:
-            slab = low_ref[a, b]
-        elif c == 3:
-            slab = high_ref[a, b]
+        x_low, x_high, y_low, y_high, z_low, z_high = around
+        if c in (0, 3):
+            slab = (z_high if c else z_low)[a, b]
+        elif b in (0, 3):
+            slab = (y_high if b else y_low)[a, c - 1]
         else:
-            slab = mid_ref[a, b, c - 1]
+            slab = (x_high if a else x_low)[b - 1, c - 1]
         slab = jnp.where(absent, MARK, slab.astype(F32)).astype(BF16)
         ghosts[s * SLAB : (s + 1) * SLAB, :] = slab
 
@@ -173,16 +185,10 @@
     nbr_ref,
     valid_ref,
     cnt_ref,
-    mid_ref,
-    low_ref,
-    high_ref,
-    idx_ref,
-    steps_ref,
-    dead_ref,
-    ghosts,
-    held,
+    *refs,
 ):
-    fill_ghosts(pos_ref, mid_ref, low_ref, high_ref, ghosts)
+    around, (idx_ref, steps_ref, dead_ref, ghosts, held) = refs[:AROUND], refs[AROUND:]
+    fill_ghosts(pos_ref, around, ghosts)
     alive = jnp.where(ghosts[...].astype(F32) < MARK * 0.5, 1.0, 0.0).astype(BF16)
     at = iota((W, GHOSTS), 1)
     bit = jnp.left_shift(1, at & 15).astype(F32)
@@ -229,7 +235,7 @@
         dead_ref[b * 8 : (b + 1) * 8, :] = dead
 
 
-def indices(pos, nbr, valid, cnt, mid, low, high):
+def indices(pos, nbr, valid, cnt, around):
     return pl.pallas_call(
         index_kernel,
         out_shape=[
@@ -237,12 +243,12 @@
             jax.ShapeDtypeStruct((32, W), I32),
             jax.ShapeDtypeStruct((32, W), F32),
         ],
-        in_specs=[smem()] + [vmem()] * 6,
+        in_specs=[smem()] + [vmem()] * (3 + AROUND),
         out_specs=[vmem()] * 3,
         scratch_shapes=[pltpu.VMEM((GHOSTS, W), BF16), pltpu.VMEM((32 * DEG, W), I32)],
         compiler_params=pltpu.CompilerParams(vmem_limit_bytes=VMEM_LIMIT),
         name="indices",
-    )(pos, nbr, valid, cnt, mid, low, high)
+    )(pos, nbr, valid, cnt, *around)
 
 
 GROUP = 16
@@ -261,27 +267,12 @@
     gidx_ref,
     dead_ref,
     state_ref,
-    mid_ref,
-    low_ref,
-    high_ref,
-    efirst_ref,
-    esecond_ref,
-    ethird_ref,
-    nfirst_ref,
-    nsecond_ref,
-    nthird_ref,
-    out_ref,
-    slab_ref,
-    table,
-    recv,
-    ghosts,
-    hidden,
-    agg,
-    full,
-    picked,
-    idx_ref,
-    sems,
+    *refs,
 ):
+    around, refs = refs[:AROUND], refs[AROUND:]
+    efirst_ref, esecond_ref, ethird_ref, nfirst_ref, nsecond_ref, nthird_ref = refs[:6]
+    out_ref, down_ref, up_ref = refs[6:9]
+    table, recv, ghosts, hidden, agg, full, picked, idx_ref, sems = refs[9:]
     copies = []
     for i, (lo, hi) in enumerate(PARTS):
         words = pl.ds(lo * DEG * W, (hi - lo) * DEG * W)
@@ -290,7 +281,7 @@
     w_recv = efirst_ref[0:W, :]
     w_send = efirst_ref[W : 2 * W, :]
     w_both = jnp.concatenate([w_recv, w_send], axis=1)
-    fill_ghosts(pos_ref, mid_ref, low_ref, high_ref, ghosts)
+    fill_ghosts(pos_ref, around, ghosts)
 
     def own(i, carry):
         rows = pl.ds(pl.multiple_of(i * 1152, 1152), 1152)
@@ -387,7 +378,7 @@
         )
         times = dot(times.astype(BF16), ones)
         alone = jnp.maximum(recv[rows, :], 0.0).astype(BF16)
-        alone = jnp.maximum(dot(alone, w_second), 0.0)
+        alone = jnp.maximum(dot(alone, w_second), 0.0).astype(BF16).astype(F32)
         summed = jnp.where(live, agg[rows, :] + times * alone, 0.0)
         top = summed.astype(BF16)
         rest = (summed - top.astype(F32)).astype(BF16)
@@ -405,19 +396,19 @@
         return carry
 
     lax.fori_loop(0, ROWS // (SPAN * W), node, 0)
-    pick_slabs(gidx_ref, full, picked)
-    slab_ref[...] = picked[...].astype(BF16)
-
-
-def one_layer(idx, pos, steps, cnt, gidx, dead, state, mid, low, high, weights):
+    pick_slabs(gidx_ref, full, picked, down_ref, up_ref)
+
+
+def one_layer(idx, pos, steps, cnt, gidx, dead, state, around, weights):
     return pl.pallas_call(
         layer_kernel,
         out_shape=[
             jax.ShapeDtypeStruct((ROWS, W), BF16),
-            jax.ShapeDtypeStruct((8 * SLAB, W), BF16),
+            jax.ShapeDtypeStruct((2, 2, SLAB, W), BF16),
+            jax.ShapeDtypeStruct((2, 2, SLAB, W), BF16),
         ],
-        in_specs=[pl.BlockSpec(memory_space=pl.ANY)] + [smem()] * 4 + [vmem()] * 11,
-        out_specs=[vmem()] * 2,
+        in_specs=[pl.BlockSpec(memory_space=pl.ANY)] + [smem()] * 4 + [vmem()] * (8 + AROUND),
+        out_specs=[vmem()] * 3,
         scratch_shapes=[
             pltpu.VMEM((NODES + 8, W), F32),
             pltpu.VMEM((ROWS, W), F32),
@@ -431,7 +422,7 @@
         ],
         compiler_params=pltpu.CompilerParams(vmem_limit_bytes=VMEM_LIMIT),
         name="layer",
-    )(idx, pos, steps, cnt, gidx, dead, state, mid, low, high, *weights)
+    )(idx, pos, steps, cnt, gidx, dead, state, *around, *weights)
 
 
 def both_ways(up, down, axis):
@@ -441,23 +432,29 @@
     return lax.ppermute(up, axis, forward), lax.ppermute(down, axis, backward)
 
 
-def migrate(buffer):
-    for dim, axis in enumerate(HALO_AXES):
-        take = lambda i: lax.index_in_dim(buffer, i, dim, keepdims=True)
-        low, high = both_ways(take(2), take(0), axis)
-        buffer = jnp.concatenate([low, take(1), high], axis=dim)
-    return buffer
-
-
-def surround(slabs):
-    block = slabs.reshape(2, 2, 2, SLAB, W)
-    for dim, axis in enumerate(HALO_AXES[:2]):
-        low, high = both_ways(
-            lax.slice_in_dim(block, 1, 2, axis=dim), lax.slice_in_dim(block, 0, 1, axis=dim), axis
+def migrate(down, mid, up):
+    low, high = both_ways(up, down, "gx")
+    buffer = jnp.stack([low, mid, high])
+    low, high = both_ways(buffer[:, 2], buffer[:, 0], "gy")
+    buffer = jnp.stack([low, buffer[:, 1], high], axis=1)
+    low, high = both_ways(buffer[:, :, 2], buffer[:, :, 0], "gz")
+    return buffer[:, :, 1], low, high
+
+
+def surround(down, up):
+    x_low, x_high = both_ways(up, down, "gx")
+    rows = (x_low, down, up, x_high)
+    y_low, y_high = both_ways(
+        jnp.stack([r[1] for r in rows]), jnp.stack([r[0] for r in rows]), "gy"
+    )
+
+    def face(c):
+        return jnp.stack(
+            [jnp.stack([y_low[a, c], r[0, c], r[1, c], y_high[a, c]]) for a, r in enumerate(rows)]
         )
-        block = jnp.concatenate([low, block, high], axis=dim)
-    low, high = both_ways(block[:, :, 1], block[:, :, 0], "gz")
-    return block, low, high
+
+    z_low, z_high = both_ways(face(1), face(0), "gz")
+    return x_low, x_high, y_low, y_high, z_low, z_high
 
 
 def body(
@@ -478,19 +475,17 @@
     mask = valid[0, 0, 0].T
     gidx = ghost_index.reshape(-1)
     pos = jnp.stack([lax.axis_index(a) for a in HALO_AXES]).astype(I32)
-    buffer = pack(dest, latent[0, 0, 0])
-    moved = migrate(buffer.reshape(3, 3, 3, W, W))
-    state, cnt, slabs = receive(gidx, moved.reshape(CODES, W, W))
+    state, cnt, down, up = receive(gidx, *migrate(*pack(dest, latent[0, 0, 0])))
     for layer in range(edge_first.shape[0]):
         weights = [
             w[layer]
             for w in (edge_first, edge_second, edge_third, node_first, node_second, node_third)
         ]
-        mid, low, high = surround(slabs)
+        around = surround(down, up)
         if layer == 0:
-            idx, steps, dead = indices(pos, nbr, mask, cnt, mid, low, high)
+            idx, steps, dead = indices(pos, nbr, mask, cnt, around)
             idx = idx.reshape(-1)
-        state, slabs = one_layer(idx, pos, steps, cnt, gidx, dead, state, mid, low, high, weights)
+        state, down, up = one_layer(idx, pos, steps, cnt, gidx, dead, state, around, weights)
     return state.reshape(1, 1, 1, ROWS, W)
 
 

time: 140 us -> 140 us (level)
  waiting for transfers between devices: 35.2 us -> 33.6 us
  Pallas kernels: 75.1 us -> 76.5 us
    unnamed x30 -> x50, local copies, waits for them, and re-layouts: 1.67 us -> 4.62 us
    pallas_call x2, Pallas kernels: 64.1 us -> 66.6 us  [one_layer(): pl.pallas_call(layer_kernel, out_shape=[jax.ShapeDtypeStruct((ROWS, W), B...]
    slice x11 -> x7, local copies, waits for them, and re-layouts: 2.99 us -> 0.79 us  [surround(): r[0]]
    ppermute x18, waiting for transfers between devices: 35.2 us -> 33.6 us  [both_ways(): return (lax.ppermute(up, axis, forward), lax.ppermute(down, axis, backward))]
    concatenate x4 -> x0, local copies, waits for them, and re-layouts: 1.49 us -> none  [surround(): block = jnp.concatenate([low, block, high], axis=dim)]
    another operation x0 -> x26, other arithmetic: none -> 1.4 us  [the longest x1 1.05 us: migrate(): buffer = jnp.stack([low, mid, high])]
where the time goes in v5:
time: 140 us; the launch traced here: 139 us
  Pallas kernels  76.5 us (55%)
  waiting for transfers between devices  33.6 us (24%)
  starting transfers between devices  16.8 us (12%)
  local copies, waits for them, and re-layouts  9.73 us (7%)
  other arithmetic  1.96 us (1%)
    pallas_call x2, Pallas kernels, one_layer(): pl.pallas_call(layer_kernel, out_shape=[jax.ShapeDtypeStruct((ROWS, W), B...  66.6 us
    ppermute x18, waiting for transfers between devices, both_ways(): return (lax.ppermute(up, axis, forward), lax.ppermute(down, axis, backward))  33.6 us
    ppermute x18, starting transfers between devices, both_ways(): return (lax.ppermute(up, axis, forward), lax.ppermute(down, axis, backward))  16.8 us
    unnamed x50, local copies, waits for them, and re-layouts  4.62 us
    pallas_call x1, Pallas kernels, pack(): pl.pallas_call(pack_kernel, out_shape=[jax.ShapeDtypeStruct((3, 3, W, W),...  4.05 us
    pallas_call x1, Pallas kernels, indices(): pl.pallas_call(index_kernel, out_shape=[jax.ShapeDtypeStruct((DEG * 32, W...  3.07 us
    pallas_call x1, Pallas kernels, receive(): pl.pallas_call(receive_kernel, out_shape=[jax.ShapeDtypeStruct((ROWS, W),...  2.87 us
  transfers between devices with their start and end apart: 18, of which 16 were waited for; matrix products, arithmetic and copies ran while one was open for 3% of the time, Pallas kernels for 0%

profile of v5, /device:TPU:106, one launch (start us, length us, event | category | flops | bytes accessed | tf_op | source)
XLA Modules:
  0.0 139.1 jit_solution(13496802196845615887)
XLA Ops:
  0.0 4.1 %pack.1 = (bf16[3,3,128,128]{3,2,1,0:T(8,128)(2,1)}, bf16[3,3,128,128]{3,2,1,0:T(8,128)(2,1)}, bf16[3,3,128,128]{3,2,1,0:T(8,128)(2,1)}) custom-call(s32[1,1024]{1,0:T(1,128)} %bitcast.228, bf16[1024,128]{1,0:T(8,128)(2,1)} %bitcast.227), custom_call_target="tpu_custom_call" | custom-call | tf_op jit(solution)/shard_map/pack/pallas_call | solution.py:78
  4.1 1.5 %collective-permute-start = (bf16[3,3,128,128]{3,2,1,0:T(8,128)(2,1)}, bf16[3,3,128,128]{3,2,1,0:T(8,128)(2,1)S(1)}, u32[]{:S(2)}, u32[]{:S(2)}) collective-permute-start(bf16[3,3,128,128]{3,2,1,0:T(8,128)(2,1)} %get-tuple-element.19), channel_id=1, source_target_pairs={{0,32},{32,64},{64,96},{96,0},{1,33},{33,65},{65,97},{97,1},{2,34}... | collective-permute-start | bytes 884744 | tf_op jit(solution)/shard_map/ppermute | solution.py:432
  6.1 6.9 %collective-permute-done = bf16[3,3,128,128]{3,2,1,0:T(8,128)(2,1)S(1)} collective-permute-done((bf16[3,3,128,128]{3,2,1,0:T(8,128)(2,1)}, bf16[3,3,128,128]{3,2,1,0:T(8,128)(2,1)S(1)}, u32[]{:S(2)}, u32[]{:S(2)}) %collective-permute-start) | collective-permute-done | bytes 294944 | tf_op jit(solution)/shard_map/ppermute | solution.py:432
  13.0 1.2 collective-permute-done.1
  14.2 1.1 pad_maximum_fusion
  15.4 1.6 %collective-permute-start.2 = (bf16[3,3,128,128]{3,2,0,1:T(8,128)(2,1)S(1)}, bf16[3,3,128,128]{3,2,0,1:T(8,128)(2,1)S(1)}, u32[]{:S(2)}, u32[]{:S(2)}) collective-permute-start(bf16[3,3,128,128]{3,2,0,1:T(8,128)(2,1)S(1)} %get-tuple-element.36), channel_id=1, source_target_pairs={{0,8},{8,16},{16,24},{24,0},{1,9},{9,17},{17,25},{25,1},{2,10},{10... | collective-permute-start | bytes 884744 | tf_op jit(solution)/shard_map/ppermute | solution.py:432
  17.4 5.5 %collective-permute-done.2 = bf16[3,3,128,128]{3,2,0,1:T(8,128)(2,1)S(1)} collective-permute-done((bf16[3,3,128,128]{3,2,0,1:T(8,128)(2,1)S(1)}, bf16[3,3,128,128]{3,2,0,1:T(8,128)(2,1)S(1)}, u32[]{:S(2)}, u32[]{:S(2)}) %collective-permute-start.2) | collective-permute-done | bytes 294944 | tf_op jit(solution)/shard_map/ppermute | solution.py:432
  23.0 1.3 collective-permute-done.3
  27.7 1.7 %collective-permute-done.5.high_ref = bf16[3,3,128,128]{3,2,1,0:T(8,128)(2,1)S(1)} collective-permute-done((bf16[3,3,128,128]{3,2,1,0:T(8,128)(2,1)S(1)}, bf16[3,3,128,128]{3,2,1,0:T(8,128)(2,1)S(1)}, u32[]{:S(2)}, u32[]{:S(2)}) %collective-permute-start.5) | collective-permute-done | bytes 294944 | tf_op jit(solution)/shard_map/ppermute | solution.py:432
  29.5 1.9 %collective-permute-done.4.low_ref = bf16[3,3,128,128]{3,2,1,0:T(8,128)(2,1)S(1)} collective-permute-done((bf16[3,3,128,128]{3,2,1,0:T(8,128)(2,1)S(1)}, bf16[3,3,128,128]{3,2,1,0:T(8,128)(2,1)S(1)}, u32[]{:S(2)}, u32[]{:S(2)}) %collective-permute-start.4) | collective-permute-done | bytes 294944 | tf_op jit(solution)/shard_map/ppermute | solution.py:432
  32.1 2.9 %receive.1 = (bf16[3456,128]{1,0:T(8,128)(2,1)}, s32[32,128]{1,0:T(8,128)}, bf16[2,2,32,128]{3,2,1,0:T(8,128)(2,1)}, bf16[2,2,32,128]{3,2,1,0:T(8,128)(2,1)}) custom-call(s32[256]{0:T(256)} %reshape.12.gidx_ref, bf16[3,3,128,128]{3,2,1,0:T(8,128)(2,1)} %get-tuple-element.35.mid_ref, bf16[3,3,128,128]{3,2,1,0:T(8,128)(2,1)} %copy-done.9, ...), custom_call_target="tpu_custom_call" | custom-call | tf_op jit(solution)/shard_map/receive/pallas_call | solution.py:128
  35.0 1.2 collective-permute-start.6
  36.2 0.8 collective-permute-start.7
  37.8 1.3 collective-permute-done.6.refs_0_
  39.1 1.2 collective-permute-done.7.refs_1_
  40.3 1.4 collective-permute-start.8
  41.7 0.8 collective-permute-start.9
  42.5 2.1 %collective-permute-done.8.refs_2_ = bf16[4,2,32,128]{3,2,1,0:T(8,128)(2,1)S(1)} collective-permute-done((bf16[4,2,32,128]{3,2,1,0:T(8,128)(2,1)S(1)}, bf16[4,2,32,128]{3,2,1,0:T(8,128)(2,1)S(1)}, u32[]{:S(2)}, u32[]{:S(2)}) %collective-permute-start.8) | collective-permute-done | bytes 65568 | tf_op jit(solution)/shard_map/ppermute | solution.py:432
  46.9 1.7 %collective-permute-start.11 = (bf16[4,4,32,128]{3,2,1,0:T(8,128)(2,1)S(1)}, bf16[4,4,32,128]{3,2,1,0:T(8,128)(2,1)S(1)}, u32[]{:S(2)}, u32[]{:S(2)}) collective-permute-start(bf16[4,4,32,128]{3,2,1,0:T(8,128)(2,1)S(1)} %pad_maximum_fusion.3), channel_id=1, source_target_pairs={{1,0},{2,1},{3,2},{4,3},{5,4},{6,5},{7,6},{0,7},{9,8},{10,9},{11,1... | collective-permute-start | bytes 393224 | tf_op jit(solution)/shard_map/ppermute | solution.py:432
  49.8 1.3 collective-permute-done.10.refs_4_
  51.8 3.1 %indices.1 = (s32[768,128]{1,0:T(8,128)}, s32[32,128]{1,0:T(8,128)}, f32[32,128]{1,0:T(8,128)}) custom-call(s32[3]{0:T(128)} %pad_add_fusion.pos_ref, s32[24,3456]{1,0:T(8,128)} %bitcast.220, s32[24,3456]{1,0:T(8,128)} %bitcast.221, s32[32,128]{1,0:T(8,128)} %get-tuple-element.22.cnt_ref, bf16[2,2,32,128]{3,2,1,0:T(8,128)(2,1)} %copy-done.2, ...), custom_call_target="tpu_custom_call" | custom-call | tf_op jit(solution)/shard_map/indices/pallas_call | solution.py:239
  54.9 33.3 %layer.2 = (bf16[3456,128]{1,0:T(8,128)(2,1)}, bf16[2,2,32,128]{3,2,1,0:T(8,128)(2,1)}, bf16[2,2,32,128]{3,2,1,0:T(8,128)(2,1)}) custom-call(s32[98304]{0:T(1024)} %bitcast.218, s32[3]{0:T(128)} %pad_add_fusion.pos_ref, s32[32,128]{1,0:T(8,128)} %get-tuple-element.26.steps_ref, s32[32,128]{1,0:T(8,128)} %get-tuple-element.22.cnt_ref, s32[256]{0:T(256)} %reshape.12.gidx_ref, ...), custom_call_target="tpu_custom_call" | custom-call | tf_op jit(solution)/shard_map/layer/pallas_call | solution.py:403
  89.0 1.4 %collective-permute-start.12 = (bf16[2,2,32,128]{3,2,1,0:T(8,128)(2,1)S(1)}, bf16[2,2,32,128]{3,2,1,0:T(8,128)(2,1)S(1)}, u32[]{:S(2)}, u32[]{:S(2)}) collective-permute-start(bf16[2,2,32,128]{3,2,1,0:T(8,128)(2,1)S(1)} %copy-done.15), channel_id=1, source_target_pairs={{0,32},{32,64},{64,96},{96,0},{1,33},{33,65},{65,97},{97,1},{2,34}... | collective-permute-start | bytes 98312 | tf_op jit(solution)/shard_map/ppermute | solution.py:432
  90.5 0.9 collective-permute-start.13
  91.4 1.8 %collective-permute-done.12.refs_0_ = bf16[2,2,32,128]{3,2,1,0:T(8,128)(2,1)S(1)} collective-permute-done((bf16[2,2,32,128]{3,2,1,0:T(8,128)(2,1)S(1)}, bf16[2,2,32,128]{3,2,1,0:T(8,128)(2,1)S(1)}, u32[]{:S(2)}, u32[]{:S(2)}) %collective-permute-start.12) | collective-permute-done | bytes 32800 | tf_op jit(solution)/shard_map/ppermute | solution.py:432
  93.2 1.3 collective-permute-done.13.refs_1_
  94.5 1.1 collective-permute-start.14
  95.6 1.1 collective-permute-start.15
  96.7 2.1 %collective-permute-done.14.refs_2_ = bf16[4,2,32,128]{3,2,1,0:T(8,128)(2,1)S(1)} collective-permute-done((bf16[4,2,32,128]{3,2,1,0:T(8,128)(2,1)S(1)}, bf16[4,2,32,128]{3,2,1,0:T(8,128)(2,1)S(1)}, u32[]{:S(2)}, u32[]{:S(2)}) %collective-permute-start.14) | collective-permute-done | bytes 65568 | tf_op jit(solution)/shard_map/ppermute | solution.py:432
  100.7 1.7 %collective-permute-start.17 = (bf16[4,4,32,128]{3,2,1,0:T(8,128)(2,1)S(1)}, bf16[4,4,32,128]{3,2,1,0:T(8,128)(2,1)S(1)}, u32[]{:S(2)}, u32[]{:S(2)}) collective-permute-start(bf16[4,4,32,128]{3,2,1,0:T(8,128)(2,1)S(1)} %pad_maximum_fusion.5), channel_id=1, source_target_pairs={{1,0},{2,1},{3,2},{4,3},{5,4},{6,5},{7,6},{0,7},{9,8},{10,9},{11,1... | collective-permute-start | bytes 393224 | tf_op jit(solution)/shard_map/ppermute | solution.py:432
  102.5 2.6 %collective-permute-done.16.refs_4_ = bf16[4,4,32,128]{3,2,1,0:T(8,128)(2,1)S(1)} collective-permute-done((bf16[4,4,32,128]{3,2,1,0:T(8,128)(2,1)S(1)}, bf16[4,4,32,128]{3,2,1,0:T(8,128)(2,1)S(1)}, u32[]{:S(2)}, u32[]{:S(2)}) %collective-permute-start.16) | collective-permute-done | bytes 131104 | tf_op jit(solution)/shard_map/ppermute | solution.py:432
  105.7 33.2 %layer.3 = (bf16[3456,128]{1,0:T(8,128)(2,1)}, bf16[2,2,32,128]{3,2,1,0:T(8,128)(2,1)}, bf16[2,2,32,128]{3,2,1,0:T(8,128)(2,1)}) custom-call(s32[98304]{0:T(1024)} %bitcast.219, s32[3]{0:T(128)} %pad_add_fusion.pos_ref, s32[32,128]{1,0:T(8,128)} %get-tuple-element.26.steps_ref, s32[32,128]{1,0:T(8,128)} %get-tuple-element.22.cnt_ref, s32[256]{0:T(256)} %reshape.12.gidx_ref, ...), custom_call_target="tpu_custom_call" | custom-call | tf_op jit(solution)/shard_map/layer/pallas_call | solution.py:403
  (110 shorter events, 13.4 us)
Async XLA Ops:
  4.1 9.0 %collective-permute-start = (bf16[3,3,128,128]{3,2,1,0:T(8,128)(2,1)}, bf16[3,3,128,128]{3,2,1,0:T(8,128)(2,1)S(1)}, u32[]{:S(2)}, u32[]{:S(2)}) collective-permute-start(bf16[3,3,128,128]{3,2,1,0:T(8,128)(2,1)} %get-tuple-element.19), channel_id=1, source_target_pairs={{0,32},{32,64},{64,96},{96,0},{1,33},{33,65},{65,97},{97,1},{2,34}... | collective-permute-start | bytes 884744 | tf_op jit(solution)/shard_map/ppermute | solution.py:432
  5.5 8.7 %collective-permute-start.1 = (bf16[3,3,128,128]{3,2,1,0:T(8,128)(2,1)}, bf16[3,3,128,128]{3,2,1,0:T(8,128)(2,1)S(1)}, u32[]{:S(2)}, u32[]{:S(2)}) collective-permute-start(bf16[3,3,128,128]{3,2,1,0:T(8,128)(2,1)} %get-tuple-element.21), channel_id=1, source_target_pairs={{32,0},{64,32},{96,64},{0,96},{33,1},{65,33},{97,65},{1,97},{34,2}... | collective-permute-start | bytes 884744 | tf_op jit(solution)/shard_map/ppermute | solution.py:432
  15.4 7.6 %collective-permute-start.2 = (bf16[3,3,128,128]{3,2,0,1:T(8,128)(2,1)S(1)}, bf16[3,3,128,128]{3,2,0,1:T(8,128)(2,1)S(1)}, u32[]{:S(2)}, u32[]{:S(2)}) collective-permute-start(bf16[3,3,128,128]{3,2,0,1:T(8,128)(2,1)S(1)} %get-tuple-element.36), channel_id=1, source_target_pairs={{0,8},{8,16},{16,24},{24,0},{1,9},{9,17},{17,25},{25,1},{2,10},{10... | collective-permute-start | bytes 884744 | tf_op jit(solution)/shard_map/ppermute | solution.py:432
  17.0 7.3 %collective-permute-start.3 = (bf16[3,3,128,128]{3,2,0,1:T(8,128)(2,1)S(1)}, bf16[3,3,128,128]{3,2,0,1:T(8,128)(2,1)S(1)}, u32[]{:S(2)}, u32[]{:S(2)}) collective-permute-start(bf16[3,3,128,128]{3,2,0,1:T(8,128)(2,1)S(1)} %get-tuple-element.37), channel_id=1, source_target_pairs={{8,0},{16,8},{24,16},{0,24},{9,1},{17,9},{25,17},{1,25},{10,2},{18... | collective-permute-start | bytes 884744 | tf_op jit(solution)/shard_map/ppermute | solution.py:432
  24.4 1.4 copy-start.20
  24.4 1.3 copy-start.21
  25.2 4.2 %collective-permute-start.5 = (bf16[3,3,128,128]{3,2,1,0:T(8,128)(2,1)S(1)}, bf16[3,3,128,128]{3,2,1,0:T(8,128)(2,1)S(1)}, u32[]{:S(2)}, u32[]{:S(2)}) collective-permute-start(bf16[3,3,128,128]{3,2,1,0:T(8,128)(2,1)S(1)} %get-tuple-element.33), channel_id=1, source_target_pairs={{1,0},{2,1},{3,2},{4,3},{5,4},{6,5},{7,6},{0,7},{9,8},{10,9},{11,1... | collective-permute-start | bytes 884744 | tf_op jit(solution)/shard_map/ppermute | solution.py:432
  25.2 1.8 %copy-start.16 = (bf16[2,256,128]{2,1,0:T(8,128)(2,1)S(1)}, bf16[2,256,128]{2,1,0:T(8,128)(2,1)}, u32[]{:S(2)}) copy-start(bf16[2,256,128]{2,1,0:T(8,128)(2,1)} %param.19) | copy-start | bytes 393220
  25.2 1.8 %copy-start.17 = (bf16[2,256,128]{2,1,0:T(8,128)(2,1)S(1)}, bf16[2,256,128]{2,1,0:T(8,128)(2,1)}, u32[]{:S(2)}) copy-start(bf16[2,256,128]{2,1,0:T(8,128)(2,1)} %param.16) | copy-start | bytes 393220
  25.2 6.2 %collective-permute-start.4 = (bf16[3,3,128,128]{3,2,1,0:T(8,128)(2,1)S(1)}, bf16[3,3,128,128]{3,2,1,0:T(8,128)(2,1)S(1)}, u32[]{:S(2)}, u32[]{:S(2)}) collective-permute-start(bf16[3,3,128,128]{3,2,1,0:T(8,128)(2,1)S(1)} %get-tuple-element.34), channel_id=1, source_target_pairs={{0,1},{1,2},{2,3},{3,4},{4,5},{5,6},{6,7},{7,0},{8,9},{9,10},{10,1... | collective-permute-start | bytes 884744 | tf_op jit(solution)/shard_map/ppermute | solution.py:432
  29.5 1.9 %copy-start.8 = (bf16[3,3,128,128]{3,2,1,0:T(8,128)(2,1)}, bf16[3,3,128,128]{3,2,1,0:T(8,128)(2,1)S(1)}, u32[]{:S(2)}) copy-start(bf16[3,3,128,128]{3,2,1,0:T(8,128)(2,1)S(1)} %collective-permute-done.5.high_ref) | copy-start | bytes 884740
  35.0 4.1 %collective-permute-start.6 = (bf16[2,2,32,128]{3,2,1,0:T(8,128)(2,1)}, bf16[2,2,32,128]{3,2,1,0:T(8,128)(2,1)S(1)}, u32[]{:S(2)}, u32[]{:S(2)}) collective-permute-start(bf16[2,2,32,128]{3,2,1,0:T(8,128)(2,1)} %get-tuple-element.23), channel_id=1, source_target_pairs={{0,32},{32,64},{64,96},{96,0},{1,33},{33,65},{65,97},{97,1},{2,34}... | collective-permute-start | bytes 98312 | tf_op jit(solution)/shard_map/ppermute | solution.py:432
  36.2 1.6 %copy-start.18 = (bf16[2,2,32,128]{3,2,1,0:T(8,128)(2,1)S(1)}, bf16[2,2,32,128]{3,2,1,0:T(8,128)(2,1)}, u32[]{:S(2)}) copy-start(bf16[2,2,32,128]{3,2,1,0:T(8,128)(2,1)} %get-tuple-element.24) | copy-start | bytes 98308
  36.2 1.6 %copy-start.19 = (bf16[2,2,32,128]{3,2,1,0:T(8,128)(2,1)S(1)}, bf16[2,2,32,128]{3,2,1,0:T(8,128)(2,1)}, u32[]{:S(2)}) copy-start(bf16[2,2,32,128]{3,2,1,0:T(8,128)(2,1)} %get-tuple-element.23) | copy-start | bytes 98308
  36.2 4.1 %collective-permute-start.7 = (bf16[2,2,32,128]{3,2,1,0:T(8,128)(2,1)}, bf16[2,2,32,128]{3,2,1,0:T(8,128)(2,1)S(1)}, u32[]{:S(2)}, u32[]{:S(2)}) collective-permute-start(bf16[2,2,32,128]{3,2,1,0:T(8,128)(2,1)} %get-tuple-element.24), channel_id=1, source_target_pairs={{32,0},{64,32},{96,64},{0,96},{33,1},{65,33},{97,65},{1,97},{34,2}... | collective-permute-start | bytes 98312 | tf_op jit(solution)/shard_map/ppermute | solution.py:432
  39.1 3.4 %copy-start.2 = (bf16[2,2,32,128]{3,2,1,0:T(8,128)(2,1)}, bf16[2,2,32,128]{3,2,1,0:T(8,128)(2,1)S(1)}, u32[]{:S(2)}) copy-start(bf16[2,2,32,128]{3,2,1,0:T(8,128)(2,1)S(1)} %collective-permute-done.6.refs_0_) | copy-start | bytes 98308
  40.3 2.2 %copy-start.3 = (bf16[2,2,32,128]{3,2,1,0:T(8,128)(2,1)}, bf16[2,2,32,128]{3,2,1,0:T(8,128)(2,1)S(1)}, u32[]{:S(2)}) copy-start(bf16[2,2,32,128]{3,2,1,0:T(8,128)(2,1)S(1)} %collective-permute-done.7.refs_1_) | copy-start | bytes 98308
  40.3 4.3 %collective-permute-start.8 = (bf16[4,2,32,128]{3,2,1,0:T(8,128)(2,1)S(1)}, bf16[4,2,32,128]{3,2,1,0:T(8,128)(2,1)S(1)}, u32[]{:S(2)}, u32[]{:S(2)}) collective-permute-start(bf16[4,2,32,128]{3,2,1,0:T(8,128)(2,1)S(1)} %pad_maximum_fusion.6), channel_id=1, source_target_pairs={{0,8},{8,16},{16,24},{24,0},{1,9},{9,17},{17,25},{25,1},{2,10},{10... | collective-permute-start | bytes 196616 | tf_op jit(solution)/shard_map/ppermute | solution.py:432
  41.7 4.3 %collective-permute-start.9 = (bf16[4,2,32,128]{3,2,1,0:T(8,128)(2,1)S(1)}, bf16[4,2,32,128]{3,2,1,0:T(8,128)(2,1)S(1)}, u32[]{:S(2)}, u32[]{:S(2)}) collective-permute-start(bf16[4,2,32,128]{3,2,1,0:T(8,128)(2,1)S(1)} %pad_maximum_fusion.7), channel_id=1, source_target_pairs={{8,0},{16,8},{24,16},{0,24},{9,1},{17,9},{25,17},{1,25},{10,2},{18... | collective-permute-start | bytes 196616 | tf_op jit(solution)/shard_map/ppermute | solution.py:432
  46.7 4.4 %collective-permute-start.10 = (bf16[4,4,32,128]{3,2,1,0:T(8,128)(2,1)S(1)}, bf16[4,4,32,128]{3,2,1,0:T(8,128)(2,1)S(1)}, u32[]{:S(2)}, u32[]{:S(2)}) collective-permute-start(bf16[4,4,32,128]{3,2,1,0:T(8,128)(2,1)S(1)} %pad_maximum_fusion.2), channel_id=1, source_target_pairs={{0,1},{1,2},{2,3},{3,4},{4,5},{5,6},{6,7},{7,0},{8,9},{9,10},{10,1... | collective-permute-start | bytes 393224 | tf_op jit(solution)/shard_map/ppermute | solution.py:432
  46.8 1.8 %copy-start.22 = (bf16[2,128,128]{2,1,0:T(8,128)(2,1)S(1)}, bf16[2,128,128]{2,1,0:T(8,128)(2,1)}, u32[]{:S(2)}) copy-start(bf16[2,128,128]{2,1,0:T(8,128)(2,1)} %param.21) | copy-start | bytes 196612
  46.8 1.8 %copy-start.23 = (bf16[2,128,128]{2,1,0:T(8,128)(2,1)S(1)}, bf16[2,128,128]{2,1,0:T(8,128)(2,1)}, u32[]{:S(2)}) copy-start(bf16[2,128,128]{2,1,0:T(8,128)(2,1)} %param.20) | copy-start | bytes 196612
  46.9 4.3 %collective-permute-start.11 = (bf16[4,4,32,128]{3,2,1,0:T(8,128)(2,1)S(1)}, bf16[4,4,32,128]{3,2,1,0:T(8,128)(2,1)S(1)}, u32[]{:S(2)}, u32[]{:S(2)}) collective-permute-start(bf16[4,4,32,128]{3,2,1,0:T(8,128)(2,1)S(1)} %pad_maximum_fusion.3), channel_id=1, source_target_pairs={{1,0},{2,1},{3,2},{4,3},{5,4},{6,5},{7,6},{0,7},{9,8},{10,9},{11,1... | collective-permute-start | bytes 393224 | tf_op jit(solution)/shard_map/ppermute | solution.py:432
  89.0 1.5 %copy-start.14 = (bf16[2,2,32,128]{3,2,1,0:T(8,128)(2,1)S(1)}, bf16[2,2,32,128]{3,2,1,0:T(8,128)(2,1)}, u32[]{:S(2)}) copy-start(bf16[2,2,32,128]{3,2,1,0:T(8,128)(2,1)} %get-tuple-element.31) | copy-start | bytes 98308
  89.0 4.2 %collective-permute-start.12 = (bf16[2,2,32,128]{3,2,1,0:T(8,128)(2,1)S(1)}, bf16[2,2,32,128]{3,2,1,0:T(8,128)(2,1)S(1)}, u32[]{:S(2)}, u32[]{:S(2)}) collective-permute-start(bf16[2,2,32,128]{3,2,1,0:T(8,128)(2,1)S(1)} %copy-done.15), channel_id=1, source_target_pairs={{0,32},{32,64},{64,96},{96,0},{1,33},{33,65},{65,97},{97,1},{2,34}... | collective-permute-start | bytes 98312 | tf_op jit(solution)/shard_map/ppermute | solution.py:432
  90.5 4.0 %collective-permute-start.13 = (bf16[2,2,32,128]{3,2,1,0:T(8,128)(2,1)S(1)}, bf16[2,2,32,128]{3,2,1,0:T(8,128)(2,1)S(1)}, u32[]{:S(2)}, u32[]{:S(2)}) collective-permute-start(bf16[2,2,32,128]{3,2,1,0:T(8,128)(2,1)S(1)} %copy-done.14), channel_id=1, source_target_pairs={{32,0},{64,32},{96,64},{0,96},{33,1},{65,33},{97,65},{1,97},{34,2}... | collective-permute-start | bytes 98312 | tf_op jit(solution)/shard_map/ppermute | solution.py:432
  93.2 3.5 %copy-start.6 = (bf16[2,2,32,128]{3,2,1,0:T(8,128)(2,1)}, bf16[2,2,32,128]{3,2,1,0:T(8,128)(2,1)S(1)}, u32[]{:S(2)}) copy-start(bf16[2,2,32,128]{3,2,1,0:T(8,128)(2,1)S(1)} %collective-permute-done.12.refs_0_) | copy-start | bytes 98308
  94.4 2.2 %copy-start.7 = (bf16[2,2,32,128]{3,2,1,0:T(8,128)(2,1)}, bf16[2,2,32,128]{3,2,1,0:T(8,128)(2,1)S(1)}, u32[]{:S(2)}) copy-start(bf16[2,2,32,128]{3,2,1,0:T(8,128)(2,1)S(1)} %collective-permute-done.13.refs_1_) | copy-start | bytes 98308
  94.5 4.3 %collective-permute-start.14 = (bf16[4,2,32,128]{3,2,1,0:T(8,128)(2,1)S(1)}, bf16[4,2,32,128]{3,2,1,0:T(8,128)(2,1)S(1)}, u32[]{:S(2)}, u32[]{:S(2)}) collective-permute-start(bf16[4,2,32,128]{3,2,1,0:T(8,128)(2,1)S(1)} %pad_maximum_fusion.8), channel_id=1, source_target_pairs={{0,8},{8,16},{16,24},{24,0},{1,9},{9,17},{17,25},{25,1},{2,10},{10... | collective-permute-start | bytes 196616 | tf_op jit(solution)/shard_map/ppermute | solution.py:432
  95.6 4.3 %collective-permute-start.15 = (bf16[4,2,32,128]{3,2,1,0:T(8,128)(2,1)S(1)}, bf16[4,2,32,128]{3,2,1,0:T(8,128)(2,1)S(1)}, u32[]{:S(2)}, u32[]{:S(2)}) collective-permute-start(bf16[4,2,32,128]{3,2,1,0:T(8,128)(2,1)S(1)} %pad_maximum_fusion.9), channel_id=1, source_target_pairs={{8,0},{16,8},{24,16},{0,24},{9,1},{17,9},{25,17},{1,25},{10,2},{18... | collective-permute-start | bytes 196616 | tf_op jit(solution)/shard_map/ppermute | solution.py:432
  100.6 4.4 %collective-permute-start.16 = (bf16[4,4,32,128]{3,2,1,0:T(8,128)(2,1)S(1)}, bf16[4,4,32,128]{3,2,1,0:T(8,128)(2,1)S(1)}, u32[]{:S(2)}, u32[]{:S(2)}) collective-permute-start(bf16[4,4,32,128]{3,2,1,0:T(8,128)(2,1)S(1)} %pad_maximum_fusion.4), channel_id=1, source_target_pairs={{0,1},{1,2},{2,3},{3,4},{4,5},{5,6},{6,7},{7,0},{8,9},{9,10},{10,1... | collective-permute-start | bytes 393224 | tf_op jit(solution)/shard_map/ppermute | solution.py:432
  100.7 4.3 %collective-permute-start.17 = (bf16[4,4,32,128]{3,2,1,0:T(8,128)(2,1)S(1)}, bf16[4,4,32,128]{3,2,1,0:T(8,128)(2,1)S(1)}, u32[]{:S(2)}, u32[]{:S(2)}) collective-permute-start(bf16[4,4,32,128]{3,2,1,0:T(8,128)(2,1)S(1)} %pad_maximum_fusion.5), channel_id=1, source_target_pairs={{1,0},{2,1},{3,2},{4,3},{5,4},{6,5},{7,6},{0,7},{9,8},{10,9},{11,1... | collective-permute-start | bytes 393224 | tf_op jit(solution)/shard_map/ppermute | solution.py:432
  (11 other events, 7.9 us)

commit v6 on v5

--- a/solution.py
+++ b/solution.py
@@ -24,7 +24,7 @@
 MARK = 2.0**100
 HALO_AXES = ("gx", "gy", "gz")
 GRID = (4, 4, 8)
-VMEM_LIMIT = 56 * 2**20
+VMEM_LIMIT = 24 * 2**20
 
 
 def dot(a, b):

time: 140 us -> 128 us (0.914)
  Pallas kernels: 76.5 us -> 68.5 us
  local copies, waits for them, and re-layouts: 9.73 us -> 2.42 us
  waiting for transfers between devices: 33.6 us -> 38 us
  other arithmetic: 1.96 us -> 0.53 us
    ppermute x18, waiting for transfers between devices: 33.6 us -> 38 us  [both_ways(): return (lax.ppermute(up, axis, forward), lax.ppermute(down, axis, backward))]
    pallas_call x2, Pallas kernels: 66.6 us -> 63.2 us  [one_layer(): pl.pallas_call(layer_kernel, out_shape=[jax.ShapeDtypeStruct((ROWS, W), B...]
    unnamed x50 -> x22, local copies, waits for them, and re-layouts: 4.62 us -> 2.08 us
    squeeze x3, local copies, waits for them, and re-layouts: 2.04 us -> 0.04 us  [body(): w[layer]]
    pallas_call x1, Pallas kernels: 4.05 us -> 2.23 us  [pack(): pl.pallas_call(pack_kernel, out_shape=[jax.ShapeDtypeStruct((3, 3, W, W),...]
    pallas_call x1, Pallas kernels: 2.87 us -> 1.35 us  [receive(): pl.pallas_call(receive_kernel, out_shape=[jax.ShapeDtypeStruct((ROWS, W),...]
  transfers between devices with their start and end apart: 18 -> 18, of which waited for: 16 -> 16; matrix products, arithmetic and copies ran while one was open for 3% -> 0% of each run, Pallas kernels for 0% -> 0%
where the time goes in v6:
time: 128 us; the launch traced here: 127 us
  Pallas kernels  68.5 us (54%)
  waiting for transfers between devices  38 us (30%)
  starting transfers between devices  16.9 us (13%)
  local copies, waits for them, and re-layouts  2.42 us (2%)
    pallas_call x2, Pallas kernels, one_layer(): pl.pallas_call(layer_kernel, out_shape=[jax.ShapeDtypeStruct((ROWS, W), B...  63.2 us
    ppermute x18, waiting for transfers between devices, both_ways(): return (lax.ppermute(up, axis, forward), lax.ppermute(down, axis, backward))  38 us
    ppermute x18, starting transfers between devices, both_ways(): return (lax.ppermute(up, axis, forward), lax.ppermute(down, axis, backward))  16.9 us
  transfers between devices with their start and end apart: 18, of which 16 were waited for; matrix products, arithmetic and copies ran while one was open for 0% of the time, Pallas kernels for 0%

profile of v6, /device:TPU:106, one launch (start us, length us, event | category | flops | bytes accessed | tf_op | source)
XLA Modules:
  0.0 126.8 jit_solution(2899271339221334943)
XLA Ops:
  0.0 0.9 copy-done.2
  1.6 2.2 %pack.1 = (bf16[3,3,128,128]{3,2,1,0:T(8,128)(2,1)S(1)}, bf16[3,3,128,128]{3,2,1,0:T(8,128)(2,1)S(1)}, bf16[3,3,128,128]{3,2,1,0:T(8,128)(2,1)S(1)}) custom-call(s32[1,1024]{1,0:T(1,128)S(1)} %bitcast.224, bf16[1024,128]{1,0:T(8,128)(2,1)S(1)} %bitcast.223), custom_call_target="tpu_custom_call" | custom-call | tf_op jit(solution)/shard_map/pack/pallas_call | solution.py:78
  3.9 1.6 %collective-permute-start = (bf16[3,3,128,128]{3,2,1,0:T(8,128)(2,1)S(1)}, bf16[3,3,128,128]{3,2,1,0:T(8,128)(2,1)S(1)}, u32[]{:S(2)}, u32[]{:S(2)}) collective-permute-start(bf16[3,3,128,128]{3,2,1,0:T(8,128)(2,1)S(1)} %get-tuple-element.19), channel_id=1, source_target_pairs={{0,32},{32,64},{64,96},{96,0},{1,33},{33,65},{65,97},{97,1},{2,34}... | collective-permute-start | bytes 884744 | tf_op jit(solution)/shard_map/ppermute | solution.py:432
  6.0 6.7 %collective-permute-done = bf16[3,3,128,128]{3,2,1,0:T(8,128)(2,1)S(1)} collective-permute-done((bf16[3,3,128,128]{3,2,1,0:T(8,128)(2,1)S(1)}, bf16[3,3,128,128]{3,2,1,0:T(8,128)(2,1)S(1)}, u32[]{:S(2)}, u32[]{:S(2)}) %collective-permute-start) | collective-permute-done | bytes 294944 | tf_op jit(solution)/shard_map/ppermute | solution.py:432
  12.7 1.2 collective-permute-done.1
  14.1 1.6 %collective-permute-start.2 = (bf16[3,3,128,128]{3,2,0,1:T(8,128)(2,1)S(1)}, bf16[3,3,128,128]{3,2,0,1:T(8,128)(2,1)S(1)}, u32[]{:S(2)}, u32[]{:S(2)}) collective-permute-start(bf16[3,3,128,128]{3,2,0,1:T(8,128)(2,1)S(1)} %get-tuple-element.36), channel_id=1, source_target_pairs={{0,8},{8,16},{16,24},{24,0},{1,9},{9,17},{17,25},{25,1},{2,10},{10... | collective-permute-start | bytes 884744 | tf_op jit(solution)/shard_map/ppermute | solution.py:432
  16.2 5.5 %collective-permute-done.2 = bf16[3,3,128,128]{3,2,0,1:T(8,128)(2,1)S(1)} collective-permute-done((bf16[3,3,128,128]{3,2,0,1:T(8,128)(2,1)S(1)}, bf16[3,3,128,128]{3,2,0,1:T(8,128)(2,1)S(1)}, u32[]{:S(2)}, u32[]{:S(2)}) %collective-permute-start.2) | collective-permute-done | bytes 294944 | tf_op jit(solution)/shard_map/ppermute | solution.py:432
  21.7 1.3 %collective-permute-done.3 = bf16[3,3,128,128]{3,2,0,1:T(8,128)(2,1)S(1)} collective-permute-done((bf16[3,3,128,128]{3,2,0,1:T(8,128)(2,1)S(1)}, bf16[3,3,128,128]{3,2,0,1:T(8,128)(2,1)S(1)}, u32[]{:S(2)}, u32[]{:S(2)}) %collective-permute-start.3) | collective-permute-done | bytes 294944 | tf_op jit(solution)/shard_map/ppermute | solution.py:432
  24.3 3.2 %collective-permute-done.5.high_ref = bf16[3,3,128,128]{3,2,1,0:T(8,128)(2,1)S(1)} collective-permute-done((bf16[3,3,128,128]{3,2,1,0:T(8,128)(2,1)S(1)}, bf16[3,3,128,128]{3,2,1,0:T(8,128)(2,1)S(1)}, u32[]{:S(2)}, u32[]{:S(2)}) %collective-permute-start.5) | collective-permute-done | bytes 294944 | tf_op jit(solution)/shard_map/ppermute | solution.py:432
  27.5 2.0 %collective-permute-done.4.low_ref = bf16[3,3,128,128]{3,2,1,0:T(8,128)(2,1)S(1)} collective-permute-done((bf16[3,3,128,128]{3,2,1,0:T(8,128)(2,1)S(1)}, bf16[3,3,128,128]{3,2,1,0:T(8,128)(2,1)S(1)}, u32[]{:S(2)}, u32[]{:S(2)}) %collective-permute-start.4) | collective-permute-done | bytes 294944 | tf_op jit(solution)/shard_map/ppermute | solution.py:432
  29.4 1.3 %receive.1 = (bf16[3456,128]{1,0:T(8,128)(2,1)S(1)}, s32[32,128]{1,0:T(8,128)S(1)}, bf16[2,2,32,128]{3,2,1,0:T(8,128)(2,1)S(1)}, bf16[2,2,32,128]{3,2,1,0:T(8,128)(2,1)S(1)}) custom-call(s32[256]{0:T(256)S(1)} %reshape.12.gidx_ref, bf16[3,3,128,128]{3,2,1,0:T(8,128)(2,1)S(1)} %get-tuple-element.35.mid_ref, ...), custom_call_target="tpu_custom_call" | custom-call | tf_op jit(solution)/shard_map/receive/pallas_call | solution.py:128
  30.8 1.3 collective-permute-start.6
  32.1 0.8 collective-permute-start.7
  32.9 1.9 %collective-permute-done.6.refs_0_ = bf16[2,2,32,128]{3,2,1,0:T(8,128)(2,1)S(1)} collective-permute-done((bf16[2,2,32,128]{3,2,1,0:T(8,128)(2,1)S(1)}, bf16[2,2,32,128]{3,2,1,0:T(8,128)(2,1)S(1)}, u32[]{:S(2)}, u32[]{:S(2)}) %collective-permute-start.6) | collective-permute-done | bytes 32800 | tf_op jit(solution)/shard_map/ppermute | solution.py:432
  34.8 1.2 collective-permute-done.7.refs_1_
  36.0 1.4 %collective-permute-start.8 = (bf16[4,2,32,128]{3,2,1,0:T(8,128)(2,1)S(1)}, bf16[4,2,32,128]{3,2,1,0:T(8,128)(2,1)S(1)}, u32[]{:S(2)}, u32[]{:S(2)}) collective-permute-start(bf16[4,2,32,128]{3,2,1,0:T(8,128)(2,1)S(1)} %pad_maximum_fusion.6), channel_id=1, source_target_pairs={{0,8},{8,16},{16,24},{24,0},{1,9},{9,17},{17,25},{25,1},{2,10},{10... | collective-permute-start | bytes 196616 | tf_op jit(solution)/shard_map/ppermute | solution.py:432
  38.2 2.1 %collective-permute-done.8.refs_2_ = bf16[4,2,32,128]{3,2,1,0:T(8,128)(2,1)S(1)} collective-permute-done((bf16[4,2,32,128]{3,2,1,0:T(8,128)(2,1)S(1)}, bf16[4,2,32,128]{3,2,1,0:T(8,128)(2,1)S(1)}, u32[]{:S(2)}, u32[]{:S(2)}) %collective-permute-start.8) | collective-permute-done | bytes 65568 | tf_op jit(solution)/shard_map/ppermute | solution.py:432
  40.3 1.4 %collective-permute-done.9.refs_3_ = bf16[4,2,32,128]{3,2,1,0:T(8,128)(2,1)S(1)} collective-permute-done((bf16[4,2,32,128]{3,2,1,0:T(8,128)(2,1)S(1)}, bf16[4,2,32,128]{3,2,1,0:T(8,128)(2,1)S(1)}, u32[]{:S(2)}, u32[]{:S(2)}) %collective-permute-start.9) | collective-permute-done | bytes 65568 | tf_op jit(solution)/shard_map/ppermute | solution.py:432
  42.0 1.7 %collective-permute-start.11 = (bf16[4,4,32,128]{3,2,1,0:T(8,128)(2,1)S(1)}, bf16[4,4,32,128]{3,2,1,0:T(8,128)(2,1)S(1)}, u32[]{:S(2)}, u32[]{:S(2)}) collective-permute-start(bf16[4,4,32,128]{3,2,1,0:T(8,128)(2,1)S(1)} %pad_maximum_fusion.3), channel_id=1, source_target_pairs={{1,0},{2,1},{3,2},{4,3},{5,4},{6,5},{7,6},{0,7},{9,8},{10,9},{11,1... | collective-permute-start | bytes 393224 | tf_op jit(solution)/shard_map/ppermute | solution.py:432
  43.8 2.4 %collective-permute-done.10.refs_4_ = bf16[4,4,32,128]{3,2,1,0:T(8,128)(2,1)S(1)} collective-permute-done((bf16[4,4,32,128]{3,2,1,0:T(8,128)(2,1)S(1)}, bf16[4,4,32,128]{3,2,1,0:T(8,128)(2,1)S(1)}, u32[]{:S(2)}, u32[]{:S(2)}) %collective-permute-start.10) | collective-permute-done | bytes 131104 | tf_op jit(solution)/shard_map/ppermute | solution.py:432
  46.2 1.7 %indices.1 = (s32[768,128]{1,0:T(8,128)S(1)}, s32[32,128]{1,0:T(8,128)S(1)}, f32[32,128]{1,0:T(8,128)S(1)}) custom-call(s32[3]{0:T(128)S(1)} %pad_add_fusion.pos_ref, s32[24,3456]{1,0:T(8,128)S(1)} %bitcast.220, s32[24,3456]{1,0:T(8,128)S(1)} %bitcast.221, s32[32,128]{1,0:T(8,128)S(1)} %get-tuple-element.22.cnt_ref, ...), custom_call_target="tpu_custom_call" | custom-call | tf_op jit(solution)/shard_map/indices/pallas_call | solution.py:239
  47.9 31.1 %layer.2 = (bf16[3456,128]{1,0:T(8,128)(2,1)S(1)}, bf16[2,2,32,128]{3,2,1,0:T(8,128)(2,1)S(1)}, bf16[2,2,32,128]{3,2,1,0:T(8,128)(2,1)S(1)}) custom-call(s32[98304]{0:T(1024)S(1)} %bitcast.218, s32[3]{0:T(128)S(1)} %pad_add_fusion.pos_ref, s32[32,128]{1,0:T(8,128)S(1)} %get-tuple-element.26.steps_ref, s32[32,128]{1,0:T(8,128)S(1)} %get-tuple-element.22.cnt_ref, ...), custom_call_target="tpu_custom_call" | custom-call | tf_op jit(solution)/shard_map/layer/pallas_call | solution.py:403
  79.1 1.6 %collective-permute-start.12 = (bf16[2,2,32,128]{3,2,1,0:T(8,128)(2,1)S(1)}, bf16[2,2,32,128]{3,2,1,0:T(8,128)(2,1)S(1)}, u32[]{:S(2)}, u32[]{:S(2)}) collective-permute-start(bf16[2,2,32,128]{3,2,1,0:T(8,128)(2,1)S(1)} %get-tuple-element.30), channel_id=1, source_target_pairs={{0,32},{32,64},{64,96},{96,0},{1,33},{33,65},{65,97},{97,1},{2,34}... | collective-permute-start | bytes 98312 | tf_op jit(solution)/shard_map/ppermute | solution.py:432
  81.4 1.9 %collective-permute-done.12.refs_0_ = bf16[2,2,32,128]{3,2,1,0:T(8,128)(2,1)S(1)} collective-permute-done((bf16[2,2,32,128]{3,2,1,0:T(8,128)(2,1)S(1)}, bf16[2,2,32,128]{3,2,1,0:T(8,128)(2,1)S(1)}, u32[]{:S(2)}, u32[]{:S(2)}) %collective-permute-start.12) | collective-permute-done | bytes 32800 | tf_op jit(solution)/shard_map/ppermute | solution.py:432
  83.3 1.3 %collective-permute-done.13.refs_1_ = bf16[2,2,32,128]{3,2,1,0:T(8,128)(2,1)S(1)} collective-permute-done((bf16[2,2,32,128]{3,2,1,0:T(8,128)(2,1)S(1)}, bf16[2,2,32,128]{3,2,1,0:T(8,128)(2,1)S(1)}, u32[]{:S(2)}, u32[]{:S(2)}) %collective-permute-start.13) | collective-permute-done | bytes 32800 | tf_op jit(solution)/shard_map/ppermute | solution.py:432
  84.6 1.1 collective-permute-start.14
  85.8 1.0 collective-permute-start.15
  86.8 2.1 %collective-permute-done.14.refs_2_ = bf16[4,2,32,128]{3,2,1,0:T(8,128)(2,1)S(1)} collective-permute-done((bf16[4,2,32,128]{3,2,1,0:T(8,128)(2,1)S(1)}, bf16[4,2,32,128]{3,2,1,0:T(8,128)(2,1)S(1)}, u32[]{:S(2)}, u32[]{:S(2)}) %collective-permute-start.14) | collective-permute-done | bytes 65568 | tf_op jit(solution)/shard_map/ppermute | solution.py:432
  89.0 1.1 collective-permute-done.15.refs_3_
  90.3 1.7 %collective-permute-start.17 = (bf16[4,4,32,128]{3,2,1,0:T(8,128)(2,1)S(1)}, bf16[4,4,32,128]{3,2,1,0:T(8,128)(2,1)S(1)}, u32[]{:S(2)}, u32[]{:S(2)}) collective-permute-start(bf16[4,4,32,128]{3,2,1,0:T(8,128)(2,1)S(1)} %pad_maximum_fusion.5), channel_id=1, source_target_pairs={{1,0},{2,1},{3,2},{4,3},{5,4},{6,5},{7,6},{0,7},{9,8},{10,9},{11,1... | collective-permute-start | bytes 393224 | tf_op jit(solution)/shard_map/ppermute | solution.py:432
  92.1 2.6 %collective-permute-done.16.refs_4_ = bf16[4,4,32,128]{3,2,1,0:T(8,128)(2,1)S(1)} collective-permute-done((bf16[4,4,32,128]{3,2,1,0:T(8,128)(2,1)S(1)}, bf16[4,4,32,128]{3,2,1,0:T(8,128)(2,1)S(1)}, u32[]{:S(2)}, u32[]{:S(2)}) %collective-permute-start.16) | collective-permute-done | bytes 131104 | tf_op jit(solution)/shard_map/ppermute | solution.py:432
  94.6 32.1 %layer.3 = (bf16[3456,128]{1,0:T(8,128)(2,1)}, bf16[2,2,32,128]{3,2,1,0:T(8,128)(2,1)}, bf16[2,2,32,128]{3,2,1,0:T(8,128)(2,1)}) custom-call(s32[98304]{0:T(1024)S(1)} %bitcast.219, s32[3]{0:T(128)S(1)} %pad_add_fusion.pos_ref, s32[32,128]{1,0:T(8,128)S(1)} %get-tuple-element.26.steps_ref, s32[32,128]{1,0:T(8,128)S(1)} %get-tuple-element.22.cnt_ref, ...), custom_call_target="tpu_custom_call" | custom-call | tf_op jit(solution)/shard_map/layer/pallas_call | solution.py:403
  (82 shorter events, 5.0 us)
Async XLA Ops:
  0.0 0.9 copy-start.2
  1.0 0.7 copy-start.3
  3.9 8.8 %collective-permute-start = (bf16[3,3,128,128]{3,2,1,0:T(8,128)(2,1)S(1)}, bf16[3,3,128,128]{3,2,1,0:T(8,128)(2,1)S(1)}, u32[]{:S(2)}, u32[]{:S(2)}) collective-permute-start(bf16[3,3,128,128]{3,2,1,0:T(8,128)(2,1)S(1)} %get-tuple-element.19), channel_id=1, source_target_pairs={{0,32},{32,64},{64,96},{96,0},{1,33},{33,65},{65,97},{97,1},{2,34}... | collective-permute-start | bytes 884744 | tf_op jit(solution)/shard_map/ppermute | solution.py:432
  5.4 8.5 %collective-permute-start.1 = (bf16[3,3,128,128]{3,2,1,0:T(8,128)(2,1)S(1)}, bf16[3,3,128,128]{3,2,1,0:T(8,128)(2,1)S(1)}, u32[]{:S(2)}, u32[]{:S(2)}) collective-permute-start(bf16[3,3,128,128]{3,2,1,0:T(8,128)(2,1)S(1)} %get-tuple-element.21), channel_id=1, source_target_pairs={{32,0},{64,32},{96,64},{0,96},{33,1},{65,33},{97,65},{1,97},{34,2}... | collective-permute-start | bytes 884744 | tf_op jit(solution)/shard_map/ppermute | solution.py:432
  14.1 7.6 %collective-permute-start.2 = (bf16[3,3,128,128]{3,2,0,1:T(8,128)(2,1)S(1)}, bf16[3,3,128,128]{3,2,0,1:T(8,128)(2,1)S(1)}, u32[]{:S(2)}, u32[]{:S(2)}) collective-permute-start(bf16[3,3,128,128]{3,2,0,1:T(8,128)(2,1)S(1)} %get-tuple-element.36), channel_id=1, source_target_pairs={{0,8},{8,16},{16,24},{24,0},{1,9},{9,17},{17,25},{25,1},{2,10},{10... | collective-permute-start | bytes 884744 | tf_op jit(solution)/shard_map/ppermute | solution.py:432
  15.7 7.3 %collective-permute-start.3 = (bf16[3,3,128,128]{3,2,0,1:T(8,128)(2,1)S(1)}, bf16[3,3,128,128]{3,2,0,1:T(8,128)(2,1)S(1)}, u32[]{:S(2)}, u32[]{:S(2)}) collective-permute-start(bf16[3,3,128,128]{3,2,0,1:T(8,128)(2,1)S(1)} %get-tuple-element.37), channel_id=1, source_target_pairs={{8,0},{16,8},{24,16},{0,24},{9,1},{17,9},{25,17},{1,25},{10,2},{18... | collective-permute-start | bytes 884744 | tf_op jit(solution)/shard_map/ppermute | solution.py:432
  23.1 0.8 copy-start.6
  23.1 0.9 copy-start.7
  23.2 4.3 %collective-permute-start.5 = (bf16[3,3,128,128]{3,2,1,0:T(8,128)(2,1)S(1)}, bf16[3,3,128,128]{3,2,1,0:T(8,128)(2,1)S(1)}, u32[]{:S(2)}, u32[]{:S(2)}) collective-permute-start(bf16[3,3,128,128]{3,2,1,0:T(8,128)(2,1)S(1)} %get-tuple-element.33), channel_id=1, source_target_pairs={{1,0},{2,1},{3,2},{4,3},{5,4},{6,5},{7,6},{0,7},{9,8},{10,9},{11,1... | collective-permute-start | bytes 884744 | tf_op jit(solution)/shard_map/ppermute | solution.py:432
  23.2 0.7 copy-start.10
  23.3 0.9 copy-start.4
  23.3 1.0 copy-start.5
  23.3 6.2 %collective-permute-start.4 = (bf16[3,3,128,128]{3,2,1,0:T(8,128)(2,1)S(1)}, bf16[3,3,128,128]{3,2,1,0:T(8,128)(2,1)S(1)}, u32[]{:S(2)}, u32[]{:S(2)}) collective-permute-start(bf16[3,3,128,128]{3,2,1,0:T(8,128)(2,1)S(1)} %get-tuple-element.34), channel_id=1, source_target_pairs={{0,1},{1,2},{2,3},{3,4},{4,5},{5,6},{6,7},{7,0},{8,9},{9,10},{10,1... | collective-permute-start | bytes 884744 | tf_op jit(solution)/shard_map/ppermute | solution.py:432
  30.8 4.0 %collective-permute-start.6 = (bf16[2,2,32,128]{3,2,1,0:T(8,128)(2,1)S(1)}, bf16[2,2,32,128]{3,2,1,0:T(8,128)(2,1)S(1)}, u32[]{:S(2)}, u32[]{:S(2)}) collective-permute-start(bf16[2,2,32,128]{3,2,1,0:T(8,128)(2,1)S(1)} %get-tuple-element.23), channel_id=1, source_target_pairs={{0,32},{32,64},{64,96},{96,0},{1,33},{33,65},{65,97},{97,1},{2,34}... | collective-permute-start | bytes 98312 | tf_op jit(solution)/shard_map/ppermute | solution.py:432
  32.1 3.9 %collective-permute-start.7 = (bf16[2,2,32,128]{3,2,1,0:T(8,128)(2,1)S(1)}, bf16[2,2,32,128]{3,2,1,0:T(8,128)(2,1)S(1)}, u32[]{:S(2)}, u32[]{:S(2)}) collective-permute-start(bf16[2,2,32,128]{3,2,1,0:T(8,128)(2,1)S(1)} %get-tuple-element.24), channel_id=1, source_target_pairs={{32,0},{64,32},{96,64},{0,96},{33,1},{65,33},{97,65},{1,97},{34,2}... | collective-permute-start | bytes 98312 | tf_op jit(solution)/shard_map/ppermute | solution.py:432
  36.0 4.3 %collective-permute-start.8 = (bf16[4,2,32,128]{3,2,1,0:T(8,128)(2,1)S(1)}, bf16[4,2,32,128]{3,2,1,0:T(8,128)(2,1)S(1)}, u32[]{:S(2)}, u32[]{:S(2)}) collective-permute-start(bf16[4,2,32,128]{3,2,1,0:T(8,128)(2,1)S(1)} %pad_maximum_fusion.6), channel_id=1, source_target_pairs={{0,8},{8,16},{16,24},{24,0},{1,9},{9,17},{17,25},{25,1},{2,10},{10... | collective-permute-start | bytes 196616 | tf_op jit(solution)/shard_map/ppermute | solution.py:432
  37.4 4.3 %collective-permute-start.9 = (bf16[4,2,32,128]{3,2,1,0:T(8,128)(2,1)S(1)}, bf16[4,2,32,128]{3,2,1,0:T(8,128)(2,1)S(1)}, u32[]{:S(2)}, u32[]{:S(2)}) collective-permute-start(bf16[4,2,32,128]{3,2,1,0:T(8,128)(2,1)S(1)} %pad_maximum_fusion.7), channel_id=1, source_target_pairs={{8,0},{16,8},{24,16},{0,24},{9,1},{17,9},{25,17},{1,25},{10,2},{18... | collective-permute-start | bytes 196616 | tf_op jit(solution)/shard_map/ppermute | solution.py:432
  41.8 4.4 %collective-permute-start.10 = (bf16[4,4,32,128]{3,2,1,0:T(8,128)(2,1)S(1)}, bf16[4,4,32,128]{3,2,1,0:T(8,128)(2,1)S(1)}, u32[]{:S(2)}, u32[]{:S(2)}) collective-permute-start(bf16[4,4,32,128]{3,2,1,0:T(8,128)(2,1)S(1)} %pad_maximum_fusion.2), channel_id=1, source_target_pairs={{0,1},{1,2},{2,3},{3,4},{4,5},{5,6},{6,7},{7,0},{8,9},{9,10},{10,1... | collective-permute-start | bytes 393224 | tf_op jit(solution)/shard_map/ppermute | solution.py:432
  41.8 1.9 %copy-start.8 = (bf16[2,128,128]{2,1,0:T(8,128)(2,1)S(1)}, bf16[2,128,128]{2,1,0:T(8,128)(2,1)}, u32[]{:S(2)}) copy-start(bf16[2,128,128]{2,1,0:T(8,128)(2,1)} %param.21) | copy-start | bytes 196612
  41.8 1.9 %copy-start.9 = (bf16[2,128,128]{2,1,0:T(8,128)(2,1)S(1)}, bf16[2,128,128]{2,1,0:T(8,128)(2,1)}, u32[]{:S(2)}) copy-start(bf16[2,128,128]{2,1,0:T(8,128)(2,1)} %param.20) | copy-start | bytes 196612
  41.9 4.3 %copy-start = (s32[1,1,1,3456,24]{3,4,2,1,0:T(8,128)S(1)}, s32[1,1,1,3456,24]{3,4,2,1,0:T(8,128)}, u32[]{:S(2)}) copy-start(s32[1,1,1,3456,24]{3,4,2,1,0:T(8,128)} %param.13) | copy-start | bytes 995332
  41.9 4.3 %copy-start.1 = (s32[1,1,1,3456,24]{3,4,2,1,0:T(8,128)S(1)}, s32[1,1,1,3456,24]{3,4,2,1,0:T(8,128)}, u32[]{:S(2)}) copy-start(s32[1,1,1,3456,24]{3,4,2,1,0:T(8,128)} %param.14) | copy-start | bytes 995332
  42.0 4.2 %collective-permute-start.11 = (bf16[4,4,32,128]{3,2,1,0:T(8,128)(2,1)S(1)}, bf16[4,4,32,128]{3,2,1,0:T(8,128)(2,1)S(1)}, u32[]{:S(2)}, u32[]{:S(2)}) collective-permute-start(bf16[4,4,32,128]{3,2,1,0:T(8,128)(2,1)S(1)} %pad_maximum_fusion.3), channel_id=1, source_target_pairs={{1,0},{2,1},{3,2},{4,3},{5,4},{6,5},{7,6},{0,7},{9,8},{10,9},{11,1... | collective-permute-start | bytes 393224 | tf_op jit(solution)/shard_map/ppermute | solution.py:432
  79.1 4.2 %collective-permute-start.12 = (bf16[2,2,32,128]{3,2,1,0:T(8,128)(2,1)S(1)}, bf16[2,2,32,128]{3,2,1,0:T(8,128)(2,1)S(1)}, u32[]{:S(2)}, u32[]{:S(2)}) collective-permute-start(bf16[2,2,32,128]{3,2,1,0:T(8,128)(2,1)S(1)} %get-tuple-element.30), channel_id=1, source_target_pairs={{0,32},{32,64},{64,96},{96,0},{1,33},{33,65},{65,97},{97,1},{2,34}... | collective-permute-start | bytes 98312 | tf_op jit(solution)/shard_map/ppermute | solution.py:432
  80.7 3.9 %collective-permute-start.13 = (bf16[2,2,32,128]{3,2,1,0:T(8,128)(2,1)S(1)}, bf16[2,2,32,128]{3,2,1,0:T(8,128)(2,1)S(1)}, u32[]{:S(2)}, u32[]{:S(2)}) collective-permute-start(bf16[2,2,32,128]{3,2,1,0:T(8,128)(2,1)S(1)} %get-tuple-element.31), channel_id=1, source_target_pairs={{32,0},{64,32},{96,64},{0,96},{33,1},{65,33},{97,65},{1,97},{34,2}... | collective-permute-start | bytes 98312 | tf_op jit(solution)/shard_map/ppermute | solution.py:432
  84.6 4.3 %collective-permute-start.14 = (bf16[4,2,32,128]{3,2,1,0:T(8,128)(2,1)S(1)}, bf16[4,2,32,128]{3,2,1,0:T(8,128)(2,1)S(1)}, u32[]{:S(2)}, u32[]{:S(2)}) collective-permute-start(bf16[4,2,32,128]{3,2,1,0:T(8,128)(2,1)S(1)} %pad_maximum_fusion.8), channel_id=1, source_target_pairs={{0,8},{8,16},{16,24},{24,0},{1,9},{9,17},{17,25},{25,1},{2,10},{10... | collective-permute-start | bytes 196616 | tf_op jit(solution)/shard_map/ppermute | solution.py:432
  85.8 4.3 %collective-permute-start.15 = (bf16[4,2,32,128]{3,2,1,0:T(8,128)(2,1)S(1)}, bf16[4,2,32,128]{3,2,1,0:T(8,128)(2,1)S(1)}, u32[]{:S(2)}, u32[]{:S(2)}) collective-permute-start(bf16[4,2,32,128]{3,2,1,0:T(8,128)(2,1)S(1)} %pad_maximum_fusion.9), channel_id=1, source_target_pairs={{8,0},{16,8},{24,16},{0,24},{9,1},{17,9},{25,17},{1,25},{10,2},{18... | collective-permute-start | bytes 196616 | tf_op jit(solution)/shard_map/ppermute | solution.py:432
  90.2 4.4 %collective-permute-start.16 = (bf16[4,4,32,128]{3,2,1,0:T(8,128)(2,1)S(1)}, bf16[4,4,32,128]{3,2,1,0:T(8,128)(2,1)S(1)}, u32[]{:S(2)}, u32[]{:S(2)}) collective-permute-start(bf16[4,4,32,128]{3,2,1,0:T(8,128)(2,1)S(1)} %pad_maximum_fusion.4), channel_id=1, source_target_pairs={{0,1},{1,2},{2,3},{3,4},{4,5},{5,6},{6,7},{7,0},{8,9},{9,10},{10,1... | collective-permute-start | bytes 393224 | tf_op jit(solution)/shard_map/ppermute | solution.py:432
  90.3 4.3 %collective-permute-start.17 = (bf16[4,4,32,128]{3,2,1,0:T(8,128)(2,1)S(1)}, bf16[4,4,32,128]{3,2,1,0:T(8,128)(2,1)S(1)}, u32[]{:S(2)}, u32[]{:S(2)}) collective-permute-start(bf16[4,4,32,128]{3,2,1,0:T(8,128)(2,1)S(1)} %pad_maximum_fusion.5), channel_id=1, source_target_pairs={{1,0},{2,1},{3,2},{4,3},{5,4},{6,5},{7,6},{0,7},{9,8},{10,9},{11,1... | collective-permute-start | bytes 393224 | tf_op jit(solution)/shard_map/ppermute | solution.py:432

commit v7 on v6

--- a/solution.py
+++ b/solution.py
@@ -13,6 +13,7 @@
 CODES = 27
 ROWS = CODES * W
 DEG = 24
+PAIRS = DEG // 2
 SLAB = 32
 OUTER = [
     p for p in range(64) if p // 16 in (0, 3) or p // 4 % 4 in (0, 3) or p % 4 in (0, 3)
@@ -187,7 +188,7 @@
     cnt_ref,
     *refs,
 ):
-    around, (idx_ref, steps_ref, dead_ref, ghosts, held) = refs[:AROUND], refs[AROUND:]
+    around, (idx_ref, steps_ref, times_ref, ghosts, held) = refs[:AROUND], refs[AROUND:]
     fill_ghosts(pos_ref, around, ghosts)
     alive = jnp.where(ghosts[...].astype(F32) < MARK * 0.5, 1.0, 0.0).astype(BF16)
     at = iota((W, GHOSTS), 1)
@@ -228,20 +229,25 @@
         used = jnp.zeros((8, W), F32)
         for k in range(DEG):
             used = used + jnp.where(keys[k] < DUMMY, 1.0, 0.0)
-            idx_ref[pl.ds(b * 8 * DEG + k, 8, stride=DEG), :] = keys[k].astype(I32)
+        for j in range(PAIRS):
+            word = keys[2 * j].astype(I32) + keys[2 * j + 1].astype(I32) * 65536
+            idx_ref[pl.ds(b * 8 * PAIRS + j, 8, stride=PAIRS), :] = word
         for shift in (1, 2, 4, 8):
             used = jnp.maximum(used, pltpu.roll(used, W - shift, 1))
         steps_ref[b * 8 : (b + 1) * 8, :] = used.astype(I32)
-        dead_ref[b * 8 : (b + 1) * 8, :] = dead
+        for c in range(b * 8, min(b * 8 + 8, CODES)):
+            row = jnp.broadcast_to(dead[c - b * 8 : c - b * 8 + 1, :], (W, W))
+            lone = jnp.where(eye, row, 0.0).astype(BF16)
+            times_ref[c * W : (c + 1) * W, :] = dot(lone, jnp.ones((W, W), BF16)).astype(BF16)
 
 
 def indices(pos, nbr, valid, cnt, around):
     return pl.pallas_call(
         index_kernel,
         out_shape=[
-            jax.ShapeDtypeStruct((DEG * 32, W), I32),
+            jax.ShapeDtypeStruct((PAIRS * 32, W), I32),
             jax.ShapeDtypeStruct((32, W), I32),
-            jax.ShapeDtypeStruct((32, W), F32),
+            jax.ShapeDtypeStruct((ROWS, W), BF16),
         ],
         in_specs=[smem()] + [vmem()] * (3 + AROUND),
         out_specs=[vmem()] * 3,
@@ -253,10 +259,66 @@
 
 GROUP = 16
 SPAN = 27
-FIRST = 13
-TAILS = (0, 1, 2, 3, 5, 7, 11)
+FIRST = 12
+TAILS = (0, 2, 4, 6, 8, 12)
 DUMP = ROWS
 PARTS = ((0, 3), (3, 11), (11, CODES))
+
+
+def project_kernel(state_ref, efirst_ref, table_ref, recv_ref):
+    w_both = jnp.concatenate([efirst_ref[0:W, :], efirst_ref[W : 2 * W, :]], axis=1)
+
+    def own(i, carry):
+        rows = pl.ds(pl.multiple_of(i * 1152, 1152), 1152)
+        both = dot(state_ref[rows, :], w_both)
+        recv_ref[rows, :] = both[:, :W]
+        table_ref[rows, :] = both[:, W:]
+        return carry
+
+    lax.fori_loop(0, ROWS // 1152, own, 0)
+    table_ref[NODES : NODES + 8, :] = jnp.full((8, W), -MARK, F32)
+
+
+def project(state, efirst):
+    return pl.pallas_call(
+        project_kernel,
+        out_shape=[
+            jax.ShapeDtypeStruct((NODES + 8, W), F32),
+            jax.ShapeDtypeStruct((ROWS, W), F32),
+        ],
+        in_specs=[vmem()] * 2,
+        out_specs=[vmem()] * 2,
+        compiler_params=pltpu.CompilerParams(vmem_limit_bytes=VMEM_LIMIT),
+        name="project",
+    )(state, efirst)
+
+
+def lone_kernel(state_ref, recv_ref, esecond_ref, nfirst_ref, alone_ref, first_ref):
+    w_second = esecond_ref[...]
+    n_state = nfirst_ref[0:W, :]
+
+    def some(i, carry):
+        rows = pl.ds(pl.multiple_of(i * 1152, 1152), 1152)
+        alone = jnp.maximum(recv_ref[rows, :], 0.0).astype(BF16)
+        alone_ref[rows, :] = jnp.maximum(dot(alone, w_second), 0.0).astype(BF16)
+        first_ref[rows, :] = dot(state_ref[rows, :], n_state)
+        return carry
+
+    lax.fori_loop(0, ROWS // 1152, some, 0)
+
+
+def lone(state, recv, esecond, nfirst):
+    return pl.pallas_call(
+        lone_kernel,
+        out_shape=[
+            jax.ShapeDtypeStruct((ROWS, W), BF16),
+            jax.ShapeDtypeStruct((ROWS, W), F32),
+        ],
+        in_specs=[vmem()] * 4,
+        out_specs=[vmem()] * 2,
+        compiler_params=pltpu.CompilerParams(vmem_limit_bytes=VMEM_LIMIT),
+        name="lone",
+    )(state, recv, esecond, nfirst)
 
 
 def layer_kernel(
@@ -265,32 +327,26 @@
     steps_ref,
     cnt_ref,
     gidx_ref,
-    dead_ref,
+    table_in,
+    recv,
+    alone_ref,
+    first_ref,
+    times_ref,
     state_ref,
     *refs,
 ):
     around, refs = refs[:AROUND], refs[AROUND:]
     efirst_ref, esecond_ref, ethird_ref, nfirst_ref, nsecond_ref, nthird_ref = refs[:6]
-    out_ref, down_ref, up_ref = refs[6:9]
-    table, recv, ghosts, hidden, agg, full, picked, idx_ref, sems = refs[9:]
+    table, out_ref, down_ref, up_ref = refs[6:10]
+    ghosts, hidden, agg, full, picked, idx_ref, sems = refs[10:]
+    del table_in
     copies = []
     for i, (lo, hi) in enumerate(PARTS):
-        words = pl.ds(lo * DEG * W, (hi - lo) * DEG * W)
+        words = pl.ds(lo * PAIRS * W, (hi - lo) * PAIRS * W)
         copies.append(pltpu.make_async_copy(idx_hbm.at[words], idx_ref.at[words], sems.at[i]))
         copies[-1].start()
-    w_recv = efirst_ref[0:W, :]
     w_send = efirst_ref[W : 2 * W, :]
-    w_both = jnp.concatenate([w_recv, w_send], axis=1)
     fill_ghosts(pos_ref, around, ghosts)
-
-    def own(i, carry):
-        rows = pl.ds(pl.multiple_of(i * 1152, 1152), 1152)
-        both = dot(state_ref[rows, :], w_both)
-        recv[rows, :] = both[:, :W]
-        table[rows, :] = both[:, W:]
-        return carry
-
-    lax.fori_loop(0, ROWS // 1152, own, 0)
 
     def far(i, carry):
         x = ghosts[pl.ds(pl.multiple_of(i * 896, 128), 896), :].astype(F32)
@@ -299,7 +355,6 @@
         return carry
 
     lax.fori_loop(0, GHOSTS // 896, far, 0)
-    table[NODES : NODES + 8, :] = jnp.full((8, W), -MARK, F32)
 
     w_second = esecond_ref[...]
     sub = iota((8, W), 0)
@@ -310,16 +365,20 @@
             d.reshape(DEG, GROUP, W), axis=0
         )
 
-    def step(base, mine, k):
-        both = []
-        for half in range(2):
-            got = None
-            for r in range(8):
-                at = idx_ref[base + (k * W + half * 8 + r)]
-                row = jnp.broadcast_to(table[pl.ds(at, 1), :], (8, W))
-                got = row if got is None else jnp.where(sub == r, row, got)
-            both.append(jnp.maximum(got + mine[half], 0.0))
-        hidden[k * GROUP : (k + 1) * GROUP, :] = jnp.concatenate(both, axis=0).astype(BF16)
+    def steps(base, mine, lo, hi):
+        for j in range(lo // 2, (hi + 1) // 2):
+            ks = [k for k in (2 * j, 2 * j + 1) if lo <= k < hi]
+            got = {}
+            for half in range(2):
+                for r in range(8):
+                    word = idx_ref[base + (j * W + half * 8 + r)]
+                    for k in ks:
+                        at = word & 65535 if k % 2 == 0 else lax.shift_right_logical(word, 16)
+                        row = jnp.broadcast_to(table[pl.ds(at, 1), :], (8, W))
+                        got[k, half] = row if r == 0 else jnp.where(sub == r, row, got[k, half])
+            for k in ks:
+                both = [jnp.maximum(got[k, half] + mine[half], 0.0) for half in range(2)]
+                hidden[k * GROUP : (k + 1) * GROUP, :] = jnp.concatenate(both, axis=0).astype(BF16)
 
     def sender(c, last):
         groups = lax.shift_right_logical(cnt_ref[c, 0] + (GROUP - 1), 4)
@@ -329,18 +388,16 @@
         def gather(g, last):
             q0 = pl.multiple_of(g * GROUP, GROUP)
             home = c * W + q0
-            base = c * (DEG * W) + q0
+            base = c * (PAIRS * W) + q0
             mine = [recv[pl.ds(pl.multiple_of(home + h * 8, 8), 8), :] for h in range(2)]
             finish(hidden[...], last)
-            for k in range(FIRST):
-                step(base, mine, k)
+            steps(base, mine, 0, FIRST)
             more = steps_ref[c, q0] - FIRST
             which = sum((more > t).astype(I32) for t in TAILS[:-1])
 
             def tail(size):
                 def run():
-                    for k in range(FIRST, FIRST + size):
-                        step(base, mine, k)
+                    steps(base, mine, FIRST, FIRST + size)
                     if FIRST + size < DEG:
                         hidden[(FIRST + size) * GROUP :, :] = jnp.zeros(
                             ((DEG - FIRST - size) * GROUP, W), BF16
@@ -357,34 +414,22 @@
     finish(hidden[...], last)
 
     w_third = ethird_ref[...]
-    n_state = nfirst_ref[0:W, :]
     n_agg = nfirst_ref[W : 2 * W, :]
     n_second = nsecond_ref[...]
     n_third = nthird_ref[...]
-    eye = iota((W, W), 0) == iota((W, W), 1)
-    ones = jnp.ones((W, W), BF16)
 
     def node(i, carry):
         rows = pl.ds(pl.multiple_of(i * (SPAN * W), SPAN * W), SPAN * W)
         live = jnp.concatenate(
             [iota((W, W), 0) < cnt_ref[i * SPAN + j, 0] for j in range(SPAN)], axis=0
         )
-        times = jnp.concatenate(
-            [
-                jnp.where(eye, jnp.broadcast_to(dead_ref[pl.ds(i * SPAN + j, 1), :], (W, W)), 0.0)
-                for j in range(SPAN)
-            ],
-            axis=0,
-        )
-        times = dot(times.astype(BF16), ones)
-        alone = jnp.maximum(recv[rows, :], 0.0).astype(BF16)
-        alone = jnp.maximum(dot(alone, w_second), 0.0).astype(BF16).astype(F32)
-        summed = jnp.where(live, agg[rows, :] + times * alone, 0.0)
+        lone_part = times_ref[rows, :].astype(F32) * alone_ref[rows, :].astype(F32)
+        summed = jnp.where(live, agg[rows, :] + lone_part, 0.0)
         top = summed.astype(BF16)
         rest = (summed - top.astype(F32)).astype(BF16)
         total = (dot(top, w_third) + dot(rest, w_third)).astype(BF16)
         state = state_ref[rows, :]
-        h = jnp.maximum(dot(state, n_state) + dot(total, n_agg), 0.0).astype(BF16)
+        h = jnp.maximum(first_ref[rows, :] + dot(total, n_agg), 0.0).astype(BF16)
         h = jnp.maximum(dot(h, n_second), 0.0).astype(BF16)
         update = dot(h, n_third)
         mean = jnp.mean(update, axis=1, keepdims=True)
@@ -399,30 +444,30 @@
     pick_slabs(gidx_ref, full, picked, down_ref, up_ref)
 
 
-def one_layer(idx, pos, steps, cnt, gidx, dead, state, around, weights):
+def one_layer(idx, pos, steps, cnt, gidx, own, times, state, around, weights):
     return pl.pallas_call(
         layer_kernel,
         out_shape=[
+            jax.ShapeDtypeStruct((NODES + 8, W), F32),
             jax.ShapeDtypeStruct((ROWS, W), BF16),
             jax.ShapeDtypeStruct((2, 2, SLAB, W), BF16),
             jax.ShapeDtypeStruct((2, 2, SLAB, W), BF16),
         ],
-        in_specs=[pl.BlockSpec(memory_space=pl.ANY)] + [smem()] * 4 + [vmem()] * (8 + AROUND),
-        out_specs=[vmem()] * 3,
+        in_specs=[pl.BlockSpec(memory_space=pl.ANY)] + [smem()] * 4 + [vmem()] * (12 + AROUND),
+        out_specs=[vmem()] * 4,
+        input_output_aliases={5: 0},
         scratch_shapes=[
-            pltpu.VMEM((NODES + 8, W), F32),
-            pltpu.VMEM((ROWS, W), F32),
             pltpu.VMEM((GHOSTS, W), BF16),
             pltpu.VMEM((DEG * GROUP, W), BF16),
             pltpu.VMEM((ROWS + GROUP, W), F32),
             pltpu.VMEM((ROWS, W), F32),
             pltpu.VMEM((8 * SLAB, W), F32),
-            pltpu.SMEM((ROWS * DEG,), I32),
+            pltpu.SMEM((ROWS * PAIRS,), I32),
             pltpu.SemaphoreType.DMA((len(PARTS),)),
         ],
         compiler_params=pltpu.CompilerParams(vmem_limit_bytes=VMEM_LIMIT),
         name="layer",
-    )(idx, pos, steps, cnt, gidx, dead, state, *around, *weights)
+    )(idx, pos, steps, cnt, gidx, *own, times, state, *around, *weights)[1:]
 
 
 def both_ways(up, down, axis):
@@ -481,11 +526,15 @@
             w[layer]
             for w in (edge_first, edge_second, edge_third, node_first, node_second, node_third)
         ]
+        table, recv = project(state, weights[0])
+        own = (table, recv, *lone(state, recv, weights[1], weights[3]))
         around = surround(down, up)
         if layer == 0:
-            idx, steps, dead = indices(pos, nbr, mask, cnt, around)
+            idx, steps, times = indices(pos, nbr, mask, cnt, around)
             idx = idx.reshape(-1)
-        state, down, up = one_layer(idx, pos, steps, cnt, gidx, dead, state, around, weights)
+        state, down, up = one_layer(
+            idx, pos, steps, cnt, gidx, own, times, state, around, weights
+        )
     return state.reshape(1, 1, 1, ROWS, W)
 
 

time: 128 us -> 130 us (1.016); the launches traced: 127 us -> 127 us
  Pallas kernels: 68.5 us -> 72 us
  waiting for transfers between devices: 38 us -> 35.2 us
    pallas_call x3 -> x7, Pallas kernels: 64.9 us -> 68.4 us  [the longest x2 63 us: one_layer(): pl.pallas_call(layer_kernel, out_shape=[jax.ShapeDtypeStruct((NODES + 8,...]
    ppermute x18, waiting for transfers between devices: 38 us -> 35.2 us  [both_ways(): return (lax.ppermute(up, axis, forward), lax.ppermute(down, axis, backward))]
  transfers between devices with their start and end apart: 18 -> 18, of which waited for: 16 -> 16; matrix products, arithmetic and copies ran while one was open for 0% -> 0% of each run, Pallas kernels for 0% -> 3%
where the time goes in v7:
time: 130 us; the launch traced here: 127 us
  Pallas kernels  72 us (55%)
  waiting for transfers between devices  35.2 us (27%)
  starting transfers between devices  16.9 us (13%)
  local copies, waits for them, and re-layouts  2.03 us (2%)
    pallas_call x2, Pallas kernels, one_layer(): pl.pallas_call(layer_kernel, out_shape=[jax.ShapeDtypeStruct((NODES + 8,...  63 us
    ppermute x18, waiting for transfers between devices, both_ways(): return (lax.ppermute(up, axis, forward), lax.ppermute(down, axis, backward))  35.2 us
    ppermute x18, starting transfers between devices, both_ways(): return (lax.ppermute(up, axis, forward), lax.ppermute(down, axis, backward))  16.9 us
  transfers between devices with their start and end apart: 18, of which 16 were waited for; matrix products, arithmetic and copies ran while one was open for 0% of the time, Pallas kernels for 3%

profile of v7, /device:TPU:106, one launch (start us, length us, event | category | flops | bytes accessed | tf_op | source)
XLA Modules:
  0.0 127.2 jit_solution(3013140982438501328)
XLA Ops:
  0.0 0.9 copy-done.2
  1.6 2.2 %pack.1 = (bf16[3,3,128,128]{3,2,1,0:T(8,128)(2,1)S(1)}, bf16[3,3,128,128]{3,2,1,0:T(8,128)(2,1)S(1)}, bf16[3,3,128,128]{3,2,1,0:T(8,128)(2,1)S(1)}) custom-call(s32[1,1024]{1,0:T(1,128)S(1)} %bitcast.224, bf16[1024,128]{1,0:T(8,128)(2,1)S(1)} %bitcast.223), custom_call_target="tpu_custom_call" | custom-call | tf_op jit(solution)/shard_map/pack/pallas_call | solution.py:79
  3.9 1.6 %collective-permute-start = (bf16[3,3,128,128]{3,2,1,0:T(8,128)(2,1)S(1)}, bf16[3,3,128,128]{3,2,1,0:T(8,128)(2,1)S(1)}, u32[]{:S(2)}, u32[]{:S(2)}) collective-permute-start(bf16[3,3,128,128]{3,2,1,0:T(8,128)(2,1)S(1)} %get-tuple-element.27), channel_id=1, source_target_pairs={{0,32},{32,64},{64,96},{96,0},{1,33},{33,65},{65,97},{97,1},{2,34}... | collective-permute-start | bytes 884744 | tf_op jit(solution)/shard_map/ppermute | solution.py:477
  6.0 6.7 %collective-permute-done = bf16[3,3,128,128]{3,2,1,0:T(8,128)(2,1)S(1)} collective-permute-done((bf16[3,3,128,128]{3,2,1,0:T(8,128)(2,1)S(1)}, bf16[3,3,128,128]{3,2,1,0:T(8,128)(2,1)S(1)}, u32[]{:S(2)}, u32[]{:S(2)}) %collective-permute-start) | collective-permute-done | bytes 294944 | tf_op jit(solution)/shard_map/ppermute | solution.py:477
  12.7 1.2 collective-permute-done.1
  14.1 1.6 %collective-permute-start.2 = (bf16[3,3,128,128]{3,2,0,1:T(8,128)(2,1)S(1)}, bf16[3,3,128,128]{3,2,0,1:T(8,128)(2,1)S(1)}, u32[]{:S(2)}, u32[]{:S(2)}) collective-permute-start(bf16[3,3,128,128]{3,2,0,1:T(8,128)(2,1)S(1)} %get-tuple-element.52), channel_id=1, source_target_pairs={{0,8},{8,16},{16,24},{24,0},{1,9},{9,17},{17,25},{25,1},{2,10},{10... | collective-permute-start | bytes 884744 | tf_op jit(solution)/shard_map/ppermute | solution.py:477
  16.2 5.5 %collective-permute-done.2 = bf16[3,3,128,128]{3,2,0,1:T(8,128)(2,1)S(1)} collective-permute-done((bf16[3,3,128,128]{3,2,0,1:T(8,128)(2,1)S(1)}, bf16[3,3,128,128]{3,2,0,1:T(8,128)(2,1)S(1)}, u32[]{:S(2)}, u32[]{:S(2)}) %collective-permute-start.2) | collective-permute-done | bytes 294944 | tf_op jit(solution)/shard_map/ppermute | solution.py:477
  21.8 1.3 %collective-permute-done.3 = bf16[3,3,128,128]{3,2,0,1:T(8,128)(2,1)S(1)} collective-permute-done((bf16[3,3,128,128]{3,2,0,1:T(8,128)(2,1)S(1)}, bf16[3,3,128,128]{3,2,0,1:T(8,128)(2,1)S(1)}, u32[]{:S(2)}, u32[]{:S(2)}) %collective-permute-start.3) | collective-permute-done | bytes 294944 | tf_op jit(solution)/shard_map/ppermute | solution.py:477
  23.9 3.6 %collective-permute-done.5.high_ref = bf16[3,3,128,128]{3,2,1,0:T(8,128)(2,1)S(1)} collective-permute-done((bf16[3,3,128,128]{3,2,1,0:T(8,128)(2,1)S(1)}, bf16[3,3,128,128]{3,2,1,0:T(8,128)(2,1)S(1)}, u32[]{:S(2)}, u32[]{:S(2)}) %collective-permute-start.5) | collective-permute-done | bytes 294944 | tf_op jit(solution)/shard_map/ppermute | solution.py:477
  27.5 1.9 %collective-permute-done.4.low_ref = bf16[3,3,128,128]{3,2,1,0:T(8,128)(2,1)S(1)} collective-permute-done((bf16[3,3,128,128]{3,2,1,0:T(8,128)(2,1)S(1)}, bf16[3,3,128,128]{3,2,1,0:T(8,128)(2,1)S(1)}, u32[]{:S(2)}, u32[]{:S(2)}) %collective-permute-start.4) | collective-permute-done | bytes 294944 | tf_op jit(solution)/shard_map/ppermute | solution.py:477
  29.4 1.3 %receive.1 = (bf16[3456,128]{1,0:T(8,128)(2,1)S(1)}, s32[32,128]{1,0:T(8,128)S(1)}, bf16[2,2,32,128]{3,2,1,0:T(8,128)(2,1)S(1)}, bf16[2,2,32,128]{3,2,1,0:T(8,128)(2,1)S(1)}) custom-call(s32[256]{0:T(256)S(1)} %reshape.12.gidx_ref, bf16[3,3,128,128]{3,2,1,0:T(8,128)(2,1)S(1)} %get-tuple-element.51.mid_ref, ...), custom_call_target="tpu_custom_call" | custom-call | tf_op jit(solution)/shard_map/receive/pallas_call | solution.py:129
  30.8 1.3 collective-permute-start.6
  32.9 1.9 %collective-permute-done.6.refs_0_ = bf16[2,2,32,128]{3,2,1,0:T(8,128)(2,1)S(1)} collective-permute-done((bf16[2,2,32,128]{3,2,1,0:T(8,128)(2,1)S(1)}, bf16[2,2,32,128]{3,2,1,0:T(8,128)(2,1)S(1)}, u32[]{:S(2)}, u32[]{:S(2)}) %collective-permute-start.6) | collective-permute-done | bytes 32800 | tf_op jit(solution)/shard_map/ppermute | solution.py:477
  34.8 1.2 collective-permute-done.7.refs_1_
  36.0 1.4 %collective-permute-start.8 = (bf16[4,2,32,128]{3,2,1,0:T(8,128)(2,1)S(1)}, bf16[4,2,32,128]{3,2,1,0:T(8,128)(2,1)S(1)}, u32[]{:S(2)}, u32[]{:S(2)}) collective-permute-start(bf16[4,2,32,128]{3,2,1,0:T(8,128)(2,1)S(1)} %pad_maximum_fusion.6), channel_id=1, source_target_pairs={{0,8},{8,16},{16,24},{24,0},{1,9},{9,17},{17,25},{25,1},{2,10},{10... | collective-permute-start | bytes 196616 | tf_op jit(solution)/shard_map/ppermute | solution.py:477
  38.2 2.1 %collective-permute-done.8.refs_2_ = bf16[4,2,32,128]{3,2,1,0:T(8,128)(2,1)S(1)} collective-permute-done((bf16[4,2,32,128]{3,2,1,0:T(8,128)(2,1)S(1)}, bf16[4,2,32,128]{3,2,1,0:T(8,128)(2,1)S(1)}, u32[]{:S(2)}, u32[]{:S(2)}) %collective-permute-start.8) | collective-permute-done | bytes 65568 | tf_op jit(solution)/shard_map/ppermute | solution.py:477
  40.3 1.4 %collective-permute-done.9.refs_3_ = bf16[4,2,32,128]{3,2,1,0:T(8,128)(2,1)S(1)} collective-permute-done((bf16[4,2,32,128]{3,2,1,0:T(8,128)(2,1)S(1)}, bf16[4,2,32,128]{3,2,1,0:T(8,128)(2,1)S(1)}, u32[]{:S(2)}, u32[]{:S(2)}) %collective-permute-start.9) | collective-permute-done | bytes 65568 | tf_op jit(solution)/shard_map/ppermute | solution.py:477
  41.9 1.7 %collective-permute-start.11 = (bf16[4,4,32,128]{3,2,1,0:T(8,128)(2,1)S(1)}, bf16[4,4,32,128]{3,2,1,0:T(8,128)(2,1)S(1)}, u32[]{:S(2)}, u32[]{:S(2)}) collective-permute-start(bf16[4,4,32,128]{3,2,1,0:T(8,128)(2,1)S(1)} %pad_maximum_fusion.3), channel_id=1, source_target_pairs={{1,0},{2,1},{3,2},{4,3},{5,4},{6,5},{7,6},{0,7},{9,8},{10,9},{11,1... | collective-permute-start | bytes 393224 | tf_op jit(solution)/shard_map/ppermute | solution.py:477
  44.6 0.9 lone.2
  46.2 1.9 %indices.1 = (s32[384,128]{1,0:T(8,128)S(1)}, s32[32,128]{1,0:T(8,128)S(1)}, bf16[3456,128]{1,0:T(8,128)(2,1)S(1)}) custom-call(s32[3]{0:T(128)S(1)} %pad_add_fusion.pos_ref, s32[24,3456]{1,0:T(8,128)S(1)} %bitcast.220, s32[24,3456]{1,0:T(8,128)S(1)} %bitcast.221, s32[32,128]{1,0:T(8,128)S(1)} %get-tuple-element.30.cnt_ref, ...), custom_call_target="tpu_custom_call" | custom-call | tf_op jit(solution)/shard_map/indices/pallas_call | solution.py:245
  48.1 31.0 %layer.2 = (f32[5256,128]{1,0:T(8,128)S(1)}, bf16[3456,128]{1,0:T(8,128)(2,1)S(1)}, bf16[2,2,32,128]{3,2,1,0:T(8,128)(2,1)S(1)}, bf16[2,2,32,128]{3,2,1,0:T(8,128)(2,1)S(1)}) custom-call(s32[49152]{0:T(1024)S(1)} %bitcast.218, s32[3]{0:T(128)S(1)} %pad_add_fusion.pos_ref, ...), custom_call_target="tpu_custom_call", output_to_operand_aliasing={{0}: (5, {})} | custom-call | tf_op jit(solution)/shard_map/layer/pallas_call | solution.py:448
  79.2 2.0 %collective-permute-start.12 = (bf16[2,2,32,128]{3,2,1,0:T(8,128)(2,1)S(1)}, bf16[2,2,32,128]{3,2,1,0:T(8,128)(2,1)S(1)}, u32[]{:S(2)}, u32[]{:S(2)}) collective-permute-start(bf16[2,2,32,128]{3,2,1,0:T(8,128)(2,1)S(1)} %get-tuple-element.46), channel_id=1, source_target_pairs={{0,32},{32,64},{64,96},{96,0},{1,33},{33,65},{65,97},{97,1},{2,34}... | collective-permute-start | bytes 98312 | tf_op jit(solution)/shard_map/ppermute | solution.py:477
  81.5 1.9 %collective-permute-done.12.refs_0_ = bf16[2,2,32,128]{3,2,1,0:T(8,128)(2,1)S(1)} collective-permute-done((bf16[2,2,32,128]{3,2,1,0:T(8,128)(2,1)S(1)}, bf16[2,2,32,128]{3,2,1,0:T(8,128)(2,1)S(1)}, u32[]{:S(2)}, u32[]{:S(2)}) %collective-permute-start.12) | collective-permute-done | bytes 32800 | tf_op jit(solution)/shard_map/ppermute | solution.py:477
  83.3 1.8 %collective-permute-done.13.refs_1_ = bf16[2,2,32,128]{3,2,1,0:T(8,128)(2,1)S(1)} collective-permute-done((bf16[2,2,32,128]{3,2,1,0:T(8,128)(2,1)S(1)}, bf16[2,2,32,128]{3,2,1,0:T(8,128)(2,1)S(1)}, u32[]{:S(2)}, u32[]{:S(2)}) %collective-permute-start.13) | collective-permute-done | bytes 32800 | tf_op jit(solution)/shard_map/ppermute | solution.py:477
  85.1 1.1 collective-permute-start.14
  86.3 1.0 collective-permute-start.15
  87.3 2.1 %collective-permute-done.14.refs_2_ = bf16[4,2,32,128]{3,2,1,0:T(8,128)(2,1)S(1)} collective-permute-done((bf16[4,2,32,128]{3,2,1,0:T(8,128)(2,1)S(1)}, bf16[4,2,32,128]{3,2,1,0:T(8,128)(2,1)S(1)}, u32[]{:S(2)}, u32[]{:S(2)}) %collective-permute-start.14) | collective-permute-done | bytes 65568 | tf_op jit(solution)/shard_map/ppermute | solution.py:477
  89.5 1.1 collective-permute-done.15.refs_3_
  90.8 1.7 %collective-permute-start.17 = (bf16[4,4,32,128]{3,2,1,0:T(8,128)(2,1)S(1)}, bf16[4,4,32,128]{3,2,1,0:T(8,128)(2,1)S(1)}, u32[]{:S(2)}, u32[]{:S(2)}) collective-permute-start(bf16[4,4,32,128]{3,2,1,0:T(8,128)(2,1)S(1)} %pad_maximum_fusion.5), channel_id=1, source_target_pairs={{1,0},{2,1},{3,2},{4,3},{5,4},{6,5},{7,6},{0,7},{9,8},{10,9},{11,1... | collective-permute-start | bytes 393224 | tf_op jit(solution)/shard_map/ppermute | solution.py:477
  92.5 0.9 project.3
  93.4 0.9 lone.3
  95.1 32.0 %layer.3 = (f32[5256,128]{1,0:T(8,128)S(1)}, bf16[3456,128]{1,0:T(8,128)(2,1)}, bf16[2,2,32,128]{3,2,1,0:T(8,128)(2,1)}, bf16[2,2,32,128]{3,2,1,0:T(8,128)(2,1)}) custom-call(s32[49152]{0:T(1024)S(1)} %bitcast.219, s32[3]{0:T(128)S(1)} %pad_add_fusion.pos_ref, s32[32,128]{1,0:T(8,128)S(1)} %get-tuple-element.34.steps_ref, ...), custom_call_target="tpu_custom_call", output_to_operand_aliasing={{0}: (5, {})} | custom-call | tf_op jit(solution)/shard_map/layer/pallas_call | solution.py:448
  (87 shorter events, 7.4 us)
Async XLA Ops:
  0.0 0.9 copy-start.2
  1.0 0.7 copy-start.3
  1.6 14.6 %copy-start.8 = (bf16[2,128,128]{2,1,0:T(8,128)(2,1)S(1)}, bf16[2,128,128]{2,1,0:T(8,128)(2,1)}, u32[]{:S(2)}) copy-start(bf16[2,128,128]{2,1,0:T(8,128)(2,1)} %param.21) | copy-start | bytes 196612
  1.6 14.6 %copy-start.9 = (bf16[2,128,128]{2,1,0:T(8,128)(2,1)S(1)}, bf16[2,128,128]{2,1,0:T(8,128)(2,1)}, u32[]{:S(2)}) copy-start(bf16[2,128,128]{2,1,0:T(8,128)(2,1)} %param.20) | copy-start | bytes 196612
  3.9 8.8 %collective-permute-start = (bf16[3,3,128,128]{3,2,1,0:T(8,128)(2,1)S(1)}, bf16[3,3,128,128]{3,2,1,0:T(8,128)(2,1)S(1)}, u32[]{:S(2)}, u32[]{:S(2)}) collective-permute-start(bf16[3,3,128,128]{3,2,1,0:T(8,128)(2,1)S(1)} %get-tuple-element.27), channel_id=1, source_target_pairs={{0,32},{32,64},{64,96},{96,0},{1,33},{33,65},{65,97},{97,1},{2,34}... | collective-permute-start | bytes 884744 | tf_op jit(solution)/shard_map/ppermute | solution.py:477
  5.4 8.5 %collective-permute-start.1 = (bf16[3,3,128,128]{3,2,1,0:T(8,128)(2,1)S(1)}, bf16[3,3,128,128]{3,2,1,0:T(8,128)(2,1)S(1)}, u32[]{:S(2)}, u32[]{:S(2)}) collective-permute-start(bf16[3,3,128,128]{3,2,1,0:T(8,128)(2,1)S(1)} %get-tuple-element.29), channel_id=1, source_target_pairs={{32,0},{64,32},{96,64},{0,96},{33,1},{65,33},{97,65},{1,97},{34,2}... | collective-permute-start | bytes 884744 | tf_op jit(solution)/shard_map/ppermute | solution.py:477
  14.0 9.8 %copy-start.6 = (bf16[2,128,128]{2,1,0:T(8,128)(2,1)S(1)}, bf16[2,128,128]{2,1,0:T(8,128)(2,1)}, u32[]{:S(2)}) copy-start(bf16[2,128,128]{2,1,0:T(8,128)(2,1)} %param.17) | copy-start | bytes 196612
  14.0 9.8 %copy-start.10 = (s32[1,1,1,8,32]{4,3,2,1,0:T(8,128)S(1)}, s32[1,1,1,8,32]{4,3,2,1,0:T(8,128)}, u32[]{:S(2)}) copy-start(s32[1,1,1,8,32]{4,3,2,1,0:T(8,128)} %param.15) | copy-start | bytes 3076
  14.0 9.8 %copy-start.4 = (bf16[2,256,128]{2,1,0:T(8,128)(2,1)S(1)}, bf16[2,256,128]{2,1,0:T(8,128)(2,1)}, u32[]{:S(2)}) copy-start(bf16[2,256,128]{2,1,0:T(8,128)(2,1)} %param.19) | copy-start | bytes 393220
  14.0 9.8 %copy-start.5 = (bf16[2,256,128]{2,1,0:T(8,128)(2,1)S(1)}, bf16[2,256,128]{2,1,0:T(8,128)(2,1)}, u32[]{:S(2)}) copy-start(bf16[2,256,128]{2,1,0:T(8,128)(2,1)} %param.16) | copy-start | bytes 393220
  14.1 7.6 %collective-permute-start.2 = (bf16[3,3,128,128]{3,2,0,1:T(8,128)(2,1)S(1)}, bf16[3,3,128,128]{3,2,0,1:T(8,128)(2,1)S(1)}, u32[]{:S(2)}, u32[]{:S(2)}) collective-permute-start(bf16[3,3,128,128]{3,2,0,1:T(8,128)(2,1)S(1)} %get-tuple-element.52), channel_id=1, source_target_pairs={{0,8},{8,16},{16,24},{24,0},{1,9},{9,17},{17,25},{25,1},{2,10},{10... | collective-permute-start | bytes 884744 | tf_op jit(solution)/shard_map/ppermute | solution.py:477
  15.8 7.3 %collective-permute-start.3 = (bf16[3,3,128,128]{3,2,0,1:T(8,128)(2,1)S(1)}, bf16[3,3,128,128]{3,2,0,1:T(8,128)(2,1)S(1)}, u32[]{:S(2)}, u32[]{:S(2)}) collective-permute-start(bf16[3,3,128,128]{3,2,0,1:T(8,128)(2,1)S(1)} %get-tuple-element.53), channel_id=1, source_target_pairs={{8,0},{16,8},{24,16},{0,24},{9,1},{17,9},{25,17},{1,25},{10,2},{18... | collective-permute-start | bytes 884744 | tf_op jit(solution)/shard_map/ppermute | solution.py:477
  23.1 20.5 %copy-start.7 = (bf16[2,128,128]{2,1,0:T(8,128)(2,1)S(1)}, bf16[2,128,128]{2,1,0:T(8,128)(2,1)}, u32[]{:S(2)}) copy-start(bf16[2,128,128]{2,1,0:T(8,128)(2,1)} %param.18) | copy-start | bytes 196612
  23.2 4.3 %collective-permute-start.5 = (bf16[3,3,128,128]{3,2,1,0:T(8,128)(2,1)S(1)}, bf16[3,3,128,128]{3,2,1,0:T(8,128)(2,1)S(1)}, u32[]{:S(2)}, u32[]{:S(2)}) collective-permute-start(bf16[3,3,128,128]{3,2,1,0:T(8,128)(2,1)S(1)} %get-tuple-element.49), channel_id=1, source_target_pairs={{1,0},{2,1},{3,2},{4,3},{5,4},{6,5},{7,6},{0,7},{9,8},{10,9},{11,1... | collective-permute-start | bytes 884744 | tf_op jit(solution)/shard_map/ppermute | solution.py:477
  23.3 6.2 %collective-permute-start.4 = (bf16[3,3,128,128]{3,2,1,0:T(8,128)(2,1)S(1)}, bf16[3,3,128,128]{3,2,1,0:T(8,128)(2,1)S(1)}, u32[]{:S(2)}, u32[]{:S(2)}) collective-permute-start(bf16[3,3,128,128]{3,2,1,0:T(8,128)(2,1)S(1)} %get-tuple-element.50), channel_id=1, source_target_pairs={{0,1},{1,2},{2,3},{3,4},{4,5},{5,6},{6,7},{7,0},{8,9},{9,10},{10,1... | collective-permute-start | bytes 884744 | tf_op jit(solution)/shard_map/ppermute | solution.py:477
  30.8 4.0 %collective-permute-start.6 = (bf16[2,2,32,128]{3,2,1,0:T(8,128)(2,1)S(1)}, bf16[2,2,32,128]{3,2,1,0:T(8,128)(2,1)S(1)}, u32[]{:S(2)}, u32[]{:S(2)}) collective-permute-start(bf16[2,2,32,128]{3,2,1,0:T(8,128)(2,1)S(1)} %get-tuple-element.31), channel_id=1, source_target_pairs={{0,32},{32,64},{64,96},{96,0},{1,33},{33,65},{65,97},{97,1},{2,34}... | collective-permute-start | bytes 98312 | tf_op jit(solution)/shard_map/ppermute | solution.py:477
  32.1 3.9 %collective-permute-start.7 = (bf16[2,2,32,128]{3,2,1,0:T(8,128)(2,1)S(1)}, bf16[2,2,32,128]{3,2,1,0:T(8,128)(2,1)S(1)}, u32[]{:S(2)}, u32[]{:S(2)}) collective-permute-start(bf16[2,2,32,128]{3,2,1,0:T(8,128)(2,1)S(1)} %get-tuple-element.32), channel_id=1, source_target_pairs={{32,0},{64,32},{96,64},{0,96},{33,1},{65,33},{97,65},{1,97},{34,2}... | collective-permute-start | bytes 98312 | tf_op jit(solution)/shard_map/ppermute | solution.py:477
  36.0 4.3 %collective-permute-start.8 = (bf16[4,2,32,128]{3,2,1,0:T(8,128)(2,1)S(1)}, bf16[4,2,32,128]{3,2,1,0:T(8,128)(2,1)S(1)}, u32[]{:S(2)}, u32[]{:S(2)}) collective-permute-start(bf16[4,2,32,128]{3,2,1,0:T(8,128)(2,1)S(1)} %pad_maximum_fusion.6), channel_id=1, source_target_pairs={{0,8},{8,16},{16,24},{24,0},{1,9},{9,17},{17,25},{25,1},{2,10},{10... | collective-permute-start | bytes 196616 | tf_op jit(solution)/shard_map/ppermute | solution.py:477
  37.4 8.9 %copy-start = (s32[1,1,1,3456,24]{3,4,2,1,0:T(8,128)S(1)}, s32[1,1,1,3456,24]{3,4,2,1,0:T(8,128)}, u32[]{:S(2)}) copy-start(s32[1,1,1,3456,24]{3,4,2,1,0:T(8,128)} %param.13) | copy-start | bytes 995332
  37.4 8.9 %copy-start.1 = (s32[1,1,1,3456,24]{3,4,2,1,0:T(8,128)S(1)}, s32[1,1,1,3456,24]{3,4,2,1,0:T(8,128)}, u32[]{:S(2)}) copy-start(s32[1,1,1,3456,24]{3,4,2,1,0:T(8,128)} %param.14) | copy-start | bytes 995332
  37.4 4.3 %collective-permute-start.9 = (bf16[4,2,32,128]{3,2,1,0:T(8,128)(2,1)S(1)}, bf16[4,2,32,128]{3,2,1,0:T(8,128)(2,1)S(1)}, u32[]{:S(2)}, u32[]{:S(2)}) collective-permute-start(bf16[4,2,32,128]{3,2,1,0:T(8,128)(2,1)S(1)} %pad_maximum_fusion.7), channel_id=1, source_target_pairs={{8,0},{16,8},{24,16},{0,24},{9,1},{17,9},{25,17},{1,25},{10,2},{18... | collective-permute-start | bytes 196616 | tf_op jit(solution)/shard_map/ppermute | solution.py:477
  41.8 4.4 %collective-permute-start.10 = (bf16[4,4,32,128]{3,2,1,0:T(8,128)(2,1)S(1)}, bf16[4,4,32,128]{3,2,1,0:T(8,128)(2,1)S(1)}, u32[]{:S(2)}, u32[]{:S(2)}) collective-permute-start(bf16[4,4,32,128]{3,2,1,0:T(8,128)(2,1)S(1)} %pad_maximum_fusion.2), channel_id=1, source_target_pairs={{0,1},{1,2},{2,3},{3,4},{4,5},{5,6},{6,7},{7,0},{8,9},{9,10},{10,1... | collective-permute-start | bytes 393224 | tf_op jit(solution)/shard_map/ppermute | solution.py:477
  41.9 4.3 %collective-permute-start.11 = (bf16[4,4,32,128]{3,2,1,0:T(8,128)(2,1)S(1)}, bf16[4,4,32,128]{3,2,1,0:T(8,128)(2,1)S(1)}, u32[]{:S(2)}, u32[]{:S(2)}) collective-permute-start(bf16[4,4,32,128]{3,2,1,0:T(8,128)(2,1)S(1)} %pad_maximum_fusion.3), channel_id=1, source_target_pairs={{1,0},{2,1},{3,2},{4,3},{5,4},{6,5},{7,6},{0,7},{9,8},{10,9},{11,1... | collective-permute-start | bytes 393224 | tf_op jit(solution)/shard_map/ppermute | solution.py:477
  79.2 4.2 %collective-permute-start.12 = (bf16[2,2,32,128]{3,2,1,0:T(8,128)(2,1)S(1)}, bf16[2,2,32,128]{3,2,1,0:T(8,128)(2,1)S(1)}, u32[]{:S(2)}, u32[]{:S(2)}) collective-permute-start(bf16[2,2,32,128]{3,2,1,0:T(8,128)(2,1)S(1)} %get-tuple-element.46), channel_id=1, source_target_pairs={{0,32},{32,64},{64,96},{96,0},{1,33},{33,65},{65,97},{97,1},{2,34}... | collective-permute-start | bytes 98312 | tf_op jit(solution)/shard_map/ppermute | solution.py:477
  81.2 3.9 %collective-permute-start.13 = (bf16[2,2,32,128]{3,2,1,0:T(8,128)(2,1)S(1)}, bf16[2,2,32,128]{3,2,1,0:T(8,128)(2,1)S(1)}, u32[]{:S(2)}, u32[]{:S(2)}) collective-permute-start(bf16[2,2,32,128]{3,2,1,0:T(8,128)(2,1)S(1)} %get-tuple-element.47), channel_id=1, source_target_pairs={{32,0},{64,32},{96,64},{0,96},{33,1},{65,33},{97,65},{1,97},{34,2}... | collective-permute-start | bytes 98312 | tf_op jit(solution)/shard_map/ppermute | solution.py:477
  85.1 4.3 %collective-permute-start.14 = (bf16[4,2,32,128]{3,2,1,0:T(8,128)(2,1)S(1)}, bf16[4,2,32,128]{3,2,1,0:T(8,128)(2,1)S(1)}, u32[]{:S(2)}, u32[]{:S(2)}) collective-permute-start(bf16[4,2,32,128]{3,2,1,0:T(8,128)(2,1)S(1)} %pad_maximum_fusion.8), channel_id=1, source_target_pairs={{0,8},{8,16},{16,24},{24,0},{1,9},{9,17},{17,25},{25,1},{2,10},{10... | collective-permute-start | bytes 196616 | tf_op jit(solution)/shard_map/ppermute | solution.py:477
  86.3 4.3 %collective-permute-start.15 = (bf16[4,2,32,128]{3,2,1,0:T(8,128)(2,1)S(1)}, bf16[4,2,32,128]{3,2,1,0:T(8,128)(2,1)S(1)}, u32[]{:S(2)}, u32[]{:S(2)}) collective-permute-start(bf16[4,2,32,128]{3,2,1,0:T(8,128)(2,1)S(1)} %pad_maximum_fusion.9), channel_id=1, source_target_pairs={{8,0},{16,8},{24,16},{0,24},{9,1},{17,9},{25,17},{1,25},{10,2},{18... | collective-permute-start | bytes 196616 | tf_op jit(solution)/shard_map/ppermute | solution.py:477
  90.7 4.4 %collective-permute-start.16 = (bf16[4,4,32,128]{3,2,1,0:T(8,128)(2,1)S(1)}, bf16[4,4,32,128]{3,2,1,0:T(8,128)(2,1)S(1)}, u32[]{:S(2)}, u32[]{:S(2)}) collective-permute-start(bf16[4,4,32,128]{3,2,1,0:T(8,128)(2,1)S(1)} %pad_maximum_fusion.4), channel_id=1, source_target_pairs={{0,1},{1,2},{2,3},{3,4},{4,5},{5,6},{6,7},{7,0},{8,9},{9,10},{10,1... | collective-permute-start | bytes 393224 | tf_op jit(solution)/shard_map/ppermute | solution.py:477
  90.8 4.3 %collective-permute-start.17 = (bf16[4,4,32,128]{3,2,1,0:T(8,128)(2,1)S(1)}, bf16[4,4,32,128]{3,2,1,0:T(8,128)(2,1)S(1)}, u32[]{:S(2)}, u32[]{:S(2)}) collective-permute-start(bf16[4,4,32,128]{3,2,1,0:T(8,128)(2,1)S(1)} %pad_maximum_fusion.5), channel_id=1, source_target_pairs={{1,0},{2,1},{3,2},{4,3},{5,4},{6,5},{7,6},{0,7},{9,8},{10,9},{11,1... | collective-permute-start | bytes 393224 | tf_op jit(solution)/shard_map/ppermute | solution.py:477

commit v8 on v7

--- a/solution.py
+++ b/solution.py
@@ -13,7 +13,6 @@
 CODES = 27
 ROWS = CODES * W
 DEG = 24
-PAIRS = DEG // 2
 SLAB = 32
 OUTER = [
     p for p in range(64) if p // 16 in (0, 3) or p // 4 % 4 in (0, 3) or p % 4 in (0, 3)
@@ -229,9 +228,7 @@
         used = jnp.zeros((8, W), F32)
         for k in range(DEG):
             used = used + jnp.where(keys[k] < DUMMY, 1.0, 0.0)
-        for j in range(PAIRS):
-            word = keys[2 * j].astype(I32) + keys[2 * j + 1].astype(I32) * 65536
-            idx_ref[pl.ds(b * 8 * PAIRS + j, 8, stride=PAIRS), :] = word
+            idx_ref[pl.ds(b * 8 * DEG + k, 8, stride=DEG), :] = keys[k].astype(I32)
         for shift in (1, 2, 4, 8):
             used = jnp.maximum(used, pltpu.roll(used, W - shift, 1))
         steps_ref[b * 8 : (b + 1) * 8, :] = used.astype(I32)
@@ -245,7 +242,7 @@
     return pl.pallas_call(
         index_kernel,
         out_shape=[
-            jax.ShapeDtypeStruct((PAIRS * 32, W), I32),
+            jax.ShapeDtypeStruct((DEG * 32, W), I32),
             jax.ShapeDtypeStruct((32, W), I32),
             jax.ShapeDtypeStruct((ROWS, W), BF16),
         ],
@@ -259,8 +256,8 @@
 
 GROUP = 16
 SPAN = 27
-FIRST = 12
-TAILS = (0, 2, 4, 6, 8, 12)
+FIRST = 13
+TAILS = (0, 1, 2, 3, 5, 7, 11)
 DUMP = ROWS
 PARTS = ((0, 3), (3, 11), (11, CODES))
 
@@ -338,11 +335,11 @@
     around, refs = refs[:AROUND], refs[AROUND:]
     efirst_ref, esecond_ref, ethird_ref, nfirst_ref, nsecond_ref, nthird_ref = refs[:6]
     table, out_ref, down_ref, up_ref = refs[6:10]
-    ghosts, hidden, agg, full, picked, idx_ref, sems = refs[10:]
+    ghosts, hidden, agg, full, picked, idx_ref, homes, sems = refs[10:]
     del table_in
     copies = []
     for i, (lo, hi) in enumerate(PARTS):
-        words = pl.ds(lo * PAIRS * W, (hi - lo) * PAIRS * W)
+        words = pl.ds(lo * DEG * W, (hi - lo) * DEG * W)
         copies.append(pltpu.make_async_copy(idx_hbm.at[words], idx_ref.at[words], sems.at[i]))
         copies[-1].start()
     w_send = efirst_ref[W : 2 * W, :]
@@ -359,58 +356,71 @@
     w_second = esecond_ref[...]
     sub = iota((8, W), 0)
 
-    def finish(h, row):
+    def listed(c, n):
+        for g in range(W // GROUP):
+            homes[n + g] = c * W + g * GROUP
+        return n + lax.shift_right_logical(cnt_ref[c, 0] + (GROUP - 1), 4)
+
+    starts = [jnp.int32(0)]
+    for lo, hi in PARTS:
+        starts.append(lax.fori_loop(lo, hi, listed, starts[-1]))
+    total = starts[-1]
+    homes[total] = homes[jnp.maximum(total - 1, 0)]
+    rounds = lax.shift_right_logical(total + 1, 1)
+    turns = [jnp.minimum(lax.shift_right_logical(n, 1), rounds) for n in starts[:-1]]
+
+    def finish(h, rows):
         d = jnp.maximum(dot(h, w_second), 0.0).astype(BF16).astype(F32)
-        agg[pl.ds(pl.multiple_of(row, GROUP), GROUP), :] = jnp.sum(
-            d.reshape(DEG, GROUP, W), axis=0
-        )
-
-    def steps(base, mine, lo, hi):
-        for j in range(lo // 2, (hi + 1) // 2):
-            ks = [k for k in (2 * j, 2 * j + 1) if lo <= k < hi]
-            got = {}
-            for half in range(2):
-                for r in range(8):
-                    word = idx_ref[base + (j * W + half * 8 + r)]
-                    for k in ks:
-                        at = word & 65535 if k % 2 == 0 else lax.shift_right_logical(word, 16)
-                        row = jnp.broadcast_to(table[pl.ds(at, 1), :], (8, W))
-                        got[k, half] = row if r == 0 else jnp.where(sub == r, row, got[k, half])
-            for k in ks:
-                both = [jnp.maximum(got[k, half] + mine[half], 0.0) for half in range(2)]
-                hidden[k * GROUP : (k + 1) * GROUP, :] = jnp.concatenate(both, axis=0).astype(BF16)
-
-    def sender(c, last):
-        groups = lax.shift_right_logical(cnt_ref[c, 0] + (GROUP - 1), 4)
-        for (lo, _), copy in zip(PARTS, copies):
-            pl.when(c == lo)(copy.wait)
-
-        def gather(g, last):
-            q0 = pl.multiple_of(g * GROUP, GROUP)
-            home = c * W + q0
-            base = c * (PAIRS * W) + q0
-            mine = [recv[pl.ds(pl.multiple_of(home + h * 8, 8), 8), :] for h in range(2)]
-            finish(hidden[...], last)
-            steps(base, mine, 0, FIRST)
-            more = steps_ref[c, q0] - FIRST
+        d = jnp.sum(d.reshape(2, DEG, GROUP, W), axis=1)
+        for slot, row in enumerate(rows):
+            agg[pl.ds(pl.multiple_of(row, GROUP), GROUP), :] = d[slot]
+
+    def step(slot, base, mine, k):
+        both = []
+        for half in range(2):
+            got = None
+            for r in range(8):
+                at = idx_ref[base + (k * W + half * 8 + r)]
+                row = jnp.broadcast_to(table[pl.ds(at, 1), :], (8, W))
+                got = row if got is None else jnp.where(sub == r, row, got)
+            both.append(jnp.maximum(got + mine[half], 0.0))
+        at = (slot * DEG + k) * GROUP
+        hidden[at : at + GROUP, :] = jnp.concatenate(both, axis=0).astype(BF16)
+
+    def gather(i, last):
+        for turn, copy in zip(turns, copies):
+            pl.when(i == turn)(copy.wait)
+        rows = [pl.multiple_of(homes[2 * i + slot], GROUP) for slot in range(2)]
+        codes = [lax.shift_right_logical(row, 7) for row in rows]
+        bases = [row + code * ((DEG - 1) * W) for row, code in zip(rows, codes)]
+        mines = [
+            [recv[pl.ds(pl.multiple_of(row + h * 8, 8), 8), :] for h in range(2)] for row in rows
+        ]
+        finish(hidden[...], last)
+        for slot in range(2):
+            for k in range(FIRST):
+                step(slot, bases[slot], mines[slot], k)
+        for slot in range(2):
+            more = steps_ref[codes[slot], rows[slot] & (W - 1)] - FIRST
             which = sum((more > t).astype(I32) for t in TAILS[:-1])
 
-            def tail(size):
+            def tail(size, slot=slot):
                 def run():
-                    steps(base, mine, FIRST, FIRST + size)
+                    for k in range(FIRST, FIRST + size):
+                        step(slot, bases[slot], mines[slot], k)
                     if FIRST + size < DEG:
-                        hidden[(FIRST + size) * GROUP :, :] = jnp.zeros(
-                            ((DEG - FIRST - size) * GROUP, W), BF16
-                        )
+                        rest = (DEG - FIRST - size) * GROUP
+                        end = (slot + 1) * DEG * GROUP
+                        hidden[end - rest : end, :] = jnp.zeros((rest, W), BF16)
 
                 return run
 
             lax.switch(which, [tail(t) for t in TAILS])
-            return home
-
-        return lax.fori_loop(0, groups, gather, last)
-
-    last = lax.fori_loop(0, CODES, sender, jnp.int32(DUMP))
+        return tuple(rows)
+
+    last = lax.fori_loop(0, rounds, gather, (jnp.int32(DUMP), jnp.int32(DUMP)))
+    for turn, copy in zip(turns, copies):
+        pl.when(turn == rounds)(copy.wait)
     finish(hidden[...], last)
 
     w_third = ethird_ref[...]
@@ -458,11 +468,12 @@
         input_output_aliases={5: 0},
         scratch_shapes=[
             pltpu.VMEM((GHOSTS, W), BF16),
-            pltpu.VMEM((DEG * GROUP, W), BF16),
+            pltpu.VMEM((2 * DEG * GROUP, W), BF16),
             pltpu.VMEM((ROWS + GROUP, W), F32),
             pltpu.VMEM((ROWS, W), F32),
             pltpu.VMEM((8 * SLAB, W), F32),
-            pltpu.SMEM((ROWS * PAIRS,), I32),
+            pltpu.SMEM((ROWS * DEG,), I32),
+            pltpu.SMEM((256,), I32),
             pltpu.SemaphoreType.DMA((len(PARTS),)),
         ],
         compiler_params=pltpu.CompilerParams(vmem_limit_bytes=VMEM_LIMIT),

time: 130 us -> 128 us (0.985); the launches traced: 127 us -> 127 us
  no operation moved by 1% of the time
where the time goes in v8:
time: 128 us; the launch traced here: 127 us
  Pallas kernels  73 us (57%)
  waiting for transfers between devices  34.5 us (27%)
  starting transfers between devices  16.7 us (13%)
  local copies, waits for them, and re-layouts  2.03 us (2%)
    pallas_call x2, Pallas kernels, one_layer(): pl.pallas_call(layer_kernel, out_shape=[jax.ShapeDtypeStruct((NODES + 8,...  63.9 us
    ppermute x18, waiting for transfers between devices, both_ways(): return (lax.ppermute(up, axis, forward), lax.ppermute(down, axis, backward))  34.5 us
    ppermute x18, starting transfers between devices, both_ways(): return (lax.ppermute(up, axis, forward), lax.ppermute(down, axis, backward))  16.7 us
  transfers between devices with their start and end apart: 18, of which 16 were waited for; matrix products, arithmetic and copies ran while one was open for 0% of the time, Pallas kernels for 3%

profile of v8, /device:TPU:106, one launch (start us, length us, event | category | flops | bytes accessed | tf_op | source)
XLA Modules:
  0.0 127.3 jit_solution(12754985140192152025)
XLA Ops:
  0.0 0.9 copy-done.2
  1.6 2.2 %pack.1 = (bf16[3,3,128,128]{3,2,1,0:T(8,128)(2,1)S(1)}, bf16[3,3,128,128]{3,2,1,0:T(8,128)(2,1)S(1)}, bf16[3,3,128,128]{3,2,1,0:T(8,128)(2,1)S(1)}) custom-call(s32[1,1024]{1,0:T(1,128)S(1)} %bitcast.224, bf16[1024,128]{1,0:T(8,128)(2,1)S(1)} %bitcast.223), custom_call_target="tpu_custom_call" | custom-call | tf_op jit(solution)/shard_map/pack/pallas_call | solution.py:78
  3.9 1.6 %collective-permute-start = (bf16[3,3,128,128]{3,2,1,0:T(8,128)(2,1)S(1)}, bf16[3,3,128,128]{3,2,1,0:T(8,128)(2,1)S(1)}, u32[]{:S(2)}, u32[]{:S(2)}) collective-permute-start(bf16[3,3,128,128]{3,2,1,0:T(8,128)(2,1)S(1)} %get-tuple-element.27), channel_id=1, source_target_pairs={{0,32},{32,64},{64,96},{96,0},{1,33},{33,65},{65,97},{97,1},{2,34}... | collective-permute-start | bytes 884744 | tf_op jit(solution)/shard_map/ppermute | solution.py:488
  6.0 6.7 %collective-permute-done = bf16[3,3,128,128]{3,2,1,0:T(8,128)(2,1)S(1)} collective-permute-done((bf16[3,3,128,128]{3,2,1,0:T(8,128)(2,1)S(1)}, bf16[3,3,128,128]{3,2,1,0:T(8,128)(2,1)S(1)}, u32[]{:S(2)}, u32[]{:S(2)}) %collective-permute-start) | collective-permute-done | bytes 294944 | tf_op jit(solution)/shard_map/ppermute | solution.py:488
  12.7 1.2 collective-permute-done.1
  14.1 1.6 %collective-permute-start.2 = (bf16[3,3,128,128]{3,2,0,1:T(8,128)(2,1)S(1)}, bf16[3,3,128,128]{3,2,0,1:T(8,128)(2,1)S(1)}, u32[]{:S(2)}, u32[]{:S(2)}) collective-permute-start(bf16[3,3,128,128]{3,2,0,1:T(8,128)(2,1)S(1)} %get-tuple-element.52), channel_id=1, source_target_pairs={{0,8},{8,16},{16,24},{24,0},{1,9},{9,17},{17,25},{25,1},{2,10},{10... | collective-permute-start | bytes 884744 | tf_op jit(solution)/shard_map/ppermute | solution.py:488
  16.2 5.5 %collective-permute-done.2 = bf16[3,3,128,128]{3,2,0,1:T(8,128)(2,1)S(1)} collective-permute-done((bf16[3,3,128,128]{3,2,0,1:T(8,128)(2,1)S(1)}, bf16[3,3,128,128]{3,2,0,1:T(8,128)(2,1)S(1)}, u32[]{:S(2)}, u32[]{:S(2)}) %collective-permute-start.2) | collective-permute-done | bytes 294944 | tf_op jit(solution)/shard_map/ppermute | solution.py:488
  21.8 1.3 %collective-permute-done.3 = bf16[3,3,128,128]{3,2,0,1:T(8,128)(2,1)S(1)} collective-permute-done((bf16[3,3,128,128]{3,2,0,1:T(8,128)(2,1)S(1)}, bf16[3,3,128,128]{3,2,0,1:T(8,128)(2,1)S(1)}, u32[]{:S(2)}, u32[]{:S(2)}) %collective-permute-start.3) | collective-permute-done | bytes 294944 | tf_op jit(solution)/shard_map/ppermute | solution.py:488
  23.9 3.6 %collective-permute-done.5.high_ref = bf16[3,3,128,128]{3,2,1,0:T(8,128)(2,1)S(1)} collective-permute-done((bf16[3,3,128,128]{3,2,1,0:T(8,128)(2,1)S(1)}, bf16[3,3,128,128]{3,2,1,0:T(8,128)(2,1)S(1)}, u32[]{:S(2)}, u32[]{:S(2)}) %collective-permute-start.5) | collective-permute-done | bytes 294944 | tf_op jit(solution)/shard_map/ppermute | solution.py:488
  27.5 1.9 %collective-permute-done.4.low_ref = bf16[3,3,128,128]{3,2,1,0:T(8,128)(2,1)S(1)} collective-permute-done((bf16[3,3,128,128]{3,2,1,0:T(8,128)(2,1)S(1)}, bf16[3,3,128,128]{3,2,1,0:T(8,128)(2,1)S(1)}, u32[]{:S(2)}, u32[]{:S(2)}) %collective-permute-start.4) | collective-permute-done | bytes 294944 | tf_op jit(solution)/shard_map/ppermute | solution.py:488
  29.4 1.3 %receive.1 = (bf16[3456,128]{1,0:T(8,128)(2,1)S(1)}, s32[32,128]{1,0:T(8,128)S(1)}, bf16[2,2,32,128]{3,2,1,0:T(8,128)(2,1)S(1)}, bf16[2,2,32,128]{3,2,1,0:T(8,128)(2,1)S(1)}) custom-call(s32[256]{0:T(256)S(1)} %reshape.12.gidx_ref, bf16[3,3,128,128]{3,2,1,0:T(8,128)(2,1)S(1)} %get-tuple-element.51.mid_ref, ...), custom_call_target="tpu_custom_call" | custom-call | tf_op jit(solution)/shard_map/receive/pallas_call | solution.py:128
  30.8 1.3 collective-permute-start.6
  32.1 0.8 collective-permute-start.7
  32.9 1.9 %collective-permute-done.6.refs_0_ = bf16[2,2,32,128]{3,2,1,0:T(8,128)(2,1)S(1)} collective-permute-done((bf16[2,2,32,128]{3,2,1,0:T(8,128)(2,1)S(1)}, bf16[2,2,32,128]{3,2,1,0:T(8,128)(2,1)S(1)}, u32[]{:S(2)}, u32[]{:S(2)}) %collective-permute-start.6) | collective-permute-done | bytes 32800 | tf_op jit(solution)/shard_map/ppermute | solution.py:488
  34.8 1.2 collective-permute-done.7.refs_1_
  36.0 1.4 %collective-permute-start.8 = (bf16[4,2,32,128]{3,2,1,0:T(8,128)(2,1)S(1)}, bf16[4,2,32,128]{3,2,1,0:T(8,128)(2,1)S(1)}, u32[]{:S(2)}, u32[]{:S(2)}) collective-permute-start(bf16[4,2,32,128]{3,2,1,0:T(8,128)(2,1)S(1)} %pad_maximum_fusion.6), channel_id=1, source_target_pairs={{0,8},{8,16},{16,24},{24,0},{1,9},{9,17},{17,25},{25,1},{2,10},{10... | collective-permute-start | bytes 196616 | tf_op jit(solution)/shard_map/ppermute | solution.py:488
  38.2 2.1 %collective-permute-done.8.refs_2_ = bf16[4,2,32,128]{3,2,1,0:T(8,128)(2,1)S(1)} collective-permute-done((bf16[4,2,32,128]{3,2,1,0:T(8,128)(2,1)S(1)}, bf16[4,2,32,128]{3,2,1,0:T(8,128)(2,1)S(1)}, u32[]{:S(2)}, u32[]{:S(2)}) %collective-permute-start.8) | collective-permute-done | bytes 65568 | tf_op jit(solution)/shard_map/ppermute | solution.py:488
  40.3 1.4 %collective-permute-done.9.refs_3_ = bf16[4,2,32,128]{3,2,1,0:T(8,128)(2,1)S(1)} collective-permute-done((bf16[4,2,32,128]{3,2,1,0:T(8,128)(2,1)S(1)}, bf16[4,2,32,128]{3,2,1,0:T(8,128)(2,1)S(1)}, u32[]{:S(2)}, u32[]{:S(2)}) %collective-permute-start.9) | collective-permute-done | bytes 65568 | tf_op jit(solution)/shard_map/ppermute | solution.py:488
  41.9 1.7 %collective-permute-start.11 = (bf16[4,4,32,128]{3,2,1,0:T(8,128)(2,1)S(1)}, bf16[4,4,32,128]{3,2,1,0:T(8,128)(2,1)S(1)}, u32[]{:S(2)}, u32[]{:S(2)}) collective-permute-start(bf16[4,4,32,128]{3,2,1,0:T(8,128)(2,1)S(1)} %pad_maximum_fusion.3), channel_id=1, source_target_pairs={{1,0},{2,1},{3,2},{4,3},{5,4},{6,5},{7,6},{0,7},{9,8},{10,9},{11,1... | collective-permute-start | bytes 393224 | tf_op jit(solution)/shard_map/ppermute | solution.py:488
  43.8 0.9 project.2
  44.6 0.9 lone.2
  46.2 1.9 %indices.1 = (s32[768,128]{1,0:T(8,128)S(1)}, s32[32,128]{1,0:T(8,128)S(1)}, bf16[3456,128]{1,0:T(8,128)(2,1)S(1)}) custom-call(s32[3]{0:T(128)S(1)} %pad_add_fusion.pos_ref, s32[24,3456]{1,0:T(8,128)S(1)} %bitcast.220, s32[24,3456]{1,0:T(8,128)S(1)} %bitcast.221, s32[32,128]{1,0:T(8,128)S(1)} %get-tuple-element.30.cnt_ref, ...), custom_call_target="tpu_custom_call" | custom-call | tf_op jit(solution)/shard_map/indices/pallas_call | solution.py:242
  48.1 31.6 %layer.2 = (f32[5256,128]{1,0:T(8,128)S(1)}, bf16[3456,128]{1,0:T(8,128)(2,1)S(1)}, bf16[2,2,32,128]{3,2,1,0:T(8,128)(2,1)S(1)}, bf16[2,2,32,128]{3,2,1,0:T(8,128)(2,1)S(1)}) custom-call(s32[98304]{0:T(1024)S(1)} %bitcast.218, s32[3]{0:T(128)S(1)} %pad_add_fusion.pos_ref, ...), custom_call_target="tpu_custom_call", output_to_operand_aliasing={{0}: (5, {})} | custom-call | tf_op jit(solution)/shard_map/layer/pallas_call | solution.py:458
  79.7 2.1 %collective-permute-start.12 = (bf16[2,2,32,128]{3,2,1,0:T(8,128)(2,1)S(1)}, bf16[2,2,32,128]{3,2,1,0:T(8,128)(2,1)S(1)}, u32[]{:S(2)}, u32[]{:S(2)}) collective-permute-start(bf16[2,2,32,128]{3,2,1,0:T(8,128)(2,1)S(1)} %get-tuple-element.46), channel_id=1, source_target_pairs={{0,32},{32,64},{64,96},{96,0},{1,33},{33,65},{65,97},{97,1},{2,34}... | collective-permute-start | bytes 98312 | tf_op jit(solution)/shard_map/ppermute | solution.py:488
  81.8 1.9 %collective-permute-done.12.refs_0_ = bf16[2,2,32,128]{3,2,1,0:T(8,128)(2,1)S(1)} collective-permute-done((bf16[2,2,32,128]{3,2,1,0:T(8,128)(2,1)S(1)}, bf16[2,2,32,128]{3,2,1,0:T(8,128)(2,1)S(1)}, u32[]{:S(2)}, u32[]{:S(2)}) %collective-permute-start.12) | collective-permute-done | bytes 32800 | tf_op jit(solution)/shard_map/ppermute | solution.py:488
  83.7 2.0 %collective-permute-done.13.refs_1_ = bf16[2,2,32,128]{3,2,1,0:T(8,128)(2,1)S(1)} collective-permute-done((bf16[2,2,32,128]{3,2,1,0:T(8,128)(2,1)S(1)}, bf16[2,2,32,128]{3,2,1,0:T(8,128)(2,1)S(1)}, u32[]{:S(2)}, u32[]{:S(2)}) %collective-permute-start.13) | collective-permute-done | bytes 32800 | tf_op jit(solution)/shard_map/ppermute | solution.py:488
  86.0 1.9 %collective-permute-start.15 = (bf16[4,2,32,128]{3,2,1,0:T(8,128)(2,1)S(1)}, bf16[4,2,32,128]{3,2,1,0:T(8,128)(2,1)S(1)}, u32[]{:S(2)}, u32[]{:S(2)}) collective-permute-start(bf16[4,2,32,128]{3,2,1,0:T(8,128)(2,1)S(1)} %pad_maximum_fusion.9), channel_id=1, source_target_pairs={{8,0},{16,8},{24,16},{0,24},{9,1},{17,9},{25,17},{1,25},{10,2},{18... | collective-permute-start | bytes 196616 | tf_op jit(solution)/shard_map/ppermute | solution.py:488
  87.9 2.1 %collective-permute-done.14.refs_2_ = bf16[4,2,32,128]{3,2,1,0:T(8,128)(2,1)S(1)} collective-permute-done((bf16[4,2,32,128]{3,2,1,0:T(8,128)(2,1)S(1)}, bf16[4,2,32,128]{3,2,1,0:T(8,128)(2,1)S(1)}, u32[]{:S(2)}, u32[]{:S(2)}) %collective-permute-start.14) | collective-permute-done | bytes 65568 | tf_op jit(solution)/shard_map/ppermute | solution.py:488
  90.5 1.7 %collective-permute-start.17 = (bf16[4,4,32,128]{3,2,1,0:T(8,128)(2,1)S(1)}, bf16[4,4,32,128]{3,2,1,0:T(8,128)(2,1)S(1)}, u32[]{:S(2)}, u32[]{:S(2)}) collective-permute-start(bf16[4,4,32,128]{3,2,1,0:T(8,128)(2,1)S(1)} %pad_maximum_fusion.5), channel_id=1, source_target_pairs={{1,0},{2,1},{3,2},{4,3},{5,4},{6,5},{7,6},{0,7},{9,8},{10,9},{11,1... | collective-permute-start | bytes 393224 | tf_op jit(solution)/shard_map/ppermute | solution.py:488
  92.3 0.9 project.3
  93.2 0.9 lone.3
  94.8 32.3 %layer.3 = (f32[5256,128]{1,0:T(8,128)S(1)}, bf16[3456,128]{1,0:T(8,128)(2,1)}, bf16[2,2,32,128]{3,2,1,0:T(8,128)(2,1)}, bf16[2,2,32,128]{3,2,1,0:T(8,128)(2,1)}) custom-call(s32[98304]{0:T(1024)S(1)} %bitcast.219, s32[3]{0:T(128)S(1)} %pad_add_fusion.pos_ref, s32[32,128]{1,0:T(8,128)S(1)} %get-tuple-element.34.steps_ref, ...), custom_call_target="tpu_custom_call", output_to_operand_aliasing={{0}: (5, {})} | custom-call | tf_op jit(solution)/shard_map/layer/pallas_call | solution.py:458
  (87 shorter events, 5.8 us)
Async XLA Ops:
  0.0 0.9 copy-start.2
  1.0 0.7 copy-start.3
  1.6 14.6 %copy-start.8 = (bf16[2,128,128]{2,1,0:T(8,128)(2,1)S(1)}, bf16[2,128,128]{2,1,0:T(8,128)(2,1)}, u32[]{:S(2)}) copy-start(bf16[2,128,128]{2,1,0:T(8,128)(2,1)} %param.21) | copy-start | bytes 196612
  1.6 14.6 %copy-start.9 = (bf16[2,128,128]{2,1,0:T(8,128)(2,1)S(1)}, bf16[2,128,128]{2,1,0:T(8,128)(2,1)}, u32[]{:S(2)}) copy-start(bf16[2,128,128]{2,1,0:T(8,128)(2,1)} %param.20) | copy-start | bytes 196612
  3.9 8.8 %collective-permute-start = (bf16[3,3,128,128]{3,2,1,0:T(8,128)(2,1)S(1)}, bf16[3,3,128,128]{3,2,1,0:T(8,128)(2,1)S(1)}, u32[]{:S(2)}, u32[]{:S(2)}) collective-permute-start(bf16[3,3,128,128]{3,2,1,0:T(8,128)(2,1)S(1)} %get-tuple-element.27), channel_id=1, source_target_pairs={{0,32},{32,64},{64,96},{96,0},{1,33},{33,65},{65,97},{97,1},{2,34}... | collective-permute-start | bytes 884744 | tf_op jit(solution)/shard_map/ppermute | solution.py:488
  5.4 8.5 %collective-permute-start.1 = (bf16[3,3,128,128]{3,2,1,0:T(8,128)(2,1)S(1)}, bf16[3,3,128,128]{3,2,1,0:T(8,128)(2,1)S(1)}, u32[]{:S(2)}, u32[]{:S(2)}) collective-permute-start(bf16[3,3,128,128]{3,2,1,0:T(8,128)(2,1)S(1)} %get-tuple-element.29), channel_id=1, source_target_pairs={{32,0},{64,32},{96,64},{0,96},{33,1},{65,33},{97,65},{1,97},{34,2}... | collective-permute-start | bytes 884744 | tf_op jit(solution)/shard_map/ppermute | solution.py:488
  14.0 9.8 %copy-start.6 = (bf16[2,128,128]{2,1,0:T(8,128)(2,1)S(1)}, bf16[2,128,128]{2,1,0:T(8,128)(2,1)}, u32[]{:S(2)}) copy-start(bf16[2,128,128]{2,1,0:T(8,128)(2,1)} %param.17) | copy-start | bytes 196612
  14.0 9.8 %copy-start.10 = (s32[1,1,1,8,32]{4,3,2,1,0:T(8,128)S(1)}, s32[1,1,1,8,32]{4,3,2,1,0:T(8,128)}, u32[]{:S(2)}) copy-start(s32[1,1,1,8,32]{4,3,2,1,0:T(8,128)} %param.15) | copy-start | bytes 3076
  14.0 9.8 %copy-start.4 = (bf16[2,256,128]{2,1,0:T(8,128)(2,1)S(1)}, bf16[2,256,128]{2,1,0:T(8,128)(2,1)}, u32[]{:S(2)}) copy-start(bf16[2,256,128]{2,1,0:T(8,128)(2,1)} %param.19) | copy-start | bytes 393220
  14.0 9.8 %copy-start.5 = (bf16[2,256,128]{2,1,0:T(8,128)(2,1)S(1)}, bf16[2,256,128]{2,1,0:T(8,128)(2,1)}, u32[]{:S(2)}) copy-start(bf16[2,256,128]{2,1,0:T(8,128)(2,1)} %param.16) | copy-start | bytes 393220
  14.1 7.6 %collective-permute-start.2 = (bf16[3,3,128,128]{3,2,0,1:T(8,128)(2,1)S(1)}, bf16[3,3,128,128]{3,2,0,1:T(8,128)(2,1)S(1)}, u32[]{:S(2)}, u32[]{:S(2)}) collective-permute-start(bf16[3,3,128,128]{3,2,0,1:T(8,128)(2,1)S(1)} %get-tuple-element.52), channel_id=1, source_target_pairs={{0,8},{8,16},{16,24},{24,0},{1,9},{9,17},{17,25},{25,1},{2,10},{10... | collective-permute-start | bytes 884744 | tf_op jit(solution)/shard_map/ppermute | solution.py:488
  15.8 7.3 %collective-permute-start.3 = (bf16[3,3,128,128]{3,2,0,1:T(8,128)(2,1)S(1)}, bf16[3,3,128,128]{3,2,0,1:T(8,128)(2,1)S(1)}, u32[]{:S(2)}, u32[]{:S(2)}) collective-permute-start(bf16[3,3,128,128]{3,2,0,1:T(8,128)(2,1)S(1)} %get-tuple-element.53), channel_id=1, source_target_pairs={{8,0},{16,8},{24,16},{0,24},{9,1},{17,9},{25,17},{1,25},{10,2},{18... | collective-permute-start | bytes 884744 | tf_op jit(solution)/shard_map/ppermute | solution.py:488
  23.1 20.5 %copy-start.7 = (bf16[2,128,128]{2,1,0:T(8,128)(2,1)S(1)}, bf16[2,128,128]{2,1,0:T(8,128)(2,1)}, u32[]{:S(2)}) copy-start(bf16[2,128,128]{2,1,0:T(8,128)(2,1)} %param.18) | copy-start | bytes 196612
  23.2 4.3 %collective-permute-start.5 = (bf16[3,3,128,128]{3,2,1,0:T(8,128)(2,1)S(1)}, bf16[3,3,128,128]{3,2,1,0:T(8,128)(2,1)S(1)}, u32[]{:S(2)}, u32[]{:S(2)}) collective-permute-start(bf16[3,3,128,128]{3,2,1,0:T(8,128)(2,1)S(1)} %get-tuple-element.49), channel_id=1, source_target_pairs={{1,0},{2,1},{3,2},{4,3},{5,4},{6,5},{7,6},{0,7},{9,8},{10,9},{11,1... | collective-permute-start | bytes 884744 | tf_op jit(solution)/shard_map/ppermute | solution.py:488
  23.3 6.2 %collective-permute-start.4 = (bf16[3,3,128,128]{3,2,1,0:T(8,128)(2,1)S(1)}, bf16[3,3,128,128]{3,2,1,0:T(8,128)(2,1)S(1)}, u32[]{:S(2)}, u32[]{:S(2)}) collective-permute-start(bf16[3,3,128,128]{3,2,1,0:T(8,128)(2,1)S(1)} %get-tuple-element.50), channel_id=1, source_target_pairs={{0,1},{1,2},{2,3},{3,4},{4,5},{5,6},{6,7},{7,0},{8,9},{9,10},{10,1... | collective-permute-start | bytes 884744 | tf_op jit(solution)/shard_map/ppermute | solution.py:488
  30.8 4.0 %collective-permute-start.6 = (bf16[2,2,32,128]{3,2,1,0:T(8,128)(2,1)S(1)}, bf16[2,2,32,128]{3,2,1,0:T(8,128)(2,1)S(1)}, u32[]{:S(2)}, u32[]{:S(2)}) collective-permute-start(bf16[2,2,32,128]{3,2,1,0:T(8,128)(2,1)S(1)} %get-tuple-element.31), channel_id=1, source_target_pairs={{0,32},{32,64},{64,96},{96,0},{1,33},{33,65},{65,97},{97,1},{2,34}... | collective-permute-start | bytes 98312 | tf_op jit(solution)/shard_map/ppermute | solution.py:488
  32.1 3.9 %collective-permute-start.7 = (bf16[2,2,32,128]{3,2,1,0:T(8,128)(2,1)S(1)}, bf16[2,2,32,128]{3,2,1,0:T(8,128)(2,1)S(1)}, u32[]{:S(2)}, u32[]{:S(2)}) collective-permute-start(bf16[2,2,32,128]{3,2,1,0:T(8,128)(2,1)S(1)} %get-tuple-element.32), channel_id=1, source_target_pairs={{32,0},{64,32},{96,64},{0,96},{33,1},{65,33},{97,65},{1,97},{34,2}... | collective-permute-start | bytes 98312 | tf_op jit(solution)/shard_map/ppermute | solution.py:488
  36.0 4.3 %collective-permute-start.8 = (bf16[4,2,32,128]{3,2,1,0:T(8,128)(2,1)S(1)}, bf16[4,2,32,128]{3,2,1,0:T(8,128)(2,1)S(1)}, u32[]{:S(2)}, u32[]{:S(2)}) collective-permute-start(bf16[4,2,32,128]{3,2,1,0:T(8,128)(2,1)S(1)} %pad_maximum_fusion.6), channel_id=1, source_target_pairs={{0,8},{8,16},{16,24},{24,0},{1,9},{9,17},{17,25},{25,1},{2,10},{10... | collective-permute-start | bytes 196616 | tf_op jit(solution)/shard_map/ppermute | solution.py:488
  37.4 8.9 %copy-start = (s32[1,1,1,3456,24]{3,4,2,1,0:T(8,128)S(1)}, s32[1,1,1,3456,24]{3,4,2,1,0:T(8,128)}, u32[]{:S(2)}) copy-start(s32[1,1,1,3456,24]{3,4,2,1,0:T(8,128)} %param.13) | copy-start | bytes 995332
  37.4 8.9 %copy-start.1 = (s32[1,1,1,3456,24]{3,4,2,1,0:T(8,128)S(1)}, s32[1,1,1,3456,24]{3,4,2,1,0:T(8,128)}, u32[]{:S(2)}) copy-start(s32[1,1,1,3456,24]{3,4,2,1,0:T(8,128)} %param.14) | copy-start | bytes 995332
  37.4 4.3 %collective-permute-start.9 = (bf16[4,2,32,128]{3,2,1,0:T(8,128)(2,1)S(1)}, bf16[4,2,32,128]{3,2,1,0:T(8,128)(2,1)S(1)}, u32[]{:S(2)}, u32[]{:S(2)}) collective-permute-start(bf16[4,2,32,128]{3,2,1,0:T(8,128)(2,1)S(1)} %pad_maximum_fusion.7), channel_id=1, source_target_pairs={{8,0},{16,8},{24,16},{0,24},{9,1},{17,9},{25,17},{1,25},{10,2},{18... | collective-permute-start | bytes 196616 | tf_op jit(solution)/shard_map/ppermute | solution.py:488
  41.8 4.4 %collective-permute-start.10 = (bf16[4,4,32,128]{3,2,1,0:T(8,128)(2,1)S(1)}, bf16[4,4,32,128]{3,2,1,0:T(8,128)(2,1)S(1)}, u32[]{:S(2)}, u32[]{:S(2)}) collective-permute-start(bf16[4,4,32,128]{3,2,1,0:T(8,128)(2,1)S(1)} %pad_maximum_fusion.2), channel_id=1, source_target_pairs={{0,1},{1,2},{2,3},{3,4},{4,5},{5,6},{6,7},{7,0},{8,9},{9,10},{10,1... | collective-permute-start | bytes 393224 | tf_op jit(solution)/shard_map/ppermute | solution.py:488
  41.9 4.3 %collective-permute-start.11 = (bf16[4,4,32,128]{3,2,1,0:T(8,128)(2,1)S(1)}, bf16[4,4,32,128]{3,2,1,0:T(8,128)(2,1)S(1)}, u32[]{:S(2)}, u32[]{:S(2)}) collective-permute-start(bf16[4,4,32,128]{3,2,1,0:T(8,128)(2,1)S(1)} %pad_maximum_fusion.3), channel_id=1, source_target_pairs={{1,0},{2,1},{3,2},{4,3},{5,4},{6,5},{7,6},{0,7},{9,8},{10,9},{11,1... | collective-permute-start | bytes 393224 | tf_op jit(solution)/shard_map/ppermute | solution.py:488
  79.7 4.0 %collective-permute-start.12 = (bf16[2,2,32,128]{3,2,1,0:T(8,128)(2,1)S(1)}, bf16[2,2,32,128]{3,2,1,0:T(8,128)(2,1)S(1)}, u32[]{:S(2)}, u32[]{:S(2)}) collective-permute-start(bf16[2,2,32,128]{3,2,1,0:T(8,128)(2,1)S(1)} %get-tuple-element.46), channel_id=1, source_target_pairs={{0,32},{32,64},{64,96},{96,0},{1,33},{33,65},{65,97},{97,1},{2,34}... | collective-permute-start | bytes 98312 | tf_op jit(solution)/shard_map/ppermute | solution.py:488
  81.8 3.9 %collective-permute-start.13 = (bf16[2,2,32,128]{3,2,1,0:T(8,128)(2,1)S(1)}, bf16[2,2,32,128]{3,2,1,0:T(8,128)(2,1)S(1)}, u32[]{:S(2)}, u32[]{:S(2)}) collective-permute-start(bf16[2,2,32,128]{3,2,1,0:T(8,128)(2,1)S(1)} %get-tuple-element.47), channel_id=1, source_target_pairs={{32,0},{64,32},{96,64},{0,96},{33,1},{65,33},{97,65},{1,97},{34,2}... | collective-permute-start | bytes 98312 | tf_op jit(solution)/shard_map/ppermute | solution.py:488
  85.8 4.3 %collective-permute-start.14 = (bf16[4,2,32,128]{3,2,1,0:T(8,128)(2,1)S(1)}, bf16[4,2,32,128]{3,2,1,0:T(8,128)(2,1)S(1)}, u32[]{:S(2)}, u32[]{:S(2)}) collective-permute-start(bf16[4,2,32,128]{3,2,1,0:T(8,128)(2,1)S(1)} %pad_maximum_fusion.8), channel_id=1, source_target_pairs={{0,8},{8,16},{16,24},{24,0},{1,9},{9,17},{17,25},{25,1},{2,10},{10... | collective-permute-start | bytes 196616 | tf_op jit(solution)/shard_map/ppermute | solution.py:488
  86.0 4.3 %collective-permute-start.15 = (bf16[4,2,32,128]{3,2,1,0:T(8,128)(2,1)S(1)}, bf16[4,2,32,128]{3,2,1,0:T(8,128)(2,1)S(1)}, u32[]{:S(2)}, u32[]{:S(2)}) collective-permute-start(bf16[4,2,32,128]{3,2,1,0:T(8,128)(2,1)S(1)} %pad_maximum_fusion.9), channel_id=1, source_target_pairs={{8,0},{16,8},{24,16},{0,24},{9,1},{17,9},{25,17},{1,25},{10,2},{18... | collective-permute-start | bytes 196616 | tf_op jit(solution)/shard_map/ppermute | solution.py:488
  90.4 4.4 %collective-permute-start.16 = (bf16[4,4,32,128]{3,2,1,0:T(8,128)(2,1)S(1)}, bf16[4,4,32,128]{3,2,1,0:T(8,128)(2,1)S(1)}, u32[]{:S(2)}, u32[]{:S(2)}) collective-permute-start(bf16[4,4,32,128]{3,2,1,0:T(8,128)(2,1)S(1)} %pad_maximum_fusion.4), channel_id=1, source_target_pairs={{0,1},{1,2},{2,3},{3,4},{4,5},{5,6},{6,7},{7,0},{8,9},{9,10},{10,1... | collective-permute-start | bytes 393224 | tf_op jit(solution)/shard_map/ppermute | solution.py:488
  90.5 4.3 %collective-permute-start.17 = (bf16[4,4,32,128]{3,2,1,0:T(8,128)(2,1)S(1)}, bf16[4,4,32,128]{3,2,1,0:T(8,128)(2,1)S(1)}, u32[]{:S(2)}, u32[]{:S(2)}) collective-permute-start(bf16[4,4,32,128]{3,2,1,0:T(8,128)(2,1)S(1)} %pad_maximum_fusion.5), channel_id=1, source_target_pairs={{1,0},{2,1},{3,2},{4,3},{5,4},{6,5},{7,6},{0,7},{9,8},{10,9},{11,1... | collective-permute-start | bytes 393224 | tf_op jit(solution)/shard_map/ppermute | solution.py:488

commit v9 on v8

--- a/solution.py
+++ b/solution.py
@@ -43,7 +43,9 @@
     return lax.broadcasted_iota(I32, shape, dim)
 
 
-def pack_kernel(dest_ref, rows_ref, down_ref, mid_ref, up_ref, slot_ref):
+def pack_kernel(dest_ref, rows_hbm, down_ref, mid_ref, up_ref, slot_ref, rows_ref, sem):
+    fetch = pltpu.make_async_copy(rows_hbm, rows_ref, sem)
+    fetch.start()
     n_y, n_z = 4, 8
     ix, iy, iz = (lax.axis_index(a) for a in HALO_AXES)
     tri = (iota((W, W), 0) < iota((W, W), 1)).astype(BF16)
@@ -63,6 +65,7 @@
         slot_ref[:, j * W : (j + 1) * W] = code * W + rank.astype(I32)
         off = off + dot(one, ones)
     slot = slot_ref[...]
+    fetch.wait()
     rows = rows_ref[...]
     for part, out_ref in enumerate((down_ref, mid_ref, up_ref)):
         first = part * 9 * W
@@ -78,9 +81,13 @@
     return pl.pallas_call(
         pack_kernel,
         out_shape=[jax.ShapeDtypeStruct((3, 3, W, W), BF16)] * 3,
-        in_specs=[vmem(), vmem()],
+        in_specs=[vmem(), pl.BlockSpec(memory_space=pltpu.HBM)],
         out_specs=[vmem()] * 3,
-        scratch_shapes=[pltpu.VMEM((1, 1024), I32)],
+        scratch_shapes=[
+            pltpu.VMEM((1, 1024), I32),
+            pltpu.VMEM((1024, W), BF16),
+            pltpu.SemaphoreType.DMA,
+        ],
         compiler_params=pltpu.CompilerParams(vmem_limit_bytes=VMEM_LIMIT),
         name="pack",
     )(dest, rows)
@@ -229,7 +236,7 @@
         for k in range(DEG):
             used = used + jnp.where(keys[k] < DUMMY, 1.0, 0.0)
             idx_ref[pl.ds(b * 8 * DEG + k, 8, stride=DEG), :] = keys[k].astype(I32)
-        for shift in (1, 2, 4, 8):
+        for shift in (1, 2, 4):
             used = jnp.maximum(used, pltpu.roll(used, W - shift, 1))
         steps_ref[b * 8 : (b + 1) * 8, :] = used.astype(I32)
         for c in range(b * 8, min(b * 8 + 8, CODES)):
@@ -256,8 +263,8 @@
 
 GROUP = 16
 SPAN = 27
-FIRST = 13
-TAILS = (0, 1, 2, 3, 5, 7, 11)
+FIRST = 12
+TAILS = (0, 1, 2, 3, 4, 6, 8, 12)
 DUMP = ROWS
 PARTS = ((0, 3), (3, 11), (11, CODES))
 
@@ -357,57 +364,59 @@
     sub = iota((8, W), 0)
 
     def listed(c, n):
-        for g in range(W // GROUP):
-            homes[n + g] = c * W + g * GROUP
-        return n + lax.shift_right_logical(cnt_ref[c, 0] + (GROUP - 1), 4)
+        for g in range(W // 8):
+            homes[n + g] = c * W + g * 8
+        return n + lax.shift_right_logical(cnt_ref[c, 0] + 7, 3)
 
     starts = [jnp.int32(0)]
     for lo, hi in PARTS:
         starts.append(lax.fori_loop(lo, hi, listed, starts[-1]))
     total = starts[-1]
-    homes[total] = homes[jnp.maximum(total - 1, 0)]
-    rounds = lax.shift_right_logical(total + 1, 1)
-    turns = [jnp.minimum(lax.shift_right_logical(n, 1), rounds) for n in starts[:-1]]
+    for extra in range(3):
+        homes[total + extra] = homes[jnp.maximum(total - 1, 0)]
+    rounds = lax.shift_right_logical(total + 3, 2)
+    turns = [jnp.minimum(lax.shift_right_logical(n, 2), rounds) for n in starts[:-1]]
 
     def finish(h, rows):
         d = jnp.maximum(dot(h, w_second), 0.0).astype(BF16).astype(F32)
         d = jnp.sum(d.reshape(2, DEG, GROUP, W), axis=1)
-        for slot, row in enumerate(rows):
-            agg[pl.ds(pl.multiple_of(row, GROUP), GROUP), :] = d[slot]
-
-    def step(slot, base, mine, k):
+        for u, row in enumerate(rows):
+            piece = d[u // 2, (u % 2) * 8 : (u % 2) * 8 + 8, :]
+            agg[pl.ds(pl.multiple_of(row, 8), 8), :] = piece
+
+    def step(slot, bases, mines, k):
         both = []
         for half in range(2):
+            base, mine = bases[2 * slot + half], mines[2 * slot + half]
             got = None
             for r in range(8):
-                at = idx_ref[base + (k * W + half * 8 + r)]
+                at = idx_ref[base + (k * W + r)]
                 row = jnp.broadcast_to(table[pl.ds(at, 1), :], (8, W))
                 got = row if got is None else jnp.where(sub == r, row, got)
-            both.append(jnp.maximum(got + mine[half], 0.0))
+            both.append(jnp.maximum(got + mine, 0.0))
         at = (slot * DEG + k) * GROUP
         hidden[at : at + GROUP, :] = jnp.concatenate(both, axis=0).astype(BF16)
 
     def gather(i, last):
         for turn, copy in zip(turns, copies):
             pl.when(i == turn)(copy.wait)
-        rows = [pl.multiple_of(homes[2 * i + slot], GROUP) for slot in range(2)]
+        rows = [pl.multiple_of(homes[4 * i + u], 8) for u in range(4)]
         codes = [lax.shift_right_logical(row, 7) for row in rows]
         bases = [row + code * ((DEG - 1) * W) for row, code in zip(rows, codes)]
-        mines = [
-            [recv[pl.ds(pl.multiple_of(row + h * 8, 8), 8), :] for h in range(2)] for row in rows
-        ]
+        mines = [recv[pl.ds(row, 8), :] for row in rows]
+        needs = [steps_ref[code, row & (W - 1)] for row, code in zip(rows, codes)]
         finish(hidden[...], last)
         for slot in range(2):
             for k in range(FIRST):
-                step(slot, bases[slot], mines[slot], k)
+                step(slot, bases, mines, k)
         for slot in range(2):
-            more = steps_ref[codes[slot], rows[slot] & (W - 1)] - FIRST
+            more = jnp.maximum(needs[2 * slot], needs[2 * slot + 1]) - FIRST
             which = sum((more > t).astype(I32) for t in TAILS[:-1])
 
             def tail(size, slot=slot):
                 def run():
                     for k in range(FIRST, FIRST + size):
-                        step(slot, bases[slot], mines[slot], k)
+                        step(slot, bases, mines, k)
                     if FIRST + size < DEG:
                         rest = (DEG - FIRST - size) * GROUP
                         end = (slot + 1) * DEG * GROUP
@@ -418,7 +427,7 @@
             lax.switch(which, [tail(t) for t in TAILS])
         return tuple(rows)
 
-    last = lax.fori_loop(0, rounds, gather, (jnp.int32(DUMP), jnp.int32(DUMP)))
+    last = lax.fori_loop(0, rounds, gather, (jnp.int32(DUMP),) * 4)
     for turn, copy in zip(turns, copies):
         pl.when(turn == rounds)(copy.wait)
     finish(hidden[...], last)
@@ -473,7 +482,7 @@
             pltpu.VMEM((ROWS, W), F32),
             pltpu.VMEM((8 * SLAB, W), F32),
             pltpu.SMEM((ROWS * DEG,), I32),
-            pltpu.SMEM((256,), I32),
+            pltpu.SMEM((512,), I32),
             pltpu.SemaphoreType.DMA((len(PARTS),)),
         ],
         compiler_params=pltpu.CompilerParams(vmem_limit_bytes=VMEM_LIMIT),

time: 128 us -> 125 us (0.977)
  Pallas kernels: 73 us -> 68.9 us
    pallas_call x2, Pallas kernels: 63.9 us -> 59.8 us  [one_layer(): pl.pallas_call(layer_kernel, out_shape=[jax.ShapeDtypeStruct((NODES + 8,...]
where the time goes in v9:
time: 125 us
  Pallas kernels  68.9 us (55%)
  waiting for transfers between devices  35.5 us (28%)
  starting transfers between devices  17.3 us (14%)
  local copies, waits for them, and re-layouts  2.03 us (2%)
    pallas_call x2, Pallas kernels, one_layer(): pl.pallas_call(layer_kernel, out_shape=[jax.ShapeDtypeStruct((NODES + 8,...  59.8 us
    ppermute x18, waiting for transfers between devices, both_ways(): return (lax.ppermute(up, axis, forward), lax.ppermute(down, axis, backward))  35.5 us
    ppermute x18, starting transfers between devices, both_ways(): return (lax.ppermute(up, axis, forward), lax.ppermute(down, axis, backward))  17.3 us
  transfers between devices with their start and end apart: 18, of which 16 were waited for; matrix products, arithmetic and copies ran while one was open for 0% of the time, Pallas kernels for 3%

profile of v9, /device:TPU:106, one launch (start us, length us, event | category | flops | bytes accessed | tf_op | source)
XLA Modules:
  0.0 124.8 jit_solution(12645216718568604451)
XLA Ops:
  0.0 0.9 copy-done.2
  1.6 2.3 %pack.1 = (bf16[3,3,128,128]{3,2,1,0:T(8,128)(2,1)S(1)}, bf16[3,3,128,128]{3,2,1,0:T(8,128)(2,1)S(1)}, bf16[3,3,128,128]{3,2,1,0:T(8,128)(2,1)S(1)}) custom-call(s32[1,1024]{1,0:T(1,128)S(1)} %bitcast.224, bf16[1024,128]{1,0:T(8,128)(2,1)S(1)} %bitcast.223), custom_call_target="tpu_custom_call" | custom-call | tf_op jit(solution)/shard_map/pack/pallas_call | solution.py:81
  4.0 1.6 %collective-permute-start = (bf16[3,3,128,128]{3,2,1,0:T(8,128)(2,1)S(1)}, bf16[3,3,128,128]{3,2,1,0:T(8,128)(2,1)S(1)}, u32[]{:S(2)}, u32[]{:S(2)}) collective-permute-start(bf16[3,3,128,128]{3,2,1,0:T(8,128)(2,1)S(1)} %get-tuple-element.27), channel_id=1, source_target_pairs={{0,32},{32,64},{64,96},{96,0},{1,33},{33,65},{65,97},{97,1},{2,34}... | collective-permute-start | bytes 884744 | tf_op jit(solution)/shard_map/ppermute | solution.py:497
  6.0 6.7 %collective-permute-done = bf16[3,3,128,128]{3,2,1,0:T(8,128)(2,1)S(1)} collective-permute-done((bf16[3,3,128,128]{3,2,1,0:T(8,128)(2,1)S(1)}, bf16[3,3,128,128]{3,2,1,0:T(8,128)(2,1)S(1)}, u32[]{:S(2)}, u32[]{:S(2)}) %collective-permute-start) | collective-permute-done | bytes 294944 | tf_op jit(solution)/shard_map/ppermute | solution.py:497
  12.8 1.2 collective-permute-done.1
  14.2 1.6 %collective-permute-start.2 = (bf16[3,3,128,128]{3,2,0,1:T(8,128)(2,1)S(1)}, bf16[3,3,128,128]{3,2,0,1:T(8,128)(2,1)S(1)}, u32[]{:S(2)}, u32[]{:S(2)}) collective-permute-start(bf16[3,3,128,128]{3,2,0,1:T(8,128)(2,1)S(1)} %get-tuple-element.52), channel_id=1, source_target_pairs={{0,8},{8,16},{16,24},{24,0},{1,9},{9,17},{17,25},{25,1},{2,10},{10... | collective-permute-start | bytes 884744 | tf_op jit(solution)/shard_map/ppermute | solution.py:497
  16.3 5.5 %collective-permute-done.2 = bf16[3,3,128,128]{3,2,0,1:T(8,128)(2,1)S(1)} collective-permute-done((bf16[3,3,128,128]{3,2,0,1:T(8,128)(2,1)S(1)}, bf16[3,3,128,128]{3,2,0,1:T(8,128)(2,1)S(1)}, u32[]{:S(2)}, u32[]{:S(2)}) %collective-permute-start.2) | collective-permute-done | bytes 294944 | tf_op jit(solution)/shard_map/ppermute | solution.py:497
  21.8 1.3 %collective-permute-done.3 = bf16[3,3,128,128]{3,2,0,1:T(8,128)(2,1)S(1)} collective-permute-done((bf16[3,3,128,128]{3,2,0,1:T(8,128)(2,1)S(1)}, bf16[3,3,128,128]{3,2,0,1:T(8,128)(2,1)S(1)}, u32[]{:S(2)}, u32[]{:S(2)}) %collective-permute-start.3) | collective-permute-done | bytes 294944 | tf_op jit(solution)/shard_map/ppermute | solution.py:497
  24.0 3.6 %collective-permute-done.5.high_ref = bf16[3,3,128,128]{3,2,1,0:T(8,128)(2,1)S(1)} collective-permute-done((bf16[3,3,128,128]{3,2,1,0:T(8,128)(2,1)S(1)}, bf16[3,3,128,128]{3,2,1,0:T(8,128)(2,1)S(1)}, u32[]{:S(2)}, u32[]{:S(2)}) %collective-permute-start.5) | collective-permute-done | bytes 294944 | tf_op jit(solution)/shard_map/ppermute | solution.py:497
  27.6 1.9 %collective-permute-done.4.low_ref = bf16[3,3,128,128]{3,2,1,0:T(8,128)(2,1)S(1)} collective-permute-done((bf16[3,3,128,128]{3,2,1,0:T(8,128)(2,1)S(1)}, bf16[3,3,128,128]{3,2,1,0:T(8,128)(2,1)S(1)}, u32[]{:S(2)}, u32[]{:S(2)}) %collective-permute-start.4) | collective-permute-done | bytes 294944 | tf_op jit(solution)/shard_map/ppermute | solution.py:497
  29.5 1.3 %receive.1 = (bf16[3456,128]{1,0:T(8,128)(2,1)S(1)}, s32[32,128]{1,0:T(8,128)S(1)}, bf16[2,2,32,128]{3,2,1,0:T(8,128)(2,1)S(1)}, bf16[2,2,32,128]{3,2,1,0:T(8,128)(2,1)S(1)}) custom-call(s32[256]{0:T(256)S(1)} %reshape.12.gidx_ref, bf16[3,3,128,128]{3,2,1,0:T(8,128)(2,1)S(1)} %get-tuple-element.51.mid_ref, ...), custom_call_target="tpu_custom_call" | custom-call | tf_op jit(solution)/shard_map/receive/pallas_call | solution.py:135
  30.9 1.3 %collective-permute-start.6 = (bf16[2,2,32,128]{3,2,1,0:T(8,128)(2,1)S(1)}, bf16[2,2,32,128]{3,2,1,0:T(8,128)(2,1)S(1)}, u32[]{:S(2)}, u32[]{:S(2)}) collective-permute-start(bf16[2,2,32,128]{3,2,1,0:T(8,128)(2,1)S(1)} %get-tuple-element.31), channel_id=1, source_target_pairs={{0,32},{32,64},{64,96},{96,0},{1,33},{33,65},{65,97},{97,1},{2,34}... | collective-permute-start | bytes 98312 | tf_op jit(solution)/shard_map/ppermute | solution.py:497
  33.0 1.9 %collective-permute-done.6.refs_0_ = bf16[2,2,32,128]{3,2,1,0:T(8,128)(2,1)S(1)} collective-permute-done((bf16[2,2,32,128]{3,2,1,0:T(8,128)(2,1)S(1)}, bf16[2,2,32,128]{3,2,1,0:T(8,128)(2,1)S(1)}, u32[]{:S(2)}, u32[]{:S(2)}) %collective-permute-start.6) | collective-permute-done | bytes 32800 | tf_op jit(solution)/shard_map/ppermute | solution.py:497
  34.9 1.2 collective-permute-done.7.refs_1_
  36.1 1.4 %collective-permute-start.8 = (bf16[4,2,32,128]{3,2,1,0:T(8,128)(2,1)S(1)}, bf16[4,2,32,128]{3,2,1,0:T(8,128)(2,1)S(1)}, u32[]{:S(2)}, u32[]{:S(2)}) collective-permute-start(bf16[4,2,32,128]{3,2,1,0:T(8,128)(2,1)S(1)} %pad_maximum_fusion.6), channel_id=1, source_target_pairs={{0,8},{8,16},{16,24},{24,0},{1,9},{9,17},{17,25},{25,1},{2,10},{10... | collective-permute-start | bytes 196616 | tf_op jit(solution)/shard_map/ppermute | solution.py:497
  38.3 2.1 %collective-permute-done.8.refs_2_ = bf16[4,2,32,128]{3,2,1,0:T(8,128)(2,1)S(1)} collective-permute-done((bf16[4,2,32,128]{3,2,1,0:T(8,128)(2,1)S(1)}, bf16[4,2,32,128]{3,2,1,0:T(8,128)(2,1)S(1)}, u32[]{:S(2)}, u32[]{:S(2)}) %collective-permute-start.8) | collective-permute-done | bytes 65568 | tf_op jit(solution)/shard_map/ppermute | solution.py:497
  40.4 1.4 %collective-permute-done.9.refs_3_ = bf16[4,2,32,128]{3,2,1,0:T(8,128)(2,1)S(1)} collective-permute-done((bf16[4,2,32,128]{3,2,1,0:T(8,128)(2,1)S(1)}, bf16[4,2,32,128]{3,2,1,0:T(8,128)(2,1)S(1)}, u32[]{:S(2)}, u32[]{:S(2)}) %collective-permute-start.9) | collective-permute-done | bytes 65568 | tf_op jit(solution)/shard_map/ppermute | solution.py:497
  42.0 1.7 %collective-permute-start.11 = (bf16[4,4,32,128]{3,2,1,0:T(8,128)(2,1)S(1)}, bf16[4,4,32,128]{3,2,1,0:T(8,128)(2,1)S(1)}, u32[]{:S(2)}, u32[]{:S(2)}) collective-permute-start(bf16[4,4,32,128]{3,2,1,0:T(8,128)(2,1)S(1)} %pad_maximum_fusion.3), channel_id=1, source_target_pairs={{1,0},{2,1},{3,2},{4,3},{5,4},{6,5},{7,6},{0,7},{9,8},{10,9},{11,1... | collective-permute-start | bytes 393224 | tf_op jit(solution)/shard_map/ppermute | solution.py:497
  43.8 0.9 project.2
  44.7 0.9 lone.2
  46.3 1.8 %indices.1 = (s32[768,128]{1,0:T(8,128)S(1)}, s32[32,128]{1,0:T(8,128)S(1)}, bf16[3456,128]{1,0:T(8,128)(2,1)S(1)}) custom-call(s32[3]{0:T(128)S(1)} %pad_add_fusion.pos_ref, s32[24,3456]{1,0:T(8,128)S(1)} %bitcast.220, s32[24,3456]{1,0:T(8,128)S(1)} %bitcast.221, s32[32,128]{1,0:T(8,128)S(1)} %get-tuple-element.30.cnt_ref, ...), custom_call_target="tpu_custom_call" | custom-call | tf_op jit(solution)/shard_map/indices/pallas_call | solution.py:249
  48.1 29.5 %layer.2 = (f32[5256,128]{1,0:T(8,128)S(1)}, bf16[3456,128]{1,0:T(8,128)(2,1)S(1)}, bf16[2,2,32,128]{3,2,1,0:T(8,128)(2,1)S(1)}, bf16[2,2,32,128]{3,2,1,0:T(8,128)(2,1)S(1)}) custom-call(s32[98304]{0:T(1024)S(1)} %bitcast.218, s32[3]{0:T(128)S(1)} %pad_add_fusion.pos_ref, ...), custom_call_target="tpu_custom_call", output_to_operand_aliasing={{0}: (5, {})} | custom-call | tf_op jit(solution)/shard_map/layer/pallas_call | solution.py:467
  77.7 1.2 collective-permute-start.12
  78.9 0.9 collective-permute-start.13
  79.8 1.9 %collective-permute-done.12.refs_0_ = bf16[2,2,32,128]{3,2,1,0:T(8,128)(2,1)S(1)} collective-permute-done((bf16[2,2,32,128]{3,2,1,0:T(8,128)(2,1)S(1)}, bf16[2,2,32,128]{3,2,1,0:T(8,128)(2,1)S(1)}, u32[]{:S(2)}, u32[]{:S(2)}) %collective-permute-start.12) | collective-permute-done | bytes 32800 | tf_op jit(solution)/shard_map/ppermute | solution.py:497
  81.7 1.1 collective-permute-done.13.refs_1_
  82.8 2.7 %collective-permute-start.14 = (bf16[4,2,32,128]{3,2,1,0:T(8,128)(2,1)S(1)}, bf16[4,2,32,128]{3,2,1,0:T(8,128)(2,1)S(1)}, u32[]{:S(2)}, u32[]{:S(2)}) collective-permute-start(bf16[4,2,32,128]{3,2,1,0:T(8,128)(2,1)S(1)} %pad_maximum_fusion.8), channel_id=1, source_target_pairs={{0,8},{8,16},{16,24},{24,0},{1,9},{9,17},{17,25},{25,1},{2,10},{10... | collective-permute-start | bytes 196616 | tf_op jit(solution)/shard_map/ppermute | solution.py:497
  85.7 1.8 %collective-permute-done.14.refs_2_ = bf16[4,2,32,128]{3,2,1,0:T(8,128)(2,1)S(1)} collective-permute-done((bf16[4,2,32,128]{3,2,1,0:T(8,128)(2,1)S(1)}, bf16[4,2,32,128]{3,2,1,0:T(8,128)(2,1)S(1)}, u32[]{:S(2)}, u32[]{:S(2)}) %collective-permute-start.14) | collective-permute-done | bytes 65568 | tf_op jit(solution)/shard_map/ppermute | solution.py:497
  87.5 2.4 %collective-permute-done.15.refs_3_ = bf16[4,2,32,128]{3,2,1,0:T(8,128)(2,1)S(1)} collective-permute-done((bf16[4,2,32,128]{3,2,1,0:T(8,128)(2,1)S(1)}, bf16[4,2,32,128]{3,2,1,0:T(8,128)(2,1)S(1)}, u32[]{:S(2)}, u32[]{:S(2)}) %collective-permute-start.15) | collective-permute-done | bytes 65568 | tf_op jit(solution)/shard_map/ppermute | solution.py:497
  90.1 1.7 %collective-permute-start.17 = (bf16[4,4,32,128]{3,2,1,0:T(8,128)(2,1)S(1)}, bf16[4,4,32,128]{3,2,1,0:T(8,128)(2,1)S(1)}, u32[]{:S(2)}, u32[]{:S(2)}) collective-permute-start(bf16[4,4,32,128]{3,2,1,0:T(8,128)(2,1)S(1)} %pad_maximum_fusion.5), channel_id=1, source_target_pairs={{1,0},{2,1},{3,2},{4,3},{5,4},{6,5},{7,6},{0,7},{9,8},{10,9},{11,1... | collective-permute-start | bytes 393224 | tf_op jit(solution)/shard_map/ppermute | solution.py:497
  92.7 0.9 lone.3
  94.4 30.3 %layer.3 = (f32[5256,128]{1,0:T(8,128)S(1)}, bf16[3456,128]{1,0:T(8,128)(2,1)}, bf16[2,2,32,128]{3,2,1,0:T(8,128)(2,1)}, bf16[2,2,32,128]{3,2,1,0:T(8,128)(2,1)}) custom-call(s32[98304]{0:T(1024)S(1)} %bitcast.219, s32[3]{0:T(128)S(1)} %pad_add_fusion.pos_ref, s32[32,128]{1,0:T(8,128)S(1)} %get-tuple-element.34.steps_ref, ...), custom_call_target="tpu_custom_call", output_to_operand_aliasing={{0}: (5, {})} | custom-call | tf_op jit(solution)/shard_map/layer/pallas_call | solution.py:467
  (87 shorter events, 7.2 us)
Async XLA Ops:
  0.0 0.9 copy-start.2
  1.0 0.7 copy-start.3
  1.6 14.7 %copy-start.8 = (bf16[2,128,128]{2,1,0:T(8,128)(2,1)S(1)}, bf16[2,128,128]{2,1,0:T(8,128)(2,1)}, u32[]{:S(2)}) copy-start(bf16[2,128,128]{2,1,0:T(8,128)(2,1)} %param.21) | copy-start | bytes 196612
  1.6 14.7 %copy-start.9 = (bf16[2,128,128]{2,1,0:T(8,128)(2,1)S(1)}, bf16[2,128,128]{2,1,0:T(8,128)(2,1)}, u32[]{:S(2)}) copy-start(bf16[2,128,128]{2,1,0:T(8,128)(2,1)} %param.20) | copy-start | bytes 196612
  4.0 8.8 %collective-permute-start = (bf16[3,3,128,128]{3,2,1,0:T(8,128)(2,1)S(1)}, bf16[3,3,128,128]{3,2,1,0:T(8,128)(2,1)S(1)}, u32[]{:S(2)}, u32[]{:S(2)}) collective-permute-start(bf16[3,3,128,128]{3,2,1,0:T(8,128)(2,1)S(1)} %get-tuple-element.27), channel_id=1, source_target_pairs={{0,32},{32,64},{64,96},{96,0},{1,33},{33,65},{65,97},{97,1},{2,34}... | collective-permute-start | bytes 884744 | tf_op jit(solution)/shard_map/ppermute | solution.py:497
  5.5 8.5 %collective-permute-start.1 = (bf16[3,3,128,128]{3,2,1,0:T(8,128)(2,1)S(1)}, bf16[3,3,128,128]{3,2,1,0:T(8,128)(2,1)S(1)}, u32[]{:S(2)}, u32[]{:S(2)}) collective-permute-start(bf16[3,3,128,128]{3,2,1,0:T(8,128)(2,1)S(1)} %get-tuple-element.29), channel_id=1, source_target_pairs={{32,0},{64,32},{96,64},{0,96},{33,1},{65,33},{97,65},{1,97},{34,2}... | collective-permute-start | bytes 884744 | tf_op jit(solution)/shard_map/ppermute | solution.py:497
  14.1 9.8 %copy-start.6 = (bf16[2,128,128]{2,1,0:T(8,128)(2,1)S(1)}, bf16[2,128,128]{2,1,0:T(8,128)(2,1)}, u32[]{:S(2)}) copy-start(bf16[2,128,128]{2,1,0:T(8,128)(2,1)} %param.17) | copy-start | bytes 196612
  14.1 9.8 %copy-start.10 = (s32[1,1,1,8,32]{4,3,2,1,0:T(8,128)S(1)}, s32[1,1,1,8,32]{4,3,2,1,0:T(8,128)}, u32[]{:S(2)}) copy-start(s32[1,1,1,8,32]{4,3,2,1,0:T(8,128)} %param.15) | copy-start | bytes 3076
  14.1 9.8 %copy-start.4 = (bf16[2,256,128]{2,1,0:T(8,128)(2,1)S(1)}, bf16[2,256,128]{2,1,0:T(8,128)(2,1)}, u32[]{:S(2)}) copy-start(bf16[2,256,128]{2,1,0:T(8,128)(2,1)} %param.19) | copy-start | bytes 393220
  14.1 9.8 %copy-start.5 = (bf16[2,256,128]{2,1,0:T(8,128)(2,1)S(1)}, bf16[2,256,128]{2,1,0:T(8,128)(2,1)}, u32[]{:S(2)}) copy-start(bf16[2,256,128]{2,1,0:T(8,128)(2,1)} %param.16) | copy-start | bytes 393220
  14.2 7.6 %collective-permute-start.2 = (bf16[3,3,128,128]{3,2,0,1:T(8,128)(2,1)S(1)}, bf16[3,3,128,128]{3,2,0,1:T(8,128)(2,1)S(1)}, u32[]{:S(2)}, u32[]{:S(2)}) collective-permute-start(bf16[3,3,128,128]{3,2,0,1:T(8,128)(2,1)S(1)} %get-tuple-element.52), channel_id=1, source_target_pairs={{0,8},{8,16},{16,24},{24,0},{1,9},{9,17},{17,25},{25,1},{2,10},{10... | collective-permute-start | bytes 884744 | tf_op jit(solution)/shard_map/ppermute | solution.py:497
  15.8 7.3 %collective-permute-start.3 = (bf16[3,3,128,128]{3,2,0,1:T(8,128)(2,1)S(1)}, bf16[3,3,128,128]{3,2,0,1:T(8,128)(2,1)S(1)}, u32[]{:S(2)}, u32[]{:S(2)}) collective-permute-start(bf16[3,3,128,128]{3,2,0,1:T(8,128)(2,1)S(1)} %get-tuple-element.53), channel_id=1, source_target_pairs={{8,0},{16,8},{24,16},{0,24},{9,1},{17,9},{25,17},{1,25},{10,2},{18... | collective-permute-start | bytes 884744 | tf_op jit(solution)/shard_map/ppermute | solution.py:497
  23.2 20.5 %copy-start.7 = (bf16[2,128,128]{2,1,0:T(8,128)(2,1)S(1)}, bf16[2,128,128]{2,1,0:T(8,128)(2,1)}, u32[]{:S(2)}) copy-start(bf16[2,128,128]{2,1,0:T(8,128)(2,1)} %param.18) | copy-start | bytes 196612
  23.3 4.3 %collective-permute-start.5 = (bf16[3,3,128,128]{3,2,1,0:T(8,128)(2,1)S(1)}, bf16[3,3,128,128]{3,2,1,0:T(8,128)(2,1)S(1)}, u32[]{:S(2)}, u32[]{:S(2)}) collective-permute-start(bf16[3,3,128,128]{3,2,1,0:T(8,128)(2,1)S(1)} %get-tuple-element.49), channel_id=1, source_target_pairs={{1,0},{2,1},{3,2},{4,3},{5,4},{6,5},{7,6},{0,7},{9,8},{10,9},{11,1... | collective-permute-start | bytes 884744 | tf_op jit(solution)/shard_map/ppermute | solution.py:497
  23.4 6.2 %collective-permute-start.4 = (bf16[3,3,128,128]{3,2,1,0:T(8,128)(2,1)S(1)}, bf16[3,3,128,128]{3,2,1,0:T(8,128)(2,1)S(1)}, u32[]{:S(2)}, u32[]{:S(2)}) collective-permute-start(bf16[3,3,128,128]{3,2,1,0:T(8,128)(2,1)S(1)} %get-tuple-element.50), channel_id=1, source_target_pairs={{0,1},{1,2},{2,3},{3,4},{4,5},{5,6},{6,7},{7,0},{8,9},{9,10},{10,1... | collective-permute-start | bytes 884744 | tf_op jit(solution)/shard_map/ppermute | solution.py:497
  30.9 4.0 %collective-permute-start.6 = (bf16[2,2,32,128]{3,2,1,0:T(8,128)(2,1)S(1)}, bf16[2,2,32,128]{3,2,1,0:T(8,128)(2,1)S(1)}, u32[]{:S(2)}, u32[]{:S(2)}) collective-permute-start(bf16[2,2,32,128]{3,2,1,0:T(8,128)(2,1)S(1)} %get-tuple-element.31), channel_id=1, source_target_pairs={{0,32},{32,64},{64,96},{96,0},{1,33},{33,65},{65,97},{97,1},{2,34}... | collective-permute-start | bytes 98312 | tf_op jit(solution)/shard_map/ppermute | solution.py:497
  32.1 3.9 %collective-permute-start.7 = (bf16[2,2,32,128]{3,2,1,0:T(8,128)(2,1)S(1)}, bf16[2,2,32,128]{3,2,1,0:T(8,128)(2,1)S(1)}, u32[]{:S(2)}, u32[]{:S(2)}) collective-permute-start(bf16[2,2,32,128]{3,2,1,0:T(8,128)(2,1)S(1)} %get-tuple-element.32), channel_id=1, source_target_pairs={{32,0},{64,32},{96,64},{0,96},{33,1},{65,33},{97,65},{1,97},{34,2}... | collective-permute-start | bytes 98312 | tf_op jit(solution)/shard_map/ppermute | solution.py:497
  36.1 4.3 %collective-permute-start.8 = (bf16[4,2,32,128]{3,2,1,0:T(8,128)(2,1)S(1)}, bf16[4,2,32,128]{3,2,1,0:T(8,128)(2,1)S(1)}, u32[]{:S(2)}, u32[]{:S(2)}) collective-permute-start(bf16[4,2,32,128]{3,2,1,0:T(8,128)(2,1)S(1)} %pad_maximum_fusion.6), channel_id=1, source_target_pairs={{0,8},{8,16},{16,24},{24,0},{1,9},{9,17},{17,25},{25,1},{2,10},{10... | collective-permute-start | bytes 196616 | tf_op jit(solution)/shard_map/ppermute | solution.py:497
  37.4 8.9 %copy-start = (s32[1,1,1,3456,24]{3,4,2,1,0:T(8,128)S(1)}, s32[1,1,1,3456,24]{3,4,2,1,0:T(8,128)}, u32[]{:S(2)}) copy-start(s32[1,1,1,3456,24]{3,4,2,1,0:T(8,128)} %param.13) | copy-start | bytes 995332
  37.4 8.9 %copy-start.1 = (s32[1,1,1,3456,24]{3,4,2,1,0:T(8,128)S(1)}, s32[1,1,1,3456,24]{3,4,2,1,0:T(8,128)}, u32[]{:S(2)}) copy-start(s32[1,1,1,3456,24]{3,4,2,1,0:T(8,128)} %param.14) | copy-start | bytes 995332
  37.4 4.3 %collective-permute-start.9 = (bf16[4,2,32,128]{3,2,1,0:T(8,128)(2,1)S(1)}, bf16[4,2,32,128]{3,2,1,0:T(8,128)(2,1)S(1)}, u32[]{:S(2)}, u32[]{:S(2)}) collective-permute-start(bf16[4,2,32,128]{3,2,1,0:T(8,128)(2,1)S(1)} %pad_maximum_fusion.7), channel_id=1, source_target_pairs={{8,0},{16,8},{24,16},{0,24},{9,1},{17,9},{25,17},{1,25},{10,2},{18... | collective-permute-start | bytes 196616 | tf_op jit(solution)/shard_map/ppermute | solution.py:497
  41.9 4.4 %collective-permute-start.10 = (bf16[4,4,32,128]{3,2,1,0:T(8,128)(2,1)S(1)}, bf16[4,4,32,128]{3,2,1,0:T(8,128)(2,1)S(1)}, u32[]{:S(2)}, u32[]{:S(2)}) collective-permute-start(bf16[4,4,32,128]{3,2,1,0:T(8,128)(2,1)S(1)} %pad_maximum_fusion.2), channel_id=1, source_target_pairs={{0,1},{1,2},{2,3},{3,4},{4,5},{5,6},{6,7},{7,0},{8,9},{9,10},{10,1... | collective-permute-start | bytes 393224 | tf_op jit(solution)/shard_map/ppermute | solution.py:497
  42.0 4.3 %collective-permute-start.11 = (bf16[4,4,32,128]{3,2,1,0:T(8,128)(2,1)S(1)}, bf16[4,4,32,128]{3,2,1,0:T(8,128)(2,1)S(1)}, u32[]{:S(2)}, u32[]{:S(2)}) collective-permute-start(bf16[4,4,32,128]{3,2,1,0:T(8,128)(2,1)S(1)} %pad_maximum_fusion.3), channel_id=1, source_target_pairs={{1,0},{2,1},{3,2},{4,3},{5,4},{6,5},{7,6},{0,7},{9,8},{10,9},{11,1... | collective-permute-start | bytes 393224 | tf_op jit(solution)/shard_map/ppermute | solution.py:497
  77.7 4.0 %collective-permute-start.12 = (bf16[2,2,32,128]{3,2,1,0:T(8,128)(2,1)S(1)}, bf16[2,2,32,128]{3,2,1,0:T(8,128)(2,1)S(1)}, u32[]{:S(2)}, u32[]{:S(2)}) collective-permute-start(bf16[2,2,32,128]{3,2,1,0:T(8,128)(2,1)S(1)} %get-tuple-element.46), channel_id=1, source_target_pairs={{0,32},{32,64},{64,96},{96,0},{1,33},{33,65},{65,97},{97,1},{2,34}... | collective-permute-start | bytes 98312 | tf_op jit(solution)/shard_map/ppermute | solution.py:497
  78.9 3.9 %collective-permute-start.13 = (bf16[2,2,32,128]{3,2,1,0:T(8,128)(2,1)S(1)}, bf16[2,2,32,128]{3,2,1,0:T(8,128)(2,1)S(1)}, u32[]{:S(2)}, u32[]{:S(2)}) collective-permute-start(bf16[2,2,32,128]{3,2,1,0:T(8,128)(2,1)S(1)} %get-tuple-element.47), channel_id=1, source_target_pairs={{32,0},{64,32},{96,64},{0,96},{33,1},{65,33},{97,65},{1,97},{34,2}... | collective-permute-start | bytes 98312 | tf_op jit(solution)/shard_map/ppermute | solution.py:497
  82.8 4.6 %collective-permute-start.14 = (bf16[4,2,32,128]{3,2,1,0:T(8,128)(2,1)S(1)}, bf16[4,2,32,128]{3,2,1,0:T(8,128)(2,1)S(1)}, u32[]{:S(2)}, u32[]{:S(2)}) collective-permute-start(bf16[4,2,32,128]{3,2,1,0:T(8,128)(2,1)S(1)} %pad_maximum_fusion.8), channel_id=1, source_target_pairs={{0,8},{8,16},{16,24},{24,0},{1,9},{9,17},{17,25},{25,1},{2,10},{10... | collective-permute-start | bytes 196616 | tf_op jit(solution)/shard_map/ppermute | solution.py:497
  85.6 4.3 %collective-permute-start.15 = (bf16[4,2,32,128]{3,2,1,0:T(8,128)(2,1)S(1)}, bf16[4,2,32,128]{3,2,1,0:T(8,128)(2,1)S(1)}, u32[]{:S(2)}, u32[]{:S(2)}) collective-permute-start(bf16[4,2,32,128]{3,2,1,0:T(8,128)(2,1)S(1)} %pad_maximum_fusion.9), channel_id=1, source_target_pairs={{8,0},{16,8},{24,16},{0,24},{9,1},{17,9},{25,17},{1,25},{10,2},{18... | collective-permute-start | bytes 196616 | tf_op jit(solution)/shard_map/ppermute | solution.py:497
  90.0 4.4 %collective-permute-start.16 = (bf16[4,4,32,128]{3,2,1,0:T(8,128)(2,1)S(1)}, bf16[4,4,32,128]{3,2,1,0:T(8,128)(2,1)S(1)}, u32[]{:S(2)}, u32[]{:S(2)}) collective-permute-start(bf16[4,4,32,128]{3,2,1,0:T(8,128)(2,1)S(1)} %pad_maximum_fusion.4), channel_id=1, source_target_pairs={{0,1},{1,2},{2,3},{3,4},{4,5},{5,6},{6,7},{7,0},{8,9},{9,10},{10,1... | collective-permute-start | bytes 393224 | tf_op jit(solution)/shard_map/ppermute | solution.py:497
  90.1 4.3 %collective-permute-start.17 = (bf16[4,4,32,128]{3,2,1,0:T(8,128)(2,1)S(1)}, bf16[4,4,32,128]{3,2,1,0:T(8,128)(2,1)S(1)}, u32[]{:S(2)}, u32[]{:S(2)}) collective-permute-start(bf16[4,4,32,128]{3,2,1,0:T(8,128)(2,1)S(1)} %pad_maximum_fusion.5), channel_id=1, source_target_pairs={{1,0},{2,1},{3,2},{4,3},{5,4},{6,5},{7,6},{0,7},{9,8},{10,9},{11,1... | collective-permute-start | bytes 393224 | tf_op jit(solution)/shard_map/ppermute | solution.py:497

commit v10 on v9

--- a/solution.py
+++ b/solution.py
@@ -187,14 +187,41 @@
         ghosts[s * SLAB : (s + 1) * SLAB, :] = slab
 
 
-def index_kernel(
-    pos_ref,
-    nbr_ref,
-    valid_ref,
-    cnt_ref,
-    *refs,
-):
-    around, (idx_ref, steps_ref, times_ref, ghosts, held) = refs[:AROUND], refs[AROUND:]
+EMPTY = -2
+NONE = -1
+
+
+def near_kernel(nbr_ref, valid_ref, cnt_ref, held_ref):
+    counts = cnt_ref[...]
+    diag = iota((32, W), 0) == iota((32, W), 1)
+    by_code = jnp.sum(jnp.where(diag, counts.astype(F32), 0.0), axis=0, keepdims=True)
+    by_code = jnp.broadcast_to(by_code.astype(I32), (DEG, W))
+    held_ref[CODES * DEG :, :] = jnp.full(((32 - CODES) * DEG, W), NONE, I32)
+    for c in range(CODES):
+        cols = slice(c * W, (c + 1) * W)
+        node = nbr_ref[:, cols]
+        near = jnp.minimum(jnp.maximum(node, 0), ROWS - 1)
+        limit = jnp.take_along_axis(by_code, lax.shift_right_logical(near, 7), axis=1)
+        node = jnp.where((node < ROWS) & ((near & (W - 1)) >= limit), EMPTY, node)
+        here = iota((DEG, W), 1) < counts[c : c + 1, :]
+        held_ref[c * DEG : (c + 1) * DEG, :] = jnp.where(
+            here & (valid_ref[:, cols] > 0), node, NONE
+        )
+
+
+def near_nodes(nbr, valid, cnt):
+    return pl.pallas_call(
+        near_kernel,
+        out_shape=jax.ShapeDtypeStruct((32 * DEG, W), I32),
+        in_specs=[vmem()] * 3,
+        out_specs=vmem(),
+        compiler_params=pltpu.CompilerParams(vmem_limit_bytes=VMEM_LIMIT),
+        name="near_nodes",
+    )(nbr, valid, cnt)
+
+
+def index_kernel(pos_ref, held, *refs):
+    around, (idx_ref, steps_ref, times_ref, ghosts) = refs[:AROUND], refs[AROUND:]
     fill_ghosts(pos_ref, around, ghosts)
     alive = jnp.where(ghosts[...].astype(F32) < MARK * 0.5, 1.0, 0.0).astype(BF16)
     at = iota((W, GHOSTS), 1)
@@ -204,18 +231,7 @@
     eye = iota((W, W), 0) == iota((W, W), 1)
     words = jnp.sum(jnp.where(eye, words, 0.0), axis=0, keepdims=True).astype(I32)
     words = jnp.broadcast_to(words, (8, W))
-    counts = cnt_ref[...]
-    diag = iota((32, W), 0) == iota((32, W), 1)
-    by_code = jnp.sum(jnp.where(diag, counts.astype(F32), 0.0), axis=0, keepdims=True)
-    by_code = jnp.broadcast_to(by_code.astype(I32), (8, W))
-
-    held[...] = jnp.zeros_like(held) - 1
-    for c in range(CODES):
-        cols = slice(c * W, (c + 1) * W)
-        held[c * DEG : (c + 1) * DEG, :] = jnp.where(valid_ref[:, cols] > 0, nbr_ref[:, cols], -1)
-
     for b in range(4):
-        here = iota((8, W), 1) < counts[b * 8 : (b + 1) * 8, :]
         keys = []
         dead = jnp.zeros((8, W), F32)
         for k in range(DEG):
@@ -223,12 +239,9 @@
             far = jnp.maximum(node - ROWS, 0)
             word = jnp.take_along_axis(words, lax.shift_right_logical(far, 4), axis=1)
             flag = lax.shift_right_logical(word, far & 15) & 1
-            near = jnp.minimum(jnp.maximum(node, 0), ROWS - 1)
-            limit = jnp.take_along_axis(by_code, lax.shift_right_logical(near, 7), axis=1)
-            lives = jnp.where(node >= ROWS, flag, jnp.where((near & (W - 1)) < limit, 1, 0))
-            real = node >= 0
-            key = jnp.where(here & real & (lives > 0), node, DUMMY)
-            dead = dead + jnp.where(here & real & (lives == 0), 1.0, 0.0)
+            lives = (node >= 0) & ((node < ROWS) | (flag > 0))
+            key = jnp.where(lives, node, DUMMY)
+            dead = dead + jnp.where((node == EMPTY) | ((node >= ROWS) & (flag == 0)), 1.0, 0.0)
             keys.append(key.astype(F32))
         for i, j in sort_pairs(DEG):
             keys[i], keys[j] = jnp.minimum(keys[i], keys[j]), jnp.maximum(keys[i], keys[j])
@@ -245,7 +258,7 @@
             times_ref[c * W : (c + 1) * W, :] = dot(lone, jnp.ones((W, W), BF16)).astype(BF16)
 
 
-def indices(pos, nbr, valid, cnt, around):
+def indices(pos, held, around):
     return pl.pallas_call(
         index_kernel,
         out_shape=[
@@ -253,12 +266,12 @@
             jax.ShapeDtypeStruct((32, W), I32),
             jax.ShapeDtypeStruct((ROWS, W), BF16),
         ],
-        in_specs=[smem()] + [vmem()] * (3 + AROUND),
+        in_specs=[smem()] + [vmem()] * (1 + AROUND),
         out_specs=[vmem()] * 3,
-        scratch_shapes=[pltpu.VMEM((GHOSTS, W), BF16), pltpu.VMEM((32 * DEG, W), I32)],
+        scratch_shapes=[pltpu.VMEM((GHOSTS, W), BF16)],
         compiler_params=pltpu.CompilerParams(vmem_limit_bytes=VMEM_LIMIT),
         name="indices",
-    )(pos, nbr, valid, cnt, *around)
+    )(pos, held, *around)
 
 
 GROUP = 16
@@ -432,7 +445,7 @@
         pl.when(turn == rounds)(copy.wait)
     finish(hidden[...], last)
 
-    w_third = ethird_ref[...]
+    w_twice = jnp.concatenate([ethird_ref[...], ethird_ref[...]], axis=0)
     n_agg = nfirst_ref[W : 2 * W, :]
     n_second = nsecond_ref[...]
     n_third = nthird_ref[...]
@@ -446,7 +459,8 @@
         summed = jnp.where(live, agg[rows, :] + lone_part, 0.0)
         top = summed.astype(BF16)
         rest = (summed - top.astype(F32)).astype(BF16)
-        total = (dot(top, w_third) + dot(rest, w_third)).astype(BF16)
+        both = jnp.concatenate([top, rest], axis=1)
+        total = dot(both, w_twice).astype(BF16)
         state = state_ref[rows, :]
         h = jnp.maximum(first_ref[rows, :] + dot(total, n_agg), 0.0).astype(BF16)
         h = jnp.maximum(dot(h, n_second), 0.0).astype(BF16)
@@ -550,7 +564,7 @@
         own = (table, recv, *lone(state, recv, weights[1], weights[3]))
         around = surround(down, up)
         if layer == 0:
-            idx, steps, times = indices(pos, nbr, mask, cnt, around)
+            idx, steps, times = indices(pos, near_nodes(nbr, mask, cnt), around)
             idx = idx.reshape(-1)
         state, down, up = one_layer(
             idx, pos, steps, cnt, gidx, own, times, state, around, weights

time: 125 us -> 125 us (level); the launches traced: 125 us -> 123 us
  no operation moved by 1% of the time
where the time goes in v10:
time: 125 us; the launch traced here: 123 us
  Pallas kernels  68.1 us (54%)
  waiting for transfers between devices  35.4 us (28%)
  starting transfers between devices  16.7 us (13%)
  local copies, waits for them, and re-layouts  2.03 us (2%)
    pallas_call x2, Pallas kernels, one_layer(): pl.pallas_call(layer_kernel, out_shape=[jax.ShapeDtypeStruct((NODES + 8,...  58.9 us
    ppermute x18, waiting for transfers between devices, both_ways(): return (lax.ppermute(up, axis, forward), lax.ppermute(down, axis, backward))  35.4 us
    ppermute x18, starting transfers between devices, both_ways(): return (lax.ppermute(up, axis, forward), lax.ppermute(down, axis, backward))  16.7 us
  transfers between devices with their start and end apart: 18, of which 16 were waited for; matrix products, arithmetic and copies ran while one was open for 0% of the time, Pallas kernels for 3%

profile of v10, /device:TPU:106, one launch (start us, length us, event | category | flops | bytes accessed | tf_op | source)
XLA Modules:
  0.0 123.4 jit_solution(5172642008462743152)
XLA Ops:
  0.0 0.9 copy-done.2
  1.6 2.3 %pack.1 = (bf16[3,3,128,128]{3,2,1,0:T(8,128)(2,1)S(1)}, bf16[3,3,128,128]{3,2,1,0:T(8,128)(2,1)S(1)}, bf16[3,3,128,128]{3,2,1,0:T(8,128)(2,1)S(1)}) custom-call(s32[1,1024]{1,0:T(1,128)S(1)} %bitcast.224, bf16[1024,128]{1,0:T(8,128)(2,1)S(1)} %bitcast.223), custom_call_target="tpu_custom_call" | custom-call | tf_op jit(solution)/shard_map/pack/pallas_call | solution.py:81
  4.0 1.6 %collective-permute-start = (bf16[3,3,128,128]{3,2,1,0:T(8,128)(2,1)S(1)}, bf16[3,3,128,128]{3,2,1,0:T(8,128)(2,1)S(1)}, u32[]{:S(2)}, u32[]{:S(2)}) collective-permute-start(bf16[3,3,128,128]{3,2,1,0:T(8,128)(2,1)S(1)} %get-tuple-element.27), channel_id=1, source_target_pairs={{0,32},{32,64},{64,96},{96,0},{1,33},{33,65},{65,97},{97,1},{2,34}... | collective-permute-start | bytes 884744 | tf_op jit(solution)/shard_map/ppermute | solution.py:511
  6.0 6.7 %collective-permute-done = bf16[3,3,128,128]{3,2,1,0:T(8,128)(2,1)S(1)} collective-permute-done((bf16[3,3,128,128]{3,2,1,0:T(8,128)(2,1)S(1)}, bf16[3,3,128,128]{3,2,1,0:T(8,128)(2,1)S(1)}, u32[]{:S(2)}, u32[]{:S(2)}) %collective-permute-start) | collective-permute-done | bytes 294944 | tf_op jit(solution)/shard_map/ppermute | solution.py:511
  12.8 1.2 collective-permute-done.1
  14.2 1.6 %collective-permute-start.2 = (bf16[3,3,128,128]{3,2,0,1:T(8,128)(2,1)S(1)}, bf16[3,3,128,128]{3,2,0,1:T(8,128)(2,1)S(1)}, u32[]{:S(2)}, u32[]{:S(2)}) collective-permute-start(bf16[3,3,128,128]{3,2,0,1:T(8,128)(2,1)S(1)} %get-tuple-element.52), channel_id=1, source_target_pairs={{0,8},{8,16},{16,24},{24,0},{1,9},{9,17},{17,25},{25,1},{2,10},{10... | collective-permute-start | bytes 884744 | tf_op jit(solution)/shard_map/ppermute | solution.py:511
  16.3 5.5 %collective-permute-done.2 = bf16[3,3,128,128]{3,2,0,1:T(8,128)(2,1)S(1)} collective-permute-done((bf16[3,3,128,128]{3,2,0,1:T(8,128)(2,1)S(1)}, bf16[3,3,128,128]{3,2,0,1:T(8,128)(2,1)S(1)}, u32[]{:S(2)}, u32[]{:S(2)}) %collective-permute-start.2) | collective-permute-done | bytes 294944 | tf_op jit(solution)/shard_map/ppermute | solution.py:511
  21.8 1.3 %collective-permute-done.3 = bf16[3,3,128,128]{3,2,0,1:T(8,128)(2,1)S(1)} collective-permute-done((bf16[3,3,128,128]{3,2,0,1:T(8,128)(2,1)S(1)}, bf16[3,3,128,128]{3,2,0,1:T(8,128)(2,1)S(1)}, u32[]{:S(2)}, u32[]{:S(2)}) %collective-permute-start.3) | collective-permute-done | bytes 294944 | tf_op jit(solution)/shard_map/ppermute | solution.py:511
  24.0 3.6 %collective-permute-done.5.high_ref = bf16[3,3,128,128]{3,2,1,0:T(8,128)(2,1)S(1)} collective-permute-done((bf16[3,3,128,128]{3,2,1,0:T(8,128)(2,1)S(1)}, bf16[3,3,128,128]{3,2,1,0:T(8,128)(2,1)S(1)}, u32[]{:S(2)}, u32[]{:S(2)}) %collective-permute-start.5) | collective-permute-done | bytes 294944 | tf_op jit(solution)/shard_map/ppermute | solution.py:511
  27.6 1.9 %collective-permute-done.4.low_ref = bf16[3,3,128,128]{3,2,1,0:T(8,128)(2,1)S(1)} collective-permute-done((bf16[3,3,128,128]{3,2,1,0:T(8,128)(2,1)S(1)}, bf16[3,3,128,128]{3,2,1,0:T(8,128)(2,1)S(1)}, u32[]{:S(2)}, u32[]{:S(2)}) %collective-permute-start.4) | collective-permute-done | bytes 294944 | tf_op jit(solution)/shard_map/ppermute | solution.py:511
  29.5 1.3 %receive.1 = (bf16[3456,128]{1,0:T(8,128)(2,1)S(1)}, s32[32,128]{1,0:T(8,128)S(1)}, bf16[2,2,32,128]{3,2,1,0:T(8,128)(2,1)S(1)}, bf16[2,2,32,128]{3,2,1,0:T(8,128)(2,1)S(1)}) custom-call(s32[256]{0:T(256)S(1)} %reshape.12.gidx_ref, bf16[3,3,128,128]{3,2,1,0:T(8,128)(2,1)S(1)} %get-tuple-element.51.mid_ref, ...), custom_call_target="tpu_custom_call" | custom-call | tf_op jit(solution)/shard_map/receive/pallas_call | solution.py:135
  30.9 1.3 %collective-permute-start.6 = (bf16[2,2,32,128]{3,2,1,0:T(8,128)(2,1)S(1)}, bf16[2,2,32,128]{3,2,1,0:T(8,128)(2,1)S(1)}, u32[]{:S(2)}, u32[]{:S(2)}) collective-permute-start(bf16[2,2,32,128]{3,2,1,0:T(8,128)(2,1)S(1)} %get-tuple-element.31), channel_id=1, source_target_pairs={{0,32},{32,64},{64,96},{96,0},{1,33},{33,65},{65,97},{97,1},{2,34}... | collective-permute-start | bytes 98312 | tf_op jit(solution)/shard_map/ppermute | solution.py:511
  33.0 1.9 %collective-permute-done.6.refs_0_ = bf16[2,2,32,128]{3,2,1,0:T(8,128)(2,1)S(1)} collective-permute-done((bf16[2,2,32,128]{3,2,1,0:T(8,128)(2,1)S(1)}, bf16[2,2,32,128]{3,2,1,0:T(8,128)(2,1)S(1)}, u32[]{:S(2)}, u32[]{:S(2)}) %collective-permute-start.6) | collective-permute-done | bytes 32800 | tf_op jit(solution)/shard_map/ppermute | solution.py:511
  34.9 1.2 collective-permute-done.7.refs_1_
  36.1 1.4 %collective-permute-start.8 = (bf16[4,2,32,128]{3,2,1,0:T(8,128)(2,1)S(1)}, bf16[4,2,32,128]{3,2,1,0:T(8,128)(2,1)S(1)}, u32[]{:S(2)}, u32[]{:S(2)}) collective-permute-start(bf16[4,2,32,128]{3,2,1,0:T(8,128)(2,1)S(1)} %pad_maximum_fusion.6), channel_id=1, source_target_pairs={{0,8},{8,16},{16,24},{24,0},{1,9},{9,17},{17,25},{25,1},{2,10},{10... | collective-permute-start | bytes 196616 | tf_op jit(solution)/shard_map/ppermute | solution.py:511
  38.3 2.1 %collective-permute-done.8.refs_2_ = bf16[4,2,32,128]{3,2,1,0:T(8,128)(2,1)S(1)} collective-permute-done((bf16[4,2,32,128]{3,2,1,0:T(8,128)(2,1)S(1)}, bf16[4,2,32,128]{3,2,1,0:T(8,128)(2,1)S(1)}, u32[]{:S(2)}, u32[]{:S(2)}) %collective-permute-start.8) | collective-permute-done | bytes 65568 | tf_op jit(solution)/shard_map/ppermute | solution.py:511
  40.4 1.4 %collective-permute-done.9.refs_3_ = bf16[4,2,32,128]{3,2,1,0:T(8,128)(2,1)S(1)} collective-permute-done((bf16[4,2,32,128]{3,2,1,0:T(8,128)(2,1)S(1)}, bf16[4,2,32,128]{3,2,1,0:T(8,128)(2,1)S(1)}, u32[]{:S(2)}, u32[]{:S(2)}) %collective-permute-start.9) | collective-permute-done | bytes 65568 | tf_op jit(solution)/shard_map/ppermute | solution.py:511
  42.0 1.7 %collective-permute-start.11 = (bf16[4,4,32,128]{3,2,1,0:T(8,128)(2,1)S(1)}, bf16[4,4,32,128]{3,2,1,0:T(8,128)(2,1)S(1)}, u32[]{:S(2)}, u32[]{:S(2)}) collective-permute-start(bf16[4,4,32,128]{3,2,1,0:T(8,128)(2,1)S(1)} %pad_maximum_fusion.3), channel_id=1, source_target_pairs={{1,0},{2,1},{3,2},{4,3},{5,4},{6,5},{7,6},{0,7},{9,8},{10,9},{11,1... | collective-permute-start | bytes 393224 | tf_op jit(solution)/shard_map/ppermute | solution.py:511
  43.8 0.9 project.2
  45.0 0.9 lone.2
  46.3 1.7 %indices.1 = (s32[768,128]{1,0:T(8,128)S(1)}, s32[32,128]{1,0:T(8,128)S(1)}, bf16[3456,128]{1,0:T(8,128)(2,1)S(1)}) custom-call(s32[3]{0:T(128)S(1)} %pad_add_fusion.pos_ref, s32[768,128]{1,0:T(8,128)S(1)} %near_nodes.1.held, bf16[2,2,32,128]{3,2,1,0:T(8,128)(2,1)S(1)} %collective-permute-done.6.refs_0_, ...), custom_call_target="tpu_custom_call" | custom-call | tf_op jit(solution)/shard_map/indices/pallas_call | solution.py:262
  48.0 29.0 %layer.2 = (f32[5256,128]{1,0:T(8,128)S(1)}, bf16[3456,128]{1,0:T(8,128)(2,1)S(1)}, bf16[2,2,32,128]{3,2,1,0:T(8,128)(2,1)S(1)}, bf16[2,2,32,128]{3,2,1,0:T(8,128)(2,1)S(1)}) custom-call(s32[98304]{0:T(1024)S(1)} %bitcast.218, s32[3]{0:T(128)S(1)} %pad_add_fusion.pos_ref, ...), custom_call_target="tpu_custom_call", output_to_operand_aliasing={{0}: (5, {})} | custom-call | tf_op jit(solution)/shard_map/layer/pallas_call | solution.py:481
  77.1 1.7 %collective-permute-start.12 = (bf16[2,2,32,128]{3,2,1,0:T(8,128)(2,1)S(1)}, bf16[2,2,32,128]{3,2,1,0:T(8,128)(2,1)S(1)}, u32[]{:S(2)}, u32[]{:S(2)}) collective-permute-start(bf16[2,2,32,128]{3,2,1,0:T(8,128)(2,1)S(1)} %get-tuple-element.46), channel_id=1, source_target_pairs={{0,32},{32,64},{64,96},{96,0},{1,33},{33,65},{65,97},{97,1},{2,34}... | collective-permute-start | bytes 98312 | tf_op jit(solution)/shard_map/ppermute | solution.py:511
  79.2 1.9 %collective-permute-done.12.refs_0_ = bf16[2,2,32,128]{3,2,1,0:T(8,128)(2,1)S(1)} collective-permute-done((bf16[2,2,32,128]{3,2,1,0:T(8,128)(2,1)S(1)}, bf16[2,2,32,128]{3,2,1,0:T(8,128)(2,1)S(1)}, u32[]{:S(2)}, u32[]{:S(2)}) %collective-permute-start.12) | collective-permute-done | bytes 32800 | tf_op jit(solution)/shard_map/ppermute | solution.py:511
  81.1 1.7 %collective-permute-done.13.refs_1_ = bf16[2,2,32,128]{3,2,1,0:T(8,128)(2,1)S(1)} collective-permute-done((bf16[2,2,32,128]{3,2,1,0:T(8,128)(2,1)S(1)}, bf16[2,2,32,128]{3,2,1,0:T(8,128)(2,1)S(1)}, u32[]{:S(2)}, u32[]{:S(2)}) %collective-permute-start.13) | collective-permute-done | bytes 32800 | tf_op jit(solution)/shard_map/ppermute | solution.py:511
  82.8 1.8 %collective-permute-start.14 = (bf16[4,2,32,128]{3,2,1,0:T(8,128)(2,1)S(1)}, bf16[4,2,32,128]{3,2,1,0:T(8,128)(2,1)S(1)}, u32[]{:S(2)}, u32[]{:S(2)}) collective-permute-start(bf16[4,2,32,128]{3,2,1,0:T(8,128)(2,1)S(1)} %pad_maximum_fusion.8), channel_id=1, source_target_pairs={{0,8},{8,16},{16,24},{24,0},{1,9},{9,17},{17,25},{25,1},{2,10},{10... | collective-permute-start | bytes 196616 | tf_op jit(solution)/shard_map/ppermute | solution.py:511
  84.9 2.1 %collective-permute-done.14.refs_2_ = bf16[4,2,32,128]{3,2,1,0:T(8,128)(2,1)S(1)} collective-permute-done((bf16[4,2,32,128]{3,2,1,0:T(8,128)(2,1)S(1)}, bf16[4,2,32,128]{3,2,1,0:T(8,128)(2,1)S(1)}, u32[]{:S(2)}, u32[]{:S(2)}) %collective-permute-start.14) | collective-permute-done | bytes 65568 | tf_op jit(solution)/shard_map/ppermute | solution.py:511
  87.1 1.9 %collective-permute-done.15.refs_3_ = bf16[4,2,32,128]{3,2,1,0:T(8,128)(2,1)S(1)} collective-permute-done((bf16[4,2,32,128]{3,2,1,0:T(8,128)(2,1)S(1)}, bf16[4,2,32,128]{3,2,1,0:T(8,128)(2,1)S(1)}, u32[]{:S(2)}, u32[]{:S(2)}) %collective-permute-start.15) | collective-permute-done | bytes 65568 | tf_op jit(solution)/shard_map/ppermute | solution.py:511
  89.2 1.7 %collective-permute-start.17 = (bf16[4,4,32,128]{3,2,1,0:T(8,128)(2,1)S(1)}, bf16[4,4,32,128]{3,2,1,0:T(8,128)(2,1)S(1)}, u32[]{:S(2)}, u32[]{:S(2)}) collective-permute-start(bf16[4,4,32,128]{3,2,1,0:T(8,128)(2,1)S(1)} %pad_maximum_fusion.5), channel_id=1, source_target_pairs={{1,0},{2,1},{3,2},{4,3},{5,4},{6,5},{7,6},{0,7},{9,8},{10,9},{11,1... | collective-permute-start | bytes 393224 | tf_op jit(solution)/shard_map/ppermute | solution.py:511
  90.9 0.9 project.3
  91.8 0.9 lone.3
  93.5 29.8 %layer.3 = (f32[5256,128]{1,0:T(8,128)S(1)}, bf16[3456,128]{1,0:T(8,128)(2,1)}, bf16[2,2,32,128]{3,2,1,0:T(8,128)(2,1)}, bf16[2,2,32,128]{3,2,1,0:T(8,128)(2,1)}) custom-call(s32[98304]{0:T(1024)S(1)} %bitcast.219, s32[3]{0:T(128)S(1)} %pad_add_fusion.pos_ref, s32[32,128]{1,0:T(8,128)S(1)} %get-tuple-element.34.steps_ref, ...), custom_call_target="tpu_custom_call", output_to_operand_aliasing={{0}: (5, {})} | custom-call | tf_op jit(solution)/shard_map/layer/pallas_call | solution.py:481
  (88 shorter events, 6.9 us)
Async XLA Ops:
  0.0 0.9 copy-start.2
  1.0 0.7 copy-start.3
  1.6 14.7 %copy-start.8 = (bf16[2,128,128]{2,1,0:T(8,128)(2,1)S(1)}, bf16[2,128,128]{2,1,0:T(8,128)(2,1)}, u32[]{:S(2)}) copy-start(bf16[2,128,128]{2,1,0:T(8,128)(2,1)} %param.21) | copy-start | bytes 196612
  1.6 14.7 %copy-start.9 = (bf16[2,128,128]{2,1,0:T(8,128)(2,1)S(1)}, bf16[2,128,128]{2,1,0:T(8,128)(2,1)}, u32[]{:S(2)}) copy-start(bf16[2,128,128]{2,1,0:T(8,128)(2,1)} %param.20) | copy-start | bytes 196612
  4.0 8.8 %collective-permute-start = (bf16[3,3,128,128]{3,2,1,0:T(8,128)(2,1)S(1)}, bf16[3,3,128,128]{3,2,1,0:T(8,128)(2,1)S(1)}, u32[]{:S(2)}, u32[]{:S(2)}) collective-permute-start(bf16[3,3,128,128]{3,2,1,0:T(8,128)(2,1)S(1)} %get-tuple-element.27), channel_id=1, source_target_pairs={{0,32},{32,64},{64,96},{96,0},{1,33},{33,65},{65,97},{97,1},{2,34}... | collective-permute-start | bytes 884744 | tf_op jit(solution)/shard_map/ppermute | solution.py:511
  5.5 8.5 %collective-permute-start.1 = (bf16[3,3,128,128]{3,2,1,0:T(8,128)(2,1)S(1)}, bf16[3,3,128,128]{3,2,1,0:T(8,128)(2,1)S(1)}, u32[]{:S(2)}, u32[]{:S(2)}) collective-permute-start(bf16[3,3,128,128]{3,2,1,0:T(8,128)(2,1)S(1)} %get-tuple-element.29), channel_id=1, source_target_pairs={{32,0},{64,32},{96,64},{0,96},{33,1},{65,33},{97,65},{1,97},{34,2}... | collective-permute-start | bytes 884744 | tf_op jit(solution)/shard_map/ppermute | solution.py:511
  14.1 9.8 %copy-start.6 = (bf16[2,128,128]{2,1,0:T(8,128)(2,1)S(1)}, bf16[2,128,128]{2,1,0:T(8,128)(2,1)}, u32[]{:S(2)}) copy-start(bf16[2,128,128]{2,1,0:T(8,128)(2,1)} %param.17) | copy-start | bytes 196612
  14.1 9.8 %copy-start.10 = (s32[1,1,1,8,32]{4,3,2,1,0:T(8,128)S(1)}, s32[1,1,1,8,32]{4,3,2,1,0:T(8,128)}, u32[]{:S(2)}) copy-start(s32[1,1,1,8,32]{4,3,2,1,0:T(8,128)} %param.15) | copy-start | bytes 3076
  14.1 9.9 %copy-start.4 = (bf16[2,256,128]{2,1,0:T(8,128)(2,1)S(1)}, bf16[2,256,128]{2,1,0:T(8,128)(2,1)}, u32[]{:S(2)}) copy-start(bf16[2,256,128]{2,1,0:T(8,128)(2,1)} %param.19) | copy-start | bytes 393220
  14.1 9.9 %copy-start.5 = (bf16[2,256,128]{2,1,0:T(8,128)(2,1)S(1)}, bf16[2,256,128]{2,1,0:T(8,128)(2,1)}, u32[]{:S(2)}) copy-start(bf16[2,256,128]{2,1,0:T(8,128)(2,1)} %param.16) | copy-start | bytes 393220
  14.2 7.6 %collective-permute-start.2 = (bf16[3,3,128,128]{3,2,0,1:T(8,128)(2,1)S(1)}, bf16[3,3,128,128]{3,2,0,1:T(8,128)(2,1)S(1)}, u32[]{:S(2)}, u32[]{:S(2)}) collective-permute-start(bf16[3,3,128,128]{3,2,0,1:T(8,128)(2,1)S(1)} %get-tuple-element.52), channel_id=1, source_target_pairs={{0,8},{8,16},{16,24},{24,0},{1,9},{9,17},{17,25},{25,1},{2,10},{10... | collective-permute-start | bytes 884744 | tf_op jit(solution)/shard_map/ppermute | solution.py:511
  15.9 7.3 %collective-permute-start.3 = (bf16[3,3,128,128]{3,2,0,1:T(8,128)(2,1)S(1)}, bf16[3,3,128,128]{3,2,0,1:T(8,128)(2,1)S(1)}, u32[]{:S(2)}, u32[]{:S(2)}) collective-permute-start(bf16[3,3,128,128]{3,2,0,1:T(8,128)(2,1)S(1)} %get-tuple-element.53), channel_id=1, source_target_pairs={{8,0},{16,8},{24,16},{0,24},{9,1},{17,9},{25,17},{1,25},{10,2},{18... | collective-permute-start | bytes 884744 | tf_op jit(solution)/shard_map/ppermute | solution.py:511
  23.2 20.5 %copy-start.7 = (bf16[2,128,128]{2,1,0:T(8,128)(2,1)S(1)}, bf16[2,128,128]{2,1,0:T(8,128)(2,1)}, u32[]{:S(2)}) copy-start(bf16[2,128,128]{2,1,0:T(8,128)(2,1)} %param.18) | copy-start | bytes 196612
  23.3 21.4 %copy-start = (s32[1,1,1,3456,24]{3,4,2,1,0:T(8,128)S(1)}, s32[1,1,1,3456,24]{3,4,2,1,0:T(8,128)}, u32[]{:S(2)}) copy-start(s32[1,1,1,3456,24]{3,4,2,1,0:T(8,128)} %param.13) | copy-start | bytes 995332
  23.3 21.4 %copy-start.1 = (s32[1,1,1,3456,24]{3,4,2,1,0:T(8,128)S(1)}, s32[1,1,1,3456,24]{3,4,2,1,0:T(8,128)}, u32[]{:S(2)}) copy-start(s32[1,1,1,3456,24]{3,4,2,1,0:T(8,128)} %param.14) | copy-start | bytes 995332
  23.4 4.3 %collective-permute-start.5 = (bf16[3,3,128,128]{3,2,1,0:T(8,128)(2,1)S(1)}, bf16[3,3,128,128]{3,2,1,0:T(8,128)(2,1)S(1)}, u32[]{:S(2)}, u32[]{:S(2)}) collective-permute-start(bf16[3,3,128,128]{3,2,1,0:T(8,128)(2,1)S(1)} %get-tuple-element.49), channel_id=1, source_target_pairs={{1,0},{2,1},{3,2},{4,3},{5,4},{6,5},{7,6},{0,7},{9,8},{10,9},{11,1... | collective-permute-start | bytes 884744 | tf_op jit(solution)/shard_map/ppermute | solution.py:511
  23.4 6.2 %collective-permute-start.4 = (bf16[3,3,128,128]{3,2,1,0:T(8,128)(2,1)S(1)}, bf16[3,3,128,128]{3,2,1,0:T(8,128)(2,1)S(1)}, u32[]{:S(2)}, u32[]{:S(2)}) collective-permute-start(bf16[3,3,128,128]{3,2,1,0:T(8,128)(2,1)S(1)} %get-tuple-element.50), channel_id=1, source_target_pairs={{0,1},{1,2},{2,3},{3,4},{4,5},{5,6},{6,7},{7,0},{8,9},{9,10},{10,1... | collective-permute-start | bytes 884744 | tf_op jit(solution)/shard_map/ppermute | solution.py:511
  30.9 4.0 %collective-permute-start.6 = (bf16[2,2,32,128]{3,2,1,0:T(8,128)(2,1)S(1)}, bf16[2,2,32,128]{3,2,1,0:T(8,128)(2,1)S(1)}, u32[]{:S(2)}, u32[]{:S(2)}) collective-permute-start(bf16[2,2,32,128]{3,2,1,0:T(8,128)(2,1)S(1)} %get-tuple-element.31), channel_id=1, source_target_pairs={{0,32},{32,64},{64,96},{96,0},{1,33},{33,65},{65,97},{97,1},{2,34}... | collective-permute-start | bytes 98312 | tf_op jit(solution)/shard_map/ppermute | solution.py:511
  32.2 3.9 %collective-permute-start.7 = (bf16[2,2,32,128]{3,2,1,0:T(8,128)(2,1)S(1)}, bf16[2,2,32,128]{3,2,1,0:T(8,128)(2,1)S(1)}, u32[]{:S(2)}, u32[]{:S(2)}) collective-permute-start(bf16[2,2,32,128]{3,2,1,0:T(8,128)(2,1)S(1)} %get-tuple-element.32), channel_id=1, source_target_pairs={{32,0},{64,32},{96,64},{0,96},{33,1},{65,33},{97,65},{1,97},{34,2}... | collective-permute-start | bytes 98312 | tf_op jit(solution)/shard_map/ppermute | solution.py:511
  36.1 4.3 %collective-permute-start.8 = (bf16[4,2,32,128]{3,2,1,0:T(8,128)(2,1)S(1)}, bf16[4,2,32,128]{3,2,1,0:T(8,128)(2,1)S(1)}, u32[]{:S(2)}, u32[]{:S(2)}) collective-permute-start(bf16[4,2,32,128]{3,2,1,0:T(8,128)(2,1)S(1)} %pad_maximum_fusion.6), channel_id=1, source_target_pairs={{0,8},{8,16},{16,24},{24,0},{1,9},{9,17},{17,25},{25,1},{2,10},{10... | collective-permute-start | bytes 196616 | tf_op jit(solution)/shard_map/ppermute | solution.py:511
  37.5 4.3 %collective-permute-start.9 = (bf16[4,2,32,128]{3,2,1,0:T(8,128)(2,1)S(1)}, bf16[4,2,32,128]{3,2,1,0:T(8,128)(2,1)S(1)}, u32[]{:S(2)}, u32[]{:S(2)}) collective-permute-start(bf16[4,2,32,128]{3,2,1,0:T(8,128)(2,1)S(1)} %pad_maximum_fusion.7), channel_id=1, source_target_pairs={{8,0},{16,8},{24,16},{0,24},{9,1},{17,9},{25,17},{1,25},{10,2},{18... | collective-permute-start | bytes 196616 | tf_op jit(solution)/shard_map/ppermute | solution.py:511
  41.9 4.4 %collective-permute-start.10 = (bf16[4,4,32,128]{3,2,1,0:T(8,128)(2,1)S(1)}, bf16[4,4,32,128]{3,2,1,0:T(8,128)(2,1)S(1)}, u32[]{:S(2)}, u32[]{:S(2)}) collective-permute-start(bf16[4,4,32,128]{3,2,1,0:T(8,128)(2,1)S(1)} %pad_maximum_fusion.2), channel_id=1, source_target_pairs={{0,1},{1,2},{2,3},{3,4},{4,5},{5,6},{6,7},{7,0},{8,9},{9,10},{10,1... | collective-permute-start | bytes 393224 | tf_op jit(solution)/shard_map/ppermute | solution.py:511
  42.0 4.3 %collective-permute-start.11 = (bf16[4,4,32,128]{3,2,1,0:T(8,128)(2,1)S(1)}, bf16[4,4,32,128]{3,2,1,0:T(8,128)(2,1)S(1)}, u32[]{:S(2)}, u32[]{:S(2)}) collective-permute-start(bf16[4,4,32,128]{3,2,1,0:T(8,128)(2,1)S(1)} %pad_maximum_fusion.3), channel_id=1, source_target_pairs={{1,0},{2,1},{3,2},{4,3},{5,4},{6,5},{7,6},{0,7},{9,8},{10,9},{11,1... | collective-permute-start | bytes 393224 | tf_op jit(solution)/shard_map/ppermute | solution.py:511
  77.1 4.0 %collective-permute-start.12 = (bf16[2,2,32,128]{3,2,1,0:T(8,128)(2,1)S(1)}, bf16[2,2,32,128]{3,2,1,0:T(8,128)(2,1)S(1)}, u32[]{:S(2)}, u32[]{:S(2)}) collective-permute-start(bf16[2,2,32,128]{3,2,1,0:T(8,128)(2,1)S(1)} %get-tuple-element.46), channel_id=1, source_target_pairs={{0,32},{32,64},{64,96},{96,0},{1,33},{33,65},{65,97},{97,1},{2,34}... | collective-permute-start | bytes 98312 | tf_op jit(solution)/shard_map/ppermute | solution.py:511
  78.8 3.9 %collective-permute-start.13 = (bf16[2,2,32,128]{3,2,1,0:T(8,128)(2,1)S(1)}, bf16[2,2,32,128]{3,2,1,0:T(8,128)(2,1)S(1)}, u32[]{:S(2)}, u32[]{:S(2)}) collective-permute-start(bf16[2,2,32,128]{3,2,1,0:T(8,128)(2,1)S(1)} %get-tuple-element.47), channel_id=1, source_target_pairs={{32,0},{64,32},{96,64},{0,96},{33,1},{65,33},{97,65},{1,97},{34,2}... | collective-permute-start | bytes 98312 | tf_op jit(solution)/shard_map/ppermute | solution.py:511
  82.8 4.3 %collective-permute-start.14 = (bf16[4,2,32,128]{3,2,1,0:T(8,128)(2,1)S(1)}, bf16[4,2,32,128]{3,2,1,0:T(8,128)(2,1)S(1)}, u32[]{:S(2)}, u32[]{:S(2)}) collective-permute-start(bf16[4,2,32,128]{3,2,1,0:T(8,128)(2,1)S(1)} %pad_maximum_fusion.8), channel_id=1, source_target_pairs={{0,8},{8,16},{16,24},{24,0},{1,9},{9,17},{17,25},{25,1},{2,10},{10... | collective-permute-start | bytes 196616 | tf_op jit(solution)/shard_map/ppermute | solution.py:511
  84.6 4.3 %collective-permute-start.15 = (bf16[4,2,32,128]{3,2,1,0:T(8,128)(2,1)S(1)}, bf16[4,2,32,128]{3,2,1,0:T(8,128)(2,1)S(1)}, u32[]{:S(2)}, u32[]{:S(2)}) collective-permute-start(bf16[4,2,32,128]{3,2,1,0:T(8,128)(2,1)S(1)} %pad_maximum_fusion.9), channel_id=1, source_target_pairs={{8,0},{16,8},{24,16},{0,24},{9,1},{17,9},{25,17},{1,25},{10,2},{18... | collective-permute-start | bytes 196616 | tf_op jit(solution)/shard_map/ppermute | solution.py:511
  89.0 4.4 %collective-permute-start.16 = (bf16[4,4,32,128]{3,2,1,0:T(8,128)(2,1)S(1)}, bf16[4,4,32,128]{3,2,1,0:T(8,128)(2,1)S(1)}, u32[]{:S(2)}, u32[]{:S(2)}) collective-permute-start(bf16[4,4,32,128]{3,2,1,0:T(8,128)(2,1)S(1)} %pad_maximum_fusion.4), channel_id=1, source_target_pairs={{0,1},{1,2},{2,3},{3,4},{4,5},{5,6},{6,7},{7,0},{8,9},{9,10},{10,1... | collective-permute-start | bytes 393224 | tf_op jit(solution)/shard_map/ppermute | solution.py:511
  89.2 4.3 %collective-permute-start.17 = (bf16[4,4,32,128]{3,2,1,0:T(8,128)(2,1)S(1)}, bf16[4,4,32,128]{3,2,1,0:T(8,128)(2,1)S(1)}, u32[]{:S(2)}, u32[]{:S(2)}) collective-permute-start(bf16[4,4,32,128]{3,2,1,0:T(8,128)(2,1)S(1)} %pad_maximum_fusion.5), channel_id=1, source_target_pairs={{1,0},{2,1},{3,2},{4,3},{5,4},{6,5},{7,6},{0,7},{9,8},{10,9},{11,1... | collective-permute-start | bytes 393224 | tf_op jit(solution)/shard_map/ppermute | solution.py:511

commit v11 on v10

--- a/solution.py
+++ b/solution.py
@@ -1,3 +1,5 @@
+import functools
+
 import jax
 import jax.numpy as jnp
 import numpy as np
@@ -339,6 +341,7 @@
 
 
 def layer_kernel(
+    final,
     idx_hbm,
     pos_ref,
     steps_ref,
@@ -354,8 +357,9 @@
 ):
     around, refs = refs[:AROUND], refs[AROUND:]
     efirst_ref, esecond_ref, ethird_ref, nfirst_ref, nsecond_ref, nthird_ref = refs[:6]
-    table, out_ref, down_ref, up_ref = refs[6:10]
-    ghosts, hidden, agg, full, picked, idx_ref, homes, sems = refs[10:]
+    table, out_ref = refs[6:8]
+    slabs, refs = ((), refs[8:]) if final else (refs[8:10], refs[10:])
+    ghosts, hidden, agg, full, picked, idx_ref, homes, sems = refs
     del table_in
     copies = []
     for i, (lo, hi) in enumerate(PARTS):
@@ -469,25 +473,26 @@
         centred = update - mean
         var = jnp.mean(centred * centred, axis=1, keepdims=True)
         new = state.astype(F32) + centred * lax.rsqrt(var + 1e-05)
-        full[rows, :] = jnp.where(live, new, MARK)
+        if not final:
+            full[rows, :] = jnp.where(live, new, MARK)
         out_ref[rows, :] = jnp.where(live, new, 0.0).astype(BF16)
         return carry
 
     lax.fori_loop(0, ROWS // (SPAN * W), node, 0)
-    pick_slabs(gidx_ref, full, picked, down_ref, up_ref)
-
-
-def one_layer(idx, pos, steps, cnt, gidx, own, times, state, around, weights):
-    return pl.pallas_call(
-        layer_kernel,
+    if not final:
+        pick_slabs(gidx_ref, full, picked, *slabs)
+
+
+def one_layer(final, idx, pos, steps, cnt, gidx, own, times, state, around, weights):
+    return pl.pallas_call(
+        functools.partial(layer_kernel, final),
         out_shape=[
             jax.ShapeDtypeStruct((NODES + 8, W), F32),
             jax.ShapeDtypeStruct((ROWS, W), BF16),
-            jax.ShapeDtypeStruct((2, 2, SLAB, W), BF16),
-            jax.ShapeDtypeStruct((2, 2, SLAB, W), BF16),
-        ],
+        ]
+        + [jax.ShapeDtypeStruct((2, 2, SLAB, W), BF16)] * (0 if final else 2),
         in_specs=[pl.BlockSpec(memory_space=pl.ANY)] + [smem()] * 4 + [vmem()] * (12 + AROUND),
-        out_specs=[vmem()] * 4,
+        out_specs=[vmem()] * (2 if final else 4),
         input_output_aliases={5: 0},
         scratch_shapes=[
             pltpu.VMEM((GHOSTS, W), BF16),
@@ -554,7 +559,7 @@
     mask = valid[0, 0, 0].T
     gidx = ghost_index.reshape(-1)
     pos = jnp.stack([lax.axis_index(a) for a in HALO_AXES]).astype(I32)
-    state, cnt, down, up = receive(gidx, *migrate(*pack(dest, latent[0, 0, 0])))
+    state, cnt, *sent = receive(gidx, *migrate(*pack(dest, latent[0, 0, 0])))
     for layer in range(edge_first.shape[0]):
         weights = [
             w[layer]
@@ -562,12 +567,13 @@
         ]
         table, recv = project(state, weights[0])
         own = (table, recv, *lone(state, recv, weights[1], weights[3]))
-        around = surround(down, up)
+        around = surround(*sent)
         if layer == 0:
             idx, steps, times = indices(pos, near_nodes(nbr, mask, cnt), around)
             idx = idx.reshape(-1)
-        state, down, up = one_layer(
-            idx, pos, steps, cnt, gidx, own, times, state, around, weights
+        final = layer == edge_first.shape[0] - 1
+        state, *sent = one_layer(
+            final, idx, pos, steps, cnt, gidx, own, times, state, around, weights
         )
     return state.reshape(1, 1, 1, ROWS, W)
 

time: 125 us -> 125 us (level); the launches traced: 123 us -> 125 us
  Pallas kernels: 68.1 us -> 70.8 us
    pallas_call x2, Pallas kernels: 58.9 us -> 61.5 us  [one_layer(): pl.pallas_call(functools.partial(layer_kernel, final), out_shape=[jax.Sha...]
where the time goes in v11:
time: 125 us
  Pallas kernels  70.8 us (57%)
  waiting for transfers between devices  34.5 us (28%)
  starting transfers between devices  16.7 us (13%)
  local copies, waits for them, and re-layouts  2.03 us (2%)
    pallas_call x2, Pallas kernels, one_layer(): pl.pallas_call(functools.partial(layer_kernel, final), out_shape=[jax.Sha...  61.5 us
    ppermute x18, waiting for transfers between devices, both_ways(): return (lax.ppermute(up, axis, forward), lax.ppermute(down, axis, backward))  34.5 us
    ppermute x18, starting transfers between devices, both_ways(): return (lax.ppermute(up, axis, forward), lax.ppermute(down, axis, backward))  16.7 us
  transfers between devices with their start and end apart: 18, of which 16 were waited for; matrix products, arithmetic and copies ran while one was open for 0% of the time, Pallas kernels for 3%

profile of v11, /device:TPU:106, one launch (start us, length us, event | category | flops | bytes accessed | tf_op | source)
XLA Modules:
  0.0 125.1 jit_solution(14499002864277646169)
XLA Ops:
  0.0 0.9 copy-done.2
  1.6 2.3 %pack.1 = (bf16[3,3,128,128]{3,2,1,0:T(8,128)(2,1)S(1)}, bf16[3,3,128,128]{3,2,1,0:T(8,128)(2,1)S(1)}, bf16[3,3,128,128]{3,2,1,0:T(8,128)(2,1)S(1)}) custom-call(s32[1,1024]{1,0:T(1,128)S(1)} %bitcast.224, bf16[1024,128]{1,0:T(8,128)(2,1)S(1)} %bitcast.223), custom_call_target="tpu_custom_call" | custom-call | tf_op jit(solution)/shard_map/pack/pallas_call | solution.py:83
  4.0 1.6 %collective-permute-start = (bf16[3,3,128,128]{3,2,1,0:T(8,128)(2,1)S(1)}, bf16[3,3,128,128]{3,2,1,0:T(8,128)(2,1)S(1)}, u32[]{:S(2)}, u32[]{:S(2)}) collective-permute-start(bf16[3,3,128,128]{3,2,1,0:T(8,128)(2,1)S(1)} %get-tuple-element.27), channel_id=1, source_target_pairs={{0,32},{32,64},{64,96},{96,0},{1,33},{33,65},{65,97},{97,1},{2,34}... | collective-permute-start | bytes 884744 | tf_op jit(solution)/shard_map/ppermute | solution.py:516
  6.0 6.7 %collective-permute-done = bf16[3,3,128,128]{3,2,1,0:T(8,128)(2,1)S(1)} collective-permute-done((bf16[3,3,128,128]{3,2,1,0:T(8,128)(2,1)S(1)}, bf16[3,3,128,128]{3,2,1,0:T(8,128)(2,1)S(1)}, u32[]{:S(2)}, u32[]{:S(2)}) %collective-permute-start) | collective-permute-done | bytes 294944 | tf_op jit(solution)/shard_map/ppermute | solution.py:516
  12.8 1.2 collective-permute-done.1
  14.2 1.6 %collective-permute-start.2 = (bf16[3,3,128,128]{3,2,0,1:T(8,128)(2,1)S(1)}, bf16[3,3,128,128]{3,2,0,1:T(8,128)(2,1)S(1)}, u32[]{:S(2)}, u32[]{:S(2)}) collective-permute-start(bf16[3,3,128,128]{3,2,0,1:T(8,128)(2,1)S(1)} %get-tuple-element.52), channel_id=1, source_target_pairs={{0,8},{8,16},{16,24},{24,0},{1,9},{9,17},{17,25},{25,1},{2,10},{10... | collective-permute-start | bytes 884744 | tf_op jit(solution)/shard_map/ppermute | solution.py:516
  16.3 5.5 %collective-permute-done.2 = bf16[3,3,128,128]{3,2,0,1:T(8,128)(2,1)S(1)} collective-permute-done((bf16[3,3,128,128]{3,2,0,1:T(8,128)(2,1)S(1)}, bf16[3,3,128,128]{3,2,0,1:T(8,128)(2,1)S(1)}, u32[]{:S(2)}, u32[]{:S(2)}) %collective-permute-start.2) | collective-permute-done | bytes 294944 | tf_op jit(solution)/shard_map/ppermute | solution.py:516
  21.8 1.3 %collective-permute-done.3 = bf16[3,3,128,128]{3,2,0,1:T(8,128)(2,1)S(1)} collective-permute-done((bf16[3,3,128,128]{3,2,0,1:T(8,128)(2,1)S(1)}, bf16[3,3,128,128]{3,2,0,1:T(8,128)(2,1)S(1)}, u32[]{:S(2)}, u32[]{:S(2)}) %collective-permute-start.3) | collective-permute-done | bytes 294944 | tf_op jit(solution)/shard_map/ppermute | solution.py:516
  24.0 3.6 %collective-permute-done.5.high_ref = bf16[3,3,128,128]{3,2,1,0:T(8,128)(2,1)S(1)} collective-permute-done((bf16[3,3,128,128]{3,2,1,0:T(8,128)(2,1)S(1)}, bf16[3,3,128,128]{3,2,1,0:T(8,128)(2,1)S(1)}, u32[]{:S(2)}, u32[]{:S(2)}) %collective-permute-start.5) | collective-permute-done | bytes 294944 | tf_op jit(solution)/shard_map/ppermute | solution.py:516
  27.6 1.9 %collective-permute-done.4.low_ref = bf16[3,3,128,128]{3,2,1,0:T(8,128)(2,1)S(1)} collective-permute-done((bf16[3,3,128,128]{3,2,1,0:T(8,128)(2,1)S(1)}, bf16[3,3,128,128]{3,2,1,0:T(8,128)(2,1)S(1)}, u32[]{:S(2)}, u32[]{:S(2)}) %collective-permute-start.4) | collective-permute-done | bytes 294944 | tf_op jit(solution)/shard_map/ppermute | solution.py:516
  29.5 1.3 %receive.1 = (bf16[3456,128]{1,0:T(8,128)(2,1)S(1)}, s32[32,128]{1,0:T(8,128)S(1)}, bf16[2,2,32,128]{3,2,1,0:T(8,128)(2,1)S(1)}, bf16[2,2,32,128]{3,2,1,0:T(8,128)(2,1)S(1)}) custom-call(s32[256]{0:T(256)S(1)} %reshape.12.gidx_ref, bf16[3,3,128,128]{3,2,1,0:T(8,128)(2,1)S(1)} %get-tuple-element.51.mid_ref, ...), custom_call_target="tpu_custom_call" | custom-call | tf_op jit(solution)/shard_map/receive/pallas_call | solution.py:137
  30.9 1.3 %collective-permute-start.6 = (bf16[2,2,32,128]{3,2,1,0:T(8,128)(2,1)S(1)}, bf16[2,2,32,128]{3,2,1,0:T(8,128)(2,1)S(1)}, u32[]{:S(2)}, u32[]{:S(2)}) collective-permute-start(bf16[2,2,32,128]{3,2,1,0:T(8,128)(2,1)S(1)} %get-tuple-element.31), channel_id=1, source_target_pairs={{0,32},{32,64},{64,96},{96,0},{1,33},{33,65},{65,97},{97,1},{2,34}... | collective-permute-start | bytes 98312 | tf_op jit(solution)/shard_map/ppermute | solution.py:516
  32.2 0.8 collective-permute-start.7
  33.0 1.9 %collective-permute-done.6.refs_0_ = bf16[2,2,32,128]{3,2,1,0:T(8,128)(2,1)S(1)} collective-permute-done((bf16[2,2,32,128]{3,2,1,0:T(8,128)(2,1)S(1)}, bf16[2,2,32,128]{3,2,1,0:T(8,128)(2,1)S(1)}, u32[]{:S(2)}, u32[]{:S(2)}) %collective-permute-start.6) | collective-permute-done | bytes 32800 | tf_op jit(solution)/shard_map/ppermute | solution.py:516
  34.9 1.2 collective-permute-done.7.refs_1_
  36.1 1.4 %collective-permute-start.8 = (bf16[4,2,32,128]{3,2,1,0:T(8,128)(2,1)S(1)}, bf16[4,2,32,128]{3,2,1,0:T(8,128)(2,1)S(1)}, u32[]{:S(2)}, u32[]{:S(2)}) collective-permute-start(bf16[4,2,32,128]{3,2,1,0:T(8,128)(2,1)S(1)} %pad_maximum_fusion.6), channel_id=1, source_target_pairs={{0,8},{8,16},{16,24},{24,0},{1,9},{9,17},{17,25},{25,1},{2,10},{10... | collective-permute-start | bytes 196616 | tf_op jit(solution)/shard_map/ppermute | solution.py:516
  38.3 2.1 %collective-permute-done.8.refs_2_ = bf16[4,2,32,128]{3,2,1,0:T(8,128)(2,1)S(1)} collective-permute-done((bf16[4,2,32,128]{3,2,1,0:T(8,128)(2,1)S(1)}, bf16[4,2,32,128]{3,2,1,0:T(8,128)(2,1)S(1)}, u32[]{:S(2)}, u32[]{:S(2)}) %collective-permute-start.8) | collective-permute-done | bytes 65568 | tf_op jit(solution)/shard_map/ppermute | solution.py:516
  40.4 1.4 %collective-permute-done.9.refs_3_ = bf16[4,2,32,128]{3,2,1,0:T(8,128)(2,1)S(1)} collective-permute-done((bf16[4,2,32,128]{3,2,1,0:T(8,128)(2,1)S(1)}, bf16[4,2,32,128]{3,2,1,0:T(8,128)(2,1)S(1)}, u32[]{:S(2)}, u32[]{:S(2)}) %collective-permute-start.9) | collective-permute-done | bytes 65568 | tf_op jit(solution)/shard_map/ppermute | solution.py:516
  42.0 1.7 %collective-permute-start.11 = (bf16[4,4,32,128]{3,2,1,0:T(8,128)(2,1)S(1)}, bf16[4,4,32,128]{3,2,1,0:T(8,128)(2,1)S(1)}, u32[]{:S(2)}, u32[]{:S(2)}) collective-permute-start(bf16[4,4,32,128]{3,2,1,0:T(8,128)(2,1)S(1)} %pad_maximum_fusion.3), channel_id=1, source_target_pairs={{1,0},{2,1},{3,2},{4,3},{5,4},{6,5},{7,6},{0,7},{9,8},{10,9},{11,1... | collective-permute-start | bytes 393224 | tf_op jit(solution)/shard_map/ppermute | solution.py:516
  43.8 0.9 project.2
  45.0 0.9 lone.2
  46.3 1.7 %indices.1 = (s32[768,128]{1,0:T(8,128)S(1)}, s32[32,128]{1,0:T(8,128)S(1)}, bf16[3456,128]{1,0:T(8,128)(2,1)S(1)}) custom-call(s32[3]{0:T(128)S(1)} %pad_add_fusion.pos_ref, s32[768,128]{1,0:T(8,128)S(1)} %near_nodes.1.held, bf16[2,2,32,128]{3,2,1,0:T(8,128)(2,1)S(1)} %collective-permute-done.6.refs_0_, ...), custom_call_target="tpu_custom_call" | custom-call | tf_op jit(solution)/shard_map/indices/pallas_call | solution.py:264
  48.0 30.5 %layer.2 = (f32[5256,128]{1,0:T(8,128)S(1)}, bf16[3456,128]{1,0:T(8,128)(2,1)S(1)}, bf16[2,2,32,128]{3,2,1,0:T(8,128)(2,1)S(1)}, bf16[2,2,32,128]{3,2,1,0:T(8,128)(2,1)S(1)}) custom-call(s32[98304]{0:T(1024)S(1)} %bitcast.218, s32[3]{0:T(128)S(1)} %pad_add_fusion.pos_ref, ...), custom_call_target="tpu_custom_call", output_to_operand_aliasing={{0}: (5, {})} | custom-call | tf_op jit(solution)/shard_map/layer/pallas_call | solution.py:487
  79.2 1.4 %collective-permute-start.13 = (bf16[2,2,32,128]{3,2,1,0:T(8,128)(2,1)S(1)}, bf16[2,2,32,128]{3,2,1,0:T(8,128)(2,1)S(1)}, u32[]{:S(2)}, u32[]{:S(2)}) collective-permute-start(bf16[2,2,32,128]{3,2,1,0:T(8,128)(2,1)S(1)} %get-tuple-element.47), channel_id=1, source_target_pairs={{32,0},{64,32},{96,64},{0,96},{33,1},{65,33},{97,65},{1,97},{34,2}... | collective-permute-start | bytes 98312 | tf_op jit(solution)/shard_map/ppermute | solution.py:516
  80.7 1.9 %collective-permute-done.12.refs_0_ = bf16[2,2,32,128]{3,2,1,0:T(8,128)(2,1)S(1)} collective-permute-done((bf16[2,2,32,128]{3,2,1,0:T(8,128)(2,1)S(1)}, bf16[2,2,32,128]{3,2,1,0:T(8,128)(2,1)S(1)}, u32[]{:S(2)}, u32[]{:S(2)}) %collective-permute-start.12) | collective-permute-done | bytes 32800 | tf_op jit(solution)/shard_map/ppermute | solution.py:516
  83.2 2.0 %collective-permute-start.14 = (bf16[4,2,32,128]{3,2,1,0:T(8,128)(2,1)S(1)}, bf16[4,2,32,128]{3,2,1,0:T(8,128)(2,1)S(1)}, u32[]{:S(2)}, u32[]{:S(2)}) collective-permute-start(bf16[4,2,32,128]{3,2,1,0:T(8,128)(2,1)S(1)} %pad_maximum_fusion.8), channel_id=1, source_target_pairs={{0,8},{8,16},{16,24},{24,0},{1,9},{9,17},{17,25},{25,1},{2,10},{10... | collective-permute-start | bytes 196616 | tf_op jit(solution)/shard_map/ppermute | solution.py:516
  85.3 2.1 %collective-permute-done.14.refs_2_ = bf16[4,2,32,128]{3,2,1,0:T(8,128)(2,1)S(1)} collective-permute-done((bf16[4,2,32,128]{3,2,1,0:T(8,128)(2,1)S(1)}, bf16[4,2,32,128]{3,2,1,0:T(8,128)(2,1)S(1)}, u32[]{:S(2)}, u32[]{:S(2)}) %collective-permute-start.14) | collective-permute-done | bytes 65568 | tf_op jit(solution)/shard_map/ppermute | solution.py:516
  87.5 2.0 %collective-permute-done.15.refs_3_ = bf16[4,2,32,128]{3,2,1,0:T(8,128)(2,1)S(1)} collective-permute-done((bf16[4,2,32,128]{3,2,1,0:T(8,128)(2,1)S(1)}, bf16[4,2,32,128]{3,2,1,0:T(8,128)(2,1)S(1)}, u32[]{:S(2)}, u32[]{:S(2)}) %collective-permute-start.15) | collective-permute-done | bytes 65568 | tf_op jit(solution)/shard_map/ppermute | solution.py:516
  89.7 1.7 %collective-permute-start.17 = (bf16[4,4,32,128]{3,2,1,0:T(8,128)(2,1)S(1)}, bf16[4,4,32,128]{3,2,1,0:T(8,128)(2,1)S(1)}, u32[]{:S(2)}, u32[]{:S(2)}) collective-permute-start(bf16[4,4,32,128]{3,2,1,0:T(8,128)(2,1)S(1)} %pad_maximum_fusion.5), channel_id=1, source_target_pairs={{1,0},{2,1},{3,2},{4,3},{5,4},{6,5},{7,6},{0,7},{9,8},{10,9},{11,1... | collective-permute-start | bytes 393224 | tf_op jit(solution)/shard_map/ppermute | solution.py:516
  91.4 0.9 project.3
  92.3 0.9 lone.3
  94.0 31.0 %layer.3 = (f32[5256,128]{1,0:T(8,128)S(1)}, bf16[3456,128]{1,0:T(8,128)(2,1)}) custom-call(s32[98304]{0:T(1024)S(1)} %bitcast.219, s32[3]{0:T(128)S(1)} %pad_add_fusion.pos_ref, s32[32,128]{1,0:T(8,128)S(1)} %get-tuple-element.34.steps_ref, s32[32,128]{1,0:T(8,128)S(1)} %get-tuple-element.30.cnt_ref, ...), custom_call_target="tpu_custom_call", output_to_operand_aliasing={{0}: (5, {})} | custom-call | tf_op jit(solution)/shard_map/layer/pallas_call | solution.py:487
  (88 shorter events, 6.8 us)
Async XLA Ops:
  0.0 0.9 copy-start.2
  1.0 0.7 copy-start.3
  1.6 14.7 %copy-start.8 = (bf16[2,128,128]{2,1,0:T(8,128)(2,1)S(1)}, bf16[2,128,128]{2,1,0:T(8,128)(2,1)}, u32[]{:S(2)}) copy-start(bf16[2,128,128]{2,1,0:T(8,128)(2,1)} %param.21) | copy-start | bytes 196612
  1.6 14.7 %copy-start.9 = (bf16[2,128,128]{2,1,0:T(8,128)(2,1)S(1)}, bf16[2,128,128]{2,1,0:T(8,128)(2,1)}, u32[]{:S(2)}) copy-start(bf16[2,128,128]{2,1,0:T(8,128)(2,1)} %param.20) | copy-start | bytes 196612
  4.0 8.8 %collective-permute-start = (bf16[3,3,128,128]{3,2,1,0:T(8,128)(2,1)S(1)}, bf16[3,3,128,128]{3,2,1,0:T(8,128)(2,1)S(1)}, u32[]{:S(2)}, u32[]{:S(2)}) collective-permute-start(bf16[3,3,128,128]{3,2,1,0:T(8,128)(2,1)S(1)} %get-tuple-element.27), channel_id=1, source_target_pairs={{0,32},{32,64},{64,96},{96,0},{1,33},{33,65},{65,97},{97,1},{2,34}... | collective-permute-start | bytes 884744 | tf_op jit(solution)/shard_map/ppermute | solution.py:516
  5.5 8.5 %collective-permute-start.1 = (bf16[3,3,128,128]{3,2,1,0:T(8,128)(2,1)S(1)}, bf16[3,3,128,128]{3,2,1,0:T(8,128)(2,1)S(1)}, u32[]{:S(2)}, u32[]{:S(2)}) collective-permute-start(bf16[3,3,128,128]{3,2,1,0:T(8,128)(2,1)S(1)} %get-tuple-element.29), channel_id=1, source_target_pairs={{32,0},{64,32},{96,64},{0,96},{33,1},{65,33},{97,65},{1,97},{34,2}... | collective-permute-start | bytes 884744 | tf_op jit(solution)/shard_map/ppermute | solution.py:516
  14.1 9.8 %copy-start.6 = (bf16[2,128,128]{2,1,0:T(8,128)(2,1)S(1)}, bf16[2,128,128]{2,1,0:T(8,128)(2,1)}, u32[]{:S(2)}) copy-start(bf16[2,128,128]{2,1,0:T(8,128)(2,1)} %param.17) | copy-start | bytes 196612
  14.1 9.8 %copy-start.10 = (s32[1,1,1,8,32]{4,3,2,1,0:T(8,128)S(1)}, s32[1,1,1,8,32]{4,3,2,1,0:T(8,128)}, u32[]{:S(2)}) copy-start(s32[1,1,1,8,32]{4,3,2,1,0:T(8,128)} %param.15) | copy-start | bytes 3076
  14.1 9.9 %copy-start.4 = (bf16[2,256,128]{2,1,0:T(8,128)(2,1)S(1)}, bf16[2,256,128]{2,1,0:T(8,128)(2,1)}, u32[]{:S(2)}) copy-start(bf16[2,256,128]{2,1,0:T(8,128)(2,1)} %param.19) | copy-start | bytes 393220
  14.1 9.9 %copy-start.5 = (bf16[2,256,128]{2,1,0:T(8,128)(2,1)S(1)}, bf16[2,256,128]{2,1,0:T(8,128)(2,1)}, u32[]{:S(2)}) copy-start(bf16[2,256,128]{2,1,0:T(8,128)(2,1)} %param.16) | copy-start | bytes 393220
  14.2 7.6 %collective-permute-start.2 = (bf16[3,3,128,128]{3,2,0,1:T(8,128)(2,1)S(1)}, bf16[3,3,128,128]{3,2,0,1:T(8,128)(2,1)S(1)}, u32[]{:S(2)}, u32[]{:S(2)}) collective-permute-start(bf16[3,3,128,128]{3,2,0,1:T(8,128)(2,1)S(1)} %get-tuple-element.52), channel_id=1, source_target_pairs={{0,8},{8,16},{16,24},{24,0},{1,9},{9,17},{17,25},{25,1},{2,10},{10... | collective-permute-start | bytes 884744 | tf_op jit(solution)/shard_map/ppermute | solution.py:516
  15.9 7.3 %collective-permute-start.3 = (bf16[3,3,128,128]{3,2,0,1:T(8,128)(2,1)S(1)}, bf16[3,3,128,128]{3,2,0,1:T(8,128)(2,1)S(1)}, u32[]{:S(2)}, u32[]{:S(2)}) collective-permute-start(bf16[3,3,128,128]{3,2,0,1:T(8,128)(2,1)S(1)} %get-tuple-element.53), channel_id=1, source_target_pairs={{8,0},{16,8},{24,16},{0,24},{9,1},{17,9},{25,17},{1,25},{10,2},{18... | collective-permute-start | bytes 884744 | tf_op jit(solution)/shard_map/ppermute | solution.py:516
  23.2 20.5 %copy-start.7 = (bf16[2,128,128]{2,1,0:T(8,128)(2,1)S(1)}, bf16[2,128,128]{2,1,0:T(8,128)(2,1)}, u32[]{:S(2)}) copy-start(bf16[2,128,128]{2,1,0:T(8,128)(2,1)} %param.18) | copy-start | bytes 196612
  23.3 21.4 %copy-start = (s32[1,1,1,3456,24]{3,4,2,1,0:T(8,128)S(1)}, s32[1,1,1,3456,24]{3,4,2,1,0:T(8,128)}, u32[]{:S(2)}) copy-start(s32[1,1,1,3456,24]{3,4,2,1,0:T(8,128)} %param.13) | copy-start | bytes 995332
  23.3 21.4 %copy-start.1 = (s32[1,1,1,3456,24]{3,4,2,1,0:T(8,128)S(1)}, s32[1,1,1,3456,24]{3,4,2,1,0:T(8,128)}, u32[]{:S(2)}) copy-start(s32[1,1,1,3456,24]{3,4,2,1,0:T(8,128)} %param.14) | copy-start | bytes 995332
  23.4 4.3 %collective-permute-start.5 = (bf16[3,3,128,128]{3,2,1,0:T(8,128)(2,1)S(1)}, bf16[3,3,128,128]{3,2,1,0:T(8,128)(2,1)S(1)}, u32[]{:S(2)}, u32[]{:S(2)}) collective-permute-start(bf16[3,3,128,128]{3,2,1,0:T(8,128)(2,1)S(1)} %get-tuple-element.49), channel_id=1, source_target_pairs={{1,0},{2,1},{3,2},{4,3},{5,4},{6,5},{7,6},{0,7},{9,8},{10,9},{11,1... | collective-permute-start | bytes 884744 | tf_op jit(solution)/shard_map/ppermute | solution.py:516
  23.4 6.2 %collective-permute-start.4 = (bf16[3,3,128,128]{3,2,1,0:T(8,128)(2,1)S(1)}, bf16[3,3,128,128]{3,2,1,0:T(8,128)(2,1)S(1)}, u32[]{:S(2)}, u32[]{:S(2)}) collective-permute-start(bf16[3,3,128,128]{3,2,1,0:T(8,128)(2,1)S(1)} %get-tuple-element.50), channel_id=1, source_target_pairs={{0,1},{1,2},{2,3},{3,4},{4,5},{5,6},{6,7},{7,0},{8,9},{9,10},{10,1... | collective-permute-start | bytes 884744 | tf_op jit(solution)/shard_map/ppermute | solution.py:516
  30.9 4.0 %collective-permute-start.6 = (bf16[2,2,32,128]{3,2,1,0:T(8,128)(2,1)S(1)}, bf16[2,2,32,128]{3,2,1,0:T(8,128)(2,1)S(1)}, u32[]{:S(2)}, u32[]{:S(2)}) collective-permute-start(bf16[2,2,32,128]{3,2,1,0:T(8,128)(2,1)S(1)} %get-tuple-element.31), channel_id=1, source_target_pairs={{0,32},{32,64},{64,96},{96,0},{1,33},{33,65},{65,97},{97,1},{2,34}... | collective-permute-start | bytes 98312 | tf_op jit(solution)/shard_map/ppermute | solution.py:516
  32.2 3.9 %collective-permute-start.7 = (bf16[2,2,32,128]{3,2,1,0:T(8,128)(2,1)S(1)}, bf16[2,2,32,128]{3,2,1,0:T(8,128)(2,1)S(1)}, u32[]{:S(2)}, u32[]{:S(2)}) collective-permute-start(bf16[2,2,32,128]{3,2,1,0:T(8,128)(2,1)S(1)} %get-tuple-element.32), channel_id=1, source_target_pairs={{32,0},{64,32},{96,64},{0,96},{33,1},{65,33},{97,65},{1,97},{34,2}... | collective-permute-start | bytes 98312 | tf_op jit(solution)/shard_map/ppermute | solution.py:516
  36.1 4.3 %collective-permute-start.8 = (bf16[4,2,32,128]{3,2,1,0:T(8,128)(2,1)S(1)}, bf16[4,2,32,128]{3,2,1,0:T(8,128)(2,1)S(1)}, u32[]{:S(2)}, u32[]{:S(2)}) collective-permute-start(bf16[4,2,32,128]{3,2,1,0:T(8,128)(2,1)S(1)} %pad_maximum_fusion.6), channel_id=1, source_target_pairs={{0,8},{8,16},{16,24},{24,0},{1,9},{9,17},{17,25},{25,1},{2,10},{10... | collective-permute-start | bytes 196616 | tf_op jit(solution)/shard_map/ppermute | solution.py:516
  37.5 4.3 %collective-permute-start.9 = (bf16[4,2,32,128]{3,2,1,0:T(8,128)(2,1)S(1)}, bf16[4,2,32,128]{3,2,1,0:T(8,128)(2,1)S(1)}, u32[]{:S(2)}, u32[]{:S(2)}) collective-permute-start(bf16[4,2,32,128]{3,2,1,0:T(8,128)(2,1)S(1)} %pad_maximum_fusion.7), channel_id=1, source_target_pairs={{8,0},{16,8},{24,16},{0,24},{9,1},{17,9},{25,17},{1,25},{10,2},{18... | collective-permute-start | bytes 196616 | tf_op jit(solution)/shard_map/ppermute | solution.py:516
  41.9 4.4 %collective-permute-start.10 = (bf16[4,4,32,128]{3,2,1,0:T(8,128)(2,1)S(1)}, bf16[4,4,32,128]{3,2,1,0:T(8,128)(2,1)S(1)}, u32[]{:S(2)}, u32[]{:S(2)}) collective-permute-start(bf16[4,4,32,128]{3,2,1,0:T(8,128)(2,1)S(1)} %pad_maximum_fusion.2), channel_id=1, source_target_pairs={{0,1},{1,2},{2,3},{3,4},{4,5},{5,6},{6,7},{7,0},{8,9},{9,10},{10,1... | collective-permute-start | bytes 393224 | tf_op jit(solution)/shard_map/ppermute | solution.py:516
  42.0 4.3 %collective-permute-start.11 = (bf16[4,4,32,128]{3,2,1,0:T(8,128)(2,1)S(1)}, bf16[4,4,32,128]{3,2,1,0:T(8,128)(2,1)S(1)}, u32[]{:S(2)}, u32[]{:S(2)}) collective-permute-start(bf16[4,4,32,128]{3,2,1,0:T(8,128)(2,1)S(1)} %pad_maximum_fusion.3), channel_id=1, source_target_pairs={{1,0},{2,1},{3,2},{4,3},{5,4},{6,5},{7,6},{0,7},{9,8},{10,9},{11,1... | collective-permute-start | bytes 393224 | tf_op jit(solution)/shard_map/ppermute | solution.py:516
  78.5 4.0 %collective-permute-start.12 = (bf16[2,2,32,128]{3,2,1,0:T(8,128)(2,1)S(1)}, bf16[2,2,32,128]{3,2,1,0:T(8,128)(2,1)S(1)}, u32[]{:S(2)}, u32[]{:S(2)}) collective-permute-start(bf16[2,2,32,128]{3,2,1,0:T(8,128)(2,1)S(1)} %get-tuple-element.46), channel_id=1, source_target_pairs={{0,32},{32,64},{64,96},{96,0},{1,33},{33,65},{65,97},{97,1},{2,34}... | collective-permute-start | bytes 98312 | tf_op jit(solution)/shard_map/ppermute | solution.py:516
  79.2 3.9 %collective-permute-start.13 = (bf16[2,2,32,128]{3,2,1,0:T(8,128)(2,1)S(1)}, bf16[2,2,32,128]{3,2,1,0:T(8,128)(2,1)S(1)}, u32[]{:S(2)}, u32[]{:S(2)}) collective-permute-start(bf16[2,2,32,128]{3,2,1,0:T(8,128)(2,1)S(1)} %get-tuple-element.47), channel_id=1, source_target_pairs={{32,0},{64,32},{96,64},{0,96},{33,1},{65,33},{97,65},{1,97},{34,2}... | collective-permute-start | bytes 98312 | tf_op jit(solution)/shard_map/ppermute | solution.py:516
  83.2 4.3 %collective-permute-start.14 = (bf16[4,2,32,128]{3,2,1,0:T(8,128)(2,1)S(1)}, bf16[4,2,32,128]{3,2,1,0:T(8,128)(2,1)S(1)}, u32[]{:S(2)}, u32[]{:S(2)}) collective-permute-start(bf16[4,2,32,128]{3,2,1,0:T(8,128)(2,1)S(1)} %pad_maximum_fusion.8), channel_id=1, source_target_pairs={{0,8},{8,16},{16,24},{24,0},{1,9},{9,17},{17,25},{25,1},{2,10},{10... | collective-permute-start | bytes 196616 | tf_op jit(solution)/shard_map/ppermute | solution.py:516
  85.1 4.3 %collective-permute-start.15 = (bf16[4,2,32,128]{3,2,1,0:T(8,128)(2,1)S(1)}, bf16[4,2,32,128]{3,2,1,0:T(8,128)(2,1)S(1)}, u32[]{:S(2)}, u32[]{:S(2)}) collective-permute-start(bf16[4,2,32,128]{3,2,1,0:T(8,128)(2,1)S(1)} %pad_maximum_fusion.9), channel_id=1, source_target_pairs={{8,0},{16,8},{24,16},{0,24},{9,1},{17,9},{25,17},{1,25},{10,2},{18... | collective-permute-start | bytes 196616 | tf_op jit(solution)/shard_map/ppermute | solution.py:516
  89.6 4.4 %collective-permute-start.16 = (bf16[4,4,32,128]{3,2,1,0:T(8,128)(2,1)S(1)}, bf16[4,4,32,128]{3,2,1,0:T(8,128)(2,1)S(1)}, u32[]{:S(2)}, u32[]{:S(2)}) collective-permute-start(bf16[4,4,32,128]{3,2,1,0:T(8,128)(2,1)S(1)} %pad_maximum_fusion.4), channel_id=1, source_target_pairs={{0,1},{1,2},{2,3},{3,4},{4,5},{5,6},{6,7},{7,0},{8,9},{9,10},{10,1... | collective-permute-start | bytes 393224 | tf_op jit(solution)/shard_map/ppermute | solution.py:516
  89.7 4.3 %collective-permute-start.17 = (bf16[4,4,32,128]{3,2,1,0:T(8,128)(2,1)S(1)}, bf16[4,4,32,128]{3,2,1,0:T(8,128)(2,1)S(1)}, u32[]{:S(2)}, u32[]{:S(2)}) collective-permute-start(bf16[4,4,32,128]{3,2,1,0:T(8,128)(2,1)S(1)} %pad_maximum_fusion.5), channel_id=1, source_target_pairs={{1,0},{2,1},{3,2},{4,3},{5,4},{6,5},{7,6},{0,7},{9,8},{10,9},{11,1... | collective-permute-start | bytes 393224 | tf_op jit(solution)/shard_map/ppermute | solution.py:516

commit v12 on v11

--- a/solution.py
+++ b/solution.py
@@ -281,7 +281,7 @@
 FIRST = 12
 TAILS = (0, 1, 2, 3, 4, 6, 8, 12)
 DUMP = ROWS
-PARTS = ((0, 3), (3, 11), (11, CODES))
+PARTS = ((0, 1), (1, 8), (8, CODES))
 
 
 def project_kernel(state_ref, efirst_ref, table_ref, recv_ref):

time: 125 us -> 125 us (level)
  no operation moved by 1% of the time
where the time goes in v12:
time: 125 us
  Pallas kernels  70.8 us (57%)
  waiting for transfers between devices  34 us (27%)
  starting transfers between devices  17.2 us (14%)
  local copies, waits for them, and re-layouts  2.03 us (2%)
    pallas_call x2, Pallas kernels, one_layer(): pl.pallas_call(functools.partial(layer_kernel, final), out_shape=[jax.Sha...  61.5 us
    ppermute x18, waiting for transfers between devices, both_ways(): return (lax.ppermute(up, axis, forward), lax.ppermute(down, axis, backward))  34 us
    ppermute x18, starting transfers between devices, both_ways(): return (lax.ppermute(up, axis, forward), lax.ppermute(down, axis, backward))  17.2 us
  transfers between devices with their start and end apart: 18, of which 16 were waited for; matrix products, arithmetic and copies ran while one was open for 0% of the time, Pallas kernels for 3%

profile of v12, /device:TPU:106, one launch (start us, length us, event | category | flops | bytes accessed | tf_op | source)
XLA Modules:
  0.0 125.2 jit_solution(14951264871827025684)
XLA Ops:
  0.0 0.9 copy-done.2
  1.6 2.3 %pack.1 = (bf16[3,3,128,128]{3,2,1,0:T(8,128)(2,1)S(1)}, bf16[3,3,128,128]{3,2,1,0:T(8,128)(2,1)S(1)}, bf16[3,3,128,128]{3,2,1,0:T(8,128)(2,1)S(1)}) custom-call(s32[1,1024]{1,0:T(1,128)S(1)} %bitcast.224, bf16[1024,128]{1,0:T(8,128)(2,1)S(1)} %bitcast.223), custom_call_target="tpu_custom_call" | custom-call | tf_op jit(solution)/shard_map/pack/pallas_call | solution.py:83
  4.0 1.6 %collective-permute-start = (bf16[3,3,128,128]{3,2,1,0:T(8,128)(2,1)S(1)}, bf16[3,3,128,128]{3,2,1,0:T(8,128)(2,1)S(1)}, u32[]{:S(2)}, u32[]{:S(2)}) collective-permute-start(bf16[3,3,128,128]{3,2,1,0:T(8,128)(2,1)S(1)} %get-tuple-element.27), channel_id=1, source_target_pairs={{0,32},{32,64},{64,96},{96,0},{1,33},{33,65},{65,97},{97,1},{2,34}... | collective-permute-start | bytes 884744 | tf_op jit(solution)/shard_map/ppermute | solution.py:516
  6.0 6.7 %collective-permute-done = bf16[3,3,128,128]{3,2,1,0:T(8,128)(2,1)S(1)} collective-permute-done((bf16[3,3,128,128]{3,2,1,0:T(8,128)(2,1)S(1)}, bf16[3,3,128,128]{3,2,1,0:T(8,128)(2,1)S(1)}, u32[]{:S(2)}, u32[]{:S(2)}) %collective-permute-start) | collective-permute-done | bytes 294944 | tf_op jit(solution)/shard_map/ppermute | solution.py:516
  12.8 1.2 collective-permute-done.1
  14.2 1.6 %collective-permute-start.2 = (bf16[3,3,128,128]{3,2,0,1:T(8,128)(2,1)S(1)}, bf16[3,3,128,128]{3,2,0,1:T(8,128)(2,1)S(1)}, u32[]{:S(2)}, u32[]{:S(2)}) collective-permute-start(bf16[3,3,128,128]{3,2,0,1:T(8,128)(2,1)S(1)} %get-tuple-element.52), channel_id=1, source_target_pairs={{0,8},{8,16},{16,24},{24,0},{1,9},{9,17},{17,25},{25,1},{2,10},{10... | collective-permute-start | bytes 884744 | tf_op jit(solution)/shard_map/ppermute | solution.py:516
  16.3 5.5 %collective-permute-done.2 = bf16[3,3,128,128]{3,2,0,1:T(8,128)(2,1)S(1)} collective-permute-done((bf16[3,3,128,128]{3,2,0,1:T(8,128)(2,1)S(1)}, bf16[3,3,128,128]{3,2,0,1:T(8,128)(2,1)S(1)}, u32[]{:S(2)}, u32[]{:S(2)}) %collective-permute-start.2) | collective-permute-done | bytes 294944 | tf_op jit(solution)/shard_map/ppermute | solution.py:516
  21.8 1.3 %collective-permute-done.3 = bf16[3,3,128,128]{3,2,0,1:T(8,128)(2,1)S(1)} collective-permute-done((bf16[3,3,128,128]{3,2,0,1:T(8,128)(2,1)S(1)}, bf16[3,3,128,128]{3,2,0,1:T(8,128)(2,1)S(1)}, u32[]{:S(2)}, u32[]{:S(2)}) %collective-permute-start.3) | collective-permute-done | bytes 294944 | tf_op jit(solution)/shard_map/ppermute | solution.py:516
  24.0 3.6 %collective-permute-done.5.high_ref = bf16[3,3,128,128]{3,2,1,0:T(8,128)(2,1)S(1)} collective-permute-done((bf16[3,3,128,128]{3,2,1,0:T(8,128)(2,1)S(1)}, bf16[3,3,128,128]{3,2,1,0:T(8,128)(2,1)S(1)}, u32[]{:S(2)}, u32[]{:S(2)}) %collective-permute-start.5) | collective-permute-done | bytes 294944 | tf_op jit(solution)/shard_map/ppermute | solution.py:516
  27.6 1.9 %collective-permute-done.4.low_ref = bf16[3,3,128,128]{3,2,1,0:T(8,128)(2,1)S(1)} collective-permute-done((bf16[3,3,128,128]{3,2,1,0:T(8,128)(2,1)S(1)}, bf16[3,3,128,128]{3,2,1,0:T(8,128)(2,1)S(1)}, u32[]{:S(2)}, u32[]{:S(2)}) %collective-permute-start.4) | collective-permute-done | bytes 294944 | tf_op jit(solution)/shard_map/ppermute | solution.py:516
  29.5 1.3 %receive.1 = (bf16[3456,128]{1,0:T(8,128)(2,1)S(1)}, s32[32,128]{1,0:T(8,128)S(1)}, bf16[2,2,32,128]{3,2,1,0:T(8,128)(2,1)S(1)}, bf16[2,2,32,128]{3,2,1,0:T(8,128)(2,1)S(1)}) custom-call(s32[256]{0:T(256)S(1)} %reshape.12.gidx_ref, bf16[3,3,128,128]{3,2,1,0:T(8,128)(2,1)S(1)} %get-tuple-element.51.mid_ref, ...), custom_call_target="tpu_custom_call" | custom-call | tf_op jit(solution)/shard_map/receive/pallas_call | solution.py:137
  30.9 1.3 %collective-permute-start.6 = (bf16[2,2,32,128]{3,2,1,0:T(8,128)(2,1)S(1)}, bf16[2,2,32,128]{3,2,1,0:T(8,128)(2,1)S(1)}, u32[]{:S(2)}, u32[]{:S(2)}) collective-permute-start(bf16[2,2,32,128]{3,2,1,0:T(8,128)(2,1)S(1)} %get-tuple-element.31), channel_id=1, source_target_pairs={{0,32},{32,64},{64,96},{96,0},{1,33},{33,65},{65,97},{97,1},{2,34}... | collective-permute-start | bytes 98312 | tf_op jit(solution)/shard_map/ppermute | solution.py:516
  32.2 0.8 collective-permute-start.7
  33.0 1.9 %collective-permute-done.6.refs_0_ = bf16[2,2,32,128]{3,2,1,0:T(8,128)(2,1)S(1)} collective-permute-done((bf16[2,2,32,128]{3,2,1,0:T(8,128)(2,1)S(1)}, bf16[2,2,32,128]{3,2,1,0:T(8,128)(2,1)S(1)}, u32[]{:S(2)}, u32[]{:S(2)}) %collective-permute-start.6) | collective-permute-done | bytes 32800 | tf_op jit(solution)/shard_map/ppermute | solution.py:516
  34.9 1.2 collective-permute-done.7.refs_1_
  36.1 1.4 %collective-permute-start.8 = (bf16[4,2,32,128]{3,2,1,0:T(8,128)(2,1)S(1)}, bf16[4,2,32,128]{3,2,1,0:T(8,128)(2,1)S(1)}, u32[]{:S(2)}, u32[]{:S(2)}) collective-permute-start(bf16[4,2,32,128]{3,2,1,0:T(8,128)(2,1)S(1)} %pad_maximum_fusion.6), channel_id=1, source_target_pairs={{0,8},{8,16},{16,24},{24,0},{1,9},{9,17},{17,25},{25,1},{2,10},{10... | collective-permute-start | bytes 196616 | tf_op jit(solution)/shard_map/ppermute | solution.py:516
  38.3 2.1 %collective-permute-done.8.refs_2_ = bf16[4,2,32,128]{3,2,1,0:T(8,128)(2,1)S(1)} collective-permute-done((bf16[4,2,32,128]{3,2,1,0:T(8,128)(2,1)S(1)}, bf16[4,2,32,128]{3,2,1,0:T(8,128)(2,1)S(1)}, u32[]{:S(2)}, u32[]{:S(2)}) %collective-permute-start.8) | collective-permute-done | bytes 65568 | tf_op jit(solution)/shard_map/ppermute | solution.py:516
  40.4 1.4 %collective-permute-done.9.refs_3_ = bf16[4,2,32,128]{3,2,1,0:T(8,128)(2,1)S(1)} collective-permute-done((bf16[4,2,32,128]{3,2,1,0:T(8,128)(2,1)S(1)}, bf16[4,2,32,128]{3,2,1,0:T(8,128)(2,1)S(1)}, u32[]{:S(2)}, u32[]{:S(2)}) %collective-permute-start.9) | collective-permute-done | bytes 65568 | tf_op jit(solution)/shard_map/ppermute | solution.py:516
  42.0 1.7 %collective-permute-start.11 = (bf16[4,4,32,128]{3,2,1,0:T(8,128)(2,1)S(1)}, bf16[4,4,32,128]{3,2,1,0:T(8,128)(2,1)S(1)}, u32[]{:S(2)}, u32[]{:S(2)}) collective-permute-start(bf16[4,4,32,128]{3,2,1,0:T(8,128)(2,1)S(1)} %pad_maximum_fusion.3), channel_id=1, source_target_pairs={{1,0},{2,1},{3,2},{4,3},{5,4},{6,5},{7,6},{0,7},{9,8},{10,9},{11,1... | collective-permute-start | bytes 393224 | tf_op jit(solution)/shard_map/ppermute | solution.py:516
  43.8 0.9 project.2
  45.0 0.9 lone.2
  46.3 1.7 %indices.1 = (s32[768,128]{1,0:T(8,128)S(1)}, s32[32,128]{1,0:T(8,128)S(1)}, bf16[3456,128]{1,0:T(8,128)(2,1)S(1)}) custom-call(s32[3]{0:T(128)S(1)} %pad_add_fusion.pos_ref, s32[768,128]{1,0:T(8,128)S(1)} %near_nodes.1.held, bf16[2,2,32,128]{3,2,1,0:T(8,128)(2,1)S(1)} %collective-permute-done.6.refs_0_, ...), custom_call_target="tpu_custom_call" | custom-call | tf_op jit(solution)/shard_map/indices/pallas_call | solution.py:264
  48.0 30.5 %layer.2 = (f32[5256,128]{1,0:T(8,128)S(1)}, bf16[3456,128]{1,0:T(8,128)(2,1)S(1)}, bf16[2,2,32,128]{3,2,1,0:T(8,128)(2,1)S(1)}, bf16[2,2,32,128]{3,2,1,0:T(8,128)(2,1)S(1)}) custom-call(s32[98304]{0:T(1024)S(1)} %bitcast.218, s32[3]{0:T(128)S(1)} %pad_add_fusion.pos_ref, ...), custom_call_target="tpu_custom_call", output_to_operand_aliasing={{0}: (5, {})} | custom-call | tf_op jit(solution)/shard_map/layer/pallas_call | solution.py:487
  78.6 2.6 %collective-permute-start.12 = (bf16[2,2,32,128]{3,2,1,0:T(8,128)(2,1)S(1)}, bf16[2,2,32,128]{3,2,1,0:T(8,128)(2,1)S(1)}, u32[]{:S(2)}, u32[]{:S(2)}) collective-permute-start(bf16[2,2,32,128]{3,2,1,0:T(8,128)(2,1)S(1)} %get-tuple-element.46), channel_id=1, source_target_pairs={{0,32},{32,64},{64,96},{96,0},{1,33},{33,65},{65,97},{97,1},{2,34}... | collective-permute-start | bytes 98312 | tf_op jit(solution)/shard_map/ppermute | solution.py:516
  81.2 1.6 %collective-permute-done.12.refs_0_ = bf16[2,2,32,128]{3,2,1,0:T(8,128)(2,1)S(1)} collective-permute-done((bf16[2,2,32,128]{3,2,1,0:T(8,128)(2,1)S(1)}, bf16[2,2,32,128]{3,2,1,0:T(8,128)(2,1)S(1)}, u32[]{:S(2)}, u32[]{:S(2)}) %collective-permute-start.12) | collective-permute-done | bytes 32800 | tf_op jit(solution)/shard_map/ppermute | solution.py:516
  82.8 2.3 %collective-permute-done.13.refs_1_ = bf16[2,2,32,128]{3,2,1,0:T(8,128)(2,1)S(1)} collective-permute-done((bf16[2,2,32,128]{3,2,1,0:T(8,128)(2,1)S(1)}, bf16[2,2,32,128]{3,2,1,0:T(8,128)(2,1)S(1)}, u32[]{:S(2)}, u32[]{:S(2)}) %collective-permute-start.13) | collective-permute-done | bytes 32800 | tf_op jit(solution)/shard_map/ppermute | solution.py:516
  85.2 2.1 %collective-permute-start.15 = (bf16[4,2,32,128]{3,2,1,0:T(8,128)(2,1)S(1)}, bf16[4,2,32,128]{3,2,1,0:T(8,128)(2,1)S(1)}, u32[]{:S(2)}, u32[]{:S(2)}) collective-permute-start(bf16[4,2,32,128]{3,2,1,0:T(8,128)(2,1)S(1)} %pad_maximum_fusion.9), channel_id=1, source_target_pairs={{8,0},{16,8},{24,16},{0,24},{9,1},{17,9},{25,17},{1,25},{10,2},{18... | collective-permute-start | bytes 196616 | tf_op jit(solution)/shard_map/ppermute | solution.py:516
  87.3 2.1 %collective-permute-done.14.refs_2_ = bf16[4,2,32,128]{3,2,1,0:T(8,128)(2,1)S(1)} collective-permute-done((bf16[4,2,32,128]{3,2,1,0:T(8,128)(2,1)S(1)}, bf16[4,2,32,128]{3,2,1,0:T(8,128)(2,1)S(1)}, u32[]{:S(2)}, u32[]{:S(2)}) %collective-permute-start.14) | collective-permute-done | bytes 65568 | tf_op jit(solution)/shard_map/ppermute | solution.py:516
  89.8 1.7 %collective-permute-start.17 = (bf16[4,4,32,128]{3,2,1,0:T(8,128)(2,1)S(1)}, bf16[4,4,32,128]{3,2,1,0:T(8,128)(2,1)S(1)}, u32[]{:S(2)}, u32[]{:S(2)}) collective-permute-start(bf16[4,4,32,128]{3,2,1,0:T(8,128)(2,1)S(1)} %pad_maximum_fusion.5), channel_id=1, source_target_pairs={{1,0},{2,1},{3,2},{4,3},{5,4},{6,5},{7,6},{0,7},{9,8},{10,9},{11,1... | collective-permute-start | bytes 393224 | tf_op jit(solution)/shard_map/ppermute | solution.py:516
  91.5 0.9 project.3
  92.4 0.9 lone.3
  94.0 31.0 %layer.3 = (f32[5256,128]{1,0:T(8,128)S(1)}, bf16[3456,128]{1,0:T(8,128)(2,1)}) custom-call(s32[98304]{0:T(1024)S(1)} %bitcast.219, s32[3]{0:T(128)S(1)} %pad_add_fusion.pos_ref, s32[32,128]{1,0:T(8,128)S(1)} %get-tuple-element.34.steps_ref, s32[32,128]{1,0:T(8,128)S(1)} %get-tuple-element.30.cnt_ref, ...), custom_call_target="tpu_custom_call", output_to_operand_aliasing={{0}: (5, {})} | custom-call | tf_op jit(solution)/shard_map/layer/pallas_call | solution.py:487
  (88 shorter events, 5.5 us)
Async XLA Ops:
  0.0 0.9 copy-start.2
  1.0 0.7 copy-start.3
  1.6 14.7 %copy-start.8 = (bf16[2,128,128]{2,1,0:T(8,128)(2,1)S(1)}, bf16[2,128,128]{2,1,0:T(8,128)(2,1)}, u32[]{:S(2)}) copy-start(bf16[2,128,128]{2,1,0:T(8,128)(2,1)} %param.21) | copy-start | bytes 196612
  1.6 14.7 %copy-start.9 = (bf16[2,128,128]{2,1,0:T(8,128)(2,1)S(1)}, bf16[2,128,128]{2,1,0:T(8,128)(2,1)}, u32[]{:S(2)}) copy-start(bf16[2,128,128]{2,1,0:T(8,128)(2,1)} %param.20) | copy-start | bytes 196612
  4.0 8.8 %collective-permute-start = (bf16[3,3,128,128]{3,2,1,0:T(8,128)(2,1)S(1)}, bf16[3,3,128,128]{3,2,1,0:T(8,128)(2,1)S(1)}, u32[]{:S(2)}, u32[]{:S(2)}) collective-permute-start(bf16[3,3,128,128]{3,2,1,0:T(8,128)(2,1)S(1)} %get-tuple-element.27), channel_id=1, source_target_pairs={{0,32},{32,64},{64,96},{96,0},{1,33},{33,65},{65,97},{97,1},{2,34}... | collective-permute-start | bytes 884744 | tf_op jit(solution)/shard_map/ppermute | solution.py:516
  5.5 8.5 %collective-permute-start.1 = (bf16[3,3,128,128]{3,2,1,0:T(8,128)(2,1)S(1)}, bf16[3,3,128,128]{3,2,1,0:T(8,128)(2,1)S(1)}, u32[]{:S(2)}, u32[]{:S(2)}) collective-permute-start(bf16[3,3,128,128]{3,2,1,0:T(8,128)(2,1)S(1)} %get-tuple-element.29), channel_id=1, source_target_pairs={{32,0},{64,32},{96,64},{0,96},{33,1},{65,33},{97,65},{1,97},{34,2}... | collective-permute-start | bytes 884744 | tf_op jit(solution)/shard_map/ppermute | solution.py:516
  14.1 9.8 %copy-start.6 = (bf16[2,128,128]{2,1,0:T(8,128)(2,1)S(1)}, bf16[2,128,128]{2,1,0:T(8,128)(2,1)}, u32[]{:S(2)}) copy-start(bf16[2,128,128]{2,1,0:T(8,128)(2,1)} %param.17) | copy-start | bytes 196612
  14.1 9.8 %copy-start.10 = (s32[1,1,1,8,32]{4,3,2,1,0:T(8,128)S(1)}, s32[1,1,1,8,32]{4,3,2,1,0:T(8,128)}, u32[]{:S(2)}) copy-start(s32[1,1,1,8,32]{4,3,2,1,0:T(8,128)} %param.15) | copy-start | bytes 3076
  14.1 9.9 %copy-start.4 = (bf16[2,256,128]{2,1,0:T(8,128)(2,1)S(1)}, bf16[2,256,128]{2,1,0:T(8,128)(2,1)}, u32[]{:S(2)}) copy-start(bf16[2,256,128]{2,1,0:T(8,128)(2,1)} %param.19) | copy-start | bytes 393220
  14.1 9.9 %copy-start.5 = (bf16[2,256,128]{2,1,0:T(8,128)(2,1)S(1)}, bf16[2,256,128]{2,1,0:T(8,128)(2,1)}, u32[]{:S(2)}) copy-start(bf16[2,256,128]{2,1,0:T(8,128)(2,1)} %param.16) | copy-start | bytes 393220
  14.2 7.6 %collective-permute-start.2 = (bf16[3,3,128,128]{3,2,0,1:T(8,128)(2,1)S(1)}, bf16[3,3,128,128]{3,2,0,1:T(8,128)(2,1)S(1)}, u32[]{:S(2)}, u32[]{:S(2)}) collective-permute-start(bf16[3,3,128,128]{3,2,0,1:T(8,128)(2,1)S(1)} %get-tuple-element.52), channel_id=1, source_target_pairs={{0,8},{8,16},{16,24},{24,0},{1,9},{9,17},{17,25},{25,1},{2,10},{10... | collective-permute-start | bytes 884744 | tf_op jit(solution)/shard_map/ppermute | solution.py:516
  15.9 7.3 %collective-permute-start.3 = (bf16[3,3,128,128]{3,2,0,1:T(8,128)(2,1)S(1)}, bf16[3,3,128,128]{3,2,0,1:T(8,128)(2,1)S(1)}, u32[]{:S(2)}, u32[]{:S(2)}) collective-permute-start(bf16[3,3,128,128]{3,2,0,1:T(8,128)(2,1)S(1)} %get-tuple-element.53), channel_id=1, source_target_pairs={{8,0},{16,8},{24,16},{0,24},{9,1},{17,9},{25,17},{1,25},{10,2},{18... | collective-permute-start | bytes 884744 | tf_op jit(solution)/shard_map/ppermute | solution.py:516
  23.2 20.5 %copy-start.7 = (bf16[2,128,128]{2,1,0:T(8,128)(2,1)S(1)}, bf16[2,128,128]{2,1,0:T(8,128)(2,1)}, u32[]{:S(2)}) copy-start(bf16[2,128,128]{2,1,0:T(8,128)(2,1)} %param.18) | copy-start | bytes 196612
  23.3 21.4 %copy-start = (s32[1,1,1,3456,24]{3,4,2,1,0:T(8,128)S(1)}, s32[1,1,1,3456,24]{3,4,2,1,0:T(8,128)}, u32[]{:S(2)}) copy-start(s32[1,1,1,3456,24]{3,4,2,1,0:T(8,128)} %param.13) | copy-start | bytes 995332
  23.3 21.4 %copy-start.1 = (s32[1,1,1,3456,24]{3,4,2,1,0:T(8,128)S(1)}, s32[1,1,1,3456,24]{3,4,2,1,0:T(8,128)}, u32[]{:S(2)}) copy-start(s32[1,1,1,3456,24]{3,4,2,1,0:T(8,128)} %param.14) | copy-start | bytes 995332
  23.4 4.3 %collective-permute-start.5 = (bf16[3,3,128,128]{3,2,1,0:T(8,128)(2,1)S(1)}, bf16[3,3,128,128]{3,2,1,0:T(8,128)(2,1)S(1)}, u32[]{:S(2)}, u32[]{:S(2)}) collective-permute-start(bf16[3,3,128,128]{3,2,1,0:T(8,128)(2,1)S(1)} %get-tuple-element.49), channel_id=1, source_target_pairs={{1,0},{2,1},{3,2},{4,3},{5,4},{6,5},{7,6},{0,7},{9,8},{10,9},{11,1... | collective-permute-start | bytes 884744 | tf_op jit(solution)/shard_map/ppermute | solution.py:516
  23.4 6.2 %collective-permute-start.4 = (bf16[3,3,128,128]{3,2,1,0:T(8,128)(2,1)S(1)}, bf16[3,3,128,128]{3,2,1,0:T(8,128)(2,1)S(1)}, u32[]{:S(2)}, u32[]{:S(2)}) collective-permute-start(bf16[3,3,128,128]{3,2,1,0:T(8,128)(2,1)S(1)} %get-tuple-element.50), channel_id=1, source_target_pairs={{0,1},{1,2},{2,3},{3,4},{4,5},{5,6},{6,7},{7,0},{8,9},{9,10},{10,1... | collective-permute-start | bytes 884744 | tf_op jit(solution)/shard_map/ppermute | solution.py:516
  30.9 4.0 %collective-permute-start.6 = (bf16[2,2,32,128]{3,2,1,0:T(8,128)(2,1)S(1)}, bf16[2,2,32,128]{3,2,1,0:T(8,128)(2,1)S(1)}, u32[]{:S(2)}, u32[]{:S(2)}) collective-permute-start(bf16[2,2,32,128]{3,2,1,0:T(8,128)(2,1)S(1)} %get-tuple-element.31), channel_id=1, source_target_pairs={{0,32},{32,64},{64,96},{96,0},{1,33},{33,65},{65,97},{97,1},{2,34}... | collective-permute-start | bytes 98312 | tf_op jit(solution)/shard_map/ppermute | solution.py:516
  32.2 3.9 %collective-permute-start.7 = (bf16[2,2,32,128]{3,2,1,0:T(8,128)(2,1)S(1)}, bf16[2,2,32,128]{3,2,1,0:T(8,128)(2,1)S(1)}, u32[]{:S(2)}, u32[]{:S(2)}) collective-permute-start(bf16[2,2,32,128]{3,2,1,0:T(8,128)(2,1)S(1)} %get-tuple-element.32), channel_id=1, source_target_pairs={{32,0},{64,32},{96,64},{0,96},{33,1},{65,33},{97,65},{1,97},{34,2}... | collective-permute-start | bytes 98312 | tf_op jit(solution)/shard_map/ppermute | solution.py:516
  36.1 4.3 %collective-permute-start.8 = (bf16[4,2,32,128]{3,2,1,0:T(8,128)(2,1)S(1)}, bf16[4,2,32,128]{3,2,1,0:T(8,128)(2,1)S(1)}, u32[]{:S(2)}, u32[]{:S(2)}) collective-permute-start(bf16[4,2,32,128]{3,2,1,0:T(8,128)(2,1)S(1)} %pad_maximum_fusion.6), channel_id=1, source_target_pairs={{0,8},{8,16},{16,24},{24,0},{1,9},{9,17},{17,25},{25,1},{2,10},{10... | collective-permute-start | bytes 196616 | tf_op jit(solution)/shard_map/ppermute | solution.py:516
  37.5 4.3 %collective-permute-start.9 = (bf16[4,2,32,128]{3,2,1,0:T(8,128)(2,1)S(1)}, bf16[4,2,32,128]{3,2,1,0:T(8,128)(2,1)S(1)}, u32[]{:S(2)}, u32[]{:S(2)}) collective-permute-start(bf16[4,2,32,128]{3,2,1,0:T(8,128)(2,1)S(1)} %pad_maximum_fusion.7), channel_id=1, source_target_pairs={{8,0},{16,8},{24,16},{0,24},{9,1},{17,9},{25,17},{1,25},{10,2},{18... | collective-permute-start | bytes 196616 | tf_op jit(solution)/shard_map/ppermute | solution.py:516
  41.9 4.4 %collective-permute-start.10 = (bf16[4,4,32,128]{3,2,1,0:T(8,128)(2,1)S(1)}, bf16[4,4,32,128]{3,2,1,0:T(8,128)(2,1)S(1)}, u32[]{:S(2)}, u32[]{:S(2)}) collective-permute-start(bf16[4,4,32,128]{3,2,1,0:T(8,128)(2,1)S(1)} %pad_maximum_fusion.2), channel_id=1, source_target_pairs={{0,1},{1,2},{2,3},{3,4},{4,5},{5,6},{6,7},{7,0},{8,9},{9,10},{10,1... | collective-permute-start | bytes 393224 | tf_op jit(solution)/shard_map/ppermute | solution.py:516
  42.0 4.3 %collective-permute-start.11 = (bf16[4,4,32,128]{3,2,1,0:T(8,128)(2,1)S(1)}, bf16[4,4,32,128]{3,2,1,0:T(8,128)(2,1)S(1)}, u32[]{:S(2)}, u32[]{:S(2)}) collective-permute-start(bf16[4,4,32,128]{3,2,1,0:T(8,128)(2,1)S(1)} %pad_maximum_fusion.3), channel_id=1, source_target_pairs={{1,0},{2,1},{3,2},{4,3},{5,4},{6,5},{7,6},{0,7},{9,8},{10,9},{11,1... | collective-permute-start | bytes 393224 | tf_op jit(solution)/shard_map/ppermute | solution.py:516
  78.6 4.2 %collective-permute-start.12 = (bf16[2,2,32,128]{3,2,1,0:T(8,128)(2,1)S(1)}, bf16[2,2,32,128]{3,2,1,0:T(8,128)(2,1)S(1)}, u32[]{:S(2)}, u32[]{:S(2)}) collective-permute-start(bf16[2,2,32,128]{3,2,1,0:T(8,128)(2,1)S(1)} %get-tuple-element.46), channel_id=1, source_target_pairs={{0,32},{32,64},{64,96},{96,0},{1,33},{33,65},{65,97},{97,1},{2,34}... | collective-permute-start | bytes 98312 | tf_op jit(solution)/shard_map/ppermute | solution.py:516
  81.2 3.9 %collective-permute-start.13 = (bf16[2,2,32,128]{3,2,1,0:T(8,128)(2,1)S(1)}, bf16[2,2,32,128]{3,2,1,0:T(8,128)(2,1)S(1)}, u32[]{:S(2)}, u32[]{:S(2)}) collective-permute-start(bf16[2,2,32,128]{3,2,1,0:T(8,128)(2,1)S(1)} %get-tuple-element.47), channel_id=1, source_target_pairs={{32,0},{64,32},{96,64},{0,96},{33,1},{65,33},{97,65},{1,97},{34,2}... | collective-permute-start | bytes 98312 | tf_op jit(solution)/shard_map/ppermute | solution.py:516
  85.1 4.3 %collective-permute-start.14 = (bf16[4,2,32,128]{3,2,1,0:T(8,128)(2,1)S(1)}, bf16[4,2,32,128]{3,2,1,0:T(8,128)(2,1)S(1)}, u32[]{:S(2)}, u32[]{:S(2)}) collective-permute-start(bf16[4,2,32,128]{3,2,1,0:T(8,128)(2,1)S(1)} %pad_maximum_fusion.8), channel_id=1, source_target_pairs={{0,8},{8,16},{16,24},{24,0},{1,9},{9,17},{17,25},{25,1},{2,10},{10... | collective-permute-start | bytes 196616 | tf_op jit(solution)/shard_map/ppermute | solution.py:516
  85.2 4.3 %collective-permute-start.15 = (bf16[4,2,32,128]{3,2,1,0:T(8,128)(2,1)S(1)}, bf16[4,2,32,128]{3,2,1,0:T(8,128)(2,1)S(1)}, u32[]{:S(2)}, u32[]{:S(2)}) collective-permute-start(bf16[4,2,32,128]{3,2,1,0:T(8,128)(2,1)S(1)} %pad_maximum_fusion.9), channel_id=1, source_target_pairs={{8,0},{16,8},{24,16},{0,24},{9,1},{17,9},{25,17},{1,25},{10,2},{18... | collective-permute-start | bytes 196616 | tf_op jit(solution)/shard_map/ppermute | solution.py:516
  89.6 4.4 %collective-permute-start.16 = (bf16[4,4,32,128]{3,2,1,0:T(8,128)(2,1)S(1)}, bf16[4,4,32,128]{3,2,1,0:T(8,128)(2,1)S(1)}, u32[]{:S(2)}, u32[]{:S(2)}) collective-permute-start(bf16[4,4,32,128]{3,2,1,0:T(8,128)(2,1)S(1)} %pad_maximum_fusion.4), channel_id=1, source_target_pairs={{0,1},{1,2},{2,3},{3,4},{4,5},{5,6},{6,7},{7,0},{8,9},{9,10},{10,1... | collective-permute-start | bytes 393224 | tf_op jit(solution)/shard_map/ppermute | solution.py:516
  89.8 4.3 %collective-permute-start.17 = (bf16[4,4,32,128]{3,2,1,0:T(8,128)(2,1)S(1)}, bf16[4,4,32,128]{3,2,1,0:T(8,128)(2,1)S(1)}, u32[]{:S(2)}, u32[]{:S(2)}) collective-permute-start(bf16[4,4,32,128]{3,2,1,0:T(8,128)(2,1)S(1)} %pad_maximum_fusion.5), channel_id=1, source_target_pairs={{1,0},{2,1},{3,2},{4,3},{5,4},{6,5},{7,6},{0,7},{9,8},{10,9},{11,1... | collective-permute-start | bytes 393224 | tf_op jit(solution)/shard_map/ppermute | solution.py:516
